TPU v7x, 32 devices: a whole 2x2x4 slice. The times are simulated.
32 devices in a mesh: groups: 2 (over y), blk: 4 (over z), heads: 2 (over x), rows: 2 (over core).
Axes of the slice: x: 2, y: 2, z: 4, core: 2. Of those that a mesh axis runs over, the one named last changes fastest.
Arguments:
- queries: bfloat16 [64, 16, 256], P(('groups', 'blk', 'rows'), 'heads'), parts along dimension 0, may hold values from -128 to 128
- src_keys: bfloat16 [12288, 8, 256], P(('groups', 'blk'), 'heads'), parts along dimension 0, may hold values from -6 to 6
- src_values: bfloat16 [12288, 8, 256], P(('groups', 'blk'), 'heads'), parts along dimension 0, may hold values from -6 to 6
- dec_state: bfloat16 [64, 3584], P('groups', ('blk', 'rows')), parts along dimension 0, may hold values from -0.59765625 to 0.59765625
- mask_embed: bfloat16 [3584], P(('blk', 'rows')), may hold values from -1.796875 to 1.796875
- out_weight: bfloat16 [4096, 3584], P('heads', ('blk', 'rows')), may hold values from -0.09375 to 0.09375
- norm_gain: bfloat16 [3584], P(('blk', 'rows')), may hold values from 0.5 to 1.5
- gate_weight: bfloat16 [3584, 14336], P('heads', ('blk', 'rows')), may hold values from -0.09375 to 0.09375
- up_weight: bfloat16 [3584, 14336], P('heads', ('blk', 'rows')), may hold values from -0.09375 to 0.09375
- down_weight: bfloat16 [14336, 3584], P(('blk', 'rows'), 'heads'), may hold values from -0.046875 to 0.046875
- cand_lengths: int32 [2], P('groups'), parts along dimension 0, may hold values from 64 to 128
- masked_pos: int32 [2, 48], P('groups'), parts along dimension 0, may hold values from 0 to 127, as said below
Outputs:
- stream: bfloat16 [64, 3584], P('groups', ('blk', 'rows')), parts along dimension 0
- branch: bfloat16 [64, 3584], P(('groups', 'blk', 'rows'), 'heads'), parts along dimension 0
There are 2 independent parts, one for each index of `groups`. A program takes and returns all parts, laid end to end along the dimension named above; an argument that names none is the same for every part. Nothing has to cross between parts.
Inputs may be any that keep to these rules, and one draw needn't show every extreme that they name: `masked_pos`: the 48 positions of one candidate are distinct.
All inputs are finite; a program needn't handle non-finite values.
Results may differ from a plain program's by a relative error of at most 0.03.
Values may be sent and summed in bfloat16 or wider, within the bound.
No kernel may reach another device: no remote copies, remote signals or barrier semaphores. Data moves between devices by JAX's collectives and lax.ppermute only.
A program may use at most 64 MiB of HBM per device.

v0:
```python
import jax
import jax.numpy as jnp
from jax import lax
from jax.sharding import PartitionSpec as P

D = 3584
LEN = 128


def token_masks(cand_lengths, masked_pos, tokens):
    positions = jnp.arange(tokens, dtype=jnp.int32) % LEN
    length_tok = jnp.repeat(cand_lengths, LEN)[:tokens]
    valid_tok = positions < length_tok
    slots = jnp.arange(LEN, dtype=jnp.int32)
    masked_tok = jnp.any(masked_pos[:, :, None] == slots[None, None, :], axis=1).reshape(-1)[
        :tokens
    ]
    return (valid_tok, masked_tok)


def shards(
    queries,
    src_keys,
    src_values,
    dec_state,
    mask_embed,
    out_weight,
    norm_gain,
    gate_weight,
    up_weight,
    down_weight,
    cand_lengths,
    masked_pos,
):
    tok_dev, local_heads, head_size = queries.shape
    kv_local = src_keys.shape[1]
    group_size = local_heads // kv_local
    score_scale = head_size ** (-0.5)
    queries_all = lax.all_gather(queries, "blk", axis=0, tiled=True)
    gathered_rows = queries_all.shape[0]
    grouped = queries_all.reshape(gathered_rows, kv_local, group_size, head_size)
    scores = (
        jnp.einsum("tgjd,kgd->tgjk", grouped, src_keys, preferred_element_type=jnp.float32)
        * score_scale
    )
    local_peak = jnp.max(scores, axis=3)
    weights = jnp.exp(scores - local_peak[..., None])
    totals = jnp.sum(weights, axis=3)
    numerator = jnp.einsum(
        "tgjk,kgd->tgjd",
        weights.astype(jnp.bfloat16),
        src_values,
        preferred_element_type=jnp.float32,
    )
    highest = lax.pmax(local_peak, "blk")
    factor = jnp.exp(local_peak - highest)
    numer_own, totals_own = (
        lax.psum_scatter(
            (numerator * factor[..., None]).astype(jnp.bfloat16),
            "blk",
            scatter_dimension=0,
            tiled=True,
        ).astype(jnp.float32),
        lax.psum_scatter(
            (totals * factor).astype(jnp.bfloat16), "blk", scatter_dimension=0, tiled=True
        ).astype(jnp.float32),
    )
    attn_own = (
        (numer_own / totals_own[..., None])
        .astype(jnp.bfloat16)
        .reshape(tok_dev, local_heads * head_size)
    )
    attn_all = lax.all_gather(attn_own, ("blk", "rows"), axis=0, tiled=True)
    tokens = attn_all.shape[0]
    projected = lax.psum(
        jnp.dot(attn_all, out_weight, preferred_element_type=jnp.float32).astype(jnp.bfloat16),
        "heads",
    ).astype(jnp.float32)
    valid_tok, masked_tok = token_masks(cand_lengths, masked_pos, tokens)
    base_state = jnp.where(masked_tok[:, None], mask_embed[None, :], dec_state).astype(jnp.float32)
    stream_mid = base_state + projected
    squares = lax.psum(jnp.sum(stream_mid * stream_mid, axis=1), ("blk", "rows"))
    inv_rms = lax.rsqrt(squares / D + 1e-06)[:, None]
    normed = (stream_mid * inv_rms * norm_gain.astype(jnp.float32)).astype(jnp.bfloat16)
    keep_mask = valid_tok.astype(jnp.float32)[:, None]
    stream = (stream_mid * keep_mask).astype(jnp.bfloat16)
    normed_full = lax.all_gather(normed, ("blk", "rows"), axis=1, tiled=True)
    feature_width = gate_weight.shape[0]
    column_block = lax.dynamic_slice_in_dim(
        normed_full, lax.axis_index("heads") * feature_width, feature_width, 1
    )
    gate_part = jnp.dot(column_block, gate_weight, preferred_element_type=jnp.float32)
    up_part = jnp.dot(column_block, up_weight, preferred_element_type=jnp.float32)
    gate_rows, up_rows = (
        lax.psum(gate_part.astype(jnp.bfloat16), "heads").astype(jnp.float32),
        lax.psum(up_part.astype(jnp.bfloat16), "heads").astype(jnp.float32),
    )
    hidden = (jax.nn.gelu(gate_rows, approximate=True) * up_rows).astype(jnp.bfloat16)
    down_out = lax.psum_scatter(
        jnp.dot(hidden, down_weight, preferred_element_type=jnp.float32),
        ("blk", "rows"),
        scatter_dimension=0,
        tiled=True,
    )
    own_start = (lax.axis_index("blk") * lax.axis_size("rows") + lax.axis_index("rows")) * tok_dev
    keep_own = lax.dynamic_slice_in_dim(keep_mask, own_start, tok_dev, 0)
    return (stream, (down_out * keep_own).astype(jnp.bfloat16))


def solution(mesh):
    placed = (
        P(("groups", "blk", "rows"), "heads", None),
        P(("groups", "blk"), "heads", None),
        P(("groups", "blk"), "heads", None),
        P("groups", ("blk", "rows")),
        P(("blk", "rows")),
        P("heads", ("blk", "rows")),
        P(("blk", "rows")),
        P("heads", ("blk", "rows")),
        P("heads", ("blk", "rows")),
        P(("blk", "rows"), "heads"),
        P("groups"),
        P("groups", None),
    )
    return jax.shard_map(
        shards,
        mesh=mesh,
        in_specs=placed,
        out_specs=(P("groups", ("blk", "rows")), P(("groups", "blk", "rows"), "heads")),
        check_vma=False,
    )
```

profile of v0, /device:TPU:0, one launch (start us, length us, event | category | flops | bytes accessed | tf_op | source)
XLA Modules:
  0.0 224.9 jit_solution(5355824614726427684)
XLA Ops:
  7.2 0.0 copy-start
  7.2 0.0 all-reduce.8.cloned.1.call-start
  7.2 15.2 %all_gather.9 = bf16[16,8,256]{2,1,0:T(8,128)(2,1)S(1)} all-gather(bf16[4,8,256]{2,1,0:T(8,128)(2,1)} %param.12), channel_id=1, replica_groups=mesh['groups'=2,'blk'=4,'heads'=2,'rows'=2] {'blk'}, dimensions={0}, use_global_device_ids=true | all-gather | bytes 81920 | tf_op jit(solution)/shard_map/all_gather | solution.py:39
  22.5 3.8 %fusion.48 = (f32[16,4,2]{0,2,1:T(2,128)S(1)}, f32[16,4,2,1536]{3,0,2,1:T(8,128)}) fusion(bf16[16,4,2,256]{3,0,2,1:T(8,128)(2,1)S(1)} %bitcast.36, bf16[1536,4,256,1]{2,1,0,3:T(4,128)(2,1)} %bitcast.37), kind=kOutput, calls=%fused_computation.59 | convolution fusion | flops 101056384 | bytes 3998208 | tf_op jit(solution)/shard_map/tgjd,kgd->tgjk/dot_general | solution.py:43
  26.3 0.0 copy-start.5
  26.3 0.0 copy-start.4
  26.3 0.0 copy-start.7
  26.3 11.8 %pmax.7 = f32[16,4,2]{0,2,1:T(2,128)S(1)} all-reduce(f32[16,4,2]{0,2,1:T(2,128)S(1)} %get-tuple-element.8), channel_id=1, replica_groups=mesh['groups'=2,'blk'=4,'heads'=2,'rows'=2] {'blk'}, use_global_device_ids=true, to_apply=%region_2.0 | all-reduce | flops 128 | bytes 1024 | tf_op jit(solution)/shard_map/pmax | solution.py:55
  38.2 1.4 fusion.19
  39.6 0.0 copy-done
  39.6 0.0 copy-start.2
  39.6 0.0 copy-start.3
  39.6 2.5 %fusion.16 = bf16[16,4,2,256]{3,0,2,1:T(8,128)(2,1)} fusion(bf16[1536,4,256,1]{2,1,0,3:T(4,128)(2,1)S(1)} %bitcast.34, f32[16,4,2,1536]{3,0,2,1:T(8,128)} %get-tuple-element.9, f32[16,4,2]{0,2,1:T(2,128)S(1)} %get-tuple-element.8, f32[16,4,2]{0,2,1:T(2,128)S(1)} %get-tuple-element.5), kind=kOutput, calls=%fused_computation.10 | convolution fusion | flops 101122048 | bytes 3998720 | tf_op jit(solution)/shard_map/tgjk,kgd->tgjd/dot_general | solution.py:49
  42.1 0.0 all-reduce.8.cloned.1.call-update
  42.1 0.0 all-reduce.12.cloned.1.call-start
  42.1 8.4 %all-reduce.1 = bf16[16,4,2]{0,2,1:T(2,128)(2,1)S(1)} all-reduce(bf16[16,4,2]{0,2,1:T(2,128)(2,1)S(1)} %get-tuple-element.4), channel_id=3, replica_groups=mesh['groups'=2,'blk'=4,'heads'=2,'rows'=2] {'blk'}, use_global_device_ids=true, to_apply=%region_5.0.clone | all-reduce | flops 128 | bytes 512
  50.5 0.0 copy-done.5
  50.5 0.1 fusion.41
  51.3 0.0 copy-done.4
  51.3 0.0 copy-done.7
  51.3 0.6 dynamic-slice.5
  52.6 0.1 dynamic-slice_convert_fusion
  52.6 21.8 %all-reduce.8.cloned.1.call-done = bf16[16,4,2,256]{3,0,2,1:T(8,128)(2,1)} async-done(((bf16[16,4,2,256]{3,0,2,1:T(8,128)(2,1)}), bf16[16,4,2,256]{3,0,2,1:T(8,128)(2,1)}) %all-reduce.8.cloned.1.call-update) | async-done | bytes 65552
  74.4 0.8 fusion.39
  75.3 14.0 %all-gather = bf16[8,4,2048]{2,1,0:T(4,128)(2,1)S(1)} all-gather(bf16[1,4,2048]{2,1,0:T(4,128)(2,1)S(1)} %bitcast.35), channel_id=1, replica_groups=mesh['groups'=2,'blk'=4,'heads'=2,'rows'=2] {'blk','rows'}, dimensions={0}, use_global_device_ids=true | all-gather | bytes 147456 | tf_op jit(solution)/shard_map/all_gather | solution.py:73
  89.3 2.1 convolution_convert_fusion.2
  91.4 8.3 %psum.28 = bf16[32,448]{1,0:T(8,128)(2,1)S(1)} all-reduce(bf16[32,448]{1,0:T(8,128)(2,1)S(1)} %convolution_convert_fusion.2), channel_id=1, replica_groups=mesh['groups'=2,'blk'=4,'heads'=2,'rows'=2] {'heads'}, use_global_device_ids=true, to_apply=%region_6.7 | all-reduce | flops 14336 | bytes 57344 | tf_op jit(solution)/shard_map/psum | solution.py:75
  99.7 0.0 copy-done.2
  99.7 0.0 copy-done.3
  99.8 0.2 multiply_reduce_fusion
  99.9 13.6 %psum.29 = f32[32]{0:T(128)S(1)} all-reduce(f32[32]{0:T(128)S(1)} %multiply_reduce_fusion), channel_id=1, replica_groups=mesh['groups'=2,'blk'=4,'heads'=2,'rows'=2] {'blk','rows'}, use_global_device_ids=true, to_apply=%region_8.9 | all-reduce | flops 32 | bytes 256 | tf_op jit(solution)/shard_map/psum | solution.py:82
  113.6 0.7 fusion.38
  114.3 14.2 %all-gather.1 = bf16[8,448,32]{1,2,0:T(8,128)(2,1)S(1)} all-gather(bf16[1,448,32]{1,2,0:T(8,128)(2,1)S(1)} %get-tuple-element.6), channel_id=1, replica_groups=mesh['groups'=2,'blk'=4,'heads'=2,'rows'=2] {'blk','rows'}, dimensions={0}, use_global_device_ids=true | all-gather | bytes 258048 | tf_op jit(solution)/shard_map/all_gather | solution.py:87
  128.5 0.1 copy.28
  128.7 0.9 reshape.80
  129.6 4.8 %convolution_convert_fusion = bf16[32,1792]{1,0:T(8,128)(2,1)} fusion(bf16[1792,1792]{1,0:T(8,128)(2,1)} %param.20, bf16[3584,32]{0,1:T(8,128)(2,1)} %reshape.80, s32[]{:T(128)S(6)} %select_n.23), kind=kOutput, calls=%fused_computation.6 | convolution fusion | flops 205578240 | bytes 6651908 | tf_op jit(solution)/shard_map/dot_general | solution.py:93
  134.4 0.0 copy-done.1
  134.4 4.7 %convolution_convert_fusion.1 = bf16[32,1792]{1,0:T(8,128)(2,1)} fusion(bf16[1792,1792]{1,0:T(8,128)(2,1)} %param.19, bf16[3584,32]{0,1:T(8,128)(2,1)S(1)} %copy-done.1, s32[]{:T(128)S(6)} %select_n.23), kind=kOutput, calls=%fused_computation.7 | convolution fusion | flops 205578240 | bytes 6651908 | tf_op jit(solution)/shard_map/dot_general | solution.py:92
  139.1 0.0 all-reduce.12.cloned.1.call-update
  139.1 0.0 all-reduce.10.cloned.1.call-start
  139.2 20.3 %all-reduce.12.cloned.1.call-done = (bf16[32,1792]{1,0:T(8,128)(2,1)}, bf16[32,1792]{1,0:T(8,128)(2,1)}) async-done(((bf16[32,1792]{1,0:T(8,128)(2,1)}, bf16[32,1792]{1,0:T(8,128)(2,1)}), (bf16[32,1792]{1,0:T(8,128)(2,1)}, bf16[32,1792]{1,0:T(8,128)(2,1)})) %all-reduce.12.cloned.1.call-update) | async-done | bytes 229392 | tf_op jit(solution)/shard_map/psum | solution.py:95
  159.5 4.7 %fusion.30 = f32[32,1792]{1,0:T(8,128)} fusion(bf16[1792,1792]{1,0:T(8,128)(2,1)} %param.21, bf16[32,1792]{1,0:T(8,128)(2,1)} %get-tuple-element.2, bf16[32,1792]{1,0:T(8,128)(2,1)} %get-tuple-element.3), kind=kOutput, calls=%fused_computation.27 | convolution fusion | flops 206209024 | bytes 6881280 | tf_op jit(solution)/shard_map/dot_general | solution.py:100
  164.2 0.0 all-reduce.10.cloned.1.call-update
  164.3 0.1 dynamic-slice.3
  164.3 0.0 copy-done.6
  164.3 0.6 dynamic-slice.9
  165.6 51.3 %all-reduce.10.cloned.1.call-done = f32[32,1792]{1,0:T(8,128)} async-done(((f32[32,1792]{1,0:T(8,128)}), f32[32,1792]{1,0:T(8,128)}) %all-reduce.10.cloned.1.call-update) | async-done | bytes 229392
  216.9 1.5 fusion.40
  (9 shorter events, 0.1 us)
Async XLA Ops:
  7.2 32.4 %copy-start = (bf16[1536,4,256]{2,1,0:T(4,128)(2,1)S(1)}, bf16[1536,4,256]{2,1,0:T(4,128)(2,1)}, u32[]{:S(2)}) copy-start(bf16[1536,4,256]{2,1,0:T(4,128)(2,1)} %param.14) | copy-start | bytes 9437188
  7.2 67.3 %all-reduce.8.cloned.1.call-start = ((), (), s32[]{:S(2)}) async-start(), calls=%async_computation | async-start | bytes 131072
  26.3 24.2 %copy-start.5 = (s32[1,48]{1,0:T(1,128)S(1)}, s32[1,48]{1,0:T(1,128)}, u32[]{:S(2)}) copy-start(s32[1,48]{1,0:T(1,128)} %param.23) | copy-start | bytes 580
  26.3 25.0 %copy-start.4 = (bf16[448]{0:T(512)(128)(2,1)S(1)}, bf16[448]{0:T(512)(128)(2,1)}, u32[]{:S(2)}) copy-start(bf16[448]{0:T(512)(128)(2,1)} %param.18) | copy-start | bytes 2692
  26.3 25.0 %copy-start.7 = (u32[32]{0:T(128)S(1)}, u32[32]{0:T(128)}, u32[]{:S(2)}) copy-start(u32[32]{0:T(128)} %constant.67) | copy-start | bytes 388
  39.6 60.2 %copy-start.2 = (bf16[32,448]{1,0:T(8,128)(2,1)S(1)}, bf16[32,448]{1,0:T(8,128)(2,1)}, u32[]{:S(2)}) copy-start(bf16[32,448]{1,0:T(8,128)(2,1)} %param.15) | copy-start | bytes 86020
  39.6 60.2 %copy-start.3 = (bf16[448]{0:T(512)(128)(2,1)S(1)}, bf16[448]{0:T(512)(128)(2,1)}, u32[]{:S(2)}) copy-start(bf16[448]{0:T(512)(128)(2,1)} %param.16) | copy-start | bytes 2692
  42.1 117.4 %all-reduce.12.cloned.1.call-start = ((), (), s32[]{:S(2)}) async-start(), calls=%async_computation.2 | async-start | bytes 458752 | tf_op jit(solution)/shard_map/psum | solution.py:95
  129.6 4.8 %copy-start.1 = (bf16[3584,32]{0,1:T(8,128)(2,1)S(1)}, bf16[3584,32]{0,1:T(8,128)(2,1)}, u32[]{:S(2)}) copy-start(bf16[3584,32]{0,1:T(8,128)(2,1)} %reshape.80) | copy-start | bytes 688132
  139.1 77.8 %all-reduce.10.cloned.1.call-start = ((), (), s32[]{:S(2)}) async-start(), calls=%async_computation.1 | async-start | bytes 458752
  159.5 4.9 %copy-start.6 = (u32[32]{0:T(128)S(1)}, u32[32]{0:T(128)}, u32[]{:S(2)}) copy-start(u32[32]{0:T(128)} %constant.75) | copy-start | bytes 388
Sparse Core Ops, SparseCore 0:
  42.2 32.1 all-reduce.7
  139.3 20.1 all-reduce.11
  164.4 52.4 all-reduce.9
where the time goes:
time: 226 us; the launch traced here: 225 us
  waiting for transfers between devices  93.5 us (41%)
  blocking collectives  85.6 us (38%)
  matrix products  22.6 us (10%)
  between operations  15.9 us (7%)
  other arithmetic  4.81 us (2%)
  local copies, waits for them, and re-layouts  2.44 us (1%)
    unnamed x5, waiting for transfers between devices  73.2 us
    psum x1, waiting for transfers between devices, shards(): lax.psum(gate_part.astype(jnp.bfloat16), 'heads').astype(jnp.float32)  20.3 us
    all_gather x1, blocking collectives, shards(): queries_all = lax.all_gather(queries, 'blk', axis=0, tiled=True)  15.2 us
    all_gather x1, blocking collectives, shards(): normed_full = lax.all_gather(normed, ('blk', 'rows'), axis=1, tiled=True)  14.2 us
    all_gather x1, blocking collectives, shards(): attn_all = lax.all_gather(attn_own, ('blk', 'rows'), axis=0, tiled=True)  14 us
    psum x1, blocking collectives, shards(): lax.psum(jnp.sum(stream_mid * stream_mid, axis=1), ('blk', 'rows'))  13.6 us
    pmax x1, blocking collectives, shards(): highest = lax.pmax(local_peak, 'blk')  11.8 us
    unnamed x1, blocking collectives  8.38 us
  transfers between devices with their start and end apart: 3, of which 3 were waited for; matrix products, arithmetic and copies ran while one was open for 1% of the time, Pallas kernels for 0%

commit v1 on v0

v1 whole, which is shorter than its diff:
```python
import jax
import jax.numpy as jnp
from jax import lax
from jax.sharding import PartitionSpec as P

LEN = 128
EPS = 1e-06
BF = jnp.bfloat16
F32 = jnp.float32


def token_masks(cand_lengths, masked_pos, tokens):
    positions = jnp.arange(tokens, dtype=jnp.int32) % LEN
    length_tok = jnp.repeat(cand_lengths, LEN)[:tokens]
    valid_tok = positions < length_tok
    slots = jnp.arange(LEN, dtype=jnp.int32)
    masked_tok = jnp.any(masked_pos[:, :, None] == slots[None, None, :], axis=1).reshape(-1)[
        :tokens
    ]
    return (valid_tok, masked_tok)


def shards_any(
    queries,
    src_keys,
    src_values,
    dec_state,
    mask_embed,
    out_weight,
    norm_gain,
    gate_weight,
    up_weight,
    down_weight,
    cand_lengths,
    masked_pos,
):
    tok_dev, local_heads, head_size = queries.shape
    kv_local = src_keys.shape[1]
    group_size = local_heads // kv_local
    score_scale = head_size ** (-0.5)
    features = dec_state.shape[1] * lax.axis_size("blk") * lax.axis_size("rows")
    queries_all = lax.all_gather(queries, "blk", axis=0, tiled=True)
    gathered_rows = queries_all.shape[0]
    grouped = queries_all.reshape(gathered_rows, kv_local, group_size, head_size)
    scores = (
        jnp.einsum("tgjd,kgd->tgjk", grouped, src_keys, preferred_element_type=F32) * score_scale
    )
    local_peak = jnp.max(scores, axis=3)
    weights = jnp.exp(scores - local_peak[..., None])
    totals = jnp.sum(weights, axis=3)
    numerator = jnp.einsum(
        "tgjk,kgd->tgjd", weights.astype(BF), src_values, preferred_element_type=F32
    )
    highest = lax.pmax(local_peak, "blk")
    factor = jnp.exp(local_peak - highest)
    numer_own, totals_own = (
        lax.psum_scatter(
            (numerator * factor[..., None]).astype(BF), "blk", scatter_dimension=0, tiled=True
        ).astype(F32),
        lax.psum_scatter(
            (totals * factor).astype(BF), "blk", scatter_dimension=0, tiled=True
        ).astype(F32),
    )
    attn_own = (
        (numer_own / totals_own[..., None]).astype(BF).reshape(tok_dev, local_heads * head_size)
    )
    attn_all = lax.all_gather(attn_own, ("blk", "rows"), axis=0, tiled=True)
    tokens = attn_all.shape[0]
    projected = lax.psum(
        jnp.dot(attn_all, out_weight, preferred_element_type=F32).astype(BF), "heads"
    ).astype(F32)
    valid_tok, masked_tok = token_masks(cand_lengths, masked_pos, tokens)
    base_state = jnp.where(masked_tok[:, None], mask_embed[None, :], dec_state).astype(F32)
    stream_mid = base_state + projected
    squares = lax.psum(jnp.sum(stream_mid * stream_mid, axis=1), ("blk", "rows"))
    inv_rms = lax.rsqrt(squares / features + EPS)[:, None]
    normed = (stream_mid * inv_rms * norm_gain.astype(F32)).astype(BF)
    keep_mask = valid_tok.astype(F32)[:, None]
    stream = (stream_mid * keep_mask).astype(BF)
    normed_full = lax.all_gather(normed, ("blk", "rows"), axis=1, tiled=True)
    feature_width = gate_weight.shape[0]
    column_block = lax.dynamic_slice_in_dim(
        normed_full, lax.axis_index("heads") * feature_width, feature_width, 1
    )
    gate_part = jnp.dot(column_block, gate_weight, preferred_element_type=F32)
    up_part = jnp.dot(column_block, up_weight, preferred_element_type=F32)
    gate_rows, up_rows = (
        lax.psum(gate_part.astype(BF), "heads").astype(F32),
        lax.psum(up_part.astype(BF), "heads").astype(F32),
    )
    hidden = (jax.nn.gelu(gate_rows, approximate=True) * up_rows).astype(BF)
    down_out = lax.psum_scatter(
        jnp.dot(hidden, down_weight, preferred_element_type=F32),
        ("blk", "rows"),
        scatter_dimension=0,
        tiled=True,
    )
    own_start = (lax.axis_index("blk") * lax.axis_size("rows") + lax.axis_index("rows")) * tok_dev
    keep_own = lax.dynamic_slice_in_dim(keep_mask, own_start, tok_dev, 0)
    return (stream, (down_out * keep_own).astype(BF))


def hop(value, axis, size, step):
    return lax.ppermute(value, axis, [(i, i ^ step) for i in range(size)])


def by_index(pieces, at):
    return [lax.select_n(at ^ k, *pieces) for k in range(len(pieces))]


def shards_direct(
    queries,
    src_keys,
    src_values,
    dec_state,
    mask_embed,
    out_weight,
    norm_gain,
    gate_weight,
    up_weight,
    down_weight,
    cand_lengths,
    masked_pos,
):
    blks, head_parts = lax.axis_size("blk"), lax.axis_size("heads")
    blk, head, row = (lax.axis_index(name) for name in ("blk", "heads", "rows"))
    tok_dev, local_heads, head_size = queries.shape
    kv_local = src_keys.shape[1]
    group_size = local_heads // kv_local
    score_scale = head_size ** (-0.5)
    width = dec_state.shape[1]
    features = width * blks * 2
    half = blks // head_parts

    pieces = [queries] + [hop(queries, "blk", blks, s) for s in range(1, blks)]
    q_all = jnp.concatenate(by_index(pieces, blk), axis=0)
    rows_in = q_all.shape[0]
    grouped = q_all.reshape(rows_in, kv_local, group_size, head_size)
    scores = (
        jnp.einsum("tgjd,kgd->tgjk", grouped, src_keys, preferred_element_type=F32) * score_scale
    )
    peak = jnp.max(scores, axis=3)
    weights = jnp.exp(scores - peak[..., None])
    totals = jnp.sum(weights, axis=3)
    numerator = jnp.einsum(
        "tgjk,kgd->tgjd", weights.astype(BF), src_values, preferred_element_type=F32
    )
    partial = (numerator / totals[..., None]).astype(BF)
    level = peak + jnp.log(totals)
    partials = [partial] + [hop(partial, "blk", blks, s) for s in range(1, blks)]
    levels = [level] + [hop(level, "blk", blks, s) for s in range(1, blks)]
    top = levels[0]
    for one in levels[1:]:
        top = jnp.maximum(top, one)
    shares = [jnp.exp(one - top) for one in levels]
    total = sum(shares)
    attn = sum(
        (share / total)[..., None] * part.astype(F32) for share, part in zip(shares, partials)
    )
    attn = attn.astype(BF).reshape(rows_in, local_heads * head_size)
    other = hop(attn, "rows", 2, 1)
    attn_all = jnp.stack(by_index([attn, other], row), axis=0)
    attn_all = attn_all.reshape(2, blks, tok_dev, -1).transpose(1, 0, 2, 3)
    tokens = rows_in * 2
    attn_all = attn_all.reshape(tokens, -1)
    projected = jnp.dot(attn_all, out_weight, preferred_element_type=F32).astype(BF)
    projected = projected.astype(F32) + hop(projected, "heads", 2, 1).astype(F32)
    valid_tok, masked_tok = token_masks(cand_lengths, masked_pos, tokens)
    base_state = jnp.where(masked_tok[:, None], mask_embed[None, :], dec_state).astype(F32)
    mid = base_state + projected
    keep_mask = valid_tok.astype(F32)[:, None]
    stream = (mid * keep_mask).astype(BF)
    squares = jnp.sum(mid * mid, axis=1)
    scaled = (mid * norm_gain.astype(F32)).astype(BF)

    def spread(value):
        got = [value]
        for s in range(1, blks):
            pairs = []
            for b in range(blks):
                h = b // half
                pairs.append((b * head_parts + h, (b ^ s) * head_parts + h))
            got.append(lax.ppermute(value, ("blk", "heads"), pairs))
        return [lax.select_n(blk ^ (head * half + k), *got) for k in range(half)]

    tiles, square_tiles = spread(scaled), spread(squares)
    mine = jnp.stack(tiles, axis=0)
    theirs = hop(mine, "rows", 2, 1)
    pair = jnp.stack(by_index([mine, theirs], row), axis=0)
    column_block = pair.transpose(2, 1, 0, 3).reshape(tokens, -1)
    squares = sum(square_tiles)
    squares = squares + hop(squares, "rows", 2, 1)
    squares = squares + hop(squares, "heads", 2, 1)
    inv_rms = lax.rsqrt(squares / features + EPS)[:, None]
    gate = jnp.dot(column_block, gate_weight, preferred_element_type=F32)
    gate = gate + hop(gate.astype(BF), "heads", 2, 1).astype(F32)
    up = jnp.dot(column_block, up_weight, preferred_element_type=F32)
    up = up + hop(up.astype(BF), "heads", 2, 1).astype(F32)
    hidden = (jax.nn.gelu(gate * inv_rms, approximate=True) * (up * inv_rms)).astype(BF)
    down = jnp.dot(hidden, down_weight, preferred_element_type=F32)
    down = down.reshape(blks, 2, tok_dev, -1)
    keep = lax.dynamic_index_in_dim(down, row, 1, keepdims=False)
    away = lax.dynamic_index_in_dim(down, 1 - row, 1, keepdims=False).astype(BF)
    keep = keep + hop(away, "rows", 2, 1).astype(F32)
    sent = keep.astype(BF)
    own = lax.dynamic_index_in_dim(keep, blk, 0, keepdims=False)
    for s in range(1, blks):
        part = lax.dynamic_index_in_dim(sent, blk ^ s, 0, keepdims=False)
        own = own + hop(part, "blk", blks, s).astype(F32)
    keep_own = lax.dynamic_slice_in_dim(keep_mask, (blk * 2 + row) * tok_dev, tok_dev, 0)
    return (stream, (own * keep_own).astype(BF))


def solution(mesh):
    size = dict(mesh.shape)
    direct = size["blk"] in (2, 4, 8) and size["heads"] == 2 and size["rows"] == 2
    placed = (
        P(("groups", "blk", "rows"), "heads", None),
        P(("groups", "blk"), "heads", None),
        P(("groups", "blk"), "heads", None),
        P("groups", ("blk", "rows")),
        P(("blk", "rows")),
        P("heads", ("blk", "rows")),
        P(("blk", "rows")),
        P("heads", ("blk", "rows")),
        P("heads", ("blk", "rows")),
        P(("blk", "rows"), "heads"),
        P("groups"),
        P("groups", None),
    )
    return jax.shard_map(
        shards_direct if direct else shards_any,
        mesh=mesh,
        in_specs=placed,
        out_specs=(P("groups", ("blk", "rows")), P(("groups", "blk", "rows"), "heads")),
        check_vma=False,
    )
```

time: 226 us -> 83.5 us (0.37)
  blocking collectives: 85.6 us -> 0 us
  waiting for transfers between devices: 93.5 us -> 18.3 us
  starting transfers between devices: 0.12 us -> 40.1 us
  between operations: 15.9 us -> 1.71 us
  matrix products: 22.6 us -> 16.1 us
    unnamed x5 -> x0, waiting for transfers between devices: 73.2 us -> none
    all_gather x3 -> x0, blocking collectives: 43.4 us -> none  [the longest x1 15.2 us: shards(): queries_all = lax.all_gather(queries, 'blk', axis=0, tiled=True)]
    ppermute x0 -> x26, starting transfers between devices: none -> 40.1 us  [the longest x20 26.4 us: hop(): return lax.ppermute(value, axis, [(i, i ^ step) for i in range(size)])]
    psum x2 -> x0, blocking collectives: 22 us -> none  [the longest x1 13.6 us: shards(): lax.psum(jnp.sum(stream_mid * stream_mid, axis=1), ('blk', 'rows'))]
    psum x1 -> x0, waiting for transfers between devices: 20.3 us -> none  [shards(): lax.psum(gate_part.astype(jnp.bfloat16), 'heads').astype(jnp.float32)]
    ppermute x0 -> x26, waiting for transfers between devices: none -> 18.3 us  [the longest x20 17.2 us: hop(): return lax.ppermute(value, axis, [(i, i ^ step) for i in range(size)])]
    pmax x1 -> x0, blocking collectives: 11.8 us -> none  [shards(): highest = lax.pmax(local_peak, 'blk')]
    unnamed x1 -> x0, blocking collectives: 8.38 us -> none
  transfers between devices with their start and end apart: 3 -> 26, of which waited for: 3 -> 11; matrix products, arithmetic and copies ran while one was open for 1% -> 12% of each run, Pallas kernels for 0% -> 0%
where the time goes in v1:
time: 83.5 us; the launch traced here: 83 us
  starting transfers between devices  40.1 us (48%)
  waiting for transfers between devices  18.3 us (22%)
  matrix products  16.1 us (19%)
  other arithmetic  4.54 us (5%)
  local copies, waits for them, and re-layouts  2.29 us (3%)
  between operations  1.71 us (2%)
    ppermute x20, starting transfers between devices, hop(): return lax.ppermute(value, axis, [(i, i ^ step) for i in range(size)])  26.4 us
    ppermute x20, waiting for transfers between devices, hop(): return lax.ppermute(value, axis, [(i, i ^ step) for i in range(size)])  17.2 us
    ppermute x6, starting transfers between devices, spread(): got.append(lax.ppermute(value, ('blk', 'heads'), pairs))  13.6 us
    dot_general x1, matrix products, shards_direct(): down = jnp.dot(hidden, down_weight, preferred_element_type=F32)  4.07 us
    dot_general x1, matrix products, shards_direct(): gate = jnp.dot(column_block, gate_weight, preferred_element_type=F32)  4.04 us
    dot_general x1, matrix products, shards_direct(): up = jnp.dot(column_block, up_weight, preferred_element_type=F32)  4.04 us
    dot_general x1, matrix products, shards_direct(): jnp.dot(attn_all, out_weight, preferred_element_type=F32).astype(BF)  2.1 us
  transfers between devices with their start and end apart: 26, of which 11 were waited for; matrix products, arithmetic and copies ran while one was open for 12% of the time, Pallas kernels for 0%

profile of v1, /device:TPU:0, one launch (start us, length us, event | category | flops | bytes accessed | tf_op | source)
XLA Modules:
  0.0 83.0 jit_solution(14094210294225003549)
XLA Ops:
  0.6 4.1 %collective-permute-start.1 = (bf16[4,8,256]{2,1,0:T(8,128)(2,1)}, bf16[4,8,256]{2,1,0:T(8,128)(2,1)S(1)}, u32[]{:S(2)}, u32[]{:S(2)}) collective-permute-start(bf16[4,8,256]{2,1,0:T(8,128)(2,1)} %param.12), channel_id=1, source_target_pairs={{0,8},{4,12},{8,0},{12,4},{1,9},{5,13},{9,1},{13,5},{2,10},{6,14},... | collective-permute-start | bytes 49160 | tf_op jit(solution)/shard_map/ppermute | solution.py:104
  4.7 1.3 %collective-permute-start.2 = (bf16[4,8,256]{2,1,0:T(8,128)(2,1)}, bf16[4,8,256]{2,1,0:T(8,128)(2,1)S(1)}, u32[]{:S(2)}, u32[]{:S(2)}) collective-permute-start(bf16[4,8,256]{2,1,0:T(8,128)(2,1)} %param.12), channel_id=1, source_target_pairs={{0,12},{4,8},{8,4},{12,0},{1,13},{5,9},{9,5},{13,1},{2,14},{6,10},... | collective-permute-start | bytes 49160 | tf_op jit(solution)/shard_map/ppermute | solution.py:104
  6.1 0.2 collective-permute-start
  6.3 0.7 fusion.44
  7.1 3.4 %collective-permute-done.2 = bf16[4,8,256]{2,1,0:T(8,128)(2,1)S(1)} collective-permute-done((bf16[4,8,256]{2,1,0:T(8,128)(2,1)}, bf16[4,8,256]{2,1,0:T(8,128)(2,1)S(1)}, u32[]{:S(2)}, u32[]{:S(2)}) %collective-permute-start.2) | collective-permute-done | bytes 16416 | tf_op jit(solution)/shard_map/ppermute | solution.py:104
  10.5 0.7 select_select_fusion.3
  11.3 1.1 %fusion.55 = (f32[16,4,2]{0,2,1:T(2,128)S(1)}, f32[16,4,2,1536]{3,0,2,1:T(8,128)S(1)}) fusion(bf16[16,4,2,256]{3,0,2,1:T(8,128)(2,1)S(1)} %bitcast.79, bf16[1536,4,256,1]{2,1,0,3:T(4,128)(2,1)S(1)} %bitcast.78), kind=kOutput, calls=%fused_computation.89 | convolution fusion | flops 101056384 | bytes 3998208 | tf_op jit(solution)/shard_map/tgjd,kgd->tgjk/dot_general | solution.py:140
  12.4 0.3 fusion.20
  12.7 2.1 %collective-permute-start.5 = (f32[16,4,2]{0,2,1:T(2,128)S(1)}, f32[16,4,2]{0,2,1:T(2,128)S(1)}, u32[]{:S(2)}, u32[]{:S(2)}) collective-permute-start(f32[16,4,2]{0,2,1:T(2,128)S(1)} %bitcast.88), channel_id=1, source_target_pairs={{0,12},{4,8},{8,4},{12,0},{1,13},{5,9},{9,5},{13,1},{2,14},{6,10},... | collective-permute-start | bytes 1544 | tf_op jit(solution)/shard_map/ppermute | solution.py:104
  14.8 2.4 %collective-permute-start.3 = (f32[16,4,2]{0,2,1:T(2,128)S(1)}, f32[16,4,2]{0,2,1:T(2,128)S(1)}, u32[]{:S(2)}, u32[]{:S(2)}) collective-permute-start(f32[16,4,2]{0,2,1:T(2,128)S(1)} %bitcast.90), channel_id=1, source_target_pairs={{0,4},{4,0},{8,12},{12,8},{1,5},{5,1},{9,13},{13,9},{2,6},{6,2},{1... | collective-permute-start | bytes 1544 | tf_op jit(solution)/shard_map/ppermute | solution.py:104
  17.2 0.7 fusion.16
  17.9 2.1 %collective-permute-start.8 = (bf16[16,4,2,256]{3,0,2,1:T(8,128)(2,1)S(1)}, bf16[16,4,2,256]{3,0,2,1:T(8,128)(2,1)S(1)}, u32[]{:S(2)}, u32[]{:S(2)}) collective-permute-start(bf16[16,4,2,256]{3,0,2,1:T(8,128)(2,1)S(1)} %fusion.16), channel_id=1, source_target_pairs={{0,12},{4,8},{8,4},{12,0},{1,13},{5,9},{9,5},{13,1},{2,14},{6,10},... | collective-permute-start | bytes 196616 | tf_op jit(solution)/shard_map/ppermute | solution.py:104
  20.0 2.4 %collective-permute-start.6 = (bf16[16,4,2,256]{3,0,2,1:T(8,128)(2,1)S(1)}, bf16[16,4,2,256]{3,0,2,1:T(8,128)(2,1)S(1)}, u32[]{:S(2)}, u32[]{:S(2)}) collective-permute-start(bf16[16,4,2,256]{3,0,2,1:T(8,128)(2,1)S(1)} %fusion.16), channel_id=1, source_target_pairs={{0,4},{4,0},{8,12},{12,8},{1,5},{5,1},{9,13},{13,9},{2,6},{6,2},{1... | collective-permute-start | bytes 196616 | tf_op jit(solution)/shard_map/ppermute | solution.py:104
  22.4 1.6 %collective-permute-done.8 = bf16[16,4,2,256]{3,0,2,1:T(8,128)(2,1)S(1)} collective-permute-done((bf16[16,4,2,256]{3,0,2,1:T(8,128)(2,1)S(1)}, bf16[16,4,2,256]{3,0,2,1:T(8,128)(2,1)S(1)}, u32[]{:S(2)}, u32[]{:S(2)}) %collective-permute-start.8) | collective-permute-done | bytes 65568 | tf_op jit(solution)/shard_map/ppermute | solution.py:104
  24.0 1.4 %collective-permute-done.7 = bf16[16,4,2,256]{3,0,2,1:T(8,128)(2,1)S(1)} collective-permute-done((bf16[16,4,2,256]{3,0,2,1:T(8,128)(2,1)S(1)}, bf16[16,4,2,256]{3,0,2,1:T(8,128)(2,1)S(1)}, u32[]{:S(2)}, u32[]{:S(2)}) %collective-permute-start.7) | collective-permute-done | bytes 65568 | tf_op jit(solution)/shard_map/ppermute | solution.py:104
  25.4 0.1 add_convert_fusion
  26.4 0.6 collective-permute-done.9
  27.0 0.1 maximum_bitcast_fusion
  27.2 2.1 %convolution_convert_fusion = bf16[32,448]{1,0:T(8,128)(2,1)S(1)} fusion(bf16[32,2048]{1,0:T(8,128)(2,1)S(1)} %reshape.95, bf16[2048,448]{0,1:T(8,128)(2,1)} %param.17), kind=kOutput, calls=%fused_computation.9 | convolution fusion | flops 58734592 | bytes 1994752 | tf_op jit(solution)/shard_map/dot_general | solution.py:166
  29.3 1.6 %collective-permute-start.10 = (bf16[32,448]{1,0:T(8,128)(2,1)S(1)}, bf16[32,448]{1,0:T(8,128)(2,1)S(1)}, u32[]{:S(2)}, u32[]{:S(2)}) collective-permute-start(bf16[32,448]{1,0:T(8,128)(2,1)S(1)} %convolution_convert_fusion), channel_id=1, source_target_pairs={{0,2},{2,0},{1,3},{3,1},{4,6},{6,4},{5,7},{7,5},{8,10},{10,8},{9,1... | collective-permute-start | bytes 86024 | tf_op jit(solution)/shard_map/ppermute | solution.py:104
  30.9 2.4 %collective-permute-done.10 = bf16[32,448]{1,0:T(8,128)(2,1)S(1)} collective-permute-done((bf16[32,448]{1,0:T(8,128)(2,1)S(1)}, bf16[32,448]{1,0:T(8,128)(2,1)S(1)}, u32[]{:S(2)}, u32[]{:S(2)}) %collective-permute-start.10) | collective-permute-done | bytes 28704 | tf_op jit(solution)/shard_map/ppermute | solution.py:104
  33.3 0.8 multiply_reduce_fusion
  34.1 3.6 %collective-permute-start.12 = (bf16[32,448]{1,0:T(8,128)(2,1)S(1)}, bf16[32,448]{1,0:T(8,128)(2,1)S(1)}, u32[]{:S(2)}, u32[]{:S(2)}) collective-permute-start(bf16[32,448]{1,0:T(8,128)(2,1)S(1)} %get-tuple-element.14), channel_id=1, source_target_pairs={{0,8},{4,12},{10,2},{14,6},{1,9},{5,13},{11,3},{15,7},{16,24},{20,... | collective-permute-start | bytes 86024 | tf_op jit(solution)/shard_map/ppermute | solution.py:183
  37.7 1.6 %collective-permute-start.13 = (bf16[32,448]{1,0:T(8,128)(2,1)S(1)}, bf16[32,448]{1,0:T(8,128)(2,1)S(1)}, u32[]{:S(2)}, u32[]{:S(2)}) collective-permute-start(bf16[32,448]{1,0:T(8,128)(2,1)S(1)} %get-tuple-element.14), channel_id=1, source_target_pairs={{0,12},{4,8},{10,6},{14,2},{1,13},{5,9},{11,7},{15,3},{16,28},{20,... | collective-permute-start | bytes 86024 | tf_op jit(solution)/shard_map/ppermute | solution.py:183
  39.3 2.5 %collective-permute-start.11 = (bf16[32,448]{1,0:T(8,128)(2,1)S(1)}, bf16[32,448]{1,0:T(8,128)(2,1)S(1)}, u32[]{:S(2)}, u32[]{:S(2)}) collective-permute-start(bf16[32,448]{1,0:T(8,128)(2,1)S(1)} %get-tuple-element.14), channel_id=1, source_target_pairs={{0,4},{4,0},{10,14},{14,10},{1,5},{5,1},{11,15},{15,11},{16,20},{2... | collective-permute-start | bytes 86024 | tf_op jit(solution)/shard_map/ppermute | solution.py:183
  41.8 3.4 %collective-permute-start.16 = (f32[32]{0:T(128)S(1)}, f32[32]{0:T(128)S(1)}, u32[]{:S(2)}, u32[]{:S(2)}) collective-permute-start(f32[32]{0:T(128)S(1)} %get-tuple-element.13), channel_id=1, source_target_pairs={{0,4},{4,0},{10,14},{14,10},{1,5},{5,1},{11,15},{15,11},{16,20},{2... | collective-permute-start | bytes 392 | tf_op jit(solution)/shard_map/ppermute | solution.py:183
  45.2 1.3 %collective-permute-start.17 = (f32[32]{0:T(128)S(1)}, f32[32]{0:T(128)S(1)}, u32[]{:S(2)}, u32[]{:S(2)}) collective-permute-start(f32[32]{0:T(128)S(1)} %get-tuple-element.13), channel_id=1, source_target_pairs={{0,8},{4,12},{10,2},{14,6},{1,9},{5,13},{11,3},{15,7},{16,24},{20,... | collective-permute-start | bytes 392 | tf_op jit(solution)/shard_map/ppermute | solution.py:183
  46.5 1.3 %collective-permute-start.18 = (f32[32]{0:T(128)S(1)}, f32[32]{0:T(128)S(1)}, u32[]{:S(2)}, u32[]{:S(2)}) collective-permute-start(f32[32]{0:T(128)S(1)} %get-tuple-element.13), channel_id=1, source_target_pairs={{0,12},{4,8},{10,6},{14,2},{1,13},{5,9},{11,7},{15,3},{16,28},{20,... | collective-permute-start | bytes 392 | tf_op jit(solution)/shard_map/ppermute | solution.py:183
  48.0 1.1 %collective-permute-done.18 = f32[32]{0:T(128)S(1)} collective-permute-done((f32[32]{0:T(128)S(1)}, f32[32]{0:T(128)S(1)}, u32[]{:S(2)}, u32[]{:S(2)}) %collective-permute-start.18) | collective-permute-done | bytes 160 | tf_op jit(solution)/shard_map/ppermute | solution.py:183
  49.1 1.1 %collective-permute-done.19 = f32[32]{0:T(128)S(1)} collective-permute-done((f32[32]{0:T(128)S(1)}, f32[32]{0:T(128)S(1)}, u32[]{:S(2)}, u32[]{:S(2)}) %collective-permute-start.19) | collective-permute-done | bytes 160 | tf_op jit(solution)/shard_map/ppermute | solution.py:104
  50.2 3.5 %collective-permute-start.20 = (f32[32]{0:T(128)S(1)}, f32[32]{0:T(128)S(1)}, u32[]{:S(2)}, u32[]{:S(2)}) collective-permute-start(f32[32]{0:T(128)S(1)} %add.124), channel_id=1, source_target_pairs={{0,2},{2,0},{1,3},{3,1},{4,6},{6,4},{5,7},{7,5},{8,10},{10,8},{9,1... | collective-permute-start | bytes 392 | tf_op jit(solution)/shard_map/ppermute | solution.py:104
  53.8 0.1 copy.30
  53.9 0.1 reshape.96
  54.1 4.0 %fusion.56 = (bf16[32,1792]{1,0:T(8,128)(2,1)S(1)}, f32[32,1792]{1,0:T(8,128)S(1)}) fusion(bf16[32,1792]{1,0:T(8,128)(2,1)S(1)} %reshape.96, bf16[1792,1792]{1,0:T(8,128)(2,1)} %param.20), kind=kOutput, calls=%fused_computation.90 | convolution fusion | flops 205578240 | bytes 6881280 | tf_op jit(solution)/shard_map/dot_general | solution.py:197
  58.2 4.0 %fusion.57 = (bf16[32,1792]{1,0:T(8,128)(2,1)S(1)}, f32[32,1792]{1,0:T(8,128)S(1)}) fusion(bf16[32,1792]{1,0:T(8,128)(2,1)S(1)} %reshape.96, bf16[1792,1792]{1,0:T(8,128)(2,1)} %param.19), kind=kOutput, calls=%fused_computation.91 | convolution fusion | flops 205578240 | bytes 6881280 | tf_op jit(solution)/shard_map/dot_general | solution.py:195
  62.2 2.0 %collective-permute-start.15 = (bf16[32,1792]{1,0:T(8,128)(2,1)S(1)}, bf16[32,1792]{1,0:T(8,128)(2,1)S(1)}, u32[]{:S(2)}, u32[]{:S(2)}) collective-permute-start(bf16[32,1792]{1,0:T(8,128)(2,1)S(1)} %get-tuple-element.30), channel_id=1, source_target_pairs={{0,2},{2,0},{1,3},{3,1},{4,6},{6,4},{5,7},{7,5},{8,10},{10,8},{9,1... | collective-permute-start | bytes 344072 | tf_op jit(solution)/shard_map/ppermute | solution.py:104
  64.3 2.9 %collective-permute-done.15 = bf16[32,1792]{1,0:T(8,128)(2,1)S(1)} collective-permute-done((bf16[32,1792]{1,0:T(8,128)(2,1)S(1)}, bf16[32,1792]{1,0:T(8,128)(2,1)S(1)}, u32[]{:S(2)}, u32[]{:S(2)}) %collective-permute-start.15) | collective-permute-done | bytes 114720 | tf_op jit(solution)/shard_map/ppermute | solution.py:104
  67.2 4.1 %fusion.32 = f32[32,1792]{1,0:T(8,128)S(1)} fusion(bf16[1792,1792]{1,0:T(8,128)(2,1)} %param.21, f32[32,1792]{1,0:T(8,128)S(1)} %get-tuple-element.29, bf16[32,1792]{1,0:T(8,128)(2,1)S(1)} %collective-permute-done.21, f32[32,1792]{1,0:T(8,128)S(1)} %get-tuple-element.31, bf16[32,1792]{1,0:T(8,128)(2,1)S(1)} %collective-permute-done.15, f32[32]{0:T(128)S(1)} %add_rsqrt_fusion), kind=kOutput, calls=%fused_computation.27 | convolution fusion | flops 206438400 | bytes 7340160 | tf_op jit(solution)/shard_map/dot_general | solution.py:200
  71.3 0.8 reshape.97
  72.1 0.9 %fusion.39 = bf16[4,4,1792]{2,1,0:T(4,128)(2,1)S(1)} fusion(f32[4,2,4,1792]{3,2,1,0:T(4,128)} %reshape.97, s32[]{:T(128)S(6)} %select_n.354), kind=kLoop, calls=%fused_computation.45 | loop fusion | bytes 114692 | tf_op jit(solution)/shard_map/convert_element_type | solution.py:203
  73.1 1.2 %collective-permute-done.22 = bf16[4,4,1792]{2,1,0:T(4,128)(2,1)S(1)} collective-permute-done((bf16[4,4,1792]{2,1,0:T(4,128)(2,1)S(1)}, bf16[4,4,1792]{2,1,0:T(4,128)(2,1)S(1)}, u32[]{:S(2)}, u32[]{:S(2)}) %collective-permute-start.22) | collective-permute-done | bytes 57376 | tf_op jit(solution)/shard_map/ppermute | solution.py:104
  74.3 0.9 %fusion.54 = (bf16[4,4,1792]{2,1,0:T(4,128)(2,1)S(1)}, f32[4,4,1792]{2,1,0:T(4,128)S(1)}) fusion(bf16[4,4,1792]{2,1,0:T(4,128)(2,1)S(1)} %collective-permute-done.22, f32[4,2,4,1792]{3,2,1,0:T(4,128)} %reshape.97, s32[]{:T(128)S(6)} %select_n.353), kind=kLoop, calls=%fused_computation.88 | loop fusion | flops 86016 | bytes 344068 | tf_op jit(solution)/shard_map/convert_element_type | solution.py:205
  75.3 2.4 %collective-permute-start.25 = (bf16[4,1792]{1,0:T(4,128)(2,1)S(1)}, bf16[4,1792]{1,0:T(4,128)(2,1)S(1)}, u32[]{:S(2)}, u32[]{:S(2)}) collective-permute-start(bf16[4,1792]{1,0:T(4,128)(2,1)S(1)} %get-tuple-element.21), channel_id=1, source_target_pairs={{0,12},{4,8},{8,4},{12,0},{1,13},{5,9},{9,5},{13,1},{2,14},{6,10},... | collective-permute-start | bytes 43016 | tf_op jit(solution)/shard_map/ppermute | solution.py:104
  77.7 2.0 %collective-permute-start.23 = (bf16[4,1792]{1,0:T(4,128)(2,1)S(1)}, bf16[4,1792]{1,0:T(4,128)(2,1)S(1)}, u32[]{:S(2)}, u32[]{:S(2)}) collective-permute-start(bf16[4,1792]{1,0:T(4,128)(2,1)S(1)} %get-tuple-element.20), channel_id=1, source_target_pairs={{0,4},{4,0},{8,12},{12,8},{1,5},{5,1},{9,13},{13,9},{2,6},{6,2},{1... | collective-permute-start | bytes 43016 | tf_op jit(solution)/shard_map/ppermute | solution.py:104
  79.7 0.1 dynamic-slice.3
  79.8 1.1 %collective-permute-done.25 = bf16[4,1792]{1,0:T(4,128)(2,1)S(1)} collective-permute-done((bf16[4,1792]{1,0:T(4,128)(2,1)S(1)}, bf16[4,1792]{1,0:T(4,128)(2,1)S(1)}, u32[]{:S(2)}, u32[]{:S(2)}) %collective-permute-start.25) | collective-permute-done | bytes 14368 | tf_op jit(solution)/shard_map/ppermute | solution.py:104
  80.8 1.5 %collective-permute-done.24 = bf16[4,1792]{1,0:T(4,128)(2,1)S(1)} collective-permute-done((bf16[4,1792]{1,0:T(4,128)(2,1)S(1)}, bf16[4,1792]{1,0:T(4,128)(2,1)S(1)}, u32[]{:S(2)}, u32[]{:S(2)}) %collective-permute-start.24) | collective-permute-done | bytes 14368 | tf_op jit(solution)/shard_map/ppermute | solution.py:104
  82.3 0.7 fusion.43
  (55 shorter events, 0.7 us)
Async XLA Ops:
  0.6 10.7 %copy-start = (bf16[1536,4,256]{2,1,0:T(4,128)(2,1)S(1)}, bf16[1536,4,256]{2,1,0:T(4,128)(2,1)}, u32[]{:S(2)}) copy-start(bf16[1536,4,256]{2,1,0:T(4,128)(2,1)} %param.13) | copy-start | bytes 9437188
  0.6 6.5 %collective-permute-start.1 = (bf16[4,8,256]{2,1,0:T(8,128)(2,1)}, bf16[4,8,256]{2,1,0:T(8,128)(2,1)S(1)}, u32[]{:S(2)}, u32[]{:S(2)}) collective-permute-start(bf16[4,8,256]{2,1,0:T(8,128)(2,1)} %param.12), channel_id=1, source_target_pairs={{0,8},{4,12},{8,0},{12,4},{1,9},{5,13},{9,1},{13,5},{2,10},{6,14},... | collective-permute-start | bytes 49160 | tf_op jit(solution)/shard_map/ppermute | solution.py:104
  4.7 5.7 %collective-permute-start.2 = (bf16[4,8,256]{2,1,0:T(8,128)(2,1)}, bf16[4,8,256]{2,1,0:T(8,128)(2,1)S(1)}, u32[]{:S(2)}, u32[]{:S(2)}) collective-permute-start(bf16[4,8,256]{2,1,0:T(8,128)(2,1)} %param.12), channel_id=1, source_target_pairs={{0,12},{4,8},{8,4},{12,0},{1,13},{5,9},{9,5},{13,1},{2,14},{6,10},... | collective-permute-start | bytes 49160 | tf_op jit(solution)/shard_map/ppermute | solution.py:104
  6.1 4.4 %collective-permute-start = (bf16[4,8,256]{2,1,0:T(8,128)(2,1)}, bf16[4,8,256]{2,1,0:T(8,128)(2,1)S(1)}, u32[]{:S(2)}, u32[]{:S(2)}) collective-permute-start(bf16[4,8,256]{2,1,0:T(8,128)(2,1)} %param.12), channel_id=1, source_target_pairs={{0,4},{4,0},{8,12},{12,8},{1,5},{5,1},{9,13},{13,9},{2,6},{6,2},{1... | collective-permute-start | bytes 49160 | tf_op jit(solution)/shard_map/ppermute | solution.py:104
  7.1 10.1 %copy-start.4 = (bf16[1536,4,256]{2,1,0:T(4,128)(2,1)S(1)}, bf16[1536,4,256]{2,1,0:T(4,128)(2,1)}, u32[]{:S(2)}) copy-start(bf16[1536,4,256]{2,1,0:T(4,128)(2,1)} %param.14) | copy-start | bytes 9437188
  12.7 7.3 %collective-permute-start.5 = (f32[16,4,2]{0,2,1:T(2,128)S(1)}, f32[16,4,2]{0,2,1:T(2,128)S(1)}, u32[]{:S(2)}, u32[]{:S(2)}) collective-permute-start(f32[16,4,2]{0,2,1:T(2,128)S(1)} %bitcast.88), channel_id=1, source_target_pairs={{0,12},{4,8},{8,4},{12,0},{1,13},{5,9},{9,5},{13,1},{2,14},{6,10},... | collective-permute-start | bytes 1544 | tf_op jit(solution)/shard_map/ppermute | solution.py:104
  14.8 7.5 %collective-permute-start.4 = (f32[16,4,2]{0,2,1:T(2,128)S(1)}, f32[16,4,2]{0,2,1:T(2,128)S(1)}, u32[]{:S(2)}, u32[]{:S(2)}) collective-permute-start(f32[16,4,2]{0,2,1:T(2,128)S(1)} %bitcast.89), channel_id=1, source_target_pairs={{0,8},{4,12},{8,0},{12,4},{1,9},{5,13},{9,1},{13,5},{2,10},{6,14},... | collective-permute-start | bytes 1544 | tf_op jit(solution)/shard_map/ppermute | solution.py:104
  14.8 7.5 %collective-permute-start.3 = (f32[16,4,2]{0,2,1:T(2,128)S(1)}, f32[16,4,2]{0,2,1:T(2,128)S(1)}, u32[]{:S(2)}, u32[]{:S(2)}) collective-permute-start(f32[16,4,2]{0,2,1:T(2,128)S(1)} %bitcast.90), channel_id=1, source_target_pairs={{0,4},{4,0},{8,12},{12,8},{1,5},{5,1},{9,13},{13,9},{2,6},{6,2},{1... | collective-permute-start | bytes 1544 | tf_op jit(solution)/shard_map/ppermute | solution.py:104
  17.2 13.7 %copy-start.3 = (bf16[448]{0:T(512)(128)(2,1)S(1)}, bf16[448]{0:T(512)(128)(2,1)}, u32[]{:S(2)}) copy-start(bf16[448]{0:T(512)(128)(2,1)} %param.18) | copy-start | bytes 2692
  17.2 16.1 %copy-start.1 = (bf16[32,448]{1,0:T(8,128)(2,1)S(1)}, bf16[32,448]{1,0:T(8,128)(2,1)}, u32[]{:S(2)}) copy-start(bf16[32,448]{1,0:T(8,128)(2,1)} %param.15) | copy-start | bytes 86020
  17.2 16.1 %copy-start.2 = (bf16[448]{0:T(512)(128)(2,1)S(1)}, bf16[448]{0:T(512)(128)(2,1)}, u32[]{:S(2)}) copy-start(bf16[448]{0:T(512)(128)(2,1)} %param.16) | copy-start | bytes 2692
  17.9 6.1 %collective-permute-start.8 = (bf16[16,4,2,256]{3,0,2,1:T(8,128)(2,1)S(1)}, bf16[16,4,2,256]{3,0,2,1:T(8,128)(2,1)S(1)}, u32[]{:S(2)}, u32[]{:S(2)}) collective-permute-start(bf16[16,4,2,256]{3,0,2,1:T(8,128)(2,1)S(1)} %fusion.16), channel_id=1, source_target_pairs={{0,12},{4,8},{8,4},{12,0},{1,13},{5,9},{9,5},{13,1},{2,14},{6,10},... | collective-permute-start | bytes 196616 | tf_op jit(solution)/shard_map/ppermute | solution.py:104
  19.9 5.4 %collective-permute-start.7 = (bf16[16,4,2,256]{3,0,2,1:T(8,128)(2,1)S(1)}, bf16[16,4,2,256]{3,0,2,1:T(8,128)(2,1)S(1)}, u32[]{:S(2)}, u32[]{:S(2)}) collective-permute-start(bf16[16,4,2,256]{3,0,2,1:T(8,128)(2,1)S(1)} %fusion.16), channel_id=1, source_target_pairs={{0,8},{4,12},{8,0},{12,4},{1,9},{5,13},{9,1},{13,5},{2,10},{6,14},... | collective-permute-start | bytes 196616 | tf_op jit(solution)/shard_map/ppermute | solution.py:104
  20.0 5.4 %collective-permute-start.6 = (bf16[16,4,2,256]{3,0,2,1:T(8,128)(2,1)S(1)}, bf16[16,4,2,256]{3,0,2,1:T(8,128)(2,1)S(1)}, u32[]{:S(2)}, u32[]{:S(2)}) collective-permute-start(bf16[16,4,2,256]{3,0,2,1:T(8,128)(2,1)S(1)} %fusion.16), channel_id=1, source_target_pairs={{0,4},{4,0},{8,12},{12,8},{1,5},{5,1},{9,13},{13,9},{2,6},{6,2},{1... | collective-permute-start | bytes 196616 | tf_op jit(solution)/shard_map/ppermute | solution.py:104
  25.6 1.3 %collective-permute-start.9 = (bf16[16,2048]{1,0:T(8,128)(2,1)S(1)}, bf16[16,2048]{1,0:T(8,128)(2,1)S(1)}, u32[]{:S(2)}, u32[]{:S(2)}) collective-permute-start(bf16[16,2048]{1,0:T(8,128)(2,1)S(1)} %reshape.94), channel_id=1, source_target_pairs={{0,1},{1,0},{2,3},{3,2},{4,5},{5,4},{6,7},{7,6},{8,9},{9,8},{10,11... | collective-permute-start | bytes 196616 | tf_op jit(solution)/shard_map/ppermute | solution.py:104
  29.3 4.0 %collective-permute-start.10 = (bf16[32,448]{1,0:T(8,128)(2,1)S(1)}, bf16[32,448]{1,0:T(8,128)(2,1)S(1)}, u32[]{:S(2)}, u32[]{:S(2)}) collective-permute-start(bf16[32,448]{1,0:T(8,128)(2,1)S(1)} %convolution_convert_fusion), channel_id=1, source_target_pairs={{0,2},{2,0},{1,3},{3,1},{4,6},{6,4},{5,7},{7,5},{8,10},{10,8},{9,1... | collective-permute-start | bytes 86024 | tf_op jit(solution)/shard_map/ppermute | solution.py:104
  34.1 12.4 %collective-permute-start.12 = (bf16[32,448]{1,0:T(8,128)(2,1)S(1)}, bf16[32,448]{1,0:T(8,128)(2,1)S(1)}, u32[]{:S(2)}, u32[]{:S(2)}) collective-permute-start(bf16[32,448]{1,0:T(8,128)(2,1)S(1)} %get-tuple-element.14), channel_id=1, source_target_pairs={{0,8},{4,12},{10,2},{14,6},{1,9},{5,13},{11,3},{15,7},{16,24},{20,... | collective-permute-start | bytes 86024 | tf_op jit(solution)/shard_map/ppermute | solution.py:183
  37.7 10.1 %collective-permute-start.13 = (bf16[32,448]{1,0:T(8,128)(2,1)S(1)}, bf16[32,448]{1,0:T(8,128)(2,1)S(1)}, u32[]{:S(2)}, u32[]{:S(2)}) collective-permute-start(bf16[32,448]{1,0:T(8,128)(2,1)S(1)} %get-tuple-element.14), channel_id=1, source_target_pairs={{0,12},{4,8},{10,6},{14,2},{1,13},{5,9},{11,7},{15,3},{16,28},{20,... | collective-permute-start | bytes 86024 | tf_op jit(solution)/shard_map/ppermute | solution.py:183
  39.3 8.5 %collective-permute-start.11 = (bf16[32,448]{1,0:T(8,128)(2,1)S(1)}, bf16[32,448]{1,0:T(8,128)(2,1)S(1)}, u32[]{:S(2)}, u32[]{:S(2)}) collective-permute-start(bf16[32,448]{1,0:T(8,128)(2,1)S(1)} %get-tuple-element.14), channel_id=1, source_target_pairs={{0,4},{4,0},{10,14},{14,10},{1,5},{5,1},{11,15},{15,11},{16,20},{2... | collective-permute-start | bytes 86024 | tf_op jit(solution)/shard_map/ppermute | solution.py:183
  41.8 6.1 %collective-permute-start.16 = (f32[32]{0:T(128)S(1)}, f32[32]{0:T(128)S(1)}, u32[]{:S(2)}, u32[]{:S(2)}) collective-permute-start(f32[32]{0:T(128)S(1)} %get-tuple-element.13), channel_id=1, source_target_pairs={{0,4},{4,0},{10,14},{14,10},{1,5},{5,1},{11,15},{15,11},{16,20},{2... | collective-permute-start | bytes 392 | tf_op jit(solution)/shard_map/ppermute | solution.py:183
  45.2 2.8 %collective-permute-start.17 = (f32[32]{0:T(128)S(1)}, f32[32]{0:T(128)S(1)}, u32[]{:S(2)}, u32[]{:S(2)}) collective-permute-start(f32[32]{0:T(128)S(1)} %get-tuple-element.13), channel_id=1, source_target_pairs={{0,8},{4,12},{10,2},{14,6},{1,9},{5,13},{11,3},{15,7},{16,24},{20,... | collective-permute-start | bytes 392 | tf_op jit(solution)/shard_map/ppermute | solution.py:183
  46.5 2.6 %collective-permute-start.18 = (f32[32]{0:T(128)S(1)}, f32[32]{0:T(128)S(1)}, u32[]{:S(2)}, u32[]{:S(2)}) collective-permute-start(f32[32]{0:T(128)S(1)} %get-tuple-element.13), channel_id=1, source_target_pairs={{0,12},{4,8},{10,6},{14,2},{1,13},{5,9},{11,7},{15,3},{16,28},{20,... | collective-permute-start | bytes 392 | tf_op jit(solution)/shard_map/ppermute | solution.py:183
  47.9 5.9 %collective-permute-start.14 = (bf16[2,32,448]{2,1,0:T(8,128)(2,1)S(1)}, bf16[2,32,448]{2,1,0:T(8,128)(2,1)S(1)}, u32[]{:S(2)}, u32[]{:S(2)}) collective-permute-start(bf16[2,32,448]{2,1,0:T(8,128)(2,1)S(1)} %pad_maximum_fusion.1), channel_id=1, source_target_pairs={{0,1},{1,0},{2,3},{3,2},{4,5},{5,4},{6,7},{7,6},{8,9},{9,8},{10,11... | collective-permute-start | bytes 172040 | tf_op jit(solution)/shard_map/ppermute | solution.py:104
  49.1 1.1 %collective-permute-start.19 = (f32[32]{0:T(128)S(1)}, f32[32]{0:T(128)S(1)}, u32[]{:S(2)}, u32[]{:S(2)}) collective-permute-start(f32[32]{0:T(128)S(1)} %fusion.45), channel_id=1, source_target_pairs={{0,1},{1,0},{2,3},{3,2},{4,5},{5,4},{6,7},{7,6},{8,9},{9,8},{10,11... | collective-permute-start | bytes 392 | tf_op jit(solution)/shard_map/ppermute | solution.py:104
  50.2 14.0 %collective-permute-start.20 = (f32[32]{0:T(128)S(1)}, f32[32]{0:T(128)S(1)}, u32[]{:S(2)}, u32[]{:S(2)}) collective-permute-start(f32[32]{0:T(128)S(1)} %add.124), channel_id=1, source_target_pairs={{0,2},{2,0},{1,3},{3,1},{4,6},{6,4},{5,7},{7,5},{8,10},{10,8},{9,1... | collective-permute-start | bytes 392 | tf_op jit(solution)/shard_map/ppermute | solution.py:104
  58.1 6.2 %collective-permute-start.21 = (bf16[32,1792]{1,0:T(8,128)(2,1)S(1)}, bf16[32,1792]{1,0:T(8,128)(2,1)S(1)}, u32[]{:S(2)}, u32[]{:S(2)}) collective-permute-start(bf16[32,1792]{1,0:T(8,128)(2,1)S(1)} %get-tuple-element.28), channel_id=1, source_target_pairs={{0,2},{2,0},{1,3},{3,1},{4,6},{6,4},{5,7},{7,5},{8,10},{10,8},{9,1... | collective-permute-start | bytes 344072 | tf_op jit(solution)/shard_map/ppermute | solution.py:104
  62.2 5.0 %collective-permute-start.15 = (bf16[32,1792]{1,0:T(8,128)(2,1)S(1)}, bf16[32,1792]{1,0:T(8,128)(2,1)S(1)}, u32[]{:S(2)}, u32[]{:S(2)}) collective-permute-start(bf16[32,1792]{1,0:T(8,128)(2,1)S(1)} %get-tuple-element.30), channel_id=1, source_target_pairs={{0,2},{2,0},{1,3},{3,1},{4,6},{6,4},{5,7},{7,5},{8,10},{10,8},{9,1... | collective-permute-start | bytes 344072 | tf_op jit(solution)/shard_map/ppermute | solution.py:104
  73.0 1.3 %collective-permute-start.22 = (bf16[4,4,1792]{2,1,0:T(4,128)(2,1)S(1)}, bf16[4,4,1792]{2,1,0:T(4,128)(2,1)S(1)}, u32[]{:S(2)}, u32[]{:S(2)}) collective-permute-start(bf16[4,4,1792]{2,1,0:T(4,128)(2,1)S(1)} %fusion.39), channel_id=1, source_target_pairs={{0,1},{1,0},{2,3},{3,2},{4,5},{5,4},{6,7},{7,6},{8,9},{9,8},{10,11... | collective-permute-start | bytes 172040 | tf_op jit(solution)/shard_map/ppermute | solution.py:104
  75.3 5.6 %collective-permute-start.25 = (bf16[4,1792]{1,0:T(4,128)(2,1)S(1)}, bf16[4,1792]{1,0:T(4,128)(2,1)S(1)}, u32[]{:S(2)}, u32[]{:S(2)}) collective-permute-start(bf16[4,1792]{1,0:T(4,128)(2,1)S(1)} %get-tuple-element.21), channel_id=1, source_target_pairs={{0,12},{4,8},{8,4},{12,0},{1,13},{5,9},{9,5},{13,1},{2,14},{6,10},... | collective-permute-start | bytes 43016 | tf_op jit(solution)/shard_map/ppermute | solution.py:104
  77.7 4.6 %collective-permute-start.24 = (bf16[4,1792]{1,0:T(4,128)(2,1)S(1)}, bf16[4,1792]{1,0:T(4,128)(2,1)S(1)}, u32[]{:S(2)}, u32[]{:S(2)}) collective-permute-start(bf16[4,1792]{1,0:T(4,128)(2,1)S(1)} %get-tuple-element.22), channel_id=1, source_target_pairs={{0,8},{4,12},{8,0},{12,4},{1,9},{5,13},{9,1},{13,5},{2,10},{6,14},... | collective-permute-start | bytes 43016 | tf_op jit(solution)/shard_map/ppermute | solution.py:104
  77.7 4.6 %collective-permute-start.23 = (bf16[4,1792]{1,0:T(4,128)(2,1)S(1)}, bf16[4,1792]{1,0:T(4,128)(2,1)S(1)}, u32[]{:S(2)}, u32[]{:S(2)}) collective-permute-start(bf16[4,1792]{1,0:T(4,128)(2,1)S(1)} %get-tuple-element.20), channel_id=1, source_target_pairs={{0,4},{4,0},{8,12},{12,8},{1,5},{5,1},{9,13},{13,9},{2,6},{6,2},{1... | collective-permute-start | bytes 43016 | tf_op jit(solution)/shard_map/ppermute | solution.py:104

commit v2 on v1

--- a/solution.py
+++ b/solution.py
@@ -1,6 +1,8 @@
 import jax
 import jax.numpy as jnp
 from jax import lax
+from jax.experimental import pallas as pl
+from jax.experimental.pallas import tpu as pltpu
 from jax.sharding import PartitionSpec as P
 
 LEN = 128
@@ -100,12 +102,75 @@
     return (stream, (down_out * keep_own).astype(BF))
 
 
+VM = pl.BlockSpec(memory_space=pltpu.VMEM)
+SM = pl.BlockSpec(memory_space=pltpu.SMEM)
+ANY = pl.BlockSpec(memory_space=pl.ANY)
+MIB = 1 << 20
+
+
 def hop(value, axis, size, step):
     return lax.ppermute(value, axis, [(i, i ^ step) for i in range(size)])
 
 
 def by_index(pieces, at):
     return [lax.select_n(at ^ k, *pieces) for k in range(len(pieces))]
+
+
+def kernel(body, name, outs, specs, args, limit=8, flops=0):
+    size = sum(a.size * a.dtype.itemsize for a in list(args) + list(outs))
+    return pl.pallas_call(
+        body,
+        out_shape=outs,
+        in_specs=specs,
+        out_specs=[VM] * len(outs),
+        compiler_params=pltpu.CompilerParams(vmem_limit_bytes=limit * MIB),
+        cost_estimate=pl.CostEstimate(flops=flops, bytes_accessed=size, transcendentals=0),
+        name=name,
+    )(*args)
+
+
+def fetch(after, arrays, name):
+    n = len(arrays)
+
+    def body(*refs):
+        sources, targets, sems = refs[1 : 1 + n], refs[1 + n : 1 + 2 * n], refs[1 + 2 * n]
+        copies = [
+            pltpu.make_async_copy(sources[i], targets[i], sems.at[i]) for i in range(n)
+        ]
+        for copy in copies:
+            copy.start()
+        for copy in copies:
+            copy.wait()
+
+    size = sum(a.size * a.dtype.itemsize for a in arrays)
+    return pl.pallas_call(
+        body,
+        out_shape=[jax.ShapeDtypeStruct(a.shape, a.dtype) for a in arrays],
+        in_specs=[ANY] * (1 + n),
+        out_specs=[VM] * n,
+        scratch_shapes=[pltpu.SemaphoreType.DMA((n,))],
+        compiler_params=pltpu.CompilerParams(vmem_limit_bytes=MIB),
+        cost_estimate=pl.CostEstimate(flops=0, bytes_accessed=2 * size, transcendentals=0),
+        name=name,
+    )(after, *[pltpu.with_memory_space_constraint(a, pltpu.HBM) for a in arrays])
+
+
+def parts_of(value, count):
+    out = []
+    for _ in range(count):
+        part = lax.reduce_precision(value, 8, 7)
+        out.append(part.astype(BF))
+        value = value - part
+    return out
+
+
+def split_in(value, count):
+    out = []
+    for _ in range(count):
+        part = value.astype(BF)
+        out.append(part)
+        value = value - part.astype(F32)
+    return out
 
 
 def shards_direct(
@@ -131,13 +196,18 @@
     width = dec_state.shape[1]
     features = width * blks * 2
     half = blks // head_parts
+    hidden_width, out_width = gate_weight.shape[1], down_weight.shape[1]
+    toks = tok_dev * blks
+    tokens = toks * 2
+    place = jnp.stack([row, blk, head]).astype(jnp.int32)
+    sds = jax.ShapeDtypeStruct
 
     pieces = [queries] + [hop(queries, "blk", blks, s) for s in range(1, blks)]
+    keys_near, proj_near = fetch(queries, [src_keys, out_weight.T], "fetch_keys_proj")
     q_all = jnp.concatenate(by_index(pieces, blk), axis=0)
-    rows_in = q_all.shape[0]
-    grouped = q_all.reshape(rows_in, kv_local, group_size, head_size)
+    grouped = q_all.reshape(toks, kv_local, group_size, head_size)
     scores = (
-        jnp.einsum("tgjd,kgd->tgjk", grouped, src_keys, preferred_element_type=F32) * score_scale
+        jnp.einsum("tgjd,kgd->tgjk", grouped, keys_near, preferred_element_type=F32) * score_scale
     )
     peak = jnp.max(scores, axis=3)
     weights = jnp.exp(scores - peak[..., None])
@@ -146,69 +216,205 @@
         "tgjk,kgd->tgjd", weights.astype(BF), src_values, preferred_element_type=F32
     )
     partial = (numerator / totals[..., None]).astype(BF)
-    level = peak + jnp.log(totals)
-    partials = [partial] + [hop(partial, "blk", blks, s) for s in range(1, blks)]
-    levels = [level] + [hop(level, "blk", blks, s) for s in range(1, blks)]
-    top = levels[0]
-    for one in levels[1:]:
-        top = jnp.maximum(top, one)
-    shares = [jnp.exp(one - top) for one in levels]
-    total = sum(shares)
-    attn = sum(
-        (share / total)[..., None] * part.astype(F32) for share, part in zip(shares, partials)
-    )
-    attn = attn.astype(BF).reshape(rows_in, local_heads * head_size)
+    partial = partial.transpose(1, 2, 0, 3).reshape(local_heads * toks, head_size)
+    level = (peak + jnp.log(totals)).reshape(toks, local_heads)
+    side = jnp.concatenate(parts_of(level, 3), axis=1)
+    side = jnp.pad(side, ((0, 0), (0, head_size - side.shape[1])))
+    note = jnp.concatenate([partial, side], axis=0)
+    notes = [note] + [hop(note, "blk", blks, s) for s in range(1, blks)]
+    (gate_near,) = fetch(note, [gate_weight], "fetch_gate")
+
+    def combine(*refs):
+        ins, out = refs[:-1], refs[-1]
+        base = local_heads * toks
+        levels = []
+        for ref in ins:
+            side = ref[base : base + toks, :].astype(F32)
+            levels.append(
+                side[:, :local_heads]
+                + side[:, local_heads : 2 * local_heads]
+                + side[:, 2 * local_heads : 3 * local_heads]
+            )
+        top = levels[0]
+        for one in levels[1:]:
+            top = jnp.maximum(top, one)
+        shares = [jnp.exp(one - top) for one in levels]
+        total = shares[0]
+        for one in shares[1:]:
+            total = total + one
+        shares = [one / total for one in shares]
+        for h in range(local_heads):
+            acc = None
+            for share, ref in zip(shares, ins):
+                term = share[:, h : h + 1] * ref[h * toks : (h + 1) * toks, :].astype(F32)
+                acc = term if acc is None else acc + term
+            out[:, h * head_size : (h + 1) * head_size] = acc.astype(BF)
+
+    (attn,) = kernel(
+        combine, "combine", [sds((toks, local_heads * head_size), BF)], [VM] * blks, notes
+    )
     other = hop(attn, "rows", 2, 1)
-    attn_all = jnp.stack(by_index([attn, other], row), axis=0)
-    attn_all = attn_all.reshape(2, blks, tok_dev, -1).transpose(1, 0, 2, 3)
-    tokens = rows_in * 2
-    attn_all = attn_all.reshape(tokens, -1)
-    projected = jnp.dot(attn_all, out_weight, preferred_element_type=F32).astype(BF)
-    projected = projected.astype(F32) + hop(projected, "heads", 2, 1).astype(F32)
+
+    def project(place_ref, own_ref, other_ref, weight_ref, out_ref):
+        first = place_ref[0] == 0
+        own, other = own_ref[...], other_ref[...]
+        rows = jnp.concatenate(
+            [jnp.where(first, own, other), jnp.where(first, other, own)], axis=0
+        )
+        out_ref[...] = lax.dot_general(
+            rows, weight_ref[...], (((1,), (1,)), ((), ())), preferred_element_type=F32
+        ).astype(BF)
+
+    (proj,) = kernel(
+        project,
+        "project",
+        [sds((tokens, width), BF)],
+        [SM, VM, VM, VM],
+        [place, attn, other, proj_near],
+    )
+    proj_other = hop(proj, "heads", 2, 1)
+    (up_near,) = fetch(proj, [up_weight], "fetch_up")
+
+    def inner(value):
+        value = value.reshape((blks, 2, tok_dev) + value.shape[1:])
+        return jnp.swapaxes(value, 0, 1).reshape((tokens,) + value.shape[3:])
+
     valid_tok, masked_tok = token_masks(cand_lengths, masked_pos, tokens)
-    base_state = jnp.where(masked_tok[:, None], mask_embed[None, :], dec_state).astype(F32)
-    mid = base_state + projected
-    keep_mask = valid_tok.astype(F32)[:, None]
-    stream = (mid * keep_mask).astype(BF)
-    squares = jnp.sum(mid * mid, axis=1)
-    scaled = (mid * norm_gain.astype(F32)).astype(BF)
-
-    def spread(value):
-        got = [value]
-        for s in range(1, blks):
-            pairs = []
-            for b in range(blks):
-                h = b // half
-                pairs.append((b * head_parts + h, (b ^ s) * head_parts + h))
-            got.append(lax.ppermute(value, ("blk", "heads"), pairs))
-        return [lax.select_n(blk ^ (head * half + k), *got) for k in range(half)]
-
-    tiles, square_tiles = spread(scaled), spread(squares)
-    mine = jnp.stack(tiles, axis=0)
+    base_state = inner(jnp.where(masked_tok[:, None], mask_embed[None, :], dec_state))
+    keep_mask = valid_tok.astype(F32)
+    keep_inner = inner(keep_mask)[:, None]
+    lanes = -(-(width + 2) // 128) * 128
+
+    def middle(base_ref, keep_ref, gain_ref, own_ref, other_ref, stream_ref, note_ref):
+        mid = base_ref[...].astype(F32) + (own_ref[...].astype(F32) + other_ref[...].astype(F32))
+        stream_ref[...] = (mid * keep_ref[...]).astype(BF)
+        note_ref[:, :width] = (mid * gain_ref[...].astype(F32)).astype(BF)
+        squares = jnp.sum(mid * mid, axis=1, keepdims=True)
+        high, low = split_in(squares, 2)
+        lane = lax.broadcasted_iota(jnp.int32, (tokens, lanes - width), 1)
+        note_ref[:, width:] = jnp.where(
+            lane == 0, high.astype(F32), jnp.where(lane == 1, low.astype(F32), 0.0)
+        ).astype(BF)
+
+    stream, note = kernel(
+        middle,
+        "middle",
+        [sds((tokens, width), BF), sds((tokens, lanes), BF)],
+        [VM] * 5,
+        [base_state, keep_inner, norm_gain[None, :], proj, proj_other],
+    )
+
+    got = [note]
+    for s in range(1, blks):
+        pairs = []
+        for b in range(blks):
+            h = b // half
+            pairs.append((b * head_parts + h, (b ^ s) * head_parts + h))
+        got.append(lax.ppermute(note, ("blk", "heads"), pairs))
+    (down_near,) = fetch(note, [down_weight], "fetch_down")
+    mine = jnp.stack([lax.select_n(blk ^ (head * half + k), *got) for k in range(half)], axis=0)
     theirs = hop(mine, "rows", 2, 1)
-    pair = jnp.stack(by_index([mine, theirs], row), axis=0)
-    column_block = pair.transpose(2, 1, 0, 3).reshape(tokens, -1)
-    squares = sum(square_tiles)
-    squares = squares + hop(squares, "rows", 2, 1)
-    squares = squares + hop(squares, "heads", 2, 1)
-    inv_rms = lax.rsqrt(squares / features + EPS)[:, None]
-    gate = jnp.dot(column_block, gate_weight, preferred_element_type=F32)
-    gate = gate + hop(gate.astype(BF), "heads", 2, 1).astype(F32)
-    up = jnp.dot(column_block, up_weight, preferred_element_type=F32)
-    up = up + hop(up.astype(BF), "heads", 2, 1).astype(F32)
-    hidden = (jax.nn.gelu(gate * inv_rms, approximate=True) * (up * inv_rms)).astype(BF)
-    down = jnp.dot(hidden, down_weight, preferred_element_type=F32)
-    down = down.reshape(blks, 2, tok_dev, -1)
-    keep = lax.dynamic_index_in_dim(down, row, 1, keepdims=False)
-    away = lax.dynamic_index_in_dim(down, 1 - row, 1, keepdims=False).astype(BF)
-    keep = keep + hop(away, "rows", 2, 1).astype(F32)
-    sent = keep.astype(BF)
-    own = lax.dynamic_index_in_dim(keep, blk, 0, keepdims=False)
+
+    def column_block(place_ref, mine_ref, theirs_ref):
+        first = place_ref[0] == 0
+        tiles = []
+        for k in range(half):
+            own, other = mine_ref[k], theirs_ref[k]
+            tiles += [jnp.where(first, own, other), jnp.where(first, other, own)]
+        return tiles
+
+    rows_in = gate_weight.shape[0]
+
+    def gates(place_ref, mine_ref, theirs_ref, weight_ref, out_ref, note_ref, x_ref):
+        tiles = column_block(place_ref, mine_ref, theirs_ref)
+        squares = None
+        for j, tile in enumerate(tiles):
+            x_ref[:, j * width : (j + 1) * width] = tile[:, :width]
+            here = tile[:, width : width + 2].astype(F32)
+            squares = here if squares is None else squares + here
+        squares = squares[:, 0:1] + squares[:, 1:2]
+        gate = jnp.dot(x_ref[...], weight_ref[...], preferred_element_type=F32)
+        out_ref[:, :hidden_width] = gate
+        note_ref[:, :hidden_width] = gate.astype(BF)
+        high, low = split_in(squares, 2)
+        lane = lax.broadcasted_iota(jnp.int32, (tokens, 128), 1)
+        out_ref[:, hidden_width:] = jnp.where(lane == 0, squares, 0.0)
+        note_ref[:, hidden_width:] = jnp.where(
+            lane == 0, high.astype(F32), jnp.where(lane == 1, low.astype(F32), 0.0)
+        ).astype(BF)
+
+    long_width = hidden_width + 128
+    gate, gate_note, column = kernel(
+        gates,
+        "gates",
+        [sds((tokens, long_width), F32), sds((tokens, long_width), BF), sds((tokens, rows_in), BF)],
+        [SM, VM, VM, VM],
+        [place, mine, theirs, gate_near],
+    )
+    gate_other = hop(gate_note, "heads", 2, 1)
+
+    def ups(x_ref, weight_ref, out_ref, note_ref):
+        up = jnp.dot(x_ref[...], weight_ref[...], preferred_element_type=F32)
+        out_ref[...] = up
+        note_ref[...] = up.astype(BF)
+
+    up, up_note = kernel(
+        ups,
+        "ups",
+        [sds((tokens, hidden_width), F32), sds((tokens, hidden_width), BF)],
+        [VM, VM],
+        [column, up_near],
+        flops=2 * tokens * rows_in * hidden_width,
+    )
+    up_other = hop(up_note, "heads", 2, 1)
+
+    def downs(
+        place_ref, gate_ref, gate_other_ref, up_ref, up_other_ref, weight_ref, keep_ref, away_ref
+    ):
+        other = gate_other_ref[:, hidden_width:].astype(F32)
+        squares = gate_ref[:, hidden_width : hidden_width + 1] + other[:, 0:1] + other[:, 1:2]
+        inv_rms = lax.rsqrt(squares / features + EPS)
+        gate = (gate_ref[:, :hidden_width] + gate_other_ref[:, :hidden_width].astype(F32)) * inv_rms
+        up = (up_ref[...] + up_other_ref[...].astype(F32)) * inv_rms
+        hidden = (jax.nn.gelu(gate, approximate=True) * up).astype(BF)
+        down = jnp.dot(hidden, weight_ref[...], preferred_element_type=F32)
+        first = place_ref[0] == 0
+        keep_ref[...] = jnp.where(first, down[:toks], down[toks:])
+        away_ref[...] = jnp.where(first, down[toks:], down[:toks]).astype(BF)
+
+    keep, away = kernel(
+        downs,
+        "downs",
+        [sds((toks, out_width), F32), sds((toks, out_width), BF)],
+        [SM] + [VM] * 5,
+        [place, gate, gate_other, up, up_other, down_near],
+        limit=12,
+    )
+    back = hop(away, "rows", 2, 1)
+
+    def owners(place_ref, keep_ref, back_ref, own_ref, *piece_refs):
+        total = keep_ref[...] + back_ref[...].astype(F32)
+        blocks = [total[k * tok_dev : (k + 1) * tok_dev] for k in range(blks)]
+        at = place_ref[1]
+        for s, ref in enumerate((own_ref,) + piece_refs):
+            value = blocks[0]
+            for k in range(1, blks):
+                value = jnp.where(at == (k ^ s), blocks[k], value)
+            ref[...] = value.astype(ref.dtype)
+
+    own, *sends = kernel(
+        owners,
+        "owners",
+        [sds((tok_dev, out_width), F32)] + [sds((tok_dev, out_width), BF)] * (blks - 1),
+        [SM, VM, VM],
+        [place, keep, back],
+    )
     for s in range(1, blks):
-        part = lax.dynamic_index_in_dim(sent, blk ^ s, 0, keepdims=False)
-        own = own + hop(part, "blk", blks, s).astype(F32)
+        own = own + hop(sends[s - 1], "blk", blks, s).astype(F32)
     keep_own = lax.dynamic_slice_in_dim(keep_mask, (blk * 2 + row) * tok_dev, tok_dev, 0)
-    return (stream, (own * keep_own).astype(BF))
+    branch = (own * keep_own[:, None]).astype(BF)
+    stream = stream.reshape(2, blks, tok_dev, width).swapaxes(0, 1).reshape(tokens, width)
+    return (stream, branch)
 
 
 def solution(mesh):

time: 83.5 us -> 73.3 us (0.88)
  Pallas kernels: 0 us -> 18 us
  starting transfers between devices: 40.1 us -> 26.4 us
  matrix products: 16.1 us -> 2.96 us
  local copies, waits for them, and re-layouts: 2.29 us -> 5.44 us
  waiting for transfers between devices: 18.3 us -> 15.7 us
  other arithmetic: 4.54 us -> 2.76 us
    pallas_call x0 -> x11, Pallas kernels: none -> 18 us  [the longest x4 11 us: fetch(): pl.pallas_call(body, out_shape=[jax.ShapeDtypeStruct(a.shape, a.dtype) fo...]
    dot_general x5 -> x1, matrix products: 15.4 us -> 1.13 us  [shards_direct(): jnp.einsum('tgjd,kgd->tgjk', grouped, keys_near, preferred_element_type=F32)]
    ppermute x20 -> x15, starting transfers between devices: 26.4 us -> 18.4 us  [hop(): return lax.ppermute(value, axis, [(i, i ^ step) for i in range(size)])]
    ppermute x6 -> x3, starting transfers between devices: 13.6 us -> 7.93 us  [shards_direct(): got.append(lax.ppermute(note, ('blk', 'heads'), pairs))]
    ppermute x20 -> x15, waiting for transfers between devices: 17.2 us -> 12.4 us  [hop(): return lax.ppermute(value, axis, [(i, i ^ step) for i in range(size)])]
    unnamed x10 -> x14, local copies, waits for them, and re-layouts: 0.03 us -> 4.39 us
    ppermute x6 -> x3, waiting for transfers between devices: 1.13 us -> 3.29 us  [shards_direct(): got.append(lax.ppermute(note, ('blk', 'heads'), pairs))]
    dot_general x1, matrix products: 0.69 us -> 1.84 us  [shards_direct(): jnp.einsum('tgjk,kgd->tgjd', weights.astype(BF), src_values, preferred_el...]
  transfers between devices with their start and end apart: 26 -> 18, of which waited for: 11 -> 10; matrix products, arithmetic and copies ran while one was open for 12% -> 4% of each run, Pallas kernels for 0% -> 17%
where the time goes in v2:
time: 73.3 us; the launch traced here: 72.8 us
  starting transfers between devices  26.4 us (36%)
  Pallas kernels  18 us (25%)
  waiting for transfers between devices  15.7 us (21%)
  local copies, waits for them, and re-layouts  5.44 us (7%)
  matrix products  2.96 us (4%)
  other arithmetic  2.76 us (4%)
  between operations  1.62 us (2%)
    ppermute x15, starting transfers between devices, hop(): return lax.ppermute(value, axis, [(i, i ^ step) for i in range(size)])  18.4 us
    ppermute x15, waiting for transfers between devices, hop(): return lax.ppermute(value, axis, [(i, i ^ step) for i in range(size)])  12.4 us
    pallas_call x4, Pallas kernels, fetch(): pl.pallas_call(body, out_shape=[jax.ShapeDtypeStruct(a.shape, a.dtype) fo...  11 us
    ppermute x3, starting transfers between devices, shards_direct(): got.append(lax.ppermute(note, ('blk', 'heads'), pairs))  7.93 us
    pallas_call x7, Pallas kernels, kernel(): pl.pallas_call(body, out_shape=outs, in_specs=specs, out_specs=[VM] * len...  7.01 us
    unnamed x14, local copies, waits for them, and re-layouts  4.39 us
    ppermute x3, waiting for transfers between devices, shards_direct(): got.append(lax.ppermute(note, ('blk', 'heads'), pairs))  3.29 us
    dot_general x1, matrix products, shards_direct(): jnp.einsum('tgjk,kgd->tgjd', weights.astype(BF), src_values, preferred_el...  1.84 us
  transfers between devices with their start and end apart: 18, of which 10 were waited for; matrix products, arithmetic and copies ran while one was open for 4% of the time, Pallas kernels for 17%

profile of v2, /device:TPU:0, one launch (start us, length us, event | category | flops | bytes accessed | tf_op | source)
XLA Modules:
  0.0 72.8 jit_solution(1341769921836627712)
XLA Ops:
  0.7 4.1 %collective-permute-start.1 = (bf16[4,8,256]{2,1,0:T(8,128)(2,1)}, bf16[4,8,256]{2,1,0:T(8,128)(2,1)S(1)}, u32[]{:S(2)}, u32[]{:S(2)}) collective-permute-start(bf16[4,8,256]{2,1,0:T(8,128)(2,1)} %refs_0_.1), channel_id=1, source_target_pairs={{0,8},{4,12},{8,0},{12,4},{1,9},{5,13},{9,1},{13,5},{2,10},{6,14},... | collective-permute-start | bytes 49160 | tf_op jit(solution)/shard_map/ppermute | solution.py:112
  4.8 1.3 %collective-permute-start.2 = (bf16[4,8,256]{2,1,0:T(8,128)(2,1)}, bf16[4,8,256]{2,1,0:T(8,128)(2,1)S(1)}, u32[]{:S(2)}, u32[]{:S(2)}) collective-permute-start(bf16[4,8,256]{2,1,0:T(8,128)(2,1)} %refs_0_.1), channel_id=1, source_target_pairs={{0,12},{4,8},{8,4},{12,0},{1,13},{5,9},{9,5},{13,1},{2,14},{6,10},... | collective-permute-start | bytes 49160 | tf_op jit(solution)/shard_map/ppermute | solution.py:112
  6.1 0.2 collective-permute-start
  6.3 0.7 %fusion.23 = pred[128]{0:T(512)(128)(4,1)S(1)} fusion(s32[48]{0:T(128)} %bitcast.49), kind=kLoop, calls=%fused_computation.25 | loop fusion | flops 12160 | bytes 320 | tf_op jit(solution)/shard_map/reduce_or | solution.py:19
  7.1 0.8 %broadcast_select_fusion = bf16[32,448]{1,0:T(8,128)(2,1)S(1)} fusion(bf16[32,448]{1,0:T(8,128)(2,1)} %param.15, pred[32]{0:T(512)(128)(4,1)S(1)} %slice_bitcast_fusion, bf16[448]{0:T(512)(128)(2,1)} %param.16), kind=kLoop, calls=%fused_computation.19 | loop fusion | flops 14336 | bytes 58272 | tf_op jit(solution)/shard_map/jit(_where)/select_n | solution.py:283
  7.9 0.7 copy-done.3
  8.6 2.5 %fetch_keys_proj.1 = (bf16[1536,4,256]{2,1,0:T(4,128)(2,1)S(1)}, bf16[448,2048]{1,0:T(8,128)(2,1)S(1)}) custom-call(bf16[4,8,256]{2,1,0:T(8,128)(2,1)S(1)} %copy-done.3, bf16[1536,4,256]{2,1,0:T(4,128)(2,1)} %refs_1_.4, bf16[448,2048]{1,0:T(8,128)(2,1)} %bitcast.39), custom_call_target="tpu_custom_call" | custom-call | bytes 9961472 | tf_op jit(solution)/shard_map/fetch_keys_proj/pallas_call | solution.py:146
  11.1 1.2 %copy-done.1 = bf16[448,2048]{1,0:T(8,128)(2,1)} copy-done((bf16[448,2048]{1,0:T(8,128)(2,1)}, bf16[448,2048]{1,0:T(8,128)(2,1)S(1)}, u32[]{:S(2)}) %copy-start.1) | copy-done | bytes 1835032
  12.5 1.1 %fusion.34 = (f32[16,4,2]{0,2,1:T(2,128)S(1)}, f32[16,4,2,1536]{3,0,2,1:T(8,128)S(1)}) fusion(bf16[16,4,2,256]{3,0,2,1:T(8,128)(2,1)S(1)} %bitcast.43, bf16[1536,4,256,1]{2,1,0,3:T(4,128)(2,1)S(1)} %bitcast.38), kind=kOutput, calls=%fused_computation.49 | convolution fusion | flops 101056384 | bytes 3998208 | tf_op jit(solution)/shard_map/tgjd,kgd->tgjk/dot_general | solution.py:210
  13.6 0.9 %copy-done.5 = f32[16,4,2,1536]{3,0,2,1:T(8,128)} copy-done((f32[16,4,2,1536]{3,0,2,1:T(8,128)}, f32[16,4,2,1536]{3,0,2,1:T(8,128)S(1)}, u32[]{:S(2)}) %copy-start.5) | copy-done | bytes 786456
  14.5 0.2 fusion.19
  14.9 1.8 %fusion.16 = bf16[4,2,16,256]{3,2,1,0:T(8,128)(2,1)S(1)} fusion(bf16[1536,4,256,1]{2,1,0,3:T(4,128)(2,1)S(1)} %bitcast.37, f32[16,4,2,1536]{3,0,2,1:T(8,128)} %copy-done.5, f32[16,4,2]{0,2,1:T(2,128)S(1)} %get-tuple-element.41, f32[4,2,16]{2,1,0:T(2,128)S(1)} %bitcast.48), kind=kOutput, calls=%fused_computation.8 | convolution fusion | flops 101122048 | bytes 3998720 | tf_op jit(solution)/shard_map/tgjk,kgd->tgjd/dot_general | solution.py:215
  16.8 0.1 fusion.33
  16.9 1.9 %collective-permute-start.3 = (bf16[144,256]{1,0:T(8,128)(2,1)S(1)}, bf16[144,256]{1,0:T(8,128)(2,1)S(1)}, u32[]{:S(2)}, u32[]{:S(2)}) collective-permute-start(bf16[144,256]{1,0:T(8,128)(2,1)S(1)} %pad_maximum_fusion.refs_0_), channel_id=1, source_target_pairs={{0,4},{4,0},{8,12},{12,8},{1,5},{5,1},{9,13},{13,9},{2,6},{6,2},{1... | collective-permute-start | bytes 221192 | tf_op jit(solution)/shard_map/ppermute | solution.py:112
  18.7 1.7 %collective-permute-start.4 = (bf16[144,256]{1,0:T(8,128)(2,1)S(1)}, bf16[144,256]{1,0:T(8,128)(2,1)S(1)}, u32[]{:S(2)}, u32[]{:S(2)}) collective-permute-start(bf16[144,256]{1,0:T(8,128)(2,1)S(1)} %pad_maximum_fusion.refs_0_), channel_id=1, source_target_pairs={{0,8},{4,12},{8,0},{12,4},{1,9},{5,13},{9,1},{13,5},{2,10},{6,14},... | collective-permute-start | bytes 221192 | tf_op jit(solution)/shard_map/ppermute | solution.py:112
  20.4 0.9 %collective-permute-start.5 = (bf16[144,256]{1,0:T(8,128)(2,1)S(1)}, bf16[144,256]{1,0:T(8,128)(2,1)S(1)}, u32[]{:S(2)}, u32[]{:S(2)}) collective-permute-start(bf16[144,256]{1,0:T(8,128)(2,1)S(1)} %pad_maximum_fusion.refs_0_), channel_id=1, source_target_pairs={{0,12},{4,8},{8,4},{12,0},{1,13},{5,9},{9,5},{13,1},{2,14},{6,10},... | collective-permute-start | bytes 221192 | tf_op jit(solution)/shard_map/ppermute | solution.py:112
  22.1 3.6 %collective-permute-done.4.refs_2_ = bf16[144,256]{1,0:T(8,128)(2,1)S(1)} collective-permute-done((bf16[144,256]{1,0:T(8,128)(2,1)S(1)}, bf16[144,256]{1,0:T(8,128)(2,1)S(1)}, u32[]{:S(2)}, u32[]{:S(2)}) %collective-permute-start.4) | collective-permute-done | bytes 73760 | tf_op jit(solution)/shard_map/ppermute | solution.py:112
  25.7 1.0 %collective-permute-done.5.refs_3_ = bf16[144,256]{1,0:T(8,128)(2,1)S(1)} collective-permute-done((bf16[144,256]{1,0:T(8,128)(2,1)S(1)}, bf16[144,256]{1,0:T(8,128)(2,1)S(1)}, u32[]{:S(2)}, u32[]{:S(2)}) %collective-permute-start.5) | collective-permute-done | bytes 73760 | tf_op jit(solution)/shard_map/ppermute | solution.py:112
  26.7 0.2 combine.1.own_ref
  27.0 0.1 pad_add_fusion.place_ref
  27.1 1.2 %collective-permute-done.6.other_ref = bf16[16,2048]{1,0:T(8,128)(2,1)S(1)} collective-permute-done((bf16[16,2048]{1,0:T(8,128)(2,1)S(1)}, bf16[16,2048]{1,0:T(8,128)(2,1)S(1)}, u32[]{:S(2)}, u32[]{:S(2)}) %collective-permute-start.6) | collective-permute-done | bytes 65568 | tf_op jit(solution)/shard_map/ppermute | solution.py:112
  28.3 1.5 %copy-done.2 = bf16[448,2048]{1,0:T(8,128)(2,1)S(1)} copy-done((bf16[448,2048]{1,0:T(8,128)(2,1)S(1)}, bf16[448,2048]{1,0:T(8,128)(2,1)}, u32[]{:S(2)}) %copy-start.2) | copy-done | bytes 1835032
  29.8 1.1 %project.1.own_ref.refs_0_ = bf16[32,448]{1,0:T(8,128)(2,1)S(1)} custom-call(s32[3]{0:T(128)S(1)} %pad_add_fusion.place_ref, bf16[16,2048]{1,0:T(8,128)(2,1)S(1)} %combine.1.own_ref, bf16[16,2048]{1,0:T(8,128)(2,1)S(1)} %collective-permute-done.6.other_ref, bf16[448,2048]{1,0:T(8,128)(2,1)S(1)} %copy-done.2), custom_call_target="tpu_custom_call" | custom-call | bytes 1994764 | tf_op jit(solution)/shard_map/project/pallas_call | solution.py:121
  30.9 1.6 %collective-permute-start.7 = (bf16[32,448]{1,0:T(8,128)(2,1)S(1)}, bf16[32,448]{1,0:T(8,128)(2,1)S(1)}, u32[]{:S(2)}, u32[]{:S(2)}) collective-permute-start(bf16[32,448]{1,0:T(8,128)(2,1)S(1)} %project.1.own_ref.refs_0_), channel_id=1, source_target_pairs={{0,2},{2,0},{1,3},{3,1},{4,6},{6,4},{5,7},{7,5},{8,10},{10,8},{9,1... | collective-permute-start | bytes 86024 | tf_op jit(solution)/shard_map/ppermute | solution.py:112
  32.6 2.3 %collective-permute-done.7.other_ref = bf16[32,448]{1,0:T(8,128)(2,1)S(1)} collective-permute-done((bf16[32,448]{1,0:T(8,128)(2,1)S(1)}, bf16[32,448]{1,0:T(8,128)(2,1)S(1)}, u32[]{:S(2)}, u32[]{:S(2)}) %collective-permute-start.7) | collective-permute-done | bytes 28704 | tf_op jit(solution)/shard_map/ppermute | solution.py:112
  34.9 0.2 middle.1
  35.1 4.1 %collective-permute-start.9 = (bf16[32,512]{1,0:T(8,128)(2,1)S(1)}, bf16[32,512]{1,0:T(8,128)(2,1)S(1)}, u32[]{:S(2)}, u32[]{:S(2)}) collective-permute-start(bf16[32,512]{1,0:T(8,128)(2,1)S(1)} %get-tuple-element.20.refs_0_), channel_id=1, source_target_pairs={{0,8},{4,12},{10,2},{14,6},{1,9},{5,13},{11,3},{15,7},{16,24},{20,... | collective-permute-start | bytes 98312 | tf_op jit(solution)/shard_map/ppermute | solution.py:313
  39.1 1.4 %collective-permute-start.10 = (bf16[32,512]{1,0:T(8,128)(2,1)S(1)}, bf16[32,512]{1,0:T(8,128)(2,1)S(1)}, u32[]{:S(2)}, u32[]{:S(2)}) collective-permute-start(bf16[32,512]{1,0:T(8,128)(2,1)S(1)} %get-tuple-element.20.refs_0_), channel_id=1, source_target_pairs={{0,12},{4,8},{10,6},{14,2},{1,13},{5,9},{11,7},{15,3},{16,28},{20,... | collective-permute-start | bytes 98312 | tf_op jit(solution)/shard_map/ppermute | solution.py:313
  40.6 2.5 %collective-permute-start.8 = (bf16[32,512]{1,0:T(8,128)(2,1)S(1)}, bf16[32,512]{1,0:T(8,128)(2,1)S(1)}, u32[]{:S(2)}, u32[]{:S(2)}) collective-permute-start(bf16[32,512]{1,0:T(8,128)(2,1)S(1)} %get-tuple-element.20.refs_0_), channel_id=1, source_target_pairs={{0,4},{4,0},{10,14},{14,10},{1,5},{5,1},{11,15},{15,11},{16,20},{2... | collective-permute-start | bytes 98312 | tf_op jit(solution)/shard_map/ppermute | solution.py:313
  43.1 3.3 %collective-permute-done.8 = bf16[32,512]{1,0:T(8,128)(2,1)S(1)} collective-permute-done((bf16[32,512]{1,0:T(8,128)(2,1)S(1)}, bf16[32,512]{1,0:T(8,128)(2,1)S(1)}, u32[]{:S(2)}, u32[]{:S(2)}) %collective-permute-start.8) | collective-permute-done | bytes 32800 | tf_op jit(solution)/shard_map/ppermute | solution.py:313
  46.5 2.8 %fetch_gate.1.weight_ref = bf16[1792,1792]{1,0:T(8,128)(2,1)S(1)} custom-call(bf16[144,256]{1,0:T(8,128)(2,1)S(1)} %pad_maximum_fusion.refs_0_, bf16[1792,1792]{1,0:T(8,128)(2,1)} %refs_1_.5), custom_call_target="tpu_custom_call" | custom-call | bytes 12845056 | tf_op jit(solution)/shard_map/fetch_gate/pallas_call | solution.py:146
  49.3 2.8 %fetch_up.1.weight_ref = bf16[1792,1792]{1,0:T(8,128)(2,1)S(1)} custom-call(bf16[32,448]{1,0:T(8,128)(2,1)S(1)} %project.1.own_ref.refs_0_, bf16[1792,1792]{1,0:T(8,128)(2,1)} %refs_1_.6), custom_call_target="tpu_custom_call" | custom-call | bytes 12845056 | tf_op jit(solution)/shard_map/fetch_up/pallas_call | solution.py:146
  52.2 1.7 %gates.1 = (f32[32,1920]{1,0:T(8,128)S(1)}, bf16[32,1920]{1,0:T(8,128)(2,1)S(1)}, bf16[32,1792]{1,0:T(8,128)(2,1)S(1)}) custom-call(s32[3]{0:T(128)S(1)} %pad_add_fusion.place_ref, bf16[2,32,512]{2,1,0:T(8,128)(2,1)S(1)} %pad_maximum_fusion.2.mine_ref, bf16[2,32,512]{2,1,0:T(8,128)(2,1)S(1)} %collective-permute-done.11.theirs_ref, ...), custom_call_target="tpu_custom_call" | custom-call | bytes 7036940 | tf_op jit(solution)/shard_map/gates/pallas_call | solution.py:121
  54.0 1.2 %ups.1 = (f32[32,1792]{1,0:T(8,128)S(1)}, bf16[32,1792]{1,0:T(8,128)(2,1)S(1)}) custom-call(bf16[32,1792]{1,0:T(8,128)(2,1)S(1)} %get-tuple-element.23.x_ref, bf16[1792,1792]{1,0:T(8,128)(2,1)S(1)} %fetch_up.1.weight_ref), custom_call_target="tpu_custom_call" | custom-call | flops 205520896 | bytes 6881280 | tf_op jit(solution)/shard_map/ups/pallas_call | solution.py:121
  55.2 2.0 %collective-permute-start.13 = (bf16[32,1792]{1,0:T(8,128)(2,1)S(1)}, bf16[32,1792]{1,0:T(8,128)(2,1)S(1)}, u32[]{:S(2)}, u32[]{:S(2)}) collective-permute-start(bf16[32,1792]{1,0:T(8,128)(2,1)S(1)} %get-tuple-element.25), channel_id=1, source_target_pairs={{0,2},{2,0},{1,3},{3,1},{4,6},{6,4},{5,7},{7,5},{8,10},{10,8},{9,1... | collective-permute-start | bytes 344072 | tf_op jit(solution)/shard_map/ppermute | solution.py:112
  57.2 2.8 %fetch_down.1.weight_ref = bf16[1792,1792]{1,0:T(8,128)(2,1)S(1)} custom-call(bf16[32,512]{1,0:T(8,128)(2,1)S(1)} %get-tuple-element.20.refs_0_, bf16[1792,1792]{1,0:T(8,128)(2,1)} %refs_1_.7), custom_call_target="tpu_custom_call" | custom-call | bytes 12845056 | tf_op jit(solution)/shard_map/fetch_down/pallas_call | solution.py:146
  60.1 2.1 %collective-permute-done.13.up_other_ref = bf16[32,1792]{1,0:T(8,128)(2,1)S(1)} collective-permute-done((bf16[32,1792]{1,0:T(8,128)(2,1)S(1)}, bf16[32,1792]{1,0:T(8,128)(2,1)S(1)}, u32[]{:S(2)}, u32[]{:S(2)}) %collective-permute-start.13) | collective-permute-done | bytes 114720 | tf_op jit(solution)/shard_map/ppermute | solution.py:112
  62.1 1.9 %downs.1 = (f32[16,1792]{1,0:T(8,128)S(1)}, bf16[16,1792]{1,0:T(8,128)(2,1)S(1)}) custom-call(s32[3]{0:T(128)S(1)} %pad_add_fusion.place_ref, f32[32,1920]{1,0:T(8,128)S(1)} %get-tuple-element.21.gate_ref, bf16[32,1920]{1,0:T(8,128)(2,1)S(1)} %collective-permute-done.12.gate_other_ref, f32[32,1792]{1,0:T(8,128)S(1)} %get-tuple-element.24.up_ref, ...), custom_call_target="tpu_custom_call" | custom-call | bytes 7307276 | tf_op jit(solution)/shard_map/downs/pallas_call | solution.py:121
  64.1 1.2 %collective-permute-done.14.back_ref = bf16[16,1792]{1,0:T(8,128)(2,1)S(1)} collective-permute-done((bf16[16,1792]{1,0:T(8,128)(2,1)S(1)}, bf16[16,1792]{1,0:T(8,128)(2,1)S(1)}, u32[]{:S(2)}, u32[]{:S(2)}) %collective-permute-start.14) | collective-permute-done | bytes 57376 | tf_op jit(solution)/shard_map/ppermute | solution.py:112
  65.3 0.6 owners.1
  65.9 1.5 %collective-permute-start.17 = (bf16[4,1792]{1,0:T(4,128)(2,1)S(1)}, bf16[4,1792]{1,0:T(4,128)(2,1)S(1)}, u32[]{:S(2)}, u32[]{:S(2)}) collective-permute-start(bf16[4,1792]{1,0:T(4,128)(2,1)S(1)} %get-tuple-element.31), channel_id=1, source_target_pairs={{0,12},{4,8},{8,4},{12,0},{1,13},{5,9},{9,5},{13,1},{2,14},{6,10},... | collective-permute-start | bytes 43016 | tf_op jit(solution)/shard_map/ppermute | solution.py:112
  67.4 0.6 collective-permute-start.16
  68.0 2.4 %collective-permute-start.15 = (bf16[4,1792]{1,0:T(4,128)(2,1)S(1)}, bf16[4,1792]{1,0:T(4,128)(2,1)S(1)}, u32[]{:S(2)}, u32[]{:S(2)}) collective-permute-start(bf16[4,1792]{1,0:T(4,128)(2,1)S(1)} %get-tuple-element.29), channel_id=1, source_target_pairs={{0,4},{4,0},{8,12},{12,8},{1,5},{5,1},{9,13},{13,9},{2,6},{6,2},{1... | collective-permute-start | bytes 43016 | tf_op jit(solution)/shard_map/ppermute | solution.py:112
  70.5 0.6 reshape.145
  71.1 0.4 collective-permute-done.17
  71.5 0.5 collective-permute-done.16
  72.0 0.1 collective-permute-done.15
  72.1 0.7 multiply_convert_fusion
  (45 shorter events, 0.8 us)
Async XLA Ops:
  0.6 14.3 %copy-start = (bf16[1536,4,256]{2,1,0:T(4,128)(2,1)S(1)}, bf16[1536,4,256]{2,1,0:T(4,128)(2,1)}, u32[]{:S(2)}) copy-start(bf16[1536,4,256]{2,1,0:T(4,128)(2,1)} %param.14) | copy-start | bytes 9437188
  0.6 11.7 %copy-start.4 = (bf16[4,8,256]{2,1,0:T(8,128)(2,1)S(1)}, bf16[4,8,256]{2,1,0:T(8,128)(2,1)}, u32[]{:S(2)}) copy-start(bf16[4,8,256]{2,1,0:T(8,128)(2,1)} %refs_0_.1) | copy-start | bytes 49156
  0.7 11.7 %collective-permute-start.1 = (bf16[4,8,256]{2,1,0:T(8,128)(2,1)}, bf16[4,8,256]{2,1,0:T(8,128)(2,1)S(1)}, u32[]{:S(2)}, u32[]{:S(2)}) collective-permute-start(bf16[4,8,256]{2,1,0:T(8,128)(2,1)} %refs_0_.1), channel_id=1, source_target_pairs={{0,8},{4,12},{8,0},{12,4},{1,9},{5,13},{9,1},{13,5},{2,10},{6,14},... | collective-permute-start | bytes 49160 | tf_op jit(solution)/shard_map/ppermute | solution.py:112
  4.8 7.6 %collective-permute-start.2 = (bf16[4,8,256]{2,1,0:T(8,128)(2,1)}, bf16[4,8,256]{2,1,0:T(8,128)(2,1)S(1)}, u32[]{:S(2)}, u32[]{:S(2)}) collective-permute-start(bf16[4,8,256]{2,1,0:T(8,128)(2,1)} %refs_0_.1), channel_id=1, source_target_pairs={{0,12},{4,8},{8,4},{12,0},{1,13},{5,9},{9,5},{13,1},{2,14},{6,10},... | collective-permute-start | bytes 49160 | tf_op jit(solution)/shard_map/ppermute | solution.py:112
  6.1 6.3 %collective-permute-start = (bf16[4,8,256]{2,1,0:T(8,128)(2,1)}, bf16[4,8,256]{2,1,0:T(8,128)(2,1)S(1)}, u32[]{:S(2)}, u32[]{:S(2)}) collective-permute-start(bf16[4,8,256]{2,1,0:T(8,128)(2,1)} %refs_0_.1), channel_id=1, source_target_pairs={{0,4},{4,0},{8,12},{12,8},{1,5},{5,1},{9,13},{13,9},{2,6},{6,2},{1... | collective-permute-start | bytes 49160 | tf_op jit(solution)/shard_map/ppermute | solution.py:112
  7.9 0.7 copy-start.3
  11.1 1.3 %copy-start.1 = (bf16[448,2048]{1,0:T(8,128)(2,1)}, bf16[448,2048]{1,0:T(8,128)(2,1)S(1)}, u32[]{:S(2)}) copy-start(bf16[448,2048]{1,0:T(8,128)(2,1)S(1)} %get-tuple-element.18.weight_ref) | copy-start | bytes 5505028
  13.6 0.9 %copy-start.5 = (f32[16,4,2,1536]{3,0,2,1:T(8,128)}, f32[16,4,2,1536]{3,0,2,1:T(8,128)S(1)}, u32[]{:S(2)}) copy-start(f32[16,4,2,1536]{3,0,2,1:T(8,128)S(1)} %get-tuple-element.42) | copy-start | bytes 2359300
  14.9 17.6 %copy-start.6 = (bf16[448]{0:T(512)(128)(2,1)S(1)}, bf16[448]{0:T(512)(128)(2,1)}, u32[]{:S(2)}) copy-start(bf16[448]{0:T(512)(128)(2,1)} %param.18) | copy-start | bytes 2692
  16.9 5.2 %collective-permute-start.3 = (bf16[144,256]{1,0:T(8,128)(2,1)S(1)}, bf16[144,256]{1,0:T(8,128)(2,1)S(1)}, u32[]{:S(2)}, u32[]{:S(2)}) collective-permute-start(bf16[144,256]{1,0:T(8,128)(2,1)S(1)} %pad_maximum_fusion.refs_0_), channel_id=1, source_target_pairs={{0,4},{4,0},{8,12},{12,8},{1,5},{5,1},{9,13},{13,9},{2,6},{6,2},{1... | collective-permute-start | bytes 221192 | tf_op jit(solution)/shard_map/ppermute | solution.py:112
  18.7 7.0 %collective-permute-start.4 = (bf16[144,256]{1,0:T(8,128)(2,1)S(1)}, bf16[144,256]{1,0:T(8,128)(2,1)S(1)}, u32[]{:S(2)}, u32[]{:S(2)}) collective-permute-start(bf16[144,256]{1,0:T(8,128)(2,1)S(1)} %pad_maximum_fusion.refs_0_), channel_id=1, source_target_pairs={{0,8},{4,12},{8,0},{12,4},{1,9},{5,13},{9,1},{13,5},{2,10},{6,14},... | collective-permute-start | bytes 221192 | tf_op jit(solution)/shard_map/ppermute | solution.py:112
  20.4 6.3 %collective-permute-start.5 = (bf16[144,256]{1,0:T(8,128)(2,1)S(1)}, bf16[144,256]{1,0:T(8,128)(2,1)S(1)}, u32[]{:S(2)}, u32[]{:S(2)}) collective-permute-start(bf16[144,256]{1,0:T(8,128)(2,1)S(1)} %pad_maximum_fusion.refs_0_), channel_id=1, source_target_pairs={{0,12},{4,8},{8,4},{12,0},{1,13},{5,9},{9,5},{13,1},{2,14},{6,10},... | collective-permute-start | bytes 221192 | tf_op jit(solution)/shard_map/ppermute | solution.py:112
  26.9 1.3 %collective-permute-start.6 = (bf16[16,2048]{1,0:T(8,128)(2,1)S(1)}, bf16[16,2048]{1,0:T(8,128)(2,1)S(1)}, u32[]{:S(2)}, u32[]{:S(2)}) collective-permute-start(bf16[16,2048]{1,0:T(8,128)(2,1)S(1)} %combine.1.own_ref), channel_id=1, source_target_pairs={{0,1},{1,0},{2,3},{3,2},{4,5},{5,4},{6,7},{7,6},{8,9},{9,8},{10,11... | collective-permute-start | bytes 196616 | tf_op jit(solution)/shard_map/ppermute | solution.py:112
  28.3 1.5 %copy-start.2 = (bf16[448,2048]{1,0:T(8,128)(2,1)S(1)}, bf16[448,2048]{1,0:T(8,128)(2,1)}, u32[]{:S(2)}) copy-start(bf16[448,2048]{1,0:T(8,128)(2,1)} %copy-done.1) | copy-start | bytes 5505028
  30.9 4.0 %collective-permute-start.7 = (bf16[32,448]{1,0:T(8,128)(2,1)S(1)}, bf16[32,448]{1,0:T(8,128)(2,1)S(1)}, u32[]{:S(2)}, u32[]{:S(2)}) collective-permute-start(bf16[32,448]{1,0:T(8,128)(2,1)S(1)} %project.1.own_ref.refs_0_), channel_id=1, source_target_pairs={{0,2},{2,0},{1,3},{3,1},{4,6},{6,4},{5,7},{7,5},{8,10},{10,8},{9,1... | collective-permute-start | bytes 86024 | tf_op jit(solution)/shard_map/ppermute | solution.py:112
  35.1 8.0 %collective-permute-start.9 = (bf16[32,512]{1,0:T(8,128)(2,1)S(1)}, bf16[32,512]{1,0:T(8,128)(2,1)S(1)}, u32[]{:S(2)}, u32[]{:S(2)}) collective-permute-start(bf16[32,512]{1,0:T(8,128)(2,1)S(1)} %get-tuple-element.20.refs_0_), channel_id=1, source_target_pairs={{0,8},{4,12},{10,2},{14,6},{1,9},{5,13},{11,3},{15,7},{16,24},{20,... | collective-permute-start | bytes 98312 | tf_op jit(solution)/shard_map/ppermute | solution.py:313
  39.1 3.9 %collective-permute-start.10 = (bf16[32,512]{1,0:T(8,128)(2,1)S(1)}, bf16[32,512]{1,0:T(8,128)(2,1)S(1)}, u32[]{:S(2)}, u32[]{:S(2)}) collective-permute-start(bf16[32,512]{1,0:T(8,128)(2,1)S(1)} %get-tuple-element.20.refs_0_), channel_id=1, source_target_pairs={{0,12},{4,8},{10,6},{14,2},{1,13},{5,9},{11,7},{15,3},{16,28},{20,... | collective-permute-start | bytes 98312 | tf_op jit(solution)/shard_map/ppermute | solution.py:313
  40.6 5.8 %collective-permute-start.8 = (bf16[32,512]{1,0:T(8,128)(2,1)S(1)}, bf16[32,512]{1,0:T(8,128)(2,1)S(1)}, u32[]{:S(2)}, u32[]{:S(2)}) collective-permute-start(bf16[32,512]{1,0:T(8,128)(2,1)S(1)} %get-tuple-element.20.refs_0_), channel_id=1, source_target_pairs={{0,4},{4,0},{10,14},{14,10},{1,5},{5,1},{11,15},{15,11},{16,20},{2... | collective-permute-start | bytes 98312 | tf_op jit(solution)/shard_map/ppermute | solution.py:313
  46.4 5.8 %collective-permute-start.11 = (bf16[2,32,512]{2,1,0:T(8,128)(2,1)S(1)}, bf16[2,32,512]{2,1,0:T(8,128)(2,1)S(1)}, u32[]{:S(2)}, u32[]{:S(2)}) collective-permute-start(bf16[2,32,512]{2,1,0:T(8,128)(2,1)S(1)} %pad_maximum_fusion.2.mine_ref), channel_id=1, source_target_pairs={{0,1},{1,0},{2,3},{3,2},{4,5},{5,4},{6,7},{7,6},{8,9},{9,8},{10,11... | collective-permute-start | bytes 196616 | tf_op jit(solution)/shard_map/ppermute | solution.py:112
  53.9 8.2 %collective-permute-start.12 = (bf16[32,1920]{1,0:T(8,128)(2,1)S(1)}, bf16[32,1920]{1,0:T(8,128)(2,1)S(1)}, u32[]{:S(2)}, u32[]{:S(2)}) collective-permute-start(bf16[32,1920]{1,0:T(8,128)(2,1)S(1)} %get-tuple-element.22), channel_id=1, source_target_pairs={{0,2},{2,0},{1,3},{3,1},{4,6},{6,4},{5,7},{7,5},{8,10},{10,8},{9,1... | collective-permute-start | bytes 368648 | tf_op jit(solution)/shard_map/ppermute | solution.py:112
  55.2 6.9 %collective-permute-start.13 = (bf16[32,1792]{1,0:T(8,128)(2,1)S(1)}, bf16[32,1792]{1,0:T(8,128)(2,1)S(1)}, u32[]{:S(2)}, u32[]{:S(2)}) collective-permute-start(bf16[32,1792]{1,0:T(8,128)(2,1)S(1)} %get-tuple-element.25), channel_id=1, source_target_pairs={{0,2},{2,0},{1,3},{3,1},{4,6},{6,4},{5,7},{7,5},{8,10},{10,8},{9,1... | collective-permute-start | bytes 344072 | tf_op jit(solution)/shard_map/ppermute | solution.py:112
  64.0 1.3 %collective-permute-start.14 = (bf16[16,1792]{1,0:T(8,128)(2,1)S(1)}, bf16[16,1792]{1,0:T(8,128)(2,1)S(1)}, u32[]{:S(2)}, u32[]{:S(2)}) collective-permute-start(bf16[16,1792]{1,0:T(8,128)(2,1)S(1)} %get-tuple-element.27), channel_id=1, source_target_pairs={{0,1},{1,0},{2,3},{3,2},{4,5},{5,4},{6,7},{7,6},{8,9},{9,8},{10,11... | collective-permute-start | bytes 172040 | tf_op jit(solution)/shard_map/ppermute | solution.py:112
  65.9 5.6 %collective-permute-start.17 = (bf16[4,1792]{1,0:T(4,128)(2,1)S(1)}, bf16[4,1792]{1,0:T(4,128)(2,1)S(1)}, u32[]{:S(2)}, u32[]{:S(2)}) collective-permute-start(bf16[4,1792]{1,0:T(4,128)(2,1)S(1)} %get-tuple-element.31), channel_id=1, source_target_pairs={{0,12},{4,8},{8,4},{12,0},{1,13},{5,9},{9,5},{13,1},{2,14},{6,10},... | collective-permute-start | bytes 43016 | tf_op jit(solution)/shard_map/ppermute | solution.py:112
  67.4 4.6 %collective-permute-start.16 = (bf16[4,1792]{1,0:T(4,128)(2,1)S(1)}, bf16[4,1792]{1,0:T(4,128)(2,1)S(1)}, u32[]{:S(2)}, u32[]{:S(2)}) collective-permute-start(bf16[4,1792]{1,0:T(4,128)(2,1)S(1)} %get-tuple-element.30), channel_id=1, source_target_pairs={{0,8},{4,12},{8,0},{12,4},{1,9},{5,13},{9,1},{13,5},{2,10},{6,14},... | collective-permute-start | bytes 43016 | tf_op jit(solution)/shard_map/ppermute | solution.py:112
  68.0 4.1 %collective-permute-start.15 = (bf16[4,1792]{1,0:T(4,128)(2,1)S(1)}, bf16[4,1792]{1,0:T(4,128)(2,1)S(1)}, u32[]{:S(2)}, u32[]{:S(2)}) collective-permute-start(bf16[4,1792]{1,0:T(4,128)(2,1)S(1)} %get-tuple-element.29), channel_id=1, source_target_pairs={{0,4},{4,0},{8,12},{12,8},{1,5},{5,1},{9,13},{13,9},{2,6},{6,2},{1... | collective-permute-start | bytes 43016 | tf_op jit(solution)/shard_map/ppermute | solution.py:112

commit v3 on v2

--- a/solution.py
+++ b/solution.py
@@ -203,11 +203,10 @@
     sds = jax.ShapeDtypeStruct
 
     pieces = [queries] + [hop(queries, "blk", blks, s) for s in range(1, blks)]
-    keys_near, proj_near = fetch(queries, [src_keys, out_weight.T], "fetch_keys_proj")
     q_all = jnp.concatenate(by_index(pieces, blk), axis=0)
     grouped = q_all.reshape(toks, kv_local, group_size, head_size)
     scores = (
-        jnp.einsum("tgjd,kgd->tgjk", grouped, keys_near, preferred_element_type=F32) * score_scale
+        jnp.einsum("tgjd,kgd->tgjk", grouped, src_keys, preferred_element_type=F32) * score_scale
     )
     peak = jnp.max(scores, axis=3)
     weights = jnp.exp(scores - peak[..., None])
@@ -217,15 +216,16 @@
     )
     partial = (numerator / totals[..., None]).astype(BF)
     partial = partial.transpose(1, 2, 0, 3).reshape(local_heads * toks, head_size)
+    partial, peak, totals = lax.optimization_barrier((partial, peak, totals))
     level = (peak + jnp.log(totals)).reshape(toks, local_heads)
     side = jnp.concatenate(parts_of(level, 3), axis=1)
     side = jnp.pad(side, ((0, 0), (0, head_size - side.shape[1])))
     note = jnp.concatenate([partial, side], axis=0)
     notes = [note] + [hop(note, "blk", blks, s) for s in range(1, blks)]
-    (gate_near,) = fetch(note, [gate_weight], "fetch_gate")
+    (proj_near,) = fetch(note, [out_weight.T], "fetch_proj")
 
     def combine(*refs):
-        ins, out = refs[:-1], refs[-1]
+        ins, out = refs[:blks], refs[-1]
         base = local_heads * toks
         levels = []
         for ref in ins:
@@ -251,29 +251,47 @@
             out[:, h * head_size : (h + 1) * head_size] = acc.astype(BF)
 
     (attn,) = kernel(
-        combine, "combine", [sds((toks, local_heads * head_size), BF)], [VM] * blks, notes
+        combine,
+        "combine",
+        [sds((toks, local_heads * head_size), BF)],
+        [VM] * blks + [ANY],
+        notes + [proj_near],
     )
     other = hop(attn, "rows", 2, 1)
+    across = (((1,), (1,)), ((), ()))
+
+    def project_own(own_ref, weight_ref, out_ref):
+        out_ref[...] = lax.dot_general(
+            own_ref[...], weight_ref[...], across, preferred_element_type=F32
+        )
+
+    (proj_own,) = kernel(
+        project_own,
+        "project_own",
+        [sds((toks, width), F32)],
+        [VM, VM],
+        [attn, proj_near],
+        flops=2 * toks * width * attn.shape[1],
+    )
 
     def project(place_ref, own_ref, other_ref, weight_ref, out_ref):
         first = place_ref[0] == 0
-        own, other = own_ref[...], other_ref[...]
-        rows = jnp.concatenate(
-            [jnp.where(first, own, other), jnp.where(first, other, own)], axis=0
+        own = own_ref[...]
+        other = lax.dot_general(
+            other_ref[...], weight_ref[...], across, preferred_element_type=F32
         )
-        out_ref[...] = lax.dot_general(
-            rows, weight_ref[...], (((1,), (1,)), ((), ())), preferred_element_type=F32
-        ).astype(BF)
+        out_ref[:toks] = jnp.where(first, own, other).astype(BF)
+        out_ref[toks:] = jnp.where(first, other, own).astype(BF)
 
     (proj,) = kernel(
         project,
         "project",
         [sds((tokens, width), BF)],
         [SM, VM, VM, VM],
-        [place, attn, other, proj_near],
+        [place, proj_own, other, proj_near],
     )
     proj_other = hop(proj, "heads", 2, 1)
-    (up_near,) = fetch(proj, [up_weight], "fetch_up")
+    (gate_near,) = fetch(proj, [gate_weight], "fetch_gate")
 
     def inner(value):
         value = value.reshape((blks, 2, tok_dev) + value.shape[1:])
@@ -285,7 +303,7 @@
     keep_inner = inner(keep_mask)[:, None]
     lanes = -(-(width + 2) // 128) * 128
 
-    def middle(base_ref, keep_ref, gain_ref, own_ref, other_ref, stream_ref, note_ref):
+    def middle(base_ref, keep_ref, gain_ref, own_ref, other_ref, near_ref, stream_ref, note_ref):
         mid = base_ref[...].astype(F32) + (own_ref[...].astype(F32) + other_ref[...].astype(F32))
         stream_ref[...] = (mid * keep_ref[...]).astype(BF)
         note_ref[:, :width] = (mid * gain_ref[...].astype(F32)).astype(BF)
@@ -300,40 +318,74 @@
         middle,
         "middle",
         [sds((tokens, width), BF), sds((tokens, lanes), BF)],
-        [VM] * 5,
-        [base_state, keep_inner, norm_gain[None, :], proj, proj_other],
-    )
-
-    got = [note]
-    for s in range(1, blks):
-        pairs = []
-        for b in range(blks):
-            h = b // half
-            pairs.append((b * head_parts + h, (b ^ s) * head_parts + h))
-        got.append(lax.ppermute(note, ("blk", "heads"), pairs))
-    (down_near,) = fetch(note, [down_weight], "fetch_down")
-    mine = jnp.stack([lax.select_n(blk ^ (head * half + k), *got) for k in range(half)], axis=0)
+        [VM] * 5 + [ANY],
+        [base_state, keep_inner, norm_gain[None, :], proj, proj_other, gate_near],
+    )
+
+    far_pairs, near_pairs = [], []
+    for b in range(blks):
+        for h in range(head_parts):
+            far_pairs.append((b * head_parts + h, (b ^ 3) * head_parts + h))
+            to = (b ^ 1, h) if b // half == h else (b ^ 2, 1 - h)
+            near_pairs.append((b * head_parts + h, to[0] * head_parts + to[1]))
+    far = lax.ppermute(note, ("blk", "heads"), far_pairs)
+    near = lax.ppermute(note, ("blk", "heads"), near_pairs)
+    (up_near,) = fetch(note, [up_weight], "fetch_up")
+    lanes_all = note.shape[1]
+
+    def pick(place_ref, own_ref, near_ref, far_ref, gate_ref, up_ref, out_ref):
+        at = place_ref[1]
+        inside = at // half == place_ref[2]
+        odd = at % 2 == 1
+        own, near_tile, far_tile = own_ref[...], near_ref[...], far_ref[...]
+        same = jnp.where(inside, own, near_tile)
+        pair = jnp.where(inside, near_tile, far_tile)
+        out_ref[0] = jnp.where(odd, pair, same)
+        out_ref[1] = jnp.where(odd, same, pair)
+
+    (mine,) = kernel(
+        pick,
+        "pick",
+        [sds((half, tokens, lanes_all), BF)],
+        [SM, VM, VM, VM, ANY, ANY],
+        [place, note, near, far, gate_near, up_near],
+    )
     theirs = hop(mine, "rows", 2, 1)
-
-    def column_block(place_ref, mine_ref, theirs_ref):
-        first = place_ref[0] == 0
-        tiles = []
+    rows_in = gate_weight.shape[0]
+
+    def tile_products(tiles_ref, weight_ref, row_at):
+        total = None
         for k in range(half):
-            own, other = mine_ref[k], theirs_ref[k]
-            tiles += [jnp.where(first, own, other), jnp.where(first, other, own)]
-        return tiles
-
-    rows_in = gate_weight.shape[0]
-
-    def gates(place_ref, mine_ref, theirs_ref, weight_ref, out_ref, note_ref, x_ref):
-        tiles = column_block(place_ref, mine_ref, theirs_ref)
+            start = pl.multiple_of((k * 2 + row_at) * width, 16)
+            term = jnp.dot(
+                tiles_ref[k, :, :width],
+                weight_ref[pl.ds(start, width), :],
+                preferred_element_type=F32,
+            )
+            total = term if total is None else total + term
+        return total
+
+    def inner_products(place_ref, mine_ref, gate_ref, up_ref, gate_out, up_out):
+        gate_out[...] = tile_products(mine_ref, gate_ref, place_ref[0])
+        up_out[...] = tile_products(mine_ref, up_ref, place_ref[0])
+
+    gate_own, up_own = kernel(
+        inner_products,
+        "inner_products",
+        [sds((tokens, hidden_width), F32)] * 2,
+        [SM, VM, VM, VM],
+        [place, mine, gate_near, up_near],
+        flops=2 * tokens * rows_in * hidden_width,
+    )
+
+    def gates(place_ref, mine_ref, theirs_ref, own_ref, weight_ref, out_ref, note_ref):
         squares = None
-        for j, tile in enumerate(tiles):
-            x_ref[:, j * width : (j + 1) * width] = tile[:, :width]
-            here = tile[:, width : width + 2].astype(F32)
-            squares = here if squares is None else squares + here
+        for k in range(half):
+            for ref in (mine_ref, theirs_ref):
+                here = ref[k, :, width : width + 2].astype(F32)
+                squares = here if squares is None else squares + here
         squares = squares[:, 0:1] + squares[:, 1:2]
-        gate = jnp.dot(x_ref[...], weight_ref[...], preferred_element_type=F32)
+        gate = own_ref[...] + tile_products(theirs_ref, weight_ref, 1 - place_ref[0])
         out_ref[:, :hidden_width] = gate
         note_ref[:, :hidden_width] = gate.astype(BF)
         high, low = split_in(squares, 2)
@@ -344,17 +396,17 @@
         ).astype(BF)
 
     long_width = hidden_width + 128
-    gate, gate_note, column = kernel(
+    gate, gate_note = kernel(
         gates,
         "gates",
-        [sds((tokens, long_width), F32), sds((tokens, long_width), BF), sds((tokens, rows_in), BF)],
-        [SM, VM, VM, VM],
-        [place, mine, theirs, gate_near],
+        [sds((tokens, long_width), F32), sds((tokens, long_width), BF)],
+        [SM, VM, VM, VM, VM],
+        [place, mine, theirs, gate_own, gate_near],
     )
     gate_other = hop(gate_note, "heads", 2, 1)
 
-    def ups(x_ref, weight_ref, out_ref, note_ref):
-        up = jnp.dot(x_ref[...], weight_ref[...], preferred_element_type=F32)
+    def ups(place_ref, theirs_ref, own_ref, weight_ref, out_ref, note_ref):
+        up = own_ref[...] + tile_products(theirs_ref, weight_ref, 1 - place_ref[0])
         out_ref[...] = up
         note_ref[...] = up.astype(BF)
 
@@ -362,11 +414,12 @@
         ups,
         "ups",
         [sds((tokens, hidden_width), F32), sds((tokens, hidden_width), BF)],
-        [VM, VM],
-        [column, up_near],
-        flops=2 * tokens * rows_in * hidden_width,
+        [SM, VM, VM, VM],
+        [place, theirs, up_own, up_near],
+        flops=tokens * rows_in * hidden_width,
     )
     up_other = hop(up_note, "heads", 2, 1)
+    (down_near,) = fetch(up_note, [down_weight], "fetch_down")
 
     def downs(
         place_ref, gate_ref, gate_other_ref, up_ref, up_other_ref, weight_ref, keep_ref, away_ref
@@ -419,7 +472,7 @@
 
 def solution(mesh):
     size = dict(mesh.shape)
-    direct = size["blk"] in (2, 4, 8) and size["heads"] == 2 and size["rows"] == 2
+    direct = size["blk"] == 4 and size["heads"] == 2 and size["rows"] == 2
     placed = (
         P(("groups", "blk", "rows"), "heads", None),
         P(("groups", "blk"), "heads", None),

time: 73.3 us -> 62.7 us (0.86)
  starting transfers between devices: 26.4 us -> 20.5 us
  local copies, waits for them, and re-layouts: 5.44 us -> 1.07 us
  Pallas kernels: 18 us -> 19.4 us
  waiting for transfers between devices: 15.7 us -> 14.4 us
  matrix products: 2.96 us -> 1.83 us
    ppermute x3 -> x2, starting transfers between devices: 7.93 us -> 1.7 us  [the longest x1 1.7 us: shards_direct(): far = lax.ppermute(note, ('blk', 'heads'), far_pairs)]
    unnamed x14 -> x6, local copies, waits for them, and re-layouts: 4.39 us -> 0.02 us
    pallas_call x7 -> x10, Pallas kernels: 7.01 us -> 9.38 us  [kernel(): pl.pallas_call(body, out_shape=outs, in_specs=specs, out_specs=[VM] * len...]
    ppermute x3 -> x2, waiting for transfers between devices: 3.29 us -> 1.49 us  [the longest x1 1.29 us: shards_direct(): far = lax.ppermute(note, ('blk', 'heads'), far_pairs)]
    dot_general x1, matrix products: 1.84 us -> 0.7 us  [shards_direct(): jnp.einsum('tgjk,kgd->tgjd', weights.astype(BF), src_values, preferred_el...]
    pallas_call x4, Pallas kernels: 11 us -> 10 us  [fetch(): pl.pallas_call(body, out_shape=[jax.ShapeDtypeStruct(a.shape, a.dtype) fo...]
  transfers between devices with their start and end apart: 18 -> 17, of which waited for: 10 -> 10; matrix products, arithmetic and copies ran while one was open for 4% -> 4% of each run, Pallas kernels for 17% -> 22%
where the time goes in v3:
time: 62.7 us; the launch traced here: 62.3 us
  starting transfers between devices  20.5 us (33%)
  Pallas kernels  19.4 us (31%)
  waiting for transfers between devices  14.4 us (23%)
  other arithmetic  3.47 us (6%)
  matrix products  1.83 us (3%)
  between operations  1.7 us (3%)
  local copies, waits for them, and re-layouts  1.07 us (2%)
    ppermute x15, starting transfers between devices, hop(): return lax.ppermute(value, axis, [(i, i ^ step) for i in range(size)])  18.8 us
    ppermute x15, waiting for transfers between devices, hop(): return lax.ppermute(value, axis, [(i, i ^ step) for i in range(size)])  12.9 us
    pallas_call x4, Pallas kernels, fetch(): pl.pallas_call(body, out_shape=[jax.ShapeDtypeStruct(a.shape, a.dtype) fo...  10 us
    pallas_call x10, Pallas kernels, kernel(): pl.pallas_call(body, out_shape=outs, in_specs=specs, out_specs=[VM] * len...  9.38 us
    ppermute x1, starting transfers between devices, shards_direct(): far = lax.ppermute(note, ('blk', 'heads'), far_pairs)  1.7 us
    ppermute x1, waiting for transfers between devices, shards_direct(): far = lax.ppermute(note, ('blk', 'heads'), far_pairs)  1.29 us
  transfers between devices with their start and end apart: 17, of which 10 were waited for; matrix products, arithmetic and copies ran while one was open for 4% of the time, Pallas kernels for 22%

profile of v3, /device:TPU:0, one launch (start us, length us, event | category | flops | bytes accessed | tf_op | source)
XLA Modules:
  0.0 62.3 jit_solution(5504914812672878549)
XLA Ops:
  0.6 3.1 %collective-permute-start = (bf16[4,8,256]{2,1,0:T(8,128)(2,1)}, bf16[4,8,256]{2,1,0:T(8,128)(2,1)S(1)}, u32[]{:S(2)}, u32[]{:S(2)}) collective-permute-start(bf16[4,8,256]{2,1,0:T(8,128)(2,1)} %param.12), channel_id=1, source_target_pairs={{0,4},{4,0},{8,12},{12,8},{1,5},{5,1},{9,13},{13,9},{2,6},{6,2},{1... | collective-permute-start | bytes 49160 | tf_op jit(solution)/shard_map/ppermute | solution.py:112
  3.7 2.6 %collective-permute-start.1 = (bf16[4,8,256]{2,1,0:T(8,128)(2,1)}, bf16[4,8,256]{2,1,0:T(8,128)(2,1)S(1)}, u32[]{:S(2)}, u32[]{:S(2)}) collective-permute-start(bf16[4,8,256]{2,1,0:T(8,128)(2,1)} %param.12), channel_id=1, source_target_pairs={{0,8},{4,12},{8,0},{12,4},{1,9},{5,13},{9,1},{13,5},{2,10},{6,14},... | collective-permute-start | bytes 49160 | tf_op jit(solution)/shard_map/ppermute | solution.py:112
  6.3 0.7 %fusion.23 = pred[128]{0:T(512)(128)(4,1)S(1)} fusion(s32[48]{0:T(128)} %bitcast.45), kind=kLoop, calls=%fused_computation.22 | loop fusion | flops 12160 | bytes 320 | tf_op jit(solution)/shard_map/reduce_or | solution.py:19
  7.1 0.8 %broadcast_select_fusion = bf16[32,448]{1,0:T(8,128)(2,1)S(1)} fusion(bf16[32,448]{1,0:T(8,128)(2,1)} %param.15, pred[32]{0:T(512)(128)(4,1)S(1)} %slice_bitcast_fusion, bf16[448]{0:T(512)(128)(2,1)} %param.16), kind=kLoop, calls=%fused_computation.16 | loop fusion | flops 14336 | bytes 58272 | tf_op jit(solution)/shard_map/jit(_where)/select_n | solution.py:301
  8.7 3.3 %collective-permute-done.2 = bf16[4,8,256]{2,1,0:T(8,128)(2,1)S(1)} collective-permute-done((bf16[4,8,256]{2,1,0:T(8,128)(2,1)}, bf16[4,8,256]{2,1,0:T(8,128)(2,1)S(1)}, u32[]{:S(2)}, u32[]{:S(2)}) %collective-permute-start.2) | collective-permute-done | bytes 16416 | tf_op jit(solution)/shard_map/ppermute | solution.py:112
  12.1 0.7 %select_select_fusion.3 = (bf16[4,8,256]{2,1,0:T(8,128)(2,1)S(1)}, bf16[4,8,256]{2,1,0:T(8,128)(2,1)S(1)}, bf16[4,8,256]{2,1,0:T(8,128)(2,1)S(1)}, bf16[4,8,256]{2,1,0:T(8,128)(2,1)S(1)}) fusion(bf16[4,8,256]{2,1,0:T(8,128)(2,1)S(1)} %collective-permute-done.1, bf16[4,8,256]{2,1,0:T(8,128)(2,1)S(1)} %collective-permute-done.2, bf16[4,8,256]{2,1,0:T(8,128)(2,1)} %param.12, ...), kind=kLoop, calls=%fused_computation.32 | loop fusion | flops 98304 | bytes 131084 | tf_op jit(solution)/shard_map/select_n | solution.py:116
  12.9 1.1 %fusion.34 = (f32[16,4,2]{0,2,1:T(2,128)S(1)}, f32[16,4,2,1536]{3,0,2,1:T(8,128)S(1)}) fusion(bf16[16,4,2,256]{3,0,2,1:T(8,128)(2,1)S(1)} %bitcast.35, bf16[1536,4,256,1]{2,1,0,3:T(4,128)(2,1)S(1)} %bitcast.33), kind=kOutput, calls=%fused_computation.46 | convolution fusion | flops 101056384 | bytes 3998208 | tf_op jit(solution)/shard_map/tgjd,kgd->tgjk/dot_general | solution.py:209
  14.0 0.3 fusion.19
  14.3 0.7 %fusion.16 = bf16[4,2,16,256]{3,2,1,0:T(8,128)(2,1)S(1)} fusion(bf16[1536,4,256,1]{2,1,0,3:T(4,128)(2,1)S(1)} %bitcast.44, f32[16,4,2,1536]{3,0,2,1:T(8,128)S(1)} %get-tuple-element.44, f32[16,4,2]{0,2,1:T(2,128)S(1)} %get-tuple-element.20, f32[4,2,16]{2,1,0:T(2,128)S(1)} %bitcast.42), kind=kOutput, calls=%fused_computation.8 | convolution fusion | flops 101122048 | bytes 3998720 | tf_op jit(solution)/shard_map/tgjk,kgd->tgjd/dot_general | solution.py:214
  15.0 0.1 copy.42
  15.1 0.1 fusion.33
  15.2 0.7 %collective-permute-start.5 = (bf16[144,256]{1,0:T(8,128)(2,1)S(1)}, bf16[144,256]{1,0:T(8,128)(2,1)S(1)}, u32[]{:S(2)}, u32[]{:S(2)}) collective-permute-start(bf16[144,256]{1,0:T(8,128)(2,1)S(1)} %pad_maximum_fusion.refs_0_), channel_id=1, source_target_pairs={{0,12},{4,8},{8,4},{12,0},{1,13},{5,9},{9,5},{13,1},{2,14},{6,10},... | collective-permute-start | bytes 221192 | tf_op jit(solution)/shard_map/ppermute | solution.py:112
  15.9 3.8 %collective-permute-start.3 = (bf16[144,256]{1,0:T(8,128)(2,1)S(1)}, bf16[144,256]{1,0:T(8,128)(2,1)S(1)}, u32[]{:S(2)}, u32[]{:S(2)}) collective-permute-start(bf16[144,256]{1,0:T(8,128)(2,1)S(1)} %pad_maximum_fusion.refs_0_), channel_id=1, source_target_pairs={{0,4},{4,0},{8,12},{12,8},{1,5},{5,1},{9,13},{13,9},{2,6},{6,2},{1... | collective-permute-start | bytes 221192 | tf_op jit(solution)/shard_map/ppermute | solution.py:112
  19.7 0.1 iota.55
  19.8 1.5 %fetch_proj.1.refs_4_.weight_ref = bf16[448,2048]{1,0:T(8,128)(2,1)S(1)} custom-call(bf16[144,256]{1,0:T(8,128)(2,1)S(1)} %pad_maximum_fusion.refs_0_, bf16[448,2048]{1,0:T(8,128)(2,1)} %bitcast.34), custom_call_target="tpu_custom_call" | custom-call | bytes 3670016 | tf_op jit(solution)/shard_map/fetch_proj/pallas_call | solution.py:146
  21.3 0.3 collective-permute-done.5.refs_3_
  21.6 1.2 %collective-permute-done.4.refs_2_ = bf16[144,256]{1,0:T(8,128)(2,1)S(1)} collective-permute-done((bf16[144,256]{1,0:T(8,128)(2,1)S(1)}, bf16[144,256]{1,0:T(8,128)(2,1)S(1)}, u32[]{:S(2)}, u32[]{:S(2)}) %collective-permute-start.4) | collective-permute-done | bytes 73760 | tf_op jit(solution)/shard_map/ppermute | solution.py:112
  22.8 0.2 combine.1.own_ref
  23.1 0.1 pad_add_fusion.place_ref
  23.2 0.6 project_own.1.own_ref
  23.8 0.6 collective-permute-done.6.other_ref
  24.3 1.1 %project.1.refs_0_.own_ref = bf16[32,448]{1,0:T(8,128)(2,1)S(1)} custom-call(s32[3]{0:T(128)S(1)} %pad_add_fusion.place_ref, f32[16,448]{1,0:T(8,128)S(1)} %project_own.1.own_ref, bf16[16,2048]{1,0:T(8,128)(2,1)S(1)} %collective-permute-done.6.other_ref, bf16[448,2048]{1,0:T(8,128)(2,1)S(1)} %fetch_proj.1.refs_4_.weight_ref), custom_call_target="tpu_custom_call" | custom-call | bytes 1957900 | tf_op jit(solution)/shard_map/project/pallas_call | solution.py:121
  25.5 1.5 %collective-permute-start.7 = (bf16[32,448]{1,0:T(8,128)(2,1)S(1)}, bf16[32,448]{1,0:T(8,128)(2,1)S(1)}, u32[]{:S(2)}, u32[]{:S(2)}) collective-permute-start(bf16[32,448]{1,0:T(8,128)(2,1)S(1)} %project.1.refs_0_.own_ref), channel_id=1, source_target_pairs={{0,2},{2,0},{1,3},{3,1},{4,6},{6,4},{5,7},{7,5},{8,10},{10,8},{9,1... | collective-permute-start | bytes 86024 | tf_op jit(solution)/shard_map/ppermute | solution.py:112
  27.1 2.8 %fetch_gate.1.near_ref.gate_ref.weight_ref = bf16[1792,1792]{1,0:T(8,128)(2,1)S(1)} custom-call(bf16[32,448]{1,0:T(8,128)(2,1)S(1)} %project.1.refs_0_.own_ref, bf16[1792,1792]{1,0:T(8,128)(2,1)} %refs_1_.3), custom_call_target="tpu_custom_call" | custom-call | bytes 12845056 | tf_op jit(solution)/shard_map/fetch_gate/pallas_call | solution.py:146
  29.9 0.2 middle.1
  30.1 1.7 %collective-permute-start.9 = (bf16[32,512]{1,0:T(8,128)(2,1)S(1)}, bf16[32,512]{1,0:T(8,128)(2,1)S(1)}, u32[]{:S(2)}, u32[]{:S(2)}) collective-permute-start(bf16[32,512]{1,0:T(8,128)(2,1)S(1)} %get-tuple-element.23.refs_0_.own_ref), channel_id=1, source_target_pairs={{0,12},{2,14},{4,8},{6,10},{8,4},{10,6},{12,0},{14,2},{1,13},{3,15... | collective-permute-start | bytes 98312 | tf_op jit(solution)/shard_map/ppermute | solution.py:331
  31.8 2.8 %fetch_up.1.up_ref.weight_ref = bf16[1792,1792]{1,0:T(8,128)(2,1)S(1)} custom-call(bf16[32,512]{1,0:T(8,128)(2,1)S(1)} %get-tuple-element.23.refs_0_.own_ref, bf16[1792,1792]{1,0:T(8,128)(2,1)} %refs_1_.4), custom_call_target="tpu_custom_call" | custom-call | bytes 12845056 | tf_op jit(solution)/shard_map/fetch_up/pallas_call | solution.py:146
  34.6 1.3 %collective-permute-done.9.far_ref = bf16[32,512]{1,0:T(8,128)(2,1)S(1)} collective-permute-done((bf16[32,512]{1,0:T(8,128)(2,1)S(1)}, bf16[32,512]{1,0:T(8,128)(2,1)S(1)}, u32[]{:S(2)}, u32[]{:S(2)}) %collective-permute-start.9) | collective-permute-done | bytes 32800 | tf_op jit(solution)/shard_map/ppermute | solution.py:331
  35.9 0.2 collective-permute-done.8.near_ref
  36.1 0.6 pick.1.mine_ref
  36.8 1.8 %inner_products.1 = (f32[32,1792]{1,0:T(8,128)S(1)}, f32[32,1792]{1,0:T(8,128)S(1)}) custom-call(s32[3]{0:T(128)S(1)} %pad_add_fusion.place_ref, bf16[2,32,512]{2,1,0:T(8,128)(2,1)S(1)} %pick.1.mine_ref, bf16[1792,1792]{1,0:T(8,128)(2,1)S(1)} %fetch_gate.1.near_ref.gate_ref.weight_ref, bf16[1792,1792]{1,0:T(8,128)(2,1)S(1)} %fetch_up.1.up_ref.weight_ref), custom_call_target="tpu_custom_call" | custom-call | flops 205520896 | bytes 13369356 | tf_op jit(solution)/shard_map/inner_products/pallas_call | solution.py:121
  38.6 1.2 %gates.1 = (f32[32,1920]{1,0:T(8,128)S(1)}, bf16[32,1920]{1,0:T(8,128)(2,1)S(1)}) custom-call(s32[3]{0:T(128)S(1)} %pad_add_fusion.place_ref, bf16[2,32,512]{2,1,0:T(8,128)(2,1)S(1)} %pick.1.mine_ref, bf16[2,32,512]{2,1,0:T(8,128)(2,1)S(1)} %collective-permute-done.10.theirs_ref, f32[32,1792]{1,0:T(8,128)S(1)} %get-tuple-element.24.own_ref, ...), custom_call_target="tpu_custom_call" | custom-call | bytes 7151628 | tf_op jit(solution)/shard_map/gates/pallas_call | solution.py:121
  39.8 2.4 %collective-permute-start.11 = (bf16[32,1920]{1,0:T(8,128)(2,1)S(1)}, bf16[32,1920]{1,0:T(8,128)(2,1)S(1)}, u32[]{:S(2)}, u32[]{:S(2)}) collective-permute-start(bf16[32,1920]{1,0:T(8,128)(2,1)S(1)} %get-tuple-element.26), channel_id=1, source_target_pairs={{0,2},{2,0},{1,3},{3,1},{4,6},{6,4},{5,7},{7,5},{8,10},{10,8},{9,1... | collective-permute-start | bytes 368648 | tf_op jit(solution)/shard_map/ppermute | solution.py:112
  42.2 1.2 %ups.1 = (f32[32,1792]{1,0:T(8,128)S(1)}, bf16[32,1792]{1,0:T(8,128)(2,1)S(1)}) custom-call(s32[3]{0:T(128)S(1)} %pad_add_fusion.place_ref, bf16[2,32,512]{2,1,0:T(8,128)(2,1)S(1)} %collective-permute-done.10.theirs_ref, f32[32,1792]{1,0:T(8,128)S(1)} %get-tuple-element.27.own_ref, bf16[1792,1792]{1,0:T(8,128)(2,1)S(1)} %fetch_up.1.up_ref.weight_ref), custom_call_target="tpu_custom_call" | custom-call | flops 102760448 | bytes 7061516 | tf_op jit(solution)/shard_map/ups/pallas_call | solution.py:121
  43.4 0.1 collective-permute-start.12
  43.5 2.8 %fetch_down.1.weight_ref = bf16[1792,1792]{1,0:T(8,128)(2,1)S(1)} custom-call(bf16[32,1792]{1,0:T(8,128)(2,1)S(1)} %get-tuple-element.29.refs_0_, bf16[1792,1792]{1,0:T(8,128)(2,1)} %refs_1_.5), custom_call_target="tpu_custom_call" | custom-call | bytes 12845056 | tf_op jit(solution)/shard_map/fetch_down/pallas_call | solution.py:146
  46.4 2.4 %collective-permute-done.12.up_other_ref = bf16[32,1792]{1,0:T(8,128)(2,1)S(1)} collective-permute-done((bf16[32,1792]{1,0:T(8,128)(2,1)S(1)}, bf16[32,1792]{1,0:T(8,128)(2,1)S(1)}, u32[]{:S(2)}, u32[]{:S(2)}) %collective-permute-start.12) | collective-permute-done | bytes 114720 | tf_op jit(solution)/shard_map/ppermute | solution.py:112
  48.8 1.9 %downs.1 = (f32[16,1792]{1,0:T(8,128)S(1)}, bf16[16,1792]{1,0:T(8,128)(2,1)S(1)}) custom-call(s32[3]{0:T(128)S(1)} %pad_add_fusion.place_ref, f32[32,1920]{1,0:T(8,128)S(1)} %get-tuple-element.25.gate_ref, bf16[32,1920]{1,0:T(8,128)(2,1)S(1)} %collective-permute-done.11.gate_other_ref, f32[32,1792]{1,0:T(8,128)S(1)} %get-tuple-element.28.up_ref, ...), custom_call_target="tpu_custom_call" | custom-call | bytes 7307276 | tf_op jit(solution)/shard_map/downs/pallas_call | solution.py:121
  50.7 1.2 %collective-permute-done.13.back_ref = bf16[16,1792]{1,0:T(8,128)(2,1)S(1)} collective-permute-done((bf16[16,1792]{1,0:T(8,128)(2,1)S(1)}, bf16[16,1792]{1,0:T(8,128)(2,1)S(1)}, u32[]{:S(2)}, u32[]{:S(2)}) %collective-permute-start.13) | collective-permute-done | bytes 57376 | tf_op jit(solution)/shard_map/ppermute | solution.py:112
  51.9 0.6 owners.1
  52.5 0.4 collective-permute-start.14
  53.0 3.2 %collective-permute-start.15 = (bf16[4,1792]{1,0:T(4,128)(2,1)S(1)}, bf16[4,1792]{1,0:T(4,128)(2,1)S(1)}, u32[]{:S(2)}, u32[]{:S(2)}) collective-permute-start(bf16[4,1792]{1,0:T(4,128)(2,1)S(1)} %get-tuple-element.34), channel_id=1, source_target_pairs={{0,8},{4,12},{8,0},{12,4},{1,9},{5,13},{9,1},{13,5},{2,10},{6,14},... | collective-permute-start | bytes 43016 | tf_op jit(solution)/shard_map/ppermute | solution.py:112
  56.1 0.9 %collective-permute-start.16 = (bf16[4,1792]{1,0:T(4,128)(2,1)S(1)}, bf16[4,1792]{1,0:T(4,128)(2,1)S(1)}, u32[]{:S(2)}, u32[]{:S(2)}) collective-permute-start(bf16[4,1792]{1,0:T(4,128)(2,1)S(1)} %get-tuple-element.35), channel_id=1, source_target_pairs={{0,12},{4,8},{8,4},{12,0},{1,13},{5,9},{9,5},{13,1},{2,14},{6,10},... | collective-permute-start | bytes 43016 | tf_op jit(solution)/shard_map/ppermute | solution.py:112
  57.0 0.1 dynamic_slice.3
  57.1 0.6 %reshape.144 = bf16[32,448]{1,0:T(8,128)(2,1)} reshape(bf16[4,2,4,448]{3,2,1,0:T(4,128)(2,1)S(1)} %copy.44) | data formatting | bytes 57344 | tf_op jit(solution)/shard_map/reshape | solution.py:469
  57.7 0.1 collective-permute-done.15
  57.8 3.8 %collective-permute-done.16 = bf16[4,1792]{1,0:T(4,128)(2,1)S(1)} collective-permute-done((bf16[4,1792]{1,0:T(4,128)(2,1)S(1)}, bf16[4,1792]{1,0:T(4,128)(2,1)S(1)}, u32[]{:S(2)}, u32[]{:S(2)}) %collective-permute-start.16) | collective-permute-done | bytes 14368 | tf_op jit(solution)/shard_map/ppermute | solution.py:112
  61.6 0.7 %multiply_convert_fusion = bf16[4,1792]{1,0:T(4,128)(2,1)} fusion(bf16[4,1792]{1,0:T(4,128)(2,1)S(1)} %collective-permute-done.16, bf16[4,1792]{1,0:T(4,128)(2,1)S(1)} %collective-permute-done.15, f32[4,1792]{1,0:T(4,128)S(1)} %get-tuple-element.32, bf16[4,1792]{1,0:T(4,128)(2,1)S(1)} %collective-permute-done.14, f32[4]{0:T(128)S(1)} %dynamic_slice.3), kind=kLoop, calls=%fused_computation.17 | loop fusion | flops 57344 | bytes 86032 | tf_op jit(solution)/shard_map/convert_element_type | solution.py:468
  (36 shorter events, 0.5 us)
Async XLA Ops:
  0.6 12.2 %copy-start = (bf16[1536,4,256]{2,1,0:T(4,128)(2,1)S(1)}, bf16[1536,4,256]{2,1,0:T(4,128)(2,1)}, u32[]{:S(2)}) copy-start(bf16[1536,4,256]{2,1,0:T(4,128)(2,1)} %param.13) | copy-start | bytes 9437188
  0.6 8.1 %collective-permute-start = (bf16[4,8,256]{2,1,0:T(8,128)(2,1)}, bf16[4,8,256]{2,1,0:T(8,128)(2,1)S(1)}, u32[]{:S(2)}, u32[]{:S(2)}) collective-permute-start(bf16[4,8,256]{2,1,0:T(8,128)(2,1)} %param.12), channel_id=1, source_target_pairs={{0,4},{4,0},{8,12},{12,8},{1,5},{5,1},{9,13},{13,9},{2,6},{6,2},{1... | collective-permute-start | bytes 49160 | tf_op jit(solution)/shard_map/ppermute | solution.py:112
  3.7 5.0 %collective-permute-start.1 = (bf16[4,8,256]{2,1,0:T(8,128)(2,1)}, bf16[4,8,256]{2,1,0:T(8,128)(2,1)S(1)}, u32[]{:S(2)}, u32[]{:S(2)}) collective-permute-start(bf16[4,8,256]{2,1,0:T(8,128)(2,1)} %param.12), channel_id=1, source_target_pairs={{0,8},{4,12},{8,0},{12,4},{1,9},{5,13},{9,1},{13,5},{2,10},{6,14},... | collective-permute-start | bytes 49160 | tf_op jit(solution)/shard_map/ppermute | solution.py:112
  6.3 5.7 %collective-permute-start.2 = (bf16[4,8,256]{2,1,0:T(8,128)(2,1)}, bf16[4,8,256]{2,1,0:T(8,128)(2,1)S(1)}, u32[]{:S(2)}, u32[]{:S(2)}) collective-permute-start(bf16[4,8,256]{2,1,0:T(8,128)(2,1)} %param.12), channel_id=1, source_target_pairs={{0,12},{4,8},{8,4},{12,0},{1,13},{5,9},{9,5},{13,1},{2,14},{6,10},... | collective-permute-start | bytes 49160 | tf_op jit(solution)/shard_map/ppermute | solution.py:112
  7.9 6.3 %copy-start.2 = (bf16[1536,4,256]{2,1,0:T(4,128)(2,1)S(1)}, bf16[1536,4,256]{2,1,0:T(4,128)(2,1)}, u32[]{:S(2)}) copy-start(bf16[1536,4,256]{2,1,0:T(4,128)(2,1)} %param.14) | copy-start | bytes 9437188
  15.2 6.4 %collective-permute-start.5 = (bf16[144,256]{1,0:T(8,128)(2,1)S(1)}, bf16[144,256]{1,0:T(8,128)(2,1)S(1)}, u32[]{:S(2)}, u32[]{:S(2)}) collective-permute-start(bf16[144,256]{1,0:T(8,128)(2,1)S(1)} %pad_maximum_fusion.refs_0_), channel_id=1, source_target_pairs={{0,12},{4,8},{8,4},{12,0},{1,13},{5,9},{9,5},{13,1},{2,14},{6,10},... | collective-permute-start | bytes 221192 | tf_op jit(solution)/shard_map/ppermute | solution.py:112
  15.9 6.8 %collective-permute-start.4 = (bf16[144,256]{1,0:T(8,128)(2,1)S(1)}, bf16[144,256]{1,0:T(8,128)(2,1)S(1)}, u32[]{:S(2)}, u32[]{:S(2)}) collective-permute-start(bf16[144,256]{1,0:T(8,128)(2,1)S(1)} %pad_maximum_fusion.refs_0_), channel_id=1, source_target_pairs={{0,8},{4,12},{8,0},{12,4},{1,9},{5,13},{9,1},{13,5},{2,10},{6,14},... | collective-permute-start | bytes 221192 | tf_op jit(solution)/shard_map/ppermute | solution.py:112
  15.9 6.8 %collective-permute-start.3 = (bf16[144,256]{1,0:T(8,128)(2,1)S(1)}, bf16[144,256]{1,0:T(8,128)(2,1)S(1)}, u32[]{:S(2)}, u32[]{:S(2)}) collective-permute-start(bf16[144,256]{1,0:T(8,128)(2,1)S(1)} %pad_maximum_fusion.refs_0_), channel_id=1, source_target_pairs={{0,4},{4,0},{8,12},{12,8},{1,5},{5,1},{9,13},{13,9},{2,6},{6,2},{1... | collective-permute-start | bytes 221192 | tf_op jit(solution)/shard_map/ppermute | solution.py:112
  21.3 5.7 %copy-start.1 = (bf16[448]{0:T(512)(128)(2,1)S(1)}, bf16[448]{0:T(512)(128)(2,1)}, u32[]{:S(2)}) copy-start(bf16[448]{0:T(512)(128)(2,1)} %param.18) | copy-start | bytes 2692
  23.0 1.3 %collective-permute-start.6 = (bf16[16,2048]{1,0:T(8,128)(2,1)S(1)}, bf16[16,2048]{1,0:T(8,128)(2,1)S(1)}, u32[]{:S(2)}, u32[]{:S(2)}) collective-permute-start(bf16[16,2048]{1,0:T(8,128)(2,1)S(1)} %combine.1.own_ref), channel_id=1, source_target_pairs={{0,1},{1,0},{2,3},{3,2},{4,5},{5,4},{6,7},{7,6},{8,9},{9,8},{10,11... | collective-permute-start | bytes 196616 | tf_op jit(solution)/shard_map/ppermute | solution.py:112
  25.5 4.5 %collective-permute-start.7 = (bf16[32,448]{1,0:T(8,128)(2,1)S(1)}, bf16[32,448]{1,0:T(8,128)(2,1)S(1)}, u32[]{:S(2)}, u32[]{:S(2)}) collective-permute-start(bf16[32,448]{1,0:T(8,128)(2,1)S(1)} %project.1.refs_0_.own_ref), channel_id=1, source_target_pairs={{0,2},{2,0},{1,3},{3,1},{4,6},{6,4},{5,7},{7,5},{8,10},{10,8},{9,1... | collective-permute-start | bytes 86024 | tf_op jit(solution)/shard_map/ppermute | solution.py:112
  30.1 5.8 %collective-permute-start.9 = (bf16[32,512]{1,0:T(8,128)(2,1)S(1)}, bf16[32,512]{1,0:T(8,128)(2,1)S(1)}, u32[]{:S(2)}, u32[]{:S(2)}) collective-permute-start(bf16[32,512]{1,0:T(8,128)(2,1)S(1)} %get-tuple-element.23.refs_0_.own_ref), channel_id=1, source_target_pairs={{0,12},{2,14},{4,8},{6,10},{8,4},{10,6},{12,0},{14,2},{1,13},{3,15... | collective-permute-start | bytes 98312 | tf_op jit(solution)/shard_map/ppermute | solution.py:331
  31.8 4.3 %collective-permute-start.8 = (bf16[32,512]{1,0:T(8,128)(2,1)S(1)}, bf16[32,512]{1,0:T(8,128)(2,1)S(1)}, u32[]{:S(2)}, u32[]{:S(2)}) collective-permute-start(bf16[32,512]{1,0:T(8,128)(2,1)S(1)} %get-tuple-element.23.refs_0_.own_ref), channel_id=1, source_target_pairs={{0,4},{2,8},{4,0},{6,12},{8,2},{10,14},{12,6},{14,10},{1,5},{3,9},... | collective-permute-start | bytes 98312 | tf_op jit(solution)/shard_map/ppermute | solution.py:332
  36.7 1.9 %collective-permute-start.10 = (bf16[2,32,512]{2,1,0:T(8,128)(2,1)S(1)}, bf16[2,32,512]{2,1,0:T(8,128)(2,1)S(1)}, u32[]{:S(2)}, u32[]{:S(2)}) collective-permute-start(bf16[2,32,512]{2,1,0:T(8,128)(2,1)S(1)} %pick.1.mine_ref), channel_id=1, source_target_pairs={{0,1},{1,0},{2,3},{3,2},{4,5},{5,4},{6,7},{7,6},{8,9},{9,8},{10,11... | collective-permute-start | bytes 196616 | tf_op jit(solution)/shard_map/ppermute | solution.py:112
  39.8 9.0 %collective-permute-start.11 = (bf16[32,1920]{1,0:T(8,128)(2,1)S(1)}, bf16[32,1920]{1,0:T(8,128)(2,1)S(1)}, u32[]{:S(2)}, u32[]{:S(2)}) collective-permute-start(bf16[32,1920]{1,0:T(8,128)(2,1)S(1)} %get-tuple-element.26), channel_id=1, source_target_pairs={{0,2},{2,0},{1,3},{3,1},{4,6},{6,4},{5,7},{7,5},{8,10},{10,8},{9,1... | collective-permute-start | bytes 368648 | tf_op jit(solution)/shard_map/ppermute | solution.py:112
  43.4 5.3 %collective-permute-start.12 = (bf16[32,1792]{1,0:T(8,128)(2,1)S(1)}, bf16[32,1792]{1,0:T(8,128)(2,1)S(1)}, u32[]{:S(2)}, u32[]{:S(2)}) collective-permute-start(bf16[32,1792]{1,0:T(8,128)(2,1)S(1)} %get-tuple-element.29.refs_0_), channel_id=1, source_target_pairs={{0,2},{2,0},{1,3},{3,1},{4,6},{6,4},{5,7},{7,5},{8,10},{10,8},{9,1... | collective-permute-start | bytes 344072 | tf_op jit(solution)/shard_map/ppermute | solution.py:112
  50.6 1.3 %collective-permute-start.13 = (bf16[16,1792]{1,0:T(8,128)(2,1)S(1)}, bf16[16,1792]{1,0:T(8,128)(2,1)S(1)}, u32[]{:S(2)}, u32[]{:S(2)}) collective-permute-start(bf16[16,1792]{1,0:T(8,128)(2,1)S(1)} %get-tuple-element.31), channel_id=1, source_target_pairs={{0,1},{1,0},{2,3},{3,2},{4,5},{5,4},{6,7},{7,6},{8,9},{9,8},{10,11... | collective-permute-start | bytes 172040 | tf_op jit(solution)/shard_map/ppermute | solution.py:112
  52.5 5.2 %collective-permute-start.14 = (bf16[4,1792]{1,0:T(4,128)(2,1)S(1)}, bf16[4,1792]{1,0:T(4,128)(2,1)S(1)}, u32[]{:S(2)}, u32[]{:S(2)}) collective-permute-start(bf16[4,1792]{1,0:T(4,128)(2,1)S(1)} %get-tuple-element.33), channel_id=1, source_target_pairs={{0,4},{4,0},{8,12},{12,8},{1,5},{5,1},{9,13},{13,9},{2,6},{6,2},{1... | collective-permute-start | bytes 43016 | tf_op jit(solution)/shard_map/ppermute | solution.py:112
  53.0 4.9 %collective-permute-start.15 = (bf16[4,1792]{1,0:T(4,128)(2,1)S(1)}, bf16[4,1792]{1,0:T(4,128)(2,1)S(1)}, u32[]{:S(2)}, u32[]{:S(2)}) collective-permute-start(bf16[4,1792]{1,0:T(4,128)(2,1)S(1)} %get-tuple-element.34), channel_id=1, source_target_pairs={{0,8},{4,12},{8,0},{12,4},{1,9},{5,13},{9,1},{13,5},{2,10},{6,14},... | collective-permute-start | bytes 43016 | tf_op jit(solution)/shard_map/ppermute | solution.py:112
  56.1 5.5 %collective-permute-start.16 = (bf16[4,1792]{1,0:T(4,128)(2,1)S(1)}, bf16[4,1792]{1,0:T(4,128)(2,1)S(1)}, u32[]{:S(2)}, u32[]{:S(2)}) collective-permute-start(bf16[4,1792]{1,0:T(4,128)(2,1)S(1)} %get-tuple-element.35), channel_id=1, source_target_pairs={{0,12},{4,8},{8,4},{12,0},{1,13},{5,9},{9,5},{13,1},{2,14},{6,10},... | collective-permute-start | bytes 43016 | tf_op jit(solution)/shard_map/ppermute | solution.py:112

commit v4 on v3

--- a/solution.py
+++ b/solution.py
@@ -103,7 +103,6 @@
 
 
 VM = pl.BlockSpec(memory_space=pltpu.VMEM)
-SM = pl.BlockSpec(memory_space=pltpu.SMEM)
 ANY = pl.BlockSpec(memory_space=pl.ANY)
 MIB = 1 << 20
 
@@ -116,13 +115,15 @@
     return [lax.select_n(at ^ k, *pieces) for k in range(len(pieces))]
 
 
-def kernel(body, name, outs, specs, args, limit=8, flops=0):
-    size = sum(a.size * a.dtype.itemsize for a in list(args) + list(outs))
+def kernel(body, name, outs, specs, args, limit=8, flops=0, aliases=None):
+    near = [a for a, spec in zip(args, specs) if spec is VM]
+    size = sum(a.size * a.dtype.itemsize for a in near + list(outs))
     return pl.pallas_call(
         body,
         out_shape=outs,
         in_specs=specs,
         out_specs=[VM] * len(outs),
+        input_output_aliases=aliases or {},
         compiler_params=pltpu.CompilerParams(vmem_limit_bytes=limit * MIB),
         cost_estimate=pl.CostEstimate(flops=flops, bytes_accessed=size, transcendentals=0),
         name=name,
@@ -130,10 +131,11 @@
 
 
 def fetch(after, arrays, name):
-    n = len(arrays)
+    n, skip = len(arrays), len(after)
 
     def body(*refs):
-        sources, targets, sems = refs[1 : 1 + n], refs[1 + n : 1 + 2 * n], refs[1 + 2 * n]
+        refs = refs[skip:]
+        sources, targets, sems = refs[:n], refs[n : 2 * n], refs[2 * n]
         copies = [
             pltpu.make_async_copy(sources[i], targets[i], sems.at[i]) for i in range(n)
         ]
@@ -146,13 +148,13 @@
     return pl.pallas_call(
         body,
         out_shape=[jax.ShapeDtypeStruct(a.shape, a.dtype) for a in arrays],
-        in_specs=[ANY] * (1 + n),
+        in_specs=[ANY] * (skip + n),
         out_specs=[VM] * n,
         scratch_shapes=[pltpu.SemaphoreType.DMA((n,))],
         compiler_params=pltpu.CompilerParams(vmem_limit_bytes=MIB),
         cost_estimate=pl.CostEstimate(flops=0, bytes_accessed=2 * size, transcendentals=0),
         name=name,
-    )(after, *[pltpu.with_memory_space_constraint(a, pltpu.HBM) for a in arrays])
+    )(*after, *[pltpu.with_memory_space_constraint(a, pltpu.HBM) for a in arrays])
 
 
 def parts_of(value, count):
@@ -199,11 +201,26 @@
     hidden_width, out_width = gate_weight.shape[1], down_weight.shape[1]
     toks = tok_dev * blks
     tokens = toks * 2
-    place = jnp.stack([row, blk, head]).astype(jnp.int32)
     sds = jax.ShapeDtypeStruct
 
-    pieces = [queries] + [hop(queries, "blk", blks, s) for s in range(1, blks)]
+    def inner(value):
+        value = value.reshape((blks, 2, tok_dev) + value.shape[1:])
+        return jnp.swapaxes(value, 0, 1).reshape((tokens,) + value.shape[3:])
+
+    valid_tok, masked_tok = token_masks(cand_lengths, masked_pos, tokens)
+    base_state = inner(jnp.where(masked_tok[:, None], mask_embed[None, :], dec_state))
+    keep_mask = valid_tok.astype(F32)
+    keep_inner = inner(keep_mask)[:, None]
+    own_start = (blk * 2 + row) * tok_dev
+    keep_own = lax.dynamic_slice_in_dim(keep_mask, own_start, tok_dev, 0)[:, None]
+    gain = norm_gain[None, :]
+
+    (queries_near,) = fetch([], [queries], "fetch_queries")
+    pieces = [queries_near] + [hop(queries, "blk", blks, s) for s in range(1, blks)]
     q_all = jnp.concatenate(by_index(pieces, blk), axis=0)
+    q_all, base_state, keep_inner, keep_own, gain = lax.optimization_barrier(
+        (q_all, base_state, keep_inner, keep_own, gain)
+    )
     grouped = q_all.reshape(toks, kv_local, group_size, head_size)
     scores = (
         jnp.einsum("tgjd,kgd->tgjk", grouped, src_keys, preferred_element_type=F32) * score_scale
@@ -222,10 +239,10 @@
     side = jnp.pad(side, ((0, 0), (0, head_size - side.shape[1])))
     note = jnp.concatenate([partial, side], axis=0)
     notes = [note] + [hop(note, "blk", blks, s) for s in range(1, blks)]
-    (proj_near,) = fetch(note, [out_weight.T], "fetch_proj")
+    (proj_near,) = fetch([note], [out_weight.T], "fetch_proj")
 
     def combine(*refs):
-        ins, out = refs[:blks], refs[-1]
+        ins, out = refs[:blks], refs[-2]
         base = local_heads * toks
         levels = []
         for ref in ins:
@@ -250,12 +267,13 @@
                 acc = term if acc is None else acc + term
             out[:, h * head_size : (h + 1) * head_size] = acc.astype(BF)
 
-    (attn,) = kernel(
+    attn, proj_near = kernel(
         combine,
         "combine",
-        [sds((toks, local_heads * head_size), BF)],
-        [VM] * blks + [ANY],
+        [sds((toks, local_heads * head_size), BF), sds(proj_near.shape, BF)],
+        [VM] * (blks + 1),
         notes + [proj_near],
+        aliases={blks: 1},
     )
     other = hop(attn, "rows", 2, 1)
     across = (((1,), (1,)), ((), ()))
@@ -274,8 +292,8 @@
         flops=2 * toks * width * attn.shape[1],
     )
 
-    def project(place_ref, own_ref, other_ref, weight_ref, out_ref):
-        first = place_ref[0] == 0
+    def project(own_ref, other_ref, weight_ref, out_ref):
+        first = lax.axis_index("rows") == 0
         own = own_ref[...]
         other = lax.dot_general(
             other_ref[...], weight_ref[...], across, preferred_element_type=F32
@@ -287,20 +305,12 @@
         project,
         "project",
         [sds((tokens, width), BF)],
-        [SM, VM, VM, VM],
-        [place, proj_own, other, proj_near],
+        [VM, VM, VM],
+        [proj_own, other, proj_near],
     )
     proj_other = hop(proj, "heads", 2, 1)
-    (gate_near,) = fetch(proj, [gate_weight], "fetch_gate")
-
-    def inner(value):
-        value = value.reshape((blks, 2, tok_dev) + value.shape[1:])
-        return jnp.swapaxes(value, 0, 1).reshape((tokens,) + value.shape[3:])
-
-    valid_tok, masked_tok = token_masks(cand_lengths, masked_pos, tokens)
-    base_state = inner(jnp.where(masked_tok[:, None], mask_embed[None, :], dec_state))
-    keep_mask = valid_tok.astype(F32)
-    keep_inner = inner(keep_mask)[:, None]
+    (gate_near,) = fetch([proj], [gate_weight], "fetch_gate")
+
     lanes = -(-(width + 2) // 128) * 128
 
     def middle(base_ref, keep_ref, gain_ref, own_ref, other_ref, near_ref, stream_ref, note_ref):
@@ -319,7 +329,7 @@
         "middle",
         [sds((tokens, width), BF), sds((tokens, lanes), BF)],
         [VM] * 5 + [ANY],
-        [base_state, keep_inner, norm_gain[None, :], proj, proj_other, gate_near],
+        [base_state, keep_inner, gain, proj, proj_other, gate_near],
     )
 
     far_pairs, near_pairs = [], []
@@ -330,12 +340,12 @@
             near_pairs.append((b * head_parts + h, to[0] * head_parts + to[1]))
     far = lax.ppermute(note, ("blk", "heads"), far_pairs)
     near = lax.ppermute(note, ("blk", "heads"), near_pairs)
-    (up_near,) = fetch(note, [up_weight], "fetch_up")
+    (up_near,) = fetch([note], [up_weight], "fetch_up")
     lanes_all = note.shape[1]
 
-    def pick(place_ref, own_ref, near_ref, far_ref, gate_ref, up_ref, out_ref):
-        at = place_ref[1]
-        inside = at // half == place_ref[2]
+    def pick(own_ref, near_ref, far_ref, gate_ref, up_ref, out_ref):
+        at = lax.axis_index("blk")
+        inside = at // half == lax.axis_index("heads")
         odd = at % 2 == 1
         own, near_tile, far_tile = own_ref[...], near_ref[...], far_ref[...]
         same = jnp.where(inside, own, near_tile)
@@ -347,8 +357,8 @@
         pick,
         "pick",
         [sds((half, tokens, lanes_all), BF)],
-        [SM, VM, VM, VM, ANY, ANY],
-        [place, note, near, far, gate_near, up_near],
+        [VM, VM, VM, ANY, ANY],
+        [note, near, far, gate_near, up_near],
     )
     theirs = hop(mine, "rows", 2, 1)
     rows_in = gate_weight.shape[0]
@@ -365,90 +375,119 @@
             total = term if total is None else total + term
         return total
 
-    def inner_products(place_ref, mine_ref, gate_ref, up_ref, gate_out, up_out):
-        gate_out[...] = tile_products(mine_ref, gate_ref, place_ref[0])
-        up_out[...] = tile_products(mine_ref, up_ref, place_ref[0])
+    def inner_products(mine_ref, gate_ref, up_ref, gate_out, up_out):
+        gate_out[...] = tile_products(mine_ref, gate_ref, lax.axis_index("rows"))
+        up_out[...] = tile_products(mine_ref, up_ref, lax.axis_index("rows"))
 
     gate_own, up_own = kernel(
         inner_products,
         "inner_products",
         [sds((tokens, hidden_width), F32)] * 2,
-        [SM, VM, VM, VM],
-        [place, mine, gate_near, up_near],
+        [VM, VM, VM],
+        [mine, gate_near, up_near],
         flops=2 * tokens * rows_in * hidden_width,
     )
 
-    def gates(place_ref, mine_ref, theirs_ref, own_ref, weight_ref, out_ref, note_ref):
-        squares = None
-        for k in range(half):
-            for ref in (mine_ref, theirs_ref):
-                here = ref[k, :, width : width + 2].astype(F32)
-                squares = here if squares is None else squares + here
-        squares = squares[:, 0:1] + squares[:, 1:2]
-        gate = own_ref[...] + tile_products(theirs_ref, weight_ref, 1 - place_ref[0])
-        out_ref[:, :hidden_width] = gate
-        note_ref[:, :hidden_width] = gate.astype(BF)
-        high, low = split_in(squares, 2)
-        lane = lax.broadcasted_iota(jnp.int32, (tokens, 128), 1)
-        out_ref[:, hidden_width:] = jnp.where(lane == 0, squares, 0.0)
-        note_ref[:, hidden_width:] = jnp.where(
-            lane == 0, high.astype(F32), jnp.where(lane == 1, low.astype(F32), 0.0)
-        ).astype(BF)
-
-    long_width = hidden_width + 128
-    gate, gate_note = kernel(
-        gates,
-        "gates",
-        [sds((tokens, long_width), F32), sds((tokens, long_width), BF)],
-        [SM, VM, VM, VM, VM],
-        [place, mine, theirs, gate_own, gate_near],
-    )
-    gate_other = hop(gate_note, "heads", 2, 1)
-
-    def ups(place_ref, theirs_ref, own_ref, weight_ref, out_ref, note_ref):
-        up = own_ref[...] + tile_products(theirs_ref, weight_ref, 1 - place_ref[0])
-        out_ref[...] = up
-        note_ref[...] = up.astype(BF)
-
-    up, up_note = kernel(
-        ups,
-        "ups",
-        [sds((tokens, hidden_width), F32), sds((tokens, hidden_width), BF)],
-        [SM, VM, VM, VM],
-        [place, theirs, up_own, up_near],
-        flops=tokens * rows_in * hidden_width,
-    )
-    up_other = hop(up_note, "heads", 2, 1)
-    (down_near,) = fetch(up_note, [down_weight], "fetch_down")
-
-    def downs(
-        place_ref, gate_ref, gate_other_ref, up_ref, up_other_ref, weight_ref, keep_ref, away_ref
+    cut = -(-hidden_width // 512) * 256
+    pieces_at = [(0, cut), (cut, hidden_width)]
+
+    def gate_up(lo, hi, with_squares):
+        span = hi - lo
+
+        def body(*refs):
+            theirs_ref, gate_in, up_in, gate_w, up_w = refs[:5]
+            out_ref, note_ref = refs[-2:]
+            row_at = 1 - lax.axis_index("rows")
+            for k, (own, weight) in enumerate(((gate_in, gate_w), (up_in, up_w))):
+                value = own[:, lo:hi] + tile_products(theirs_ref, weight.at[:, lo:hi], row_at)
+                out_ref[:, k * span : (k + 1) * span] = value
+                note_ref[:, k * span : (k + 1) * span] = value.astype(BF)
+            if with_squares:
+                squares = None
+                for k in range(half):
+                    for ref in (refs[5], theirs_ref):
+                        here = ref[k, :, width : width + 2].astype(F32)
+                        squares = here if squares is None else squares + here
+                squares = squares[:, 0:1] + squares[:, 1:2]
+                high, low = split_in(squares, 2)
+                lane = lax.broadcasted_iota(jnp.int32, (tokens, 128), 1)
+                out_ref[:, 2 * span :] = jnp.where(lane == 0, squares, 0.0)
+                note_ref[:, 2 * span :] = jnp.where(
+                    lane == 0, high.astype(F32), jnp.where(lane == 1, low.astype(F32), 0.0)
+                ).astype(BF)
+
+        return body
+
+    sums, sum_notes = [], []
+    for c, (lo, hi) in enumerate(pieces_at):
+        operands = [theirs, gate_own, up_own, gate_near, up_near] + [mine] * (c == 0)
+        long_width = 2 * (hi - lo) + 128 * (c == 0)
+        value, value_note = kernel(
+            gate_up(lo, hi, c == 0),
+            f"gate_up_{c}",
+            [sds((tokens, long_width), F32), sds((tokens, long_width), BF)],
+            [VM] * len(operands),
+            operands,
+            flops=tokens * rows_in * hidden_width,
+        )
+        sums.append(value)
+        sum_notes.append(value_note)
+    sum_others = [hop(value, "heads", 2, 1) for value in sum_notes]
+    (down_near,) = fetch([sum_notes[-1]], [down_weight], "fetch_down")
+
+    def down_piece(c, own_ref, other_ref, first_ref, first_other_ref, weight_ref):
+        lo, hi = pieces_at[c]
+        span, at = hi - lo, 2 * cut
+        other = first_other_ref[:, at:].astype(F32)
+        squares = first_ref[:, at : at + 1] + other[:, 0:1] + other[:, 1:2]
+        inv_rms = lax.rsqrt(squares / features + EPS)
+        gate, up = [
+            (
+                own_ref[:, k * span : (k + 1) * span]
+                + other_ref[:, k * span : (k + 1) * span].astype(F32)
+            )
+            * inv_rms
+            for k in range(2)
+        ]
+        hidden = (jax.nn.gelu(gate, approximate=True) * up).astype(BF)
+        return jnp.dot(hidden, weight_ref[lo:hi, :], preferred_element_type=F32)
+
+    def down_first(own_ref, other_ref, weight_ref, out_ref):
+        out_ref[...] = down_piece(0, own_ref, other_ref, own_ref, other_ref, weight_ref)
+
+    (down_part,) = kernel(
+        down_first,
+        "down_first",
+        [sds((tokens, out_width), F32)],
+        [VM] * 3,
+        [sums[0], sum_others[0], down_near],
+        flops=tokens * hidden_width * out_width,
+    )
+
+    def down_last(
+        own_ref, other_ref, first_ref, first_other_ref, part_ref, weight_ref, keep_ref, away_ref
     ):
-        other = gate_other_ref[:, hidden_width:].astype(F32)
-        squares = gate_ref[:, hidden_width : hidden_width + 1] + other[:, 0:1] + other[:, 1:2]
-        inv_rms = lax.rsqrt(squares / features + EPS)
-        gate = (gate_ref[:, :hidden_width] + gate_other_ref[:, :hidden_width].astype(F32)) * inv_rms
-        up = (up_ref[...] + up_other_ref[...].astype(F32)) * inv_rms
-        hidden = (jax.nn.gelu(gate, approximate=True) * up).astype(BF)
-        down = jnp.dot(hidden, weight_ref[...], preferred_element_type=F32)
-        first = place_ref[0] == 0
+        down = part_ref[...] + down_piece(
+            1, own_ref, other_ref, first_ref, first_other_ref, weight_ref
+        )
+        first = lax.axis_index("rows") == 0
         keep_ref[...] = jnp.where(first, down[:toks], down[toks:])
         away_ref[...] = jnp.where(first, down[toks:], down[:toks]).astype(BF)
 
     keep, away = kernel(
-        downs,
-        "downs",
+        down_last,
+        "down_last",
         [sds((toks, out_width), F32), sds((toks, out_width), BF)],
-        [SM] + [VM] * 5,
-        [place, gate, gate_other, up, up_other, down_near],
+        [VM] * 6,
+        [sums[1], sum_others[1], sums[0], sum_others[0], down_part, down_near],
         limit=12,
     )
     back = hop(away, "rows", 2, 1)
 
-    def owners(place_ref, keep_ref, back_ref, own_ref, *piece_refs):
+    def owners(keep_ref, back_ref, own_ref, *piece_refs):
         total = keep_ref[...] + back_ref[...].astype(F32)
         blocks = [total[k * tok_dev : (k + 1) * tok_dev] for k in range(blks)]
-        at = place_ref[1]
+        at = lax.axis_index("blk")
         for s, ref in enumerate((own_ref,) + piece_refs):
             value = blocks[0]
             for k in range(1, blks):
@@ -459,13 +498,12 @@
         owners,
         "owners",
         [sds((tok_dev, out_width), F32)] + [sds((tok_dev, out_width), BF)] * (blks - 1),
-        [SM, VM, VM],
-        [place, keep, back],
+        [VM, VM],
+        [keep, back],
     )
     for s in range(1, blks):
         own = own + hop(sends[s - 1], "blk", blks, s).astype(F32)
-    keep_own = lax.dynamic_slice_in_dim(keep_mask, (blk * 2 + row) * tok_dev, tok_dev, 0)
-    branch = (own * keep_own[:, None]).astype(BF)
+    branch = (own * keep_own).astype(BF)
     stream = stream.reshape(2, blks, tok_dev, width).swapaxes(0, 1).reshape(tokens, width)
     return (stream, branch)
 

time: 62.7 us -> 58.6 us (0.935)
  Pallas kernels: 19.4 us -> 16.5 us
  waiting for transfers between devices: 14.4 us -> 12.6 us
  starting transfers between devices: 20.5 us -> 21.3 us
  other arithmetic: 3.47 us -> 2.68 us
  local copies, waits for them, and re-layouts: 1.07 us -> 1.74 us
    pallas_call x10 -> x11, Pallas kernels: 9.38 us -> 5.82 us  [kernel(): pl.pallas_call(body, out_shape=outs, in_specs=specs, out_specs=[VM] * len...]
    ppermute x15, waiting for transfers between devices: 12.9 us -> 11.2 us  [hop(): return lax.ppermute(value, axis, [(i, i ^ step) for i in range(size)])]
    broadcast_in_dim x1 -> x2, local copies, waits for them, and re-layouts: 0.01 us -> 0.76 us  [the longest x1 0.68 us: shards_direct(): gain = norm_gain[None, :]]
    pallas_call x4 -> x5, Pallas kernels: 10 us -> 10.7 us  [fetch(): pl.pallas_call(body, out_shape=[jax.ShapeDtypeStruct(a.shape, a.dtype) fo...]
    select_n x1, other arithmetic: 0.73 us -> 0.02 us  [by_index(): return [lax.select_n(at ^ k, *pieces) for k in range(len(pieces))]]
    ppermute x1, waiting for transfers between devices: 1.29 us -> 0.6 us  [shards_direct(): far = lax.ppermute(note, ('blk', 'heads'), far_pairs)]
  transfers between devices with their start and end apart: 17 -> 17, of which waited for: 10 -> 10; matrix products, arithmetic and copies ran while one was open for 4% -> 5% of each run, Pallas kernels for 22% -> 24%
where the time goes in v4:
time: 58.6 us; the launch traced here: 58.2 us
  starting transfers between devices  21.3 us (36%)
  Pallas kernels  16.5 us (28%)
  waiting for transfers between devices  12.6 us (22%)
  other arithmetic  2.68 us (5%)
  matrix products  1.83 us (3%)
  local copies, waits for them, and re-layouts  1.74 us (3%)
  between operations  1.52 us (3%)
    ppermute x15, starting transfers between devices, hop(): return lax.ppermute(value, axis, [(i, i ^ step) for i in range(size)])  19 us
    ppermute x15, waiting for transfers between devices, hop(): return lax.ppermute(value, axis, [(i, i ^ step) for i in range(size)])  11.2 us
    pallas_call x5, Pallas kernels, fetch(): pl.pallas_call(body, out_shape=[jax.ShapeDtypeStruct(a.shape, a.dtype) fo...  10.7 us
    pallas_call x11, Pallas kernels, kernel(): pl.pallas_call(body, out_shape=outs, in_specs=specs, out_specs=[VM] * len...  5.82 us
    ppermute x1, starting transfers between devices, shards_direct(): far = lax.ppermute(note, ('blk', 'heads'), far_pairs)  2.31 us
  transfers between devices with their start and end apart: 17, of which 10 were waited for; matrix products, arithmetic and copies ran while one was open for 5% of the time, Pallas kernels for 24%

profile of v4, /device:TPU:0, one launch (start us, length us, event | category | flops | bytes accessed | tf_op | source)
XLA Modules:
  0.0 58.2 jit_solution(1076097464454889907)
XLA Ops:
  0.6 3.1 %collective-permute-start = (bf16[4,8,256]{2,1,0:T(8,128)(2,1)}, bf16[4,8,256]{2,1,0:T(8,128)(2,1)S(1)}, u32[]{:S(2)}, u32[]{:S(2)}) collective-permute-start(bf16[4,8,256]{2,1,0:T(8,128)(2,1)} %refs_0_.1), channel_id=1, source_target_pairs={{0,4},{4,0},{8,12},{12,8},{1,5},{5,1},{9,13},{13,9},{2,6},{6,2},{1... | collective-permute-start | bytes 49160 | tf_op jit(solution)/shard_map/ppermute | solution.py:111
  3.7 2.5 %collective-permute-start.2 = (bf16[4,8,256]{2,1,0:T(8,128)(2,1)}, bf16[4,8,256]{2,1,0:T(8,128)(2,1)S(1)}, u32[]{:S(2)}, u32[]{:S(2)}) collective-permute-start(bf16[4,8,256]{2,1,0:T(8,128)(2,1)} %refs_0_.1), channel_id=1, source_target_pairs={{0,12},{4,8},{8,4},{12,0},{1,13},{5,9},{9,5},{13,1},{2,14},{6,10},... | collective-permute-start | bytes 49160 | tf_op jit(solution)/shard_map/ppermute | solution.py:111
  6.2 0.1 collective-permute-start.1
  7.0 0.7 %fusion.23 = pred[128]{0:T(512)(128)(4,1)S(1)} fusion(s32[48]{0:T(128)} %bitcast.46), kind=kLoop, calls=%fused_computation.22 | loop fusion | flops 12160 | bytes 320 | tf_op jit(solution)/shard_map/reduce_or | solution.py:19
  7.7 0.1 iota.55
  7.8 0.8 %broadcast_select_fusion = bf16[32,448]{1,0:T(8,128)(2,1)S(1)} fusion(bf16[32,448]{1,0:T(8,128)(2,1)} %param.15, pred[32]{0:T(512)(128)(4,1)S(1)} %slice_bitcast_fusion, bf16[448]{0:T(512)(128)(2,1)} %param.16), kind=kLoop, calls=%fused_computation.16 | loop fusion | flops 14336 | bytes 58272 | tf_op jit(solution)/shard_map/jit(_where)/select_n | solution.py:211
  8.7 0.1 dynamic-slice_bitcast_fusion
  8.8 0.7 %fetch_queries.1 = bf16[4,8,256]{2,1,0:T(8,128)(2,1)S(1)} custom-call(bf16[4,8,256]{2,1,0:T(8,128)(2,1)} %refs_0_.1), custom_call_target="tpu_custom_call" | custom-call | bytes 32768 | tf_op jit(solution)/shard_map/fetch_queries/pallas_call | solution.py:148
  9.5 0.7 %broadcast_in_dim.35.gain_ref = bf16[1,448]{1,0:T(2,128)(2,1)S(1)} reshape(bf16[448]{0:T(512)(128)(2,1)} %param.18) | data formatting | bytes 1792 | tf_op jit(solution)/shard_map/broadcast_in_dim | solution.py:216
  10.3 0.8 %collective-permute-done.1 = bf16[4,8,256]{2,1,0:T(8,128)(2,1)S(1)} collective-permute-done((bf16[4,8,256]{2,1,0:T(8,128)(2,1)}, bf16[4,8,256]{2,1,0:T(8,128)(2,1)S(1)}, u32[]{:S(2)}, u32[]{:S(2)}) %collective-permute-start.1) | collective-permute-done | bytes 16416 | tf_op jit(solution)/shard_map/ppermute | solution.py:111
  11.1 1.1 %fusion.34 = (f32[16,4,2]{0,2,1:T(2,128)S(1)}, f32[16,4,2,1536]{3,0,2,1:T(8,128)S(1)}) fusion(bf16[16,4,2,256]{3,0,2,1:T(8,128)(2,1)S(1)} %bitcast.35, bf16[1536,4,256,1]{2,1,0,3:T(4,128)(2,1)S(1)} %bitcast.33), kind=kOutput, calls=%fused_computation.46 | convolution fusion | flops 101056384 | bytes 3998208 | tf_op jit(solution)/shard_map/tgjd,kgd->tgjk/dot_general | solution.py:226
  12.3 0.3 fusion.19
  12.5 0.7 %fusion.16 = bf16[4,2,16,256]{3,2,1,0:T(8,128)(2,1)S(1)} fusion(bf16[1536,4,256,1]{2,1,0,3:T(4,128)(2,1)S(1)} %bitcast.45, f32[16,4,2,1536]{3,0,2,1:T(8,128)S(1)} %get-tuple-element.58, f32[16,4,2]{0,2,1:T(2,128)S(1)} %get-tuple-element.31, f32[4,2,16]{2,1,0:T(2,128)S(1)} %bitcast.42), kind=kOutput, calls=%fused_computation.8 | convolution fusion | flops 101122048 | bytes 3998720 | tf_op jit(solution)/shard_map/tgjk,kgd->tgjd/dot_general | solution.py:231
  13.3 0.1 copy.43
  13.4 0.1 fusion.33
  13.5 2.6 %collective-permute-start.5 = (bf16[144,256]{1,0:T(8,128)(2,1)S(1)}, bf16[144,256]{1,0:T(8,128)(2,1)S(1)}, u32[]{:S(2)}, u32[]{:S(2)}) collective-permute-start(bf16[144,256]{1,0:T(8,128)(2,1)S(1)} %pad_maximum_fusion.refs_0_), channel_id=1, source_target_pairs={{0,12},{4,8},{8,4},{12,0},{1,13},{5,9},{9,5},{13,1},{2,14},{6,10},... | collective-permute-start | bytes 221192 | tf_op jit(solution)/shard_map/ppermute | solution.py:111
  16.1 0.3 collective-permute-start.4
  16.4 1.6 %collective-permute-start.3 = (bf16[144,256]{1,0:T(8,128)(2,1)S(1)}, bf16[144,256]{1,0:T(8,128)(2,1)S(1)}, u32[]{:S(2)}, u32[]{:S(2)}) collective-permute-start(bf16[144,256]{1,0:T(8,128)(2,1)S(1)} %pad_maximum_fusion.refs_0_), channel_id=1, source_target_pairs={{0,4},{4,0},{8,12},{12,8},{1,5},{5,1},{9,13},{13,9},{2,6},{6,2},{1... | collective-permute-start | bytes 221192 | tf_op jit(solution)/shard_map/ppermute | solution.py:111
  18.0 1.5 %fetch_proj.1.refs_4_ = bf16[448,2048]{1,0:T(8,128)(2,1)S(1)} custom-call(bf16[144,256]{1,0:T(8,128)(2,1)S(1)} %pad_maximum_fusion.refs_0_, bf16[448,2048]{1,0:T(8,128)(2,1)} %bitcast.34), custom_call_target="tpu_custom_call" | custom-call | bytes 3670016 | tf_op jit(solution)/shard_map/fetch_proj/pallas_call | solution.py:148
  19.5 0.8 %collective-permute-done.5.refs_3_ = bf16[144,256]{1,0:T(8,128)(2,1)S(1)} collective-permute-done((bf16[144,256]{1,0:T(8,128)(2,1)S(1)}, bf16[144,256]{1,0:T(8,128)(2,1)S(1)}, u32[]{:S(2)}, u32[]{:S(2)}) %collective-permute-start.5) | collective-permute-done | bytes 73760 | tf_op jit(solution)/shard_map/ppermute | solution.py:111
  20.3 2.4 %collective-permute-done.4.refs_2_ = bf16[144,256]{1,0:T(8,128)(2,1)S(1)} collective-permute-done((bf16[144,256]{1,0:T(8,128)(2,1)S(1)}, bf16[144,256]{1,0:T(8,128)(2,1)S(1)}, u32[]{:S(2)}, u32[]{:S(2)}) %collective-permute-start.4) | collective-permute-done | bytes 73760 | tf_op jit(solution)/shard_map/ppermute | solution.py:111
  22.7 0.2 combine.1
  23.0 0.6 project_own.1.own_ref
  23.6 0.7 %collective-permute-done.6.other_ref = bf16[16,2048]{1,0:T(8,128)(2,1)S(1)} collective-permute-done((bf16[16,2048]{1,0:T(8,128)(2,1)S(1)}, bf16[16,2048]{1,0:T(8,128)(2,1)S(1)}, u32[]{:S(2)}, u32[]{:S(2)}) %collective-permute-start.6) | collective-permute-done | bytes 65568 | tf_op jit(solution)/shard_map/ppermute | solution.py:111
  24.3 0.6 project.1.refs_0_.own_ref
  24.9 1.5 %collective-permute-start.7 = (bf16[32,448]{1,0:T(8,128)(2,1)S(1)}, bf16[32,448]{1,0:T(8,128)(2,1)S(1)}, u32[]{:S(2)}, u32[]{:S(2)}) collective-permute-start(bf16[32,448]{1,0:T(8,128)(2,1)S(1)} %project.1.refs_0_.own_ref), channel_id=1, source_target_pairs={{0,2},{2,0},{1,3},{3,1},{4,6},{6,4},{5,7},{7,5},{8,10},{10,8},{9,1... | collective-permute-start | bytes 86024 | tf_op jit(solution)/shard_map/ppermute | solution.py:111
  26.4 2.8 %fetch_gate.1.near_ref.gate_ref.refs_3_ = bf16[1792,1792]{1,0:T(8,128)(2,1)S(1)} custom-call(bf16[32,448]{1,0:T(8,128)(2,1)S(1)} %project.1.refs_0_.own_ref, bf16[1792,1792]{1,0:T(8,128)(2,1)} %refs_1_.3), custom_call_target="tpu_custom_call" | custom-call | bytes 12845056 | tf_op jit(solution)/shard_map/fetch_gate/pallas_call | solution.py:148
  29.2 0.2 middle.1
  29.4 2.3 %collective-permute-start.9 = (bf16[32,512]{1,0:T(8,128)(2,1)S(1)}, bf16[32,512]{1,0:T(8,128)(2,1)S(1)}, u32[]{:S(2)}, u32[]{:S(2)}) collective-permute-start(bf16[32,512]{1,0:T(8,128)(2,1)S(1)} %get-tuple-element.36.refs_0_.own_ref), channel_id=1, source_target_pairs={{0,12},{2,14},{4,8},{6,10},{8,4},{10,6},{12,0},{14,2},{1,13},{3,15... | collective-permute-start | bytes 98312 | tf_op jit(solution)/shard_map/ppermute | solution.py:341
  31.7 2.8 %fetch_up.1.up_ref.refs_4_ = bf16[1792,1792]{1,0:T(8,128)(2,1)S(1)} custom-call(bf16[32,512]{1,0:T(8,128)(2,1)S(1)} %get-tuple-element.36.refs_0_.own_ref, bf16[1792,1792]{1,0:T(8,128)(2,1)} %refs_1_.4), custom_call_target="tpu_custom_call" | custom-call | bytes 12845056 | tf_op jit(solution)/shard_map/fetch_up/pallas_call | solution.py:148
  34.6 0.6 %collective-permute-done.9.far_ref = bf16[32,512]{1,0:T(8,128)(2,1)S(1)} collective-permute-done((bf16[32,512]{1,0:T(8,128)(2,1)S(1)}, bf16[32,512]{1,0:T(8,128)(2,1)S(1)}, u32[]{:S(2)}, u32[]{:S(2)}) %collective-permute-start.9) | collective-permute-done | bytes 32800 | tf_op jit(solution)/shard_map/ppermute | solution.py:341
  35.2 0.8 %collective-permute-done.8.near_ref = bf16[32,512]{1,0:T(8,128)(2,1)S(1)} collective-permute-done((bf16[32,512]{1,0:T(8,128)(2,1)S(1)}, bf16[32,512]{1,0:T(8,128)(2,1)S(1)}, u32[]{:S(2)}, u32[]{:S(2)}) %collective-permute-start.8) | collective-permute-done | bytes 32800 | tf_op jit(solution)/shard_map/ppermute | solution.py:342
  36.0 1.2 %inner_products.1 = (f32[32,1792]{1,0:T(8,128)S(1)}, f32[32,1792]{1,0:T(8,128)S(1)}) custom-call(bf16[2,32,512]{2,1,0:T(8,128)(2,1)S(1)} %pick.1.mine_ref.refs_5_, bf16[1792,1792]{1,0:T(8,128)(2,1)S(1)} %fetch_gate.1.near_ref.gate_ref.refs_3_, bf16[1792,1792]{1,0:T(8,128)(2,1)S(1)} %fetch_up.1.up_ref.refs_4_), custom_call_target="tpu_custom_call" | custom-call | flops 205520896 | bytes 13369344 | tf_op jit(solution)/shard_map/inner_products/pallas_call | solution.py:121
  37.3 0.8 %gate_up_0.1 = (f32[32,2176]{1,0:T(8,128)S(1)}, bf16[32,2176]{1,0:T(8,128)(2,1)S(1)}) custom-call(bf16[2,32,512]{2,1,0:T(8,128)(2,1)S(1)} %collective-permute-done.10.refs_0_, f32[32,1792]{1,0:T(8,128)S(1)} %get-tuple-element.37.refs_1_, f32[32,1792]{1,0:T(8,128)S(1)} %get-tuple-element.38.refs_2_, ...), custom_call_target="tpu_custom_call" | custom-call | flops 102760448 | bytes 13852672 | tf_op jit(solution)/shard_map/gate_up_0/pallas_call | solution.py:121
  38.0 2.6 %collective-permute-start.12 = (bf16[32,2176]{1,0:T(8,128)(2,1)S(1)}, bf16[32,2176]{1,0:T(8,128)(2,1)S(1)}, u32[]{:S(2)}, u32[]{:S(2)}) collective-permute-start(bf16[32,2176]{1,0:T(8,128)(2,1)S(1)} %get-tuple-element.42), channel_id=1, source_target_pairs={{0,2},{2,0},{1,3},{3,1},{4,6},{6,4},{5,7},{7,5},{8,10},{10,8},{9,1... | collective-permute-start | bytes 417800 | tf_op jit(solution)/shard_map/ppermute | solution.py:111
  40.7 0.6 %gate_up_1.1 = (f32[32,1536]{1,0:T(8,128)S(1)}, bf16[32,1536]{1,0:T(8,128)(2,1)S(1)}) custom-call(bf16[2,32,512]{2,1,0:T(8,128)(2,1)S(1)} %collective-permute-done.10.refs_0_, f32[32,1792]{1,0:T(8,128)S(1)} %get-tuple-element.37.refs_1_, f32[32,1792]{1,0:T(8,128)S(1)} %get-tuple-element.38.refs_2_, ...), custom_call_target="tpu_custom_call" | custom-call | flops 102760448 | bytes 13664256 | tf_op jit(solution)/shard_map/gate_up_1/pallas_call | solution.py:121
  41.3 0.1 collective-permute-start.11
  41.3 2.8 %fetch_down.1.weight_ref = bf16[1792,1792]{1,0:T(8,128)(2,1)S(1)} custom-call(bf16[32,1536]{1,0:T(8,128)(2,1)S(1)} %get-tuple-element.40.refs_0_, bf16[1792,1792]{1,0:T(8,128)(2,1)} %refs_1_.5), custom_call_target="tpu_custom_call" | custom-call | bytes 12845056 | tf_op jit(solution)/shard_map/fetch_down/pallas_call | solution.py:148
  44.2 1.0 %collective-permute-done.12.other_ref.first_other_ref = bf16[32,2176]{1,0:T(8,128)(2,1)S(1)} collective-permute-done((bf16[32,2176]{1,0:T(8,128)(2,1)S(1)}, bf16[32,2176]{1,0:T(8,128)(2,1)S(1)}, u32[]{:S(2)}, u32[]{:S(2)}) %collective-permute-start.12) | collective-permute-done | bytes 139296 | tf_op jit(solution)/shard_map/ppermute | solution.py:111
  45.2 0.8 %down_first.1.part_ref = f32[32,1792]{1,0:T(8,128)S(1)} custom-call(f32[32,2176]{1,0:T(8,128)S(1)} %get-tuple-element.41.own_ref.first_ref, bf16[32,2176]{1,0:T(8,128)(2,1)S(1)} %collective-permute-done.12.other_ref.first_other_ref, bf16[1792,1792]{1,0:T(8,128)(2,1)S(1)} %fetch_down.1.weight_ref), custom_call_target="tpu_custom_call" | custom-call | flops 102760448 | bytes 7069696 | tf_op jit(solution)/shard_map/down_first/pallas_call | solution.py:121
  46.0 1.1 %collective-permute-done.11.other_ref = bf16[32,1536]{1,0:T(8,128)(2,1)S(1)} collective-permute-done((bf16[32,1536]{1,0:T(8,128)(2,1)S(1)}, bf16[32,1536]{1,0:T(8,128)(2,1)S(1)}, u32[]{:S(2)}, u32[]{:S(2)}) %collective-permute-start.11) | collective-permute-done | bytes 98336 | tf_op jit(solution)/shard_map/ppermute | solution.py:111
  47.1 0.7 %down_last.1 = (f32[16,1792]{1,0:T(8,128)S(1)}, bf16[16,1792]{1,0:T(8,128)(2,1)S(1)}) custom-call(f32[32,1536]{1,0:T(8,128)S(1)} %get-tuple-element.39.own_ref, bf16[32,1536]{1,0:T(8,128)(2,1)S(1)} %collective-permute-done.11.other_ref, f32[32,2176]{1,0:T(8,128)S(1)} %get-tuple-element.41.own_ref.first_ref, ...), custom_call_target="tpu_custom_call" | custom-call | bytes 7536640 | tf_op jit(solution)/shard_map/down_last/pallas_call | solution.py:121
  47.9 1.2 %collective-permute-done.13.back_ref = bf16[16,1792]{1,0:T(8,128)(2,1)S(1)} collective-permute-done((bf16[16,1792]{1,0:T(8,128)(2,1)S(1)}, bf16[16,1792]{1,0:T(8,128)(2,1)S(1)}, u32[]{:S(2)}, u32[]{:S(2)}) %collective-permute-start.13) | collective-permute-done | bytes 57376 | tf_op jit(solution)/shard_map/ppermute | solution.py:111
  49.2 2.7 %collective-permute-start.15 = (bf16[4,1792]{1,0:T(4,128)(2,1)S(1)}, bf16[4,1792]{1,0:T(4,128)(2,1)S(1)}, u32[]{:S(2)}, u32[]{:S(2)}) collective-permute-start(bf16[4,1792]{1,0:T(4,128)(2,1)S(1)} %get-tuple-element.47), channel_id=1, source_target_pairs={{0,8},{4,12},{8,0},{12,4},{1,9},{5,13},{9,1},{13,5},{2,10},{6,14},... | collective-permute-start | bytes 43016 | tf_op jit(solution)/shard_map/ppermute | solution.py:111
  52.0 1.6 %collective-permute-start.16 = (bf16[4,1792]{1,0:T(4,128)(2,1)S(1)}, bf16[4,1792]{1,0:T(4,128)(2,1)S(1)}, u32[]{:S(2)}, u32[]{:S(2)}) collective-permute-start(bf16[4,1792]{1,0:T(4,128)(2,1)S(1)} %get-tuple-element.48), channel_id=1, source_target_pairs={{0,12},{4,8},{8,4},{12,0},{1,13},{5,9},{9,5},{13,1},{2,14},{6,10},... | collective-permute-start | bytes 43016 | tf_op jit(solution)/shard_map/ppermute | solution.py:111
  53.7 0.6 %reshape.143 = bf16[32,448]{1,0:T(8,128)(2,1)} reshape(bf16[4,2,4,448]{3,2,1,0:T(4,128)(2,1)S(1)} %copy.45) | data formatting | bytes 57344 | tf_op jit(solution)/shard_map/reshape | solution.py:507
  54.3 3.2 %collective-permute-done.16 = bf16[4,1792]{1,0:T(4,128)(2,1)S(1)} collective-permute-done((bf16[4,1792]{1,0:T(4,128)(2,1)S(1)}, bf16[4,1792]{1,0:T(4,128)(2,1)S(1)}, u32[]{:S(2)}, u32[]{:S(2)}) %collective-permute-start.16) | collective-permute-done | bytes 14368 | tf_op jit(solution)/shard_map/ppermute | solution.py:111
  57.5 0.7 %multiply_convert_fusion = bf16[4,1792]{1,0:T(4,128)(2,1)} fusion(bf16[4,1792]{1,0:T(4,128)(2,1)S(1)} %collective-permute-done.16, bf16[4,1792]{1,0:T(4,128)(2,1)S(1)} %collective-permute-done.15, f32[4,1792]{1,0:T(4,128)S(1)} %get-tuple-element.45, bf16[4,1792]{1,0:T(4,128)(2,1)S(1)} %collective-permute-done.14, f32[4]{0:T(128)S(1)} %bitcast.44), kind=kLoop, calls=%fused_computation.17 | loop fusion | flops 57344 | bytes 86032 | tf_op jit(solution)/shard_map/convert_element_type | solution.py:506
  (35 shorter events, 0.6 us)
Async XLA Ops:
  0.6 10.5 %copy-start = (bf16[1536,4,256]{2,1,0:T(4,128)(2,1)S(1)}, bf16[1536,4,256]{2,1,0:T(4,128)(2,1)}, u32[]{:S(2)}) copy-start(bf16[1536,4,256]{2,1,0:T(4,128)(2,1)} %param.13) | copy-start | bytes 9437188
  0.6 9.6 %collective-permute-start = (bf16[4,8,256]{2,1,0:T(8,128)(2,1)}, bf16[4,8,256]{2,1,0:T(8,128)(2,1)S(1)}, u32[]{:S(2)}, u32[]{:S(2)}) collective-permute-start(bf16[4,8,256]{2,1,0:T(8,128)(2,1)} %refs_0_.1), channel_id=1, source_target_pairs={{0,4},{4,0},{8,12},{12,8},{1,5},{5,1},{9,13},{13,9},{2,6},{6,2},{1... | collective-permute-start | bytes 49160 | tf_op jit(solution)/shard_map/ppermute | solution.py:111
  3.7 6.5 %collective-permute-start.2 = (bf16[4,8,256]{2,1,0:T(8,128)(2,1)}, bf16[4,8,256]{2,1,0:T(8,128)(2,1)S(1)}, u32[]{:S(2)}, u32[]{:S(2)}) collective-permute-start(bf16[4,8,256]{2,1,0:T(8,128)(2,1)} %refs_0_.1), channel_id=1, source_target_pairs={{0,12},{4,8},{8,4},{12,0},{1,13},{5,9},{9,5},{13,1},{2,14},{6,10},... | collective-permute-start | bytes 49160 | tf_op jit(solution)/shard_map/ppermute | solution.py:111
  6.2 4.9 %collective-permute-start.1 = (bf16[4,8,256]{2,1,0:T(8,128)(2,1)}, bf16[4,8,256]{2,1,0:T(8,128)(2,1)S(1)}, u32[]{:S(2)}, u32[]{:S(2)}) collective-permute-start(bf16[4,8,256]{2,1,0:T(8,128)(2,1)} %refs_0_.1), channel_id=1, source_target_pairs={{0,8},{4,12},{8,0},{12,4},{1,9},{5,13},{9,1},{13,5},{2,10},{6,14},... | collective-permute-start | bytes 49160 | tf_op jit(solution)/shard_map/ppermute | solution.py:111
  10.2 2.3 %copy-start.1 = (bf16[1536,4,256]{2,1,0:T(4,128)(2,1)S(1)}, bf16[1536,4,256]{2,1,0:T(4,128)(2,1)}, u32[]{:S(2)}) copy-start(bf16[1536,4,256]{2,1,0:T(4,128)(2,1)} %param.14) | copy-start | bytes 9437188
  13.5 6.7 %collective-permute-start.5 = (bf16[144,256]{1,0:T(8,128)(2,1)S(1)}, bf16[144,256]{1,0:T(8,128)(2,1)S(1)}, u32[]{:S(2)}, u32[]{:S(2)}) collective-permute-start(bf16[144,256]{1,0:T(8,128)(2,1)S(1)} %pad_maximum_fusion.refs_0_), channel_id=1, source_target_pairs={{0,12},{4,8},{8,4},{12,0},{1,13},{5,9},{9,5},{13,1},{2,14},{6,10},... | collective-permute-start | bytes 221192 | tf_op jit(solution)/shard_map/ppermute | solution.py:111
  16.1 6.6 %collective-permute-start.4 = (bf16[144,256]{1,0:T(8,128)(2,1)S(1)}, bf16[144,256]{1,0:T(8,128)(2,1)S(1)}, u32[]{:S(2)}, u32[]{:S(2)}) collective-permute-start(bf16[144,256]{1,0:T(8,128)(2,1)S(1)} %pad_maximum_fusion.refs_0_), channel_id=1, source_target_pairs={{0,8},{4,12},{8,0},{12,4},{1,9},{5,13},{9,1},{13,5},{2,10},{6,14},... | collective-permute-start | bytes 221192 | tf_op jit(solution)/shard_map/ppermute | solution.py:111
  16.4 6.3 %collective-permute-start.3 = (bf16[144,256]{1,0:T(8,128)(2,1)S(1)}, bf16[144,256]{1,0:T(8,128)(2,1)S(1)}, u32[]{:S(2)}, u32[]{:S(2)}) collective-permute-start(bf16[144,256]{1,0:T(8,128)(2,1)S(1)} %pad_maximum_fusion.refs_0_), channel_id=1, source_target_pairs={{0,4},{4,0},{8,12},{12,8},{1,5},{5,1},{9,13},{13,9},{2,6},{6,2},{1... | collective-permute-start | bytes 221192 | tf_op jit(solution)/shard_map/ppermute | solution.py:111
  23.0 1.3 %collective-permute-start.6 = (bf16[16,2048]{1,0:T(8,128)(2,1)S(1)}, bf16[16,2048]{1,0:T(8,128)(2,1)S(1)}, u32[]{:S(2)}, u32[]{:S(2)}) collective-permute-start(bf16[16,2048]{1,0:T(8,128)(2,1)S(1)} %get-tuple-element.33.own_ref), channel_id=1, source_target_pairs={{0,1},{1,0},{2,3},{3,2},{4,5},{5,4},{6,7},{7,6},{8,9},{9,8},{10,11... | collective-permute-start | bytes 196616 | tf_op jit(solution)/shard_map/ppermute | solution.py:111
  24.9 4.4 %collective-permute-start.7 = (bf16[32,448]{1,0:T(8,128)(2,1)S(1)}, bf16[32,448]{1,0:T(8,128)(2,1)S(1)}, u32[]{:S(2)}, u32[]{:S(2)}) collective-permute-start(bf16[32,448]{1,0:T(8,128)(2,1)S(1)} %project.1.refs_0_.own_ref), channel_id=1, source_target_pairs={{0,2},{2,0},{1,3},{3,1},{4,6},{6,4},{5,7},{7,5},{8,10},{10,8},{9,1... | collective-permute-start | bytes 86024 | tf_op jit(solution)/shard_map/ppermute | solution.py:111
  29.4 5.8 %collective-permute-start.9 = (bf16[32,512]{1,0:T(8,128)(2,1)S(1)}, bf16[32,512]{1,0:T(8,128)(2,1)S(1)}, u32[]{:S(2)}, u32[]{:S(2)}) collective-permute-start(bf16[32,512]{1,0:T(8,128)(2,1)S(1)} %get-tuple-element.36.refs_0_.own_ref), channel_id=1, source_target_pairs={{0,12},{2,14},{4,8},{6,10},{8,4},{10,6},{12,0},{14,2},{1,13},{3,15... | collective-permute-start | bytes 98312 | tf_op jit(solution)/shard_map/ppermute | solution.py:341
  31.7 4.2 %collective-permute-start.8 = (bf16[32,512]{1,0:T(8,128)(2,1)S(1)}, bf16[32,512]{1,0:T(8,128)(2,1)S(1)}, u32[]{:S(2)}, u32[]{:S(2)}) collective-permute-start(bf16[32,512]{1,0:T(8,128)(2,1)S(1)} %get-tuple-element.36.refs_0_.own_ref), channel_id=1, source_target_pairs={{0,4},{2,8},{4,0},{6,12},{8,2},{10,14},{12,6},{14,10},{1,5},{3,9},... | collective-permute-start | bytes 98312 | tf_op jit(solution)/shard_map/ppermute | solution.py:342
  35.9 1.3 %collective-permute-start.10 = (bf16[2,32,512]{2,1,0:T(8,128)(2,1)S(1)}, bf16[2,32,512]{2,1,0:T(8,128)(2,1)S(1)}, u32[]{:S(2)}, u32[]{:S(2)}) collective-permute-start(bf16[2,32,512]{2,1,0:T(8,128)(2,1)S(1)} %pick.1.mine_ref.refs_5_), channel_id=1, source_target_pairs={{0,1},{1,0},{2,3},{3,2},{4,5},{5,4},{6,7},{7,6},{8,9},{9,8},{10,11... | collective-permute-start | bytes 196616 | tf_op jit(solution)/shard_map/ppermute | solution.py:111
  38.0 7.2 %collective-permute-start.12 = (bf16[32,2176]{1,0:T(8,128)(2,1)S(1)}, bf16[32,2176]{1,0:T(8,128)(2,1)S(1)}, u32[]{:S(2)}, u32[]{:S(2)}) collective-permute-start(bf16[32,2176]{1,0:T(8,128)(2,1)S(1)} %get-tuple-element.42), channel_id=1, source_target_pairs={{0,2},{2,0},{1,3},{3,1},{4,6},{6,4},{5,7},{7,5},{8,10},{10,8},{9,1... | collective-permute-start | bytes 417800 | tf_op jit(solution)/shard_map/ppermute | solution.py:111
  41.3 5.8 %collective-permute-start.11 = (bf16[32,1536]{1,0:T(8,128)(2,1)S(1)}, bf16[32,1536]{1,0:T(8,128)(2,1)S(1)}, u32[]{:S(2)}, u32[]{:S(2)}) collective-permute-start(bf16[32,1536]{1,0:T(8,128)(2,1)S(1)} %get-tuple-element.40.refs_0_), channel_id=1, source_target_pairs={{0,2},{2,0},{1,3},{3,1},{4,6},{6,4},{5,7},{7,5},{8,10},{10,8},{9,1... | collective-permute-start | bytes 294920 | tf_op jit(solution)/shard_map/ppermute | solution.py:111
  47.8 1.3 %collective-permute-start.13 = (bf16[16,1792]{1,0:T(8,128)(2,1)S(1)}, bf16[16,1792]{1,0:T(8,128)(2,1)S(1)}, u32[]{:S(2)}, u32[]{:S(2)}) collective-permute-start(bf16[16,1792]{1,0:T(8,128)(2,1)S(1)} %get-tuple-element.44), channel_id=1, source_target_pairs={{0,1},{1,0},{2,3},{3,2},{4,5},{5,4},{6,7},{7,6},{8,9},{9,8},{10,11... | collective-permute-start | bytes 172040 | tf_op jit(solution)/shard_map/ppermute | solution.py:111
  49.2 5.1 %collective-permute-start.14 = (bf16[4,1792]{1,0:T(4,128)(2,1)S(1)}, bf16[4,1792]{1,0:T(4,128)(2,1)S(1)}, u32[]{:S(2)}, u32[]{:S(2)}) collective-permute-start(bf16[4,1792]{1,0:T(4,128)(2,1)S(1)} %get-tuple-element.46), channel_id=1, source_target_pairs={{0,4},{4,0},{8,12},{12,8},{1,5},{5,1},{9,13},{13,9},{2,6},{6,2},{1... | collective-permute-start | bytes 43016 | tf_op jit(solution)/shard_map/ppermute | solution.py:111
  49.2 5.1 %collective-permute-start.15 = (bf16[4,1792]{1,0:T(4,128)(2,1)S(1)}, bf16[4,1792]{1,0:T(4,128)(2,1)S(1)}, u32[]{:S(2)}, u32[]{:S(2)}) collective-permute-start(bf16[4,1792]{1,0:T(4,128)(2,1)S(1)} %get-tuple-element.47), channel_id=1, source_target_pairs={{0,8},{4,12},{8,0},{12,4},{1,9},{5,13},{9,1},{13,5},{2,10},{6,14},... | collective-permute-start | bytes 43016 | tf_op jit(solution)/shard_map/ppermute | solution.py:111
  52.0 5.5 %collective-permute-start.16 = (bf16[4,1792]{1,0:T(4,128)(2,1)S(1)}, bf16[4,1792]{1,0:T(4,128)(2,1)S(1)}, u32[]{:S(2)}, u32[]{:S(2)}) collective-permute-start(bf16[4,1792]{1,0:T(4,128)(2,1)S(1)} %get-tuple-element.48), channel_id=1, source_target_pairs={{0,12},{4,8},{8,4},{12,0},{1,13},{5,9},{9,5},{13,1},{2,14},{6,10},... | collective-permute-start | bytes 43016 | tf_op jit(solution)/shard_map/ppermute | solution.py:111

commit v5 on v4

--- a/solution.py
+++ b/solution.py
@@ -109,10 +109,6 @@
 
 def hop(value, axis, size, step):
     return lax.ppermute(value, axis, [(i, i ^ step) for i in range(size)])
-
-
-def by_index(pieces, at):
-    return [lax.select_n(at ^ k, *pieces) for k in range(len(pieces))]
 
 
 def kernel(body, name, outs, specs, args, limit=8, flops=0, aliases=None):
@@ -216,8 +212,12 @@
     gain = norm_gain[None, :]
 
     (queries_near,) = fetch([], [queries], "fetch_queries")
-    pieces = [queries_near] + [hop(queries, "blk", blks, s) for s in range(1, blks)]
-    q_all = jnp.concatenate(by_index(pieces, blk), axis=0)
+    blocks = [queries_near] * blks
+    for s in [1] + list(reversed(range(2, blks))):
+        piece = hop(queries, "blk", blks, s)
+        blocks = [jnp.where(blk == (k ^ s), piece, block) for k, block in enumerate(blocks)]
+        blocks = list(lax.optimization_barrier(tuple(blocks)))
+    q_all = jnp.concatenate(blocks, axis=0)
     q_all, base_state, keep_inner, keep_own, gain = lax.optimization_barrier(
         (q_all, base_state, keep_inner, keep_own, gain)
     )
@@ -278,19 +278,33 @@
     other = hop(attn, "rows", 2, 1)
     across = (((1,), (1,)), ((), ()))
 
-    def project_own(own_ref, weight_ref, out_ref):
+    gate_cut = gate_weight.shape[0] // 64 * 16
+
+    def project_own(own_ref, weight_ref, gate_ref, out_ref, near_ref, sem):
+        copy = pltpu.make_async_copy(
+            gate_ref.at[pl.ds(0, gate_cut)], near_ref.at[pl.ds(0, gate_cut)], sem
+        )
+        copy.start()
         out_ref[...] = lax.dot_general(
             own_ref[...], weight_ref[...], across, preferred_element_type=F32
         )
-
-    (proj_own,) = kernel(
+        copy.wait()
+
+    gate_far = pltpu.with_memory_space_constraint(gate_weight, pltpu.HBM)
+    proj_own, gate_near = pl.pallas_call(
         project_own,
-        "project_own",
-        [sds((toks, width), F32)],
-        [VM, VM],
-        [attn, proj_near],
-        flops=2 * toks * width * attn.shape[1],
-    )
+        out_shape=[sds((toks, width), F32), sds(gate_weight.shape, BF)],
+        in_specs=[VM, VM, ANY],
+        out_specs=[VM] * 2,
+        scratch_shapes=[pltpu.SemaphoreType.DMA],
+        compiler_params=pltpu.CompilerParams(vmem_limit_bytes=8 * MIB),
+        cost_estimate=pl.CostEstimate(
+            flops=2 * toks * width * attn.shape[1],
+            bytes_accessed=2 * gate_cut * gate_weight.shape[1] * 2,
+            transcendentals=0,
+        ),
+        name="project_own",
+    )(attn, proj_near, gate_far)
 
     def project(own_ref, other_ref, weight_ref, out_ref):
         first = lax.axis_index("rows") == 0
@@ -309,8 +323,26 @@
         [proj_own, other, proj_near],
     )
     proj_other = hop(proj, "heads", 2, 1)
-    (gate_near,) = fetch([proj], [gate_weight], "fetch_gate")
-
+
+    def fetch_gate(proj_ref, gate_ref, part_ref, near_ref, sem):
+        rest = pl.ds(gate_cut, gate_weight.shape[0] - gate_cut)
+        copy = pltpu.make_async_copy(gate_ref.at[rest], near_ref.at[rest], sem)
+        copy.start()
+        copy.wait()
+
+    gate_near = pl.pallas_call(
+        fetch_gate,
+        out_shape=sds(gate_weight.shape, BF),
+        in_specs=[ANY, ANY, VM],
+        out_specs=VM,
+        input_output_aliases={2: 0},
+        scratch_shapes=[pltpu.SemaphoreType.DMA],
+        compiler_params=pltpu.CompilerParams(vmem_limit_bytes=MIB),
+        cost_estimate=pl.CostEstimate(
+            flops=0, bytes_accessed=2 * gate_weight.size * 2, transcendentals=0
+        ),
+        name="fetch_gate",
+    )(proj, gate_far, gate_near)
     lanes = -(-(width + 2) // 128) * 128
 
     def middle(base_ref, keep_ref, gain_ref, own_ref, other_ref, near_ref, stream_ref, note_ref):
@@ -335,11 +367,11 @@
     far_pairs, near_pairs = [], []
     for b in range(blks):
         for h in range(head_parts):
-            far_pairs.append((b * head_parts + h, (b ^ 3) * head_parts + h))
-            to = (b ^ 1, h) if b // half == h else (b ^ 2, 1 - h)
+            far_pairs.append((b * head_parts + h, (b ^ 2) * head_parts + h))
+            to = (b ^ 1, h) if b // half == h else (b ^ 3, 1 - h)
             near_pairs.append((b * head_parts + h, to[0] * head_parts + to[1]))
+    near = lax.ppermute(note, ("blk", "heads"), near_pairs)
     far = lax.ppermute(note, ("blk", "heads"), far_pairs)
-    near = lax.ppermute(note, ("blk", "heads"), near_pairs)
     (up_near,) = fetch([note], [up_weight], "fetch_up")
     lanes_all = note.shape[1]
 
@@ -347,9 +379,8 @@
         at = lax.axis_index("blk")
         inside = at // half == lax.axis_index("heads")
         odd = at % 2 == 1
-        own, near_tile, far_tile = own_ref[...], near_ref[...], far_ref[...]
-        same = jnp.where(inside, own, near_tile)
-        pair = jnp.where(inside, near_tile, far_tile)
+        same = jnp.where(inside, own_ref[...], far_ref[...])
+        pair = near_ref[...]
         out_ref[0] = jnp.where(odd, pair, same)
         out_ref[1] = jnp.where(odd, same, pair)
 
@@ -501,7 +532,7 @@
         [VM, VM],
         [keep, back],
     )
-    for s in range(1, blks):
+    for s in reversed(range(1, blks)):
         own = own + hop(sends[s - 1], "blk", blks, s).astype(F32)
     branch = (own * keep_own).astype(BF)
     stream = stream.reshape(2, blks, tok_dev, width).swapaxes(0, 1).reshape(tokens, width)

time: 58.6 us -> 57.5 us (0.981)
  waiting for transfers between devices: 12.6 us -> 8.38 us
  starting transfers between devices: 21.3 us -> 23.3 us
  Pallas kernels: 16.5 us -> 17.4 us
    pallas_call x0 -> x2, Pallas kernels: none -> 4.24 us  [the longest x1 2.37 us: shards_direct(): pl.pallas_call(fetch_gate, out_shape=sds(gate_weight.shape, BF), in_specs...]
    pallas_call x5 -> x4, Pallas kernels: 10.7 us -> 7.89 us  [fetch(): pl.pallas_call(body, out_shape=[jax.ShapeDtypeStruct(a.shape, a.dtype) fo...]
    ppermute x15, waiting for transfers between devices: 11.2 us -> 8.37 us  [hop(): return lax.ppermute(value, axis, [(i, i ^ step) for i in range(size)])]
    ppermute x1, starting transfers between devices: 0.01 us -> 1.39 us  [shards_direct(): near = lax.ppermute(note, ('blk', 'heads'), near_pairs)]
    ppermute x15, starting transfers between devices: 19 us -> 20.4 us  [hop(): return lax.ppermute(value, axis, [(i, i ^ step) for i in range(size)])]
    ppermute x1, waiting for transfers between devices: 0.77 us -> 0.01 us  [shards_direct(): near = lax.ppermute(note, ('blk', 'heads'), near_pairs)]
    ppermute x1, starting transfers between devices: 2.31 us -> 1.56 us  [shards_direct(): far = lax.ppermute(note, ('blk', 'heads'), far_pairs)]
    ppermute x1, waiting for transfers between devices: 0.6 us -> 0.01 us  [shards_direct(): far = lax.ppermute(note, ('blk', 'heads'), far_pairs)]
  transfers between devices with their start and end apart: 17 -> 17, of which waited for: 10 -> 9; matrix products, arithmetic and copies ran while one was open for 5% -> 6% of each run, Pallas kernels for 24% -> 26%
where the time goes in v5:
time: 57.5 us; the launch traced here: 57 us
  starting transfers between devices  23.3 us (41%)
  Pallas kernels  17.4 us (30%)
  waiting for transfers between devices  8.38 us (15%)
  other arithmetic  2.7 us (5%)
  local copies, waits for them, and re-layouts  1.9 us (3%)
  matrix products  1.81 us (3%)
  between operations  1.55 us (3%)
    ppermute x15, starting transfers between devices, hop(): return lax.ppermute(value, axis, [(i, i ^ step) for i in range(size)])  20.4 us
    ppermute x15, waiting for transfers between devices, hop(): return lax.ppermute(value, axis, [(i, i ^ step) for i in range(size)])  8.37 us
    pallas_call x4, Pallas kernels, fetch(): pl.pallas_call(body, out_shape=[jax.ShapeDtypeStruct(a.shape, a.dtype) fo...  7.89 us
    pallas_call x10, Pallas kernels, kernel(): pl.pallas_call(body, out_shape=outs, in_specs=specs, out_specs=[VM] * len...  5.26 us
    pallas_call x1, Pallas kernels, shards_direct(): pl.pallas_call(fetch_gate, out_shape=sds(gate_weight.shape, BF), in_specs...  2.37 us
    pallas_call x1, Pallas kernels, shards_direct(): pl.pallas_call(project_own, out_shape=[sds((toks, width), F32), sds(gate_...  1.86 us
    ppermute x1, starting transfers between devices, shards_direct(): far = lax.ppermute(note, ('blk', 'heads'), far_pairs)  1.56 us
    ppermute x1, starting transfers between devices, shards_direct(): near = lax.ppermute(note, ('blk', 'heads'), near_pairs)  1.39 us
  transfers between devices with their start and end apart: 17, of which 9 were waited for; matrix products, arithmetic and copies ran while one was open for 6% of the time, Pallas kernels for 26%

profile of v5, /device:TPU:0, one launch (start us, length us, event | category | flops | bytes accessed | tf_op | source)
XLA Modules:
  0.0 57.0 jit_solution(17426196770578796158)
XLA Ops:
  0.6 5.1 %collective-permute-start.1 = (bf16[4,8,256]{2,1,0:T(8,128)(2,1)}, bf16[4,8,256]{2,1,0:T(8,128)(2,1)S(1)}, u32[]{:S(2)}, u32[]{:S(2)}) collective-permute-start(bf16[4,8,256]{2,1,0:T(8,128)(2,1)} %refs_0_.1), channel_id=1, source_target_pairs={{0,12},{4,8},{8,4},{12,0},{1,13},{5,9},{9,5},{13,1},{2,14},{6,10},... | collective-permute-start | bytes 49160 | tf_op jit(solution)/shard_map/ppermute | solution.py:111
  5.8 0.6 %collective-permute-start.2 = (bf16[4,8,256]{2,1,0:T(8,128)(2,1)}, bf16[4,8,256]{2,1,0:T(8,128)(2,1)S(1)}, u32[]{:S(2)}, u32[]{:S(2)}) collective-permute-start(bf16[4,8,256]{2,1,0:T(8,128)(2,1)} %refs_0_.1), channel_id=1, source_target_pairs={{0,4},{4,0},{8,12},{12,8},{1,5},{5,1},{9,13},{13,9},{2,6},{6,2},{1... | collective-permute-start | bytes 49160 | tf_op jit(solution)/shard_map/ppermute | solution.py:111
  7.1 0.7 %fusion.23 = pred[128]{0:T(512)(128)(4,1)S(1)} fusion(s32[48]{0:T(128)} %bitcast.46), kind=kLoop, calls=%fused_computation.22 | loop fusion | flops 12160 | bytes 320 | tf_op jit(solution)/shard_map/reduce_or | solution.py:19
  7.8 0.1 iota.55
  7.9 0.8 %broadcast_select_fusion = bf16[32,448]{1,0:T(8,128)(2,1)S(1)} fusion(bf16[32,448]{1,0:T(8,128)(2,1)} %param.15, pred[32]{0:T(512)(128)(4,1)S(1)} %slice_bitcast_fusion, bf16[448]{0:T(512)(128)(2,1)} %param.16), kind=kLoop, calls=%fused_computation.16 | loop fusion | flops 14336 | bytes 58272 | tf_op jit(solution)/shard_map/jit(_where)/select_n | solution.py:207
  8.8 0.1 dynamic-slice_bitcast_fusion
  8.8 0.7 %fetch_queries.1 = bf16[4,8,256]{2,1,0:T(8,128)(2,1)S(1)} custom-call(bf16[4,8,256]{2,1,0:T(8,128)(2,1)} %refs_0_.1), custom_call_target="tpu_custom_call" | custom-call | bytes 32768 | tf_op jit(solution)/shard_map/fetch_queries/pallas_call | solution.py:144
  9.6 0.7 %broadcast_in_dim.35.gain_ref = bf16[1,448]{1,0:T(2,128)(2,1)S(1)} reshape(bf16[448]{0:T(512)(128)(2,1)} %param.18) | data formatting | bytes 1792 | tf_op jit(solution)/shard_map/broadcast_in_dim | solution.py:212
  10.4 0.2 collective-permute-done
  10.7 1.1 %fusion.34 = (f32[16,4,2]{0,2,1:T(2,128)S(1)}, f32[16,4,2,1536]{3,0,2,1:T(8,128)S(1)}) fusion(bf16[16,4,2,256]{3,0,2,1:T(8,128)(2,1)S(1)} %bitcast.35, bf16[1536,4,256,1]{2,1,0,3:T(4,128)(2,1)S(1)} %bitcast.33), kind=kOutput, calls=%fused_computation.54 | convolution fusion | flops 101056384 | bytes 3998208 | tf_op jit(solution)/shard_map/tgjd,kgd->tgjk/dot_general | solution.py:226
  11.8 0.3 fusion.19
  12.1 0.2 copy-done.1
  12.2 0.7 %fusion.16 = bf16[4,2,16,256]{3,2,1,0:T(8,128)(2,1)S(1)} fusion(bf16[1536,4,256,1]{2,1,0,3:T(4,128)(2,1)S(1)} %bitcast.45, f32[16,4,2,1536]{3,0,2,1:T(8,128)S(1)} %get-tuple-element.94, f32[16,4,2]{0,2,1:T(2,128)S(1)} %get-tuple-element.57, f32[4,2,16]{2,1,0:T(2,128)S(1)} %bitcast.42), kind=kOutput, calls=%fused_computation.8 | convolution fusion | flops 101122048 | bytes 3998720 | tf_op jit(solution)/shard_map/tgjk,kgd->tgjd/dot_general | solution.py:231
  12.9 0.1 copy.44
  13.0 0.1 copy.43
  13.1 0.1 fusion.33
  13.2 3.8 %collective-permute-start.5 = (bf16[144,256]{1,0:T(8,128)(2,1)S(1)}, bf16[144,256]{1,0:T(8,128)(2,1)S(1)}, u32[]{:S(2)}, u32[]{:S(2)}) collective-permute-start(bf16[144,256]{1,0:T(8,128)(2,1)S(1)} %pad_maximum_fusion.refs_0_), channel_id=1, source_target_pairs={{0,12},{4,8},{8,4},{12,0},{1,13},{5,9},{9,5},{13,1},{2,14},{6,10},... | collective-permute-start | bytes 221192 | tf_op jit(solution)/shard_map/ppermute | solution.py:111
  17.0 0.6 %collective-permute-start.3 = (bf16[144,256]{1,0:T(8,128)(2,1)S(1)}, bf16[144,256]{1,0:T(8,128)(2,1)S(1)}, u32[]{:S(2)}, u32[]{:S(2)}) collective-permute-start(bf16[144,256]{1,0:T(8,128)(2,1)S(1)} %pad_maximum_fusion.refs_0_), channel_id=1, source_target_pairs={{0,4},{4,0},{8,12},{12,8},{1,5},{5,1},{9,13},{13,9},{2,6},{6,2},{1... | collective-permute-start | bytes 221192 | tf_op jit(solution)/shard_map/ppermute | solution.py:111
  17.6 1.5 %fetch_proj.1.refs_4_ = bf16[448,2048]{1,0:T(8,128)(2,1)S(1)} custom-call(bf16[144,256]{1,0:T(8,128)(2,1)S(1)} %pad_maximum_fusion.refs_0_, bf16[448,2048]{1,0:T(8,128)(2,1)} %bitcast.34), custom_call_target="tpu_custom_call" | custom-call | bytes 3670016 | tf_op jit(solution)/shard_map/fetch_proj/pallas_call | solution.py:144
  19.2 0.6 collective-permute-done.5.refs_3_
  19.7 2.8 %collective-permute-done.4.refs_2_ = bf16[144,256]{1,0:T(8,128)(2,1)S(1)} collective-permute-done((bf16[144,256]{1,0:T(8,128)(2,1)S(1)}, bf16[144,256]{1,0:T(8,128)(2,1)S(1)}, u32[]{:S(2)}, u32[]{:S(2)}) %collective-permute-start.4) | collective-permute-done | bytes 73760 | tf_op jit(solution)/shard_map/ppermute | solution.py:111
  22.5 0.2 collective-permute-done.3.refs_1_
  22.7 0.2 combine.1
  23.1 1.9 %project_own.1 = (f32[16,448]{1,0:T(8,128)S(1)}, bf16[1792,1792]{1,0:T(8,128)(2,1)S(1)}) custom-call(bf16[16,2048]{1,0:T(8,128)(2,1)S(1)} %get-tuple-element.59.own_ref, bf16[448,2048]{1,0:T(8,128)(2,1)S(1)} %get-tuple-element.60.weight_ref, bf16[1792,1792]{1,0:T(8,128)(2,1)} %gate_ref.3), custom_call_target="tpu_custom_call" | custom-call | flops 29360128 | bytes 3211264 | tf_op jit(solution)/shard_map/project_own/pallas_call | solution.py:294
  24.9 0.6 %project.1.proj_ref.own_ref = bf16[32,448]{1,0:T(8,128)(2,1)S(1)} custom-call(f32[16,448]{1,0:T(8,128)S(1)} %get-tuple-element.61.own_ref, bf16[16,2048]{1,0:T(8,128)(2,1)S(1)} %collective-permute-done.6.other_ref, bf16[448,2048]{1,0:T(8,128)(2,1)S(1)} %get-tuple-element.60.weight_ref), custom_call_target="tpu_custom_call" | custom-call | bytes 1957888 | tf_op jit(solution)/shard_map/project/pallas_call | solution.py:117
  25.5 1.5 %collective-permute-start.7 = (bf16[32,448]{1,0:T(8,128)(2,1)S(1)}, bf16[32,448]{1,0:T(8,128)(2,1)S(1)}, u32[]{:S(2)}, u32[]{:S(2)}) collective-permute-start(bf16[32,448]{1,0:T(8,128)(2,1)S(1)} %project.1.proj_ref.own_ref), channel_id=1, source_target_pairs={{0,2},{2,0},{1,3},{3,1},{4,6},{6,4},{5,7},{7,5},{8,10},{10,8},{9,1... | collective-permute-start | bytes 86024 | tf_op jit(solution)/shard_map/ppermute | solution.py:111
  27.0 2.4 %fetch_gate.1.near_ref.gate_ref.refs_3_ = bf16[1792,1792]{1,0:T(8,128)(2,1)S(1)} custom-call(bf16[32,448]{1,0:T(8,128)(2,1)S(1)} %project.1.proj_ref.own_ref, bf16[1792,1792]{1,0:T(8,128)(2,1)} %gate_ref.3, bf16[1792,1792]{1,0:T(8,128)(2,1)S(1)} %get-tuple-element.62.part_ref), custom_call_target="tpu_custom_call", output_to_operand_aliasing={{}: (2, {})} | custom-call | bytes 12845056 | tf_op jit(solution)/shard_map/fetch_gate/pallas_call | solution.py:333
  29.5 0.2 middle.1
  29.6 1.6 %collective-permute-start.9 = (bf16[32,512]{1,0:T(8,128)(2,1)S(1)}, bf16[32,512]{1,0:T(8,128)(2,1)S(1)}, u32[]{:S(2)}, u32[]{:S(2)}) collective-permute-start(bf16[32,512]{1,0:T(8,128)(2,1)S(1)} %get-tuple-element.64.refs_0_.own_ref), channel_id=1, source_target_pairs={{0,8},{2,10},{4,12},{6,14},{8,0},{10,2},{12,4},{14,6},{1,9},{3,11}... | collective-permute-start | bytes 98312 | tf_op jit(solution)/shard_map/ppermute | solution.py:374
  31.2 1.4 %collective-permute-start.8 = (bf16[32,512]{1,0:T(8,128)(2,1)S(1)}, bf16[32,512]{1,0:T(8,128)(2,1)S(1)}, u32[]{:S(2)}, u32[]{:S(2)}) collective-permute-start(bf16[32,512]{1,0:T(8,128)(2,1)S(1)} %get-tuple-element.64.refs_0_.own_ref), channel_id=1, source_target_pairs={{0,4},{2,12},{4,0},{6,8},{8,6},{10,14},{12,2},{14,10},{1,5},{3,13}... | collective-permute-start | bytes 98312 | tf_op jit(solution)/shard_map/ppermute | solution.py:373
  32.6 2.8 %fetch_up.1.up_ref.refs_4_ = bf16[1792,1792]{1,0:T(8,128)(2,1)S(1)} custom-call(bf16[32,512]{1,0:T(8,128)(2,1)S(1)} %get-tuple-element.64.refs_0_.own_ref, bf16[1792,1792]{1,0:T(8,128)(2,1)} %refs_1_.2), custom_call_target="tpu_custom_call" | custom-call | bytes 12845056 | tf_op jit(solution)/shard_map/fetch_up/pallas_call | solution.py:144
  35.6 1.2 %inner_products.1 = (f32[32,1792]{1,0:T(8,128)S(1)}, f32[32,1792]{1,0:T(8,128)S(1)}) custom-call(bf16[2,32,512]{2,1,0:T(8,128)(2,1)S(1)} %pick.1.mine_ref.refs_5_, bf16[1792,1792]{1,0:T(8,128)(2,1)S(1)} %fetch_gate.1.near_ref.gate_ref.refs_3_, bf16[1792,1792]{1,0:T(8,128)(2,1)S(1)} %fetch_up.1.up_ref.refs_4_), custom_call_target="tpu_custom_call" | custom-call | flops 205520896 | bytes 13369344 | tf_op jit(solution)/shard_map/inner_products/pallas_call | solution.py:117
  36.8 0.8 %gate_up_0.1 = (f32[32,2176]{1,0:T(8,128)S(1)}, bf16[32,2176]{1,0:T(8,128)(2,1)S(1)}) custom-call(bf16[2,32,512]{2,1,0:T(8,128)(2,1)S(1)} %collective-permute-done.10.refs_0_, f32[32,1792]{1,0:T(8,128)S(1)} %get-tuple-element.65.refs_1_, f32[32,1792]{1,0:T(8,128)S(1)} %get-tuple-element.66.refs_2_, ...), custom_call_target="tpu_custom_call" | custom-call | flops 102760448 | bytes 13852672 | tf_op jit(solution)/shard_map/gate_up_0/pallas_call | solution.py:117
  37.6 3.9 %collective-permute-start.12 = (bf16[32,2176]{1,0:T(8,128)(2,1)S(1)}, bf16[32,2176]{1,0:T(8,128)(2,1)S(1)}, u32[]{:S(2)}, u32[]{:S(2)}) collective-permute-start(bf16[32,2176]{1,0:T(8,128)(2,1)S(1)} %get-tuple-element.70), channel_id=1, source_target_pairs={{0,2},{2,0},{1,3},{3,1},{4,6},{6,4},{5,7},{7,5},{8,10},{10,8},{9,1... | collective-permute-start | bytes 417800 | tf_op jit(solution)/shard_map/ppermute | solution.py:111
  41.5 0.6 %gate_up_1.1 = (f32[32,1536]{1,0:T(8,128)S(1)}, bf16[32,1536]{1,0:T(8,128)(2,1)S(1)}) custom-call(bf16[2,32,512]{2,1,0:T(8,128)(2,1)S(1)} %collective-permute-done.10.refs_0_, f32[32,1792]{1,0:T(8,128)S(1)} %get-tuple-element.65.refs_1_, f32[32,1792]{1,0:T(8,128)S(1)} %get-tuple-element.66.refs_2_, ...), custom_call_target="tpu_custom_call" | custom-call | flops 102760448 | bytes 13664256 | tf_op jit(solution)/shard_map/gate_up_1/pallas_call | solution.py:117
  42.1 0.1 collective-permute-start.11
  42.2 2.8 %fetch_down.1.weight_ref = bf16[1792,1792]{1,0:T(8,128)(2,1)S(1)} custom-call(bf16[32,1536]{1,0:T(8,128)(2,1)S(1)} %get-tuple-element.68.refs_0_, bf16[1792,1792]{1,0:T(8,128)(2,1)} %refs_1_.3), custom_call_target="tpu_custom_call" | custom-call | bytes 12845056 | tf_op jit(solution)/shard_map/fetch_down/pallas_call | solution.py:144
  45.0 1.0 %collective-permute-done.12.other_ref.first_other_ref = bf16[32,2176]{1,0:T(8,128)(2,1)S(1)} collective-permute-done((bf16[32,2176]{1,0:T(8,128)(2,1)S(1)}, bf16[32,2176]{1,0:T(8,128)(2,1)S(1)}, u32[]{:S(2)}, u32[]{:S(2)}) %collective-permute-start.12) | collective-permute-done | bytes 139296 | tf_op jit(solution)/shard_map/ppermute | solution.py:111
  46.0 0.8 %down_first.1.part_ref = f32[32,1792]{1,0:T(8,128)S(1)} custom-call(f32[32,2176]{1,0:T(8,128)S(1)} %get-tuple-element.69.own_ref.first_ref, bf16[32,2176]{1,0:T(8,128)(2,1)S(1)} %collective-permute-done.12.other_ref.first_other_ref, bf16[1792,1792]{1,0:T(8,128)(2,1)S(1)} %fetch_down.1.weight_ref), custom_call_target="tpu_custom_call" | custom-call | flops 102760448 | bytes 7069696 | tf_op jit(solution)/shard_map/down_first/pallas_call | solution.py:117
  46.8 1.1 %collective-permute-done.11.other_ref = bf16[32,1536]{1,0:T(8,128)(2,1)S(1)} collective-permute-done((bf16[32,1536]{1,0:T(8,128)(2,1)S(1)}, bf16[32,1536]{1,0:T(8,128)(2,1)S(1)}, u32[]{:S(2)}, u32[]{:S(2)}) %collective-permute-start.11) | collective-permute-done | bytes 98336 | tf_op jit(solution)/shard_map/ppermute | solution.py:111
  47.9 0.7 %down_last.1 = (f32[16,1792]{1,0:T(8,128)S(1)}, bf16[16,1792]{1,0:T(8,128)(2,1)S(1)}) custom-call(f32[32,1536]{1,0:T(8,128)S(1)} %get-tuple-element.67.own_ref, bf16[32,1536]{1,0:T(8,128)(2,1)S(1)} %collective-permute-done.11.other_ref, f32[32,2176]{1,0:T(8,128)S(1)} %get-tuple-element.69.own_ref.first_ref, ...), custom_call_target="tpu_custom_call" | custom-call | bytes 7536640 | tf_op jit(solution)/shard_map/down_last/pallas_call | solution.py:117
  48.7 1.2 %collective-permute-done.13.back_ref = bf16[16,1792]{1,0:T(8,128)(2,1)S(1)} collective-permute-done((bf16[16,1792]{1,0:T(8,128)(2,1)S(1)}, bf16[16,1792]{1,0:T(8,128)(2,1)S(1)}, u32[]{:S(2)}, u32[]{:S(2)}) %collective-permute-start.13) | collective-permute-done | bytes 57376 | tf_op jit(solution)/shard_map/ppermute | solution.py:111
  50.0 1.8 %collective-permute-start.14 = (bf16[4,1792]{1,0:T(4,128)(2,1)S(1)}, bf16[4,1792]{1,0:T(4,128)(2,1)S(1)}, u32[]{:S(2)}, u32[]{:S(2)}) collective-permute-start(bf16[4,1792]{1,0:T(4,128)(2,1)S(1)} %get-tuple-element.74), channel_id=1, source_target_pairs={{0,12},{4,8},{8,4},{12,0},{1,13},{5,9},{9,5},{13,1},{2,14},{6,10},... | collective-permute-start | bytes 43016 | tf_op jit(solution)/shard_map/ppermute | solution.py:111
  51.7 2.7 %collective-permute-start.16 = (bf16[4,1792]{1,0:T(4,128)(2,1)S(1)}, bf16[4,1792]{1,0:T(4,128)(2,1)S(1)}, u32[]{:S(2)}, u32[]{:S(2)}) collective-permute-start(bf16[4,1792]{1,0:T(4,128)(2,1)S(1)} %get-tuple-element.76), channel_id=1, source_target_pairs={{0,4},{4,0},{8,12},{12,8},{1,5},{5,1},{9,13},{13,9},{2,6},{6,2},{1... | collective-permute-start | bytes 43016 | tf_op jit(solution)/shard_map/ppermute | solution.py:111
  54.5 0.6 %reshape.143 = bf16[32,448]{1,0:T(8,128)(2,1)} reshape(bf16[4,2,4,448]{3,2,1,0:T(4,128)(2,1)S(1)} %copy.46) | data formatting | bytes 57344 | tf_op jit(solution)/shard_map/reshape | solution.py:538
  55.1 0.4 collective-permute-done.14
  55.5 0.8 %collective-permute-done.15 = bf16[4,1792]{1,0:T(4,128)(2,1)S(1)} collective-permute-done((bf16[4,1792]{1,0:T(4,128)(2,1)S(1)}, bf16[4,1792]{1,0:T(4,128)(2,1)S(1)}, u32[]{:S(2)}, u32[]{:S(2)}) %collective-permute-start.15) | collective-permute-done | bytes 14368 | tf_op jit(solution)/shard_map/ppermute | solution.py:111
  56.4 0.7 %multiply_convert_fusion = bf16[4,1792]{1,0:T(4,128)(2,1)} fusion(bf16[4,1792]{1,0:T(4,128)(2,1)S(1)} %collective-permute-done.16, bf16[4,1792]{1,0:T(4,128)(2,1)S(1)} %collective-permute-done.15, f32[4,1792]{1,0:T(4,128)S(1)} %get-tuple-element.73, bf16[4,1792]{1,0:T(4,128)(2,1)S(1)} %collective-permute-done.14, f32[4]{0:T(128)S(1)} %bitcast.44), kind=kLoop, calls=%fused_computation.17 | loop fusion | flops 57344 | bytes 86032 | tf_op jit(solution)/shard_map/convert_element_type | solution.py:537
  (37 shorter events, 0.6 us)
Async XLA Ops:
  0.6 10.0 %copy-start = (bf16[1536,4,256]{2,1,0:T(4,128)(2,1)S(1)}, bf16[1536,4,256]{2,1,0:T(4,128)(2,1)}, u32[]{:S(2)}) copy-start(bf16[1536,4,256]{2,1,0:T(4,128)(2,1)} %param.13) | copy-start | bytes 9437188
  0.6 9.7 %collective-permute-start.1 = (bf16[4,8,256]{2,1,0:T(8,128)(2,1)}, bf16[4,8,256]{2,1,0:T(8,128)(2,1)S(1)}, u32[]{:S(2)}, u32[]{:S(2)}) collective-permute-start(bf16[4,8,256]{2,1,0:T(8,128)(2,1)} %refs_0_.1), channel_id=1, source_target_pairs={{0,12},{4,8},{8,4},{12,0},{1,13},{5,9},{9,5},{13,1},{2,14},{6,10},... | collective-permute-start | bytes 49160 | tf_op jit(solution)/shard_map/ppermute | solution.py:111
  5.8 4.8 %collective-permute-start = (bf16[4,8,256]{2,1,0:T(8,128)(2,1)}, bf16[4,8,256]{2,1,0:T(8,128)(2,1)S(1)}, u32[]{:S(2)}, u32[]{:S(2)}) collective-permute-start(bf16[4,8,256]{2,1,0:T(8,128)(2,1)} %refs_0_.1), channel_id=1, source_target_pairs={{0,8},{4,12},{8,0},{12,4},{1,9},{5,13},{9,1},{13,5},{2,10},{6,14},... | collective-permute-start | bytes 49160 | tf_op jit(solution)/shard_map/ppermute | solution.py:111
  5.8 4.6 %collective-permute-start.2 = (bf16[4,8,256]{2,1,0:T(8,128)(2,1)}, bf16[4,8,256]{2,1,0:T(8,128)(2,1)S(1)}, u32[]{:S(2)}, u32[]{:S(2)}) collective-permute-start(bf16[4,8,256]{2,1,0:T(8,128)(2,1)} %refs_0_.1), channel_id=1, source_target_pairs={{0,4},{4,0},{8,12},{12,8},{1,5},{5,1},{9,13},{13,9},{2,6},{6,2},{1... | collective-permute-start | bytes 49160 | tf_op jit(solution)/shard_map/ppermute | solution.py:111
  10.3 1.9 %copy-start.1 = (bf16[1536,4,256]{2,1,0:T(4,128)(2,1)S(1)}, bf16[1536,4,256]{2,1,0:T(4,128)(2,1)}, u32[]{:S(2)}) copy-start(bf16[1536,4,256]{2,1,0:T(4,128)(2,1)} %param.14) | copy-start | bytes 9437188
  13.2 6.5 %collective-permute-start.5 = (bf16[144,256]{1,0:T(8,128)(2,1)S(1)}, bf16[144,256]{1,0:T(8,128)(2,1)S(1)}, u32[]{:S(2)}, u32[]{:S(2)}) collective-permute-start(bf16[144,256]{1,0:T(8,128)(2,1)S(1)} %pad_maximum_fusion.refs_0_), channel_id=1, source_target_pairs={{0,12},{4,8},{8,4},{12,0},{1,13},{5,9},{9,5},{13,1},{2,14},{6,10},... | collective-permute-start | bytes 221192 | tf_op jit(solution)/shard_map/ppermute | solution.py:111
  17.0 5.5 %collective-permute-start.4 = (bf16[144,256]{1,0:T(8,128)(2,1)S(1)}, bf16[144,256]{1,0:T(8,128)(2,1)S(1)}, u32[]{:S(2)}, u32[]{:S(2)}) collective-permute-start(bf16[144,256]{1,0:T(8,128)(2,1)S(1)} %pad_maximum_fusion.refs_0_), channel_id=1, source_target_pairs={{0,8},{4,12},{8,0},{12,4},{1,9},{5,13},{9,1},{13,5},{2,10},{6,14},... | collective-permute-start | bytes 221192 | tf_op jit(solution)/shard_map/ppermute | solution.py:111
  17.0 5.7 %collective-permute-start.3 = (bf16[144,256]{1,0:T(8,128)(2,1)S(1)}, bf16[144,256]{1,0:T(8,128)(2,1)S(1)}, u32[]{:S(2)}, u32[]{:S(2)}) collective-permute-start(bf16[144,256]{1,0:T(8,128)(2,1)S(1)} %pad_maximum_fusion.refs_0_), channel_id=1, source_target_pairs={{0,4},{4,0},{8,12},{12,8},{1,5},{5,1},{9,13},{13,9},{2,6},{6,2},{1... | collective-permute-start | bytes 221192 | tf_op jit(solution)/shard_map/ppermute | solution.py:111
  23.0 2.0 %collective-permute-start.6 = (bf16[16,2048]{1,0:T(8,128)(2,1)S(1)}, bf16[16,2048]{1,0:T(8,128)(2,1)S(1)}, u32[]{:S(2)}, u32[]{:S(2)}) collective-permute-start(bf16[16,2048]{1,0:T(8,128)(2,1)S(1)} %get-tuple-element.59.own_ref), channel_id=1, source_target_pairs={{0,1},{1,0},{2,3},{3,2},{4,5},{5,4},{6,7},{7,6},{8,9},{9,8},{10,11... | collective-permute-start | bytes 196616 | tf_op jit(solution)/shard_map/ppermute | solution.py:111
  25.5 3.9 %collective-permute-start.7 = (bf16[32,448]{1,0:T(8,128)(2,1)S(1)}, bf16[32,448]{1,0:T(8,128)(2,1)S(1)}, u32[]{:S(2)}, u32[]{:S(2)}) collective-permute-start(bf16[32,448]{1,0:T(8,128)(2,1)S(1)} %project.1.proj_ref.own_ref), channel_id=1, source_target_pairs={{0,2},{2,0},{1,3},{3,1},{4,6},{6,4},{5,7},{7,5},{8,10},{10,8},{9,1... | collective-permute-start | bytes 86024 | tf_op jit(solution)/shard_map/ppermute | solution.py:111
  29.6 5.8 %collective-permute-start.9 = (bf16[32,512]{1,0:T(8,128)(2,1)S(1)}, bf16[32,512]{1,0:T(8,128)(2,1)S(1)}, u32[]{:S(2)}, u32[]{:S(2)}) collective-permute-start(bf16[32,512]{1,0:T(8,128)(2,1)S(1)} %get-tuple-element.64.refs_0_.own_ref), channel_id=1, source_target_pairs={{0,8},{2,10},{4,12},{6,14},{8,0},{10,2},{12,4},{14,6},{1,9},{3,11}... | collective-permute-start | bytes 98312 | tf_op jit(solution)/shard_map/ppermute | solution.py:374
  31.2 4.2 %collective-permute-start.8 = (bf16[32,512]{1,0:T(8,128)(2,1)S(1)}, bf16[32,512]{1,0:T(8,128)(2,1)S(1)}, u32[]{:S(2)}, u32[]{:S(2)}) collective-permute-start(bf16[32,512]{1,0:T(8,128)(2,1)S(1)} %get-tuple-element.64.refs_0_.own_ref), channel_id=1, source_target_pairs={{0,4},{2,12},{4,0},{6,8},{8,6},{10,14},{12,2},{14,10},{1,5},{3,13}... | collective-permute-start | bytes 98312 | tf_op jit(solution)/shard_map/ppermute | solution.py:373
  35.5 1.3 %collective-permute-start.10 = (bf16[2,32,512]{2,1,0:T(8,128)(2,1)S(1)}, bf16[2,32,512]{2,1,0:T(8,128)(2,1)S(1)}, u32[]{:S(2)}, u32[]{:S(2)}) collective-permute-start(bf16[2,32,512]{2,1,0:T(8,128)(2,1)S(1)} %pick.1.mine_ref.refs_5_), channel_id=1, source_target_pairs={{0,1},{1,0},{2,3},{3,2},{4,5},{5,4},{6,7},{7,6},{8,9},{9,8},{10,11... | collective-permute-start | bytes 196616 | tf_op jit(solution)/shard_map/ppermute | solution.py:111
  37.6 8.4 %collective-permute-start.12 = (bf16[32,2176]{1,0:T(8,128)(2,1)S(1)}, bf16[32,2176]{1,0:T(8,128)(2,1)S(1)}, u32[]{:S(2)}, u32[]{:S(2)}) collective-permute-start(bf16[32,2176]{1,0:T(8,128)(2,1)S(1)} %get-tuple-element.70), channel_id=1, source_target_pairs={{0,2},{2,0},{1,3},{3,1},{4,6},{6,4},{5,7},{7,5},{8,10},{10,8},{9,1... | collective-permute-start | bytes 417800 | tf_op jit(solution)/shard_map/ppermute | solution.py:111
  42.1 5.8 %collective-permute-start.11 = (bf16[32,1536]{1,0:T(8,128)(2,1)S(1)}, bf16[32,1536]{1,0:T(8,128)(2,1)S(1)}, u32[]{:S(2)}, u32[]{:S(2)}) collective-permute-start(bf16[32,1536]{1,0:T(8,128)(2,1)S(1)} %get-tuple-element.68.refs_0_), channel_id=1, source_target_pairs={{0,2},{2,0},{1,3},{3,1},{4,6},{6,4},{5,7},{7,5},{8,10},{10,8},{9,1... | collective-permute-start | bytes 294920 | tf_op jit(solution)/shard_map/ppermute | solution.py:111
  48.6 1.3 %collective-permute-start.13 = (bf16[16,1792]{1,0:T(8,128)(2,1)S(1)}, bf16[16,1792]{1,0:T(8,128)(2,1)S(1)}, u32[]{:S(2)}, u32[]{:S(2)}) collective-permute-start(bf16[16,1792]{1,0:T(8,128)(2,1)S(1)} %get-tuple-element.72), channel_id=1, source_target_pairs={{0,1},{1,0},{2,3},{3,2},{4,5},{5,4},{6,7},{7,6},{8,9},{9,8},{10,11... | collective-permute-start | bytes 172040 | tf_op jit(solution)/shard_map/ppermute | solution.py:111
  50.0 5.6 %collective-permute-start.14 = (bf16[4,1792]{1,0:T(4,128)(2,1)S(1)}, bf16[4,1792]{1,0:T(4,128)(2,1)S(1)}, u32[]{:S(2)}, u32[]{:S(2)}) collective-permute-start(bf16[4,1792]{1,0:T(4,128)(2,1)S(1)} %get-tuple-element.74), channel_id=1, source_target_pairs={{0,12},{4,8},{8,4},{12,0},{1,13},{5,9},{9,5},{13,1},{2,14},{6,10},... | collective-permute-start | bytes 43016 | tf_op jit(solution)/shard_map/ppermute | solution.py:111
  51.7 4.6 %collective-permute-start.15 = (bf16[4,1792]{1,0:T(4,128)(2,1)S(1)}, bf16[4,1792]{1,0:T(4,128)(2,1)S(1)}, u32[]{:S(2)}, u32[]{:S(2)}) collective-permute-start(bf16[4,1792]{1,0:T(4,128)(2,1)S(1)} %get-tuple-element.75), channel_id=1, source_target_pairs={{0,8},{4,12},{8,0},{12,4},{1,9},{5,13},{9,1},{13,5},{2,10},{6,14},... | collective-permute-start | bytes 43016 | tf_op jit(solution)/shard_map/ppermute | solution.py:111
  51.7 4.6 %collective-permute-start.16 = (bf16[4,1792]{1,0:T(4,128)(2,1)S(1)}, bf16[4,1792]{1,0:T(4,128)(2,1)S(1)}, u32[]{:S(2)}, u32[]{:S(2)}) collective-permute-start(bf16[4,1792]{1,0:T(4,128)(2,1)S(1)} %get-tuple-element.76), channel_id=1, source_target_pairs={{0,4},{4,0},{8,12},{12,8},{1,5},{5,1},{9,13},{13,9},{2,6},{6,2},{1... | collective-permute-start | bytes 43016 | tf_op jit(solution)/shard_map/ppermute | solution.py:111

commit v6 on v4

--- a/solution.py
+++ b/solution.py
@@ -111,10 +111,6 @@
     return lax.ppermute(value, axis, [(i, i ^ step) for i in range(size)])
 
 
-def by_index(pieces, at):
-    return [lax.select_n(at ^ k, *pieces) for k in range(len(pieces))]
-
-
 def kernel(body, name, outs, specs, args, limit=8, flops=0, aliases=None):
     near = [a for a, spec in zip(args, specs) if spec is VM]
     size = sum(a.size * a.dtype.itemsize for a in near + list(outs))
@@ -130,15 +126,18 @@
     )(*args)
 
 
-def fetch(after, arrays, name):
+def fetch(after, arrays, name, rows=None, into=None):
     n, skip = len(arrays), len(after)
+    begun = list(into or [])
 
     def body(*refs):
-        refs = refs[skip:]
-        sources, targets, sems = refs[:n], refs[n : 2 * n], refs[2 * n]
-        copies = [
-            pltpu.make_async_copy(sources[i], targets[i], sems.at[i]) for i in range(n)
-        ]
+        sources = refs[skip : skip + n]
+        targets, sems = refs[-1 - n : -1], refs[-1]
+        copies = []
+        for i, (source, target) in enumerate(zip(sources, targets)):
+            if rows is not None:
+                source, target = source.at[pl.ds(*rows)], target.at[pl.ds(*rows)]
+            copies.append(pltpu.make_async_copy(source, target, sems.at[i]))
         for copy in copies:
             copy.start()
         for copy in copies:
@@ -148,13 +147,14 @@
     return pl.pallas_call(
         body,
         out_shape=[jax.ShapeDtypeStruct(a.shape, a.dtype) for a in arrays],
-        in_specs=[ANY] * (skip + n),
+        in_specs=[ANY] * (skip + n) + [VM] * len(begun),
         out_specs=[VM] * n,
+        input_output_aliases={skip + n + i: i for i in range(len(begun))},
         scratch_shapes=[pltpu.SemaphoreType.DMA((n,))],
         compiler_params=pltpu.CompilerParams(vmem_limit_bytes=MIB),
         cost_estimate=pl.CostEstimate(flops=0, bytes_accessed=2 * size, transcendentals=0),
         name=name,
-    )(*after, *[pltpu.with_memory_space_constraint(a, pltpu.HBM) for a in arrays])
+    )(*after, *[pltpu.with_memory_space_constraint(a, pltpu.HBM) for a in arrays], *begun)
 
 
 def parts_of(value, count):
@@ -216,8 +216,12 @@
     gain = norm_gain[None, :]
 
     (queries_near,) = fetch([], [queries], "fetch_queries")
-    pieces = [queries_near] + [hop(queries, "blk", blks, s) for s in range(1, blks)]
-    q_all = jnp.concatenate(by_index(pieces, blk), axis=0)
+    blocks = [queries_near] * blks
+    for s in [1] + list(reversed(range(2, blks))):
+        piece = hop(queries, "blk", blks, s)
+        blocks = [jnp.where(blk == (k ^ s), piece, block) for k, block in enumerate(blocks)]
+        blocks = list(lax.optimization_barrier(tuple(blocks)))
+    q_all = jnp.concatenate(blocks, axis=0)
     q_all, base_state, keep_inner, keep_own, gain = lax.optimization_barrier(
         (q_all, base_state, keep_inner, keep_own, gain)
     )
@@ -239,10 +243,10 @@
     side = jnp.pad(side, ((0, 0), (0, head_size - side.shape[1])))
     note = jnp.concatenate([partial, side], axis=0)
     notes = [note] + [hop(note, "blk", blks, s) for s in range(1, blks)]
-    (proj_near,) = fetch([note], [out_weight.T], "fetch_proj")
+    proj_near, gate_near = fetch([note], [out_weight.T, gate_weight], "fetch_proj_gate")
 
     def combine(*refs):
-        ins, out = refs[:blks], refs[-2]
+        ins, out = refs[:blks], refs[blks + 2]
         base = local_heads * toks
         levels = []
         for ref in ins:
@@ -267,32 +271,32 @@
                 acc = term if acc is None else acc + term
             out[:, h * head_size : (h + 1) * head_size] = acc.astype(BF)
 
-    attn, proj_near = kernel(
+    attn, proj_near, gate_near = kernel(
         combine,
         "combine",
-        [sds((toks, local_heads * head_size), BF), sds(proj_near.shape, BF)],
-        [VM] * (blks + 1),
-        notes + [proj_near],
-        aliases={blks: 1},
+        [sds((toks, local_heads * head_size), BF), sds(proj_near.shape, BF), sds(gate_near.shape, BF)],
+        [VM] * (blks + 2),
+        notes + [proj_near, gate_near],
+        aliases={blks: 1, blks + 1: 2},
     )
     other = hop(attn, "rows", 2, 1)
     across = (((1,), (1,)), ((), ()))
 
-    def project_own(own_ref, weight_ref, out_ref):
+    def project_own(own_ref, weight_ref, gate_ref, out_ref, gate_out):
         out_ref[...] = lax.dot_general(
             own_ref[...], weight_ref[...], across, preferred_element_type=F32
         )
 
-    (proj_own,) = kernel(
+    proj_own, gate_near = kernel(
         project_own,
         "project_own",
-        [sds((toks, width), F32)],
-        [VM, VM],
-        [attn, proj_near],
-        flops=2 * toks * width * attn.shape[1],
-    )
-
-    def project(own_ref, other_ref, weight_ref, out_ref):
+        [sds((toks, width), F32), sds(gate_near.shape, BF)],
+        [VM] * 3,
+        [attn, proj_near, gate_near],
+        aliases={2: 1},
+    )
+
+    def project(own_ref, other_ref, weight_ref, gate_ref, out_ref, gate_out):
         first = lax.axis_index("rows") == 0
         own = own_ref[...]
         other = lax.dot_general(
@@ -301,19 +305,23 @@
         out_ref[:toks] = jnp.where(first, own, other).astype(BF)
         out_ref[toks:] = jnp.where(first, other, own).astype(BF)
 
-    (proj,) = kernel(
+    proj, gate_near = kernel(
         project,
         "project",
-        [sds((tokens, width), BF)],
-        [VM, VM, VM],
-        [proj_own, other, proj_near],
+        [sds((tokens, width), BF), sds(gate_near.shape, BF)],
+        [VM] * 4,
+        [proj_own, other, proj_near, gate_near],
+        aliases={3: 1},
     )
     proj_other = hop(proj, "heads", 2, 1)
-    (gate_near,) = fetch([proj], [gate_weight], "fetch_gate")
+    up_cut = up_weight.shape[0] // 32 * 16
+    (up_near,) = fetch([proj], [up_weight], "fetch_up_first", rows=(0, up_cut))
 
     lanes = -(-(width + 2) // 128) * 128
 
-    def middle(base_ref, keep_ref, gain_ref, own_ref, other_ref, near_ref, stream_ref, note_ref):
+    def middle(
+        base_ref, keep_ref, gain_ref, own_ref, other_ref, gate_ref, up_ref, stream_ref, note_ref, *_
+    ):
         mid = base_ref[...].astype(F32) + (own_ref[...].astype(F32) + other_ref[...].astype(F32))
         stream_ref[...] = (mid * keep_ref[...]).astype(BF)
         note_ref[:, :width] = (mid * gain_ref[...].astype(F32)).astype(BF)
@@ -324,12 +332,18 @@
             lane == 0, high.astype(F32), jnp.where(lane == 1, low.astype(F32), 0.0)
         ).astype(BF)
 
-    stream, note = kernel(
+    stream, note, gate_near, up_near = kernel(
         middle,
         "middle",
-        [sds((tokens, width), BF), sds((tokens, lanes), BF)],
-        [VM] * 5 + [ANY],
-        [base_state, keep_inner, gain, proj, proj_other, gate_near],
+        [
+            sds((tokens, width), BF),
+            sds((tokens, lanes), BF),
+            sds(gate_near.shape, BF),
+            sds(up_near.shape, BF),
+        ],
+        [VM] * 7,
+        [base_state, keep_inner, gain, proj, proj_other, gate_near, up_near],
+        aliases={5: 2, 6: 3},
     )
 
     far_pairs, near_pairs = [], []
@@ -338,18 +352,23 @@
             far_pairs.append((b * head_parts + h, (b ^ 3) * head_parts + h))
             to = (b ^ 1, h) if b // half == h else (b ^ 2, 1 - h)
             near_pairs.append((b * head_parts + h, to[0] * head_parts + to[1]))
+    near = lax.ppermute(note, ("blk", "heads"), near_pairs)
     far = lax.ppermute(note, ("blk", "heads"), far_pairs)
-    near = lax.ppermute(note, ("blk", "heads"), near_pairs)
-    (up_near,) = fetch([note], [up_weight], "fetch_up")
+    (up_near,) = fetch(
+        [note],
+        [up_weight],
+        "fetch_up_last",
+        rows=(up_cut, up_weight.shape[0] - up_cut),
+        into=[up_near],
+    )
     lanes_all = note.shape[1]
 
     def pick(own_ref, near_ref, far_ref, gate_ref, up_ref, out_ref):
         at = lax.axis_index("blk")
         inside = at // half == lax.axis_index("heads")
         odd = at % 2 == 1
-        own, near_tile, far_tile = own_ref[...], near_ref[...], far_ref[...]
-        same = jnp.where(inside, own, near_tile)
-        pair = jnp.where(inside, near_tile, far_tile)
+        same = jnp.where(inside, own_ref[...], near_ref[...])
+        pair = jnp.where(inside, near_ref[...], far_ref[...])
         out_ref[0] = jnp.where(odd, pair, same)
         out_ref[1] = jnp.where(odd, same, pair)
 
@@ -501,7 +520,7 @@
         [VM, VM],
         [keep, back],
     )
-    for s in range(1, blks):
+    for s in reversed(range(1, blks)):
         own = own + hop(sends[s - 1], "blk", blks, s).astype(F32)
     branch = (own * keep_own).astype(BF)
     stream = stream.reshape(2, blks, tok_dev, width).swapaxes(0, 1).reshape(tokens, width)

time: 58.6 us -> 56.9 us (0.971)
  waiting for transfers between devices: 12.6 us -> 9.88 us
  starting transfers between devices: 21.3 us -> 22.1 us
    ppermute x15, waiting for transfers between devices: 11.2 us -> 7.77 us  [hop(): return lax.ppermute(value, axis, [(i, i ^ step) for i in range(size)])]
    ppermute x1, waiting for transfers between devices: 0.6 us -> 1.43 us  [shards_direct(): far = lax.ppermute(note, ('blk', 'heads'), far_pairs)]
    ppermute x15, starting transfers between devices: 19 us -> 19.7 us  [hop(): return lax.ppermute(value, axis, [(i, i ^ step) for i in range(size)])]
  transfers between devices with their start and end apart: 17 -> 17, of which waited for: 10 -> 12; matrix products, arithmetic and copies ran while one was open for 5% -> 6% of each run, Pallas kernels for 24% -> 25%
where the time goes in v6:
time: 56.9 us; the launch traced here: 56.5 us
  starting transfers between devices  22.1 us (39%)
  Pallas kernels  16.6 us (29%)
  waiting for transfers between devices  9.88 us (17%)
  other arithmetic  2.7 us (5%)
  local copies, waits for them, and re-layouts  1.9 us (3%)
  matrix products  1.81 us (3%)
  between operations  1.53 us (3%)
    ppermute x15, starting transfers between devices, hop(): return lax.ppermute(value, axis, [(i, i ^ step) for i in range(size)])  19.7 us
    pallas_call x5, Pallas kernels, fetch(): pl.pallas_call(body, out_shape=[jax.ShapeDtypeStruct(a.shape, a.dtype) fo...  10.8 us
    ppermute x15, waiting for transfers between devices, hop(): return lax.ppermute(value, axis, [(i, i ^ step) for i in range(size)])  7.77 us
    pallas_call x11, Pallas kernels, kernel(): pl.pallas_call(body, out_shape=outs, in_specs=specs, out_specs=[VM] * len...  5.82 us
    ppermute x1, starting transfers between devices, shards_direct(): far = lax.ppermute(note, ('blk', 'heads'), far_pairs)  2.38 us
    ppermute x1, waiting for transfers between devices, shards_direct(): far = lax.ppermute(note, ('blk', 'heads'), far_pairs)  1.43 us
  transfers between devices with their start and end apart: 17, of which 12 were waited for; matrix products, arithmetic and copies ran while one was open for 6% of the time, Pallas kernels for 25%

profile of v6, /device:TPU:0, one launch (start us, length us, event | category | flops | bytes accessed | tf_op | source)
XLA Modules:
  0.0 56.5 jit_solution(11461572857353394382)
XLA Ops:
  0.6 5.1 %collective-permute-start.1 = (bf16[4,8,256]{2,1,0:T(8,128)(2,1)}, bf16[4,8,256]{2,1,0:T(8,128)(2,1)S(1)}, u32[]{:S(2)}, u32[]{:S(2)}) collective-permute-start(bf16[4,8,256]{2,1,0:T(8,128)(2,1)} %refs_0_.1), channel_id=1, source_target_pairs={{0,12},{4,8},{8,4},{12,0},{1,13},{5,9},{9,5},{13,1},{2,14},{6,10},... | collective-permute-start | bytes 49160 | tf_op jit(solution)/shard_map/ppermute | solution.py:111
  5.8 0.6 %collective-permute-start.2 = (bf16[4,8,256]{2,1,0:T(8,128)(2,1)}, bf16[4,8,256]{2,1,0:T(8,128)(2,1)S(1)}, u32[]{:S(2)}, u32[]{:S(2)}) collective-permute-start(bf16[4,8,256]{2,1,0:T(8,128)(2,1)} %refs_0_.1), channel_id=1, source_target_pairs={{0,4},{4,0},{8,12},{12,8},{1,5},{5,1},{9,13},{13,9},{2,6},{6,2},{1... | collective-permute-start | bytes 49160 | tf_op jit(solution)/shard_map/ppermute | solution.py:111
  7.1 0.7 %fusion.23 = pred[128]{0:T(512)(128)(4,1)S(1)} fusion(s32[48]{0:T(128)} %bitcast.46), kind=kLoop, calls=%fused_computation.22 | loop fusion | flops 12160 | bytes 320 | tf_op jit(solution)/shard_map/reduce_or | solution.py:19
  7.8 0.1 iota.55
  7.9 0.8 %broadcast_select_fusion = bf16[32,448]{1,0:T(8,128)(2,1)S(1)} fusion(bf16[32,448]{1,0:T(8,128)(2,1)} %param.15, pred[32]{0:T(512)(128)(4,1)S(1)} %slice_bitcast_fusion, bf16[448]{0:T(512)(128)(2,1)} %param.16), kind=kLoop, calls=%fused_computation.16 | loop fusion | flops 14336 | bytes 58272 | tf_op jit(solution)/shard_map/jit(_where)/select_n | solution.py:211
  8.8 0.1 dynamic-slice_bitcast_fusion
  8.8 0.7 %fetch_queries.1 = bf16[4,8,256]{2,1,0:T(8,128)(2,1)S(1)} custom-call(bf16[4,8,256]{2,1,0:T(8,128)(2,1)} %refs_0_.1), custom_call_target="tpu_custom_call" | custom-call | bytes 32768 | tf_op jit(solution)/shard_map/fetch_queries/pallas_call | solution.py:147
  9.6 0.7 %broadcast_in_dim.35.gain_ref = bf16[1,448]{1,0:T(2,128)(2,1)S(1)} reshape(bf16[448]{0:T(512)(128)(2,1)} %param.18) | data formatting | bytes 1792 | tf_op jit(solution)/shard_map/broadcast_in_dim | solution.py:216
  10.4 0.2 collective-permute-done
  10.7 1.1 %fusion.34 = (f32[16,4,2]{0,2,1:T(2,128)S(1)}, f32[16,4,2,1536]{3,0,2,1:T(8,128)S(1)}) fusion(bf16[16,4,2,256]{3,0,2,1:T(8,128)(2,1)S(1)} %bitcast.35, bf16[1536,4,256,1]{2,1,0,3:T(4,128)(2,1)S(1)} %bitcast.33), kind=kOutput, calls=%fused_computation.54 | convolution fusion | flops 101056384 | bytes 3998208 | tf_op jit(solution)/shard_map/tgjd,kgd->tgjk/dot_general | solution.py:230
  11.8 0.3 fusion.19
  12.1 0.2 copy-done.1
  12.2 0.7 %fusion.16 = bf16[4,2,16,256]{3,2,1,0:T(8,128)(2,1)S(1)} fusion(bf16[1536,4,256,1]{2,1,0,3:T(4,128)(2,1)S(1)} %bitcast.45, f32[16,4,2,1536]{3,0,2,1:T(8,128)S(1)} %get-tuple-element.108, f32[16,4,2]{0,2,1:T(2,128)S(1)} %get-tuple-element.64, f32[4,2,16]{2,1,0:T(2,128)S(1)} %bitcast.42), kind=kOutput, calls=%fused_computation.8 | convolution fusion | flops 101122048 | bytes 3998720 | tf_op jit(solution)/shard_map/tgjk,kgd->tgjd/dot_general | solution.py:235
  13.1 0.1 fusion.33
  13.2 3.8 %collective-permute-start.5 = (bf16[144,256]{1,0:T(8,128)(2,1)S(1)}, bf16[144,256]{1,0:T(8,128)(2,1)S(1)}, u32[]{:S(2)}, u32[]{:S(2)}) collective-permute-start(bf16[144,256]{1,0:T(8,128)(2,1)S(1)} %pad_maximum_fusion.refs_0_), channel_id=1, source_target_pairs={{0,12},{4,8},{8,4},{12,0},{1,13},{5,9},{9,5},{13,1},{2,14},{6,10},... | collective-permute-start | bytes 221192 | tf_op jit(solution)/shard_map/ppermute | solution.py:111
  17.0 0.6 %collective-permute-start.3 = (bf16[144,256]{1,0:T(8,128)(2,1)S(1)}, bf16[144,256]{1,0:T(8,128)(2,1)S(1)}, u32[]{:S(2)}, u32[]{:S(2)}) collective-permute-start(bf16[144,256]{1,0:T(8,128)(2,1)S(1)} %pad_maximum_fusion.refs_0_), channel_id=1, source_target_pairs={{0,4},{4,0},{8,12},{12,8},{1,5},{5,1},{9,13},{13,9},{2,6},{6,2},{1... | collective-permute-start | bytes 221192 | tf_op jit(solution)/shard_map/ppermute | solution.py:111
  17.6 3.4 %fetch_proj_gate.1 = (bf16[448,2048]{1,0:T(8,128)(2,1)S(1)}, bf16[1792,1792]{1,0:T(8,128)(2,1)S(1)}) custom-call(bf16[144,256]{1,0:T(8,128)(2,1)S(1)} %pad_maximum_fusion.refs_0_, bf16[448,2048]{1,0:T(8,128)(2,1)} %bitcast.34, bf16[1792,1792]{1,0:T(8,128)(2,1)} %refs_2_.1), custom_call_target="tpu_custom_call" | custom-call | bytes 16515072 | tf_op jit(solution)/shard_map/fetch_proj_gate/pallas_call | solution.py:147
  21.1 1.4 %collective-permute-done.4.refs_2_ = bf16[144,256]{1,0:T(8,128)(2,1)S(1)} collective-permute-done((bf16[144,256]{1,0:T(8,128)(2,1)S(1)}, bf16[144,256]{1,0:T(8,128)(2,1)S(1)}, u32[]{:S(2)}, u32[]{:S(2)}) %collective-permute-start.4) | collective-permute-done | bytes 73760 | tf_op jit(solution)/shard_map/ppermute | solution.py:111
  22.5 0.2 collective-permute-done.3.refs_1_
  22.7 0.2 combine.1
  23.1 0.6 %project_own.1 = (f32[16,448]{1,0:T(8,128)S(1)}, bf16[1792,1792]{1,0:T(8,128)(2,1)S(1)}) custom-call(bf16[16,2048]{1,0:T(8,128)(2,1)S(1)} %get-tuple-element.68.own_ref, bf16[448,2048]{1,0:T(8,128)(2,1)S(1)} %get-tuple-element.69.weight_ref, bf16[1792,1792]{1,0:T(8,128)(2,1)S(1)} %get-tuple-element.70.gate_ref), custom_call_target="tpu_custom_call", output_to_operand_aliasing={{1}: (2, {})} | custom-call | bytes 14774272 | tf_op jit(solution)/shard_map/project_own/pallas_call | solution.py:117
  23.6 0.7 %collective-permute-done.6.other_ref = bf16[16,2048]{1,0:T(8,128)(2,1)S(1)} collective-permute-done((bf16[16,2048]{1,0:T(8,128)(2,1)S(1)}, bf16[16,2048]{1,0:T(8,128)(2,1)S(1)}, u32[]{:S(2)}, u32[]{:S(2)}) %collective-permute-start.6) | collective-permute-done | bytes 65568 | tf_op jit(solution)/shard_map/ppermute | solution.py:111
  24.3 0.6 %project.1 = (bf16[32,448]{1,0:T(8,128)(2,1)S(1)}, bf16[1792,1792]{1,0:T(8,128)(2,1)S(1)}) custom-call(f32[16,448]{1,0:T(8,128)S(1)} %get-tuple-element.71.own_ref, bf16[16,2048]{1,0:T(8,128)(2,1)S(1)} %collective-permute-done.6.other_ref, bf16[448,2048]{1,0:T(8,128)(2,1)S(1)} %get-tuple-element.69.weight_ref, ...), custom_call_target="tpu_custom_call", output_to_operand_aliasing={{1}: (3, {})} | custom-call | bytes 14802944 | tf_op jit(solution)/shard_map/project/pallas_call | solution.py:117
  24.9 1.5 %collective-permute-start.7 = (bf16[32,448]{1,0:T(8,128)(2,1)S(1)}, bf16[32,448]{1,0:T(8,128)(2,1)S(1)}, u32[]{:S(2)}, u32[]{:S(2)}) collective-permute-start(bf16[32,448]{1,0:T(8,128)(2,1)S(1)} %get-tuple-element.73.refs_0_.own_ref), channel_id=1, source_target_pairs={{0,2},{2,0},{1,3},{3,1},{4,6},{6,4},{5,7},{7,5},{8,10},{10,8},{9,1... | collective-permute-start | bytes 86024 | tf_op jit(solution)/shard_map/ppermute | solution.py:111
  26.4 1.9 %fetch_up_first.1.up_ref = bf16[1792,1792]{1,0:T(8,128)(2,1)S(1)} custom-call(bf16[32,448]{1,0:T(8,128)(2,1)S(1)} %get-tuple-element.73.refs_0_.own_ref, bf16[1792,1792]{1,0:T(8,128)(2,1)} %refs_1_.4), custom_call_target="tpu_custom_call" | custom-call | bytes 12845056 | tf_op jit(solution)/shard_map/fetch_up_first/pallas_call | solution.py:147
  28.3 0.5 collective-permute-done.7.other_ref
  28.8 0.2 middle.1
  29.0 2.4 %collective-permute-start.9 = (bf16[32,512]{1,0:T(8,128)(2,1)S(1)}, bf16[32,512]{1,0:T(8,128)(2,1)S(1)}, u32[]{:S(2)}, u32[]{:S(2)}) collective-permute-start(bf16[32,512]{1,0:T(8,128)(2,1)S(1)} %get-tuple-element.76.refs_0_.own_ref), channel_id=1, source_target_pairs={{0,12},{2,14},{4,8},{6,10},{8,4},{10,6},{12,0},{14,2},{1,13},{3,15... | collective-permute-start | bytes 98312 | tf_op jit(solution)/shard_map/ppermute | solution.py:356
  31.4 1.9 %fetch_up_last.1.up_ref.refs_4_ = bf16[1792,1792]{1,0:T(8,128)(2,1)S(1)} custom-call(bf16[32,512]{1,0:T(8,128)(2,1)S(1)} %get-tuple-element.76.refs_0_.own_ref, bf16[1792,1792]{1,0:T(8,128)(2,1)} %refs_1_.4, bf16[1792,1792]{1,0:T(8,128)(2,1)S(1)} %get-tuple-element.78.refs_2_), custom_call_target="tpu_custom_call", output_to_operand_aliasing={{}: (2, {})} | custom-call | bytes 12845056 | tf_op jit(solution)/shard_map/fetch_up_last/pallas_call | solution.py:147
  33.3 1.4 %collective-permute-done.9.far_ref = bf16[32,512]{1,0:T(8,128)(2,1)S(1)} collective-permute-done((bf16[32,512]{1,0:T(8,128)(2,1)S(1)}, bf16[32,512]{1,0:T(8,128)(2,1)S(1)}, u32[]{:S(2)}, u32[]{:S(2)}) %collective-permute-start.9) | collective-permute-done | bytes 32800 | tf_op jit(solution)/shard_map/ppermute | solution.py:356
  34.7 0.7 %collective-permute-done.8.near_ref = bf16[32,512]{1,0:T(8,128)(2,1)S(1)} collective-permute-done((bf16[32,512]{1,0:T(8,128)(2,1)S(1)}, bf16[32,512]{1,0:T(8,128)(2,1)S(1)}, u32[]{:S(2)}, u32[]{:S(2)}) %collective-permute-start.8) | collective-permute-done | bytes 32800 | tf_op jit(solution)/shard_map/ppermute | solution.py:355
  35.5 1.2 %inner_products.1 = (f32[32,1792]{1,0:T(8,128)S(1)}, f32[32,1792]{1,0:T(8,128)S(1)}) custom-call(bf16[2,32,512]{2,1,0:T(8,128)(2,1)S(1)} %pick.1.mine_ref.refs_5_, bf16[1792,1792]{1,0:T(8,128)(2,1)S(1)} %get-tuple-element.77.gate_ref.refs_3_, bf16[1792,1792]{1,0:T(8,128)(2,1)S(1)} %fetch_up_last.1.up_ref.refs_4_), custom_call_target="tpu_custom_call" | custom-call | flops 205520896 | bytes 13369344 | tf_op jit(solution)/shard_map/inner_products/pallas_call | solution.py:117
  36.8 0.8 %gate_up_0.1 = (f32[32,2176]{1,0:T(8,128)S(1)}, bf16[32,2176]{1,0:T(8,128)(2,1)S(1)}) custom-call(bf16[2,32,512]{2,1,0:T(8,128)(2,1)S(1)} %collective-permute-done.10.refs_0_, f32[32,1792]{1,0:T(8,128)S(1)} %get-tuple-element.79.refs_1_, f32[32,1792]{1,0:T(8,128)S(1)} %get-tuple-element.80.refs_2_, ...), custom_call_target="tpu_custom_call" | custom-call | flops 102760448 | bytes 13852672 | tf_op jit(solution)/shard_map/gate_up_0/pallas_call | solution.py:117
  37.5 3.2 %collective-permute-start.12 = (bf16[32,2176]{1,0:T(8,128)(2,1)S(1)}, bf16[32,2176]{1,0:T(8,128)(2,1)S(1)}, u32[]{:S(2)}, u32[]{:S(2)}) collective-permute-start(bf16[32,2176]{1,0:T(8,128)(2,1)S(1)} %get-tuple-element.84), channel_id=1, source_target_pairs={{0,2},{2,0},{1,3},{3,1},{4,6},{6,4},{5,7},{7,5},{8,10},{10,8},{9,1... | collective-permute-start | bytes 417800 | tf_op jit(solution)/shard_map/ppermute | solution.py:111
  40.8 0.6 %gate_up_1.1 = (f32[32,1536]{1,0:T(8,128)S(1)}, bf16[32,1536]{1,0:T(8,128)(2,1)S(1)}) custom-call(bf16[2,32,512]{2,1,0:T(8,128)(2,1)S(1)} %collective-permute-done.10.refs_0_, f32[32,1792]{1,0:T(8,128)S(1)} %get-tuple-element.79.refs_1_, f32[32,1792]{1,0:T(8,128)S(1)} %get-tuple-element.80.refs_2_, ...), custom_call_target="tpu_custom_call" | custom-call | flops 102760448 | bytes 13664256 | tf_op jit(solution)/shard_map/gate_up_1/pallas_call | solution.py:117
  41.3 0.1 collective-permute-start.11
  41.4 2.8 %fetch_down.1.weight_ref = bf16[1792,1792]{1,0:T(8,128)(2,1)S(1)} custom-call(bf16[32,1536]{1,0:T(8,128)(2,1)S(1)} %get-tuple-element.82.refs_0_, bf16[1792,1792]{1,0:T(8,128)(2,1)} %refs_1_.5), custom_call_target="tpu_custom_call" | custom-call | bytes 12845056 | tf_op jit(solution)/shard_map/fetch_down/pallas_call | solution.py:147
  44.3 1.0 %collective-permute-done.12.other_ref.first_other_ref = bf16[32,2176]{1,0:T(8,128)(2,1)S(1)} collective-permute-done((bf16[32,2176]{1,0:T(8,128)(2,1)S(1)}, bf16[32,2176]{1,0:T(8,128)(2,1)S(1)}, u32[]{:S(2)}, u32[]{:S(2)}) %collective-permute-start.12) | collective-permute-done | bytes 139296 | tf_op jit(solution)/shard_map/ppermute | solution.py:111
  45.3 0.8 %down_first.1.part_ref = f32[32,1792]{1,0:T(8,128)S(1)} custom-call(f32[32,2176]{1,0:T(8,128)S(1)} %get-tuple-element.83.own_ref.first_ref, bf16[32,2176]{1,0:T(8,128)(2,1)S(1)} %collective-permute-done.12.other_ref.first_other_ref, bf16[1792,1792]{1,0:T(8,128)(2,1)S(1)} %fetch_down.1.weight_ref), custom_call_target="tpu_custom_call" | custom-call | flops 102760448 | bytes 7069696 | tf_op jit(solution)/shard_map/down_first/pallas_call | solution.py:117
  46.1 1.1 %collective-permute-done.11.other_ref = bf16[32,1536]{1,0:T(8,128)(2,1)S(1)} collective-permute-done((bf16[32,1536]{1,0:T(8,128)(2,1)S(1)}, bf16[32,1536]{1,0:T(8,128)(2,1)S(1)}, u32[]{:S(2)}, u32[]{:S(2)}) %collective-permute-start.11) | collective-permute-done | bytes 98336 | tf_op jit(solution)/shard_map/ppermute | solution.py:111
  47.2 0.7 %down_last.1 = (f32[16,1792]{1,0:T(8,128)S(1)}, bf16[16,1792]{1,0:T(8,128)(2,1)S(1)}) custom-call(f32[32,1536]{1,0:T(8,128)S(1)} %get-tuple-element.81.own_ref, bf16[32,1536]{1,0:T(8,128)(2,1)S(1)} %collective-permute-done.11.other_ref, f32[32,2176]{1,0:T(8,128)S(1)} %get-tuple-element.83.own_ref.first_ref, ...), custom_call_target="tpu_custom_call" | custom-call | bytes 7536640 | tf_op jit(solution)/shard_map/down_last/pallas_call | solution.py:117
  48.0 1.2 %collective-permute-done.13.back_ref = bf16[16,1792]{1,0:T(8,128)(2,1)S(1)} collective-permute-done((bf16[16,1792]{1,0:T(8,128)(2,1)S(1)}, bf16[16,1792]{1,0:T(8,128)(2,1)S(1)}, u32[]{:S(2)}, u32[]{:S(2)}) %collective-permute-start.13) | collective-permute-done | bytes 57376 | tf_op jit(solution)/shard_map/ppermute | solution.py:111
  49.2 1.9 %collective-permute-start.14 = (bf16[4,1792]{1,0:T(4,128)(2,1)S(1)}, bf16[4,1792]{1,0:T(4,128)(2,1)S(1)}, u32[]{:S(2)}, u32[]{:S(2)}) collective-permute-start(bf16[4,1792]{1,0:T(4,128)(2,1)S(1)} %get-tuple-element.88), channel_id=1, source_target_pairs={{0,12},{4,8},{8,4},{12,0},{1,13},{5,9},{9,5},{13,1},{2,14},{6,10},... | collective-permute-start | bytes 43016 | tf_op jit(solution)/shard_map/ppermute | solution.py:111
  51.2 2.5 %collective-permute-start.16 = (bf16[4,1792]{1,0:T(4,128)(2,1)S(1)}, bf16[4,1792]{1,0:T(4,128)(2,1)S(1)}, u32[]{:S(2)}, u32[]{:S(2)}) collective-permute-start(bf16[4,1792]{1,0:T(4,128)(2,1)S(1)} %get-tuple-element.90), channel_id=1, source_target_pairs={{0,4},{4,0},{8,12},{12,8},{1,5},{5,1},{9,13},{13,9},{2,6},{6,2},{1... | collective-permute-start | bytes 43016 | tf_op jit(solution)/shard_map/ppermute | solution.py:111
  53.7 0.6 %reshape.143 = bf16[32,448]{1,0:T(8,128)(2,1)} reshape(bf16[4,2,4,448]{3,2,1,0:T(4,128)(2,1)S(1)} %copy.51) | data formatting | bytes 57344 | tf_op jit(solution)/shard_map/reshape | solution.py:526
  54.4 0.5 collective-permute-done.14
  54.9 0.9 %collective-permute-done.15 = bf16[4,1792]{1,0:T(4,128)(2,1)S(1)} collective-permute-done((bf16[4,1792]{1,0:T(4,128)(2,1)S(1)}, bf16[4,1792]{1,0:T(4,128)(2,1)S(1)}, u32[]{:S(2)}, u32[]{:S(2)}) %collective-permute-start.15) | collective-permute-done | bytes 14368 | tf_op jit(solution)/shard_map/ppermute | solution.py:111
  55.8 0.7 %multiply_convert_fusion = bf16[4,1792]{1,0:T(4,128)(2,1)} fusion(bf16[4,1792]{1,0:T(4,128)(2,1)S(1)} %collective-permute-done.16, bf16[4,1792]{1,0:T(4,128)(2,1)S(1)} %collective-permute-done.15, f32[4,1792]{1,0:T(4,128)S(1)} %get-tuple-element.87, bf16[4,1792]{1,0:T(4,128)(2,1)S(1)} %collective-permute-done.14, f32[4]{0:T(128)S(1)} %bitcast.44), kind=kLoop, calls=%fused_computation.17 | loop fusion | flops 57344 | bytes 86032 | tf_op jit(solution)/shard_map/convert_element_type | solution.py:525
  (37 shorter events, 0.7 us)
Async XLA Ops:
  0.6 10.0 %copy-start = (bf16[1536,4,256]{2,1,0:T(4,128)(2,1)S(1)}, bf16[1536,4,256]{2,1,0:T(4,128)(2,1)}, u32[]{:S(2)}) copy-start(bf16[1536,4,256]{2,1,0:T(4,128)(2,1)} %param.13) | copy-start | bytes 9437188
  0.6 9.7 %collective-permute-start.1 = (bf16[4,8,256]{2,1,0:T(8,128)(2,1)}, bf16[4,8,256]{2,1,0:T(8,128)(2,1)S(1)}, u32[]{:S(2)}, u32[]{:S(2)}) collective-permute-start(bf16[4,8,256]{2,1,0:T(8,128)(2,1)} %refs_0_.1), channel_id=1, source_target_pairs={{0,12},{4,8},{8,4},{12,0},{1,13},{5,9},{9,5},{13,1},{2,14},{6,10},... | collective-permute-start | bytes 49160 | tf_op jit(solution)/shard_map/ppermute | solution.py:111
  5.8 4.8 %collective-permute-start = (bf16[4,8,256]{2,1,0:T(8,128)(2,1)}, bf16[4,8,256]{2,1,0:T(8,128)(2,1)S(1)}, u32[]{:S(2)}, u32[]{:S(2)}) collective-permute-start(bf16[4,8,256]{2,1,0:T(8,128)(2,1)} %refs_0_.1), channel_id=1, source_target_pairs={{0,8},{4,12},{8,0},{12,4},{1,9},{5,13},{9,1},{13,5},{2,10},{6,14},... | collective-permute-start | bytes 49160 | tf_op jit(solution)/shard_map/ppermute | solution.py:111
  5.8 4.6 %collective-permute-start.2 = (bf16[4,8,256]{2,1,0:T(8,128)(2,1)}, bf16[4,8,256]{2,1,0:T(8,128)(2,1)S(1)}, u32[]{:S(2)}, u32[]{:S(2)}) collective-permute-start(bf16[4,8,256]{2,1,0:T(8,128)(2,1)} %refs_0_.1), channel_id=1, source_target_pairs={{0,4},{4,0},{8,12},{12,8},{1,5},{5,1},{9,13},{13,9},{2,6},{6,2},{1... | collective-permute-start | bytes 49160 | tf_op jit(solution)/shard_map/ppermute | solution.py:111
  10.3 1.9 %copy-start.1 = (bf16[1536,4,256]{2,1,0:T(4,128)(2,1)S(1)}, bf16[1536,4,256]{2,1,0:T(4,128)(2,1)}, u32[]{:S(2)}) copy-start(bf16[1536,4,256]{2,1,0:T(4,128)(2,1)} %param.14) | copy-start | bytes 9437188
  13.2 7.9 %collective-permute-start.5 = (bf16[144,256]{1,0:T(8,128)(2,1)S(1)}, bf16[144,256]{1,0:T(8,128)(2,1)S(1)}, u32[]{:S(2)}, u32[]{:S(2)}) collective-permute-start(bf16[144,256]{1,0:T(8,128)(2,1)S(1)} %pad_maximum_fusion.refs_0_), channel_id=1, source_target_pairs={{0,12},{4,8},{8,4},{12,0},{1,13},{5,9},{9,5},{13,1},{2,14},{6,10},... | collective-permute-start | bytes 221192 | tf_op jit(solution)/shard_map/ppermute | solution.py:111
  17.0 5.5 %collective-permute-start.4 = (bf16[144,256]{1,0:T(8,128)(2,1)S(1)}, bf16[144,256]{1,0:T(8,128)(2,1)S(1)}, u32[]{:S(2)}, u32[]{:S(2)}) collective-permute-start(bf16[144,256]{1,0:T(8,128)(2,1)S(1)} %pad_maximum_fusion.refs_0_), channel_id=1, source_target_pairs={{0,8},{4,12},{8,0},{12,4},{1,9},{5,13},{9,1},{13,5},{2,10},{6,14},... | collective-permute-start | bytes 221192 | tf_op jit(solution)/shard_map/ppermute | solution.py:111
  17.0 5.7 %collective-permute-start.3 = (bf16[144,256]{1,0:T(8,128)(2,1)S(1)}, bf16[144,256]{1,0:T(8,128)(2,1)S(1)}, u32[]{:S(2)}, u32[]{:S(2)}) collective-permute-start(bf16[144,256]{1,0:T(8,128)(2,1)S(1)} %pad_maximum_fusion.refs_0_), channel_id=1, source_target_pairs={{0,4},{4,0},{8,12},{12,8},{1,5},{5,1},{9,13},{13,9},{2,6},{6,2},{1... | collective-permute-start | bytes 221192 | tf_op jit(solution)/shard_map/ppermute | solution.py:111
  23.0 1.3 %collective-permute-start.6 = (bf16[16,2048]{1,0:T(8,128)(2,1)S(1)}, bf16[16,2048]{1,0:T(8,128)(2,1)S(1)}, u32[]{:S(2)}, u32[]{:S(2)}) collective-permute-start(bf16[16,2048]{1,0:T(8,128)(2,1)S(1)} %get-tuple-element.68.own_ref), channel_id=1, source_target_pairs={{0,1},{1,0},{2,3},{3,2},{4,5},{5,4},{6,7},{7,6},{8,9},{9,8},{10,11... | collective-permute-start | bytes 196616 | tf_op jit(solution)/shard_map/ppermute | solution.py:111
  24.9 3.9 %collective-permute-start.7 = (bf16[32,448]{1,0:T(8,128)(2,1)S(1)}, bf16[32,448]{1,0:T(8,128)(2,1)S(1)}, u32[]{:S(2)}, u32[]{:S(2)}) collective-permute-start(bf16[32,448]{1,0:T(8,128)(2,1)S(1)} %get-tuple-element.73.refs_0_.own_ref), channel_id=1, source_target_pairs={{0,2},{2,0},{1,3},{3,1},{4,6},{6,4},{5,7},{7,5},{8,10},{10,8},{9,1... | collective-permute-start | bytes 86024 | tf_op jit(solution)/shard_map/ppermute | solution.py:111
  29.0 5.7 %collective-permute-start.9 = (bf16[32,512]{1,0:T(8,128)(2,1)S(1)}, bf16[32,512]{1,0:T(8,128)(2,1)S(1)}, u32[]{:S(2)}, u32[]{:S(2)}) collective-permute-start(bf16[32,512]{1,0:T(8,128)(2,1)S(1)} %get-tuple-element.76.refs_0_.own_ref), channel_id=1, source_target_pairs={{0,12},{2,14},{4,8},{6,10},{8,4},{10,6},{12,0},{14,2},{1,13},{3,15... | collective-permute-start | bytes 98312 | tf_op jit(solution)/shard_map/ppermute | solution.py:356
  31.4 4.0 %collective-permute-start.8 = (bf16[32,512]{1,0:T(8,128)(2,1)S(1)}, bf16[32,512]{1,0:T(8,128)(2,1)S(1)}, u32[]{:S(2)}, u32[]{:S(2)}) collective-permute-start(bf16[32,512]{1,0:T(8,128)(2,1)S(1)} %get-tuple-element.76.refs_0_.own_ref), channel_id=1, source_target_pairs={{0,4},{2,8},{4,0},{6,12},{8,2},{10,14},{12,6},{14,10},{1,5},{3,9},... | collective-permute-start | bytes 98312 | tf_op jit(solution)/shard_map/ppermute | solution.py:355
  35.4 1.3 %collective-permute-start.10 = (bf16[2,32,512]{2,1,0:T(8,128)(2,1)S(1)}, bf16[2,32,512]{2,1,0:T(8,128)(2,1)S(1)}, u32[]{:S(2)}, u32[]{:S(2)}) collective-permute-start(bf16[2,32,512]{2,1,0:T(8,128)(2,1)S(1)} %pick.1.mine_ref.refs_5_), channel_id=1, source_target_pairs={{0,1},{1,0},{2,3},{3,2},{4,5},{5,4},{6,7},{7,6},{8,9},{9,8},{10,11... | collective-permute-start | bytes 196616 | tf_op jit(solution)/shard_map/ppermute | solution.py:111
  37.5 7.7 %collective-permute-start.12 = (bf16[32,2176]{1,0:T(8,128)(2,1)S(1)}, bf16[32,2176]{1,0:T(8,128)(2,1)S(1)}, u32[]{:S(2)}, u32[]{:S(2)}) collective-permute-start(bf16[32,2176]{1,0:T(8,128)(2,1)S(1)} %get-tuple-element.84), channel_id=1, source_target_pairs={{0,2},{2,0},{1,3},{3,1},{4,6},{6,4},{5,7},{7,5},{8,10},{10,8},{9,1... | collective-permute-start | bytes 417800 | tf_op jit(solution)/shard_map/ppermute | solution.py:111
  41.3 5.8 %collective-permute-start.11 = (bf16[32,1536]{1,0:T(8,128)(2,1)S(1)}, bf16[32,1536]{1,0:T(8,128)(2,1)S(1)}, u32[]{:S(2)}, u32[]{:S(2)}) collective-permute-start(bf16[32,1536]{1,0:T(8,128)(2,1)S(1)} %get-tuple-element.82.refs_0_), channel_id=1, source_target_pairs={{0,2},{2,0},{1,3},{3,1},{4,6},{6,4},{5,7},{7,5},{8,10},{10,8},{9,1... | collective-permute-start | bytes 294920 | tf_op jit(solution)/shard_map/ppermute | solution.py:111
  47.9 1.3 %collective-permute-start.13 = (bf16[16,1792]{1,0:T(8,128)(2,1)S(1)}, bf16[16,1792]{1,0:T(8,128)(2,1)S(1)}, u32[]{:S(2)}, u32[]{:S(2)}) collective-permute-start(bf16[16,1792]{1,0:T(8,128)(2,1)S(1)} %get-tuple-element.86), channel_id=1, source_target_pairs={{0,1},{1,0},{2,3},{3,2},{4,5},{5,4},{6,7},{7,6},{8,9},{9,8},{10,11... | collective-permute-start | bytes 172040 | tf_op jit(solution)/shard_map/ppermute | solution.py:111
  49.2 5.6 %collective-permute-start.14 = (bf16[4,1792]{1,0:T(4,128)(2,1)S(1)}, bf16[4,1792]{1,0:T(4,128)(2,1)S(1)}, u32[]{:S(2)}, u32[]{:S(2)}) collective-permute-start(bf16[4,1792]{1,0:T(4,128)(2,1)S(1)} %get-tuple-element.88), channel_id=1, source_target_pairs={{0,12},{4,8},{8,4},{12,0},{1,13},{5,9},{9,5},{13,1},{2,14},{6,10},... | collective-permute-start | bytes 43016 | tf_op jit(solution)/shard_map/ppermute | solution.py:111
  51.2 4.6 %collective-permute-start.15 = (bf16[4,1792]{1,0:T(4,128)(2,1)S(1)}, bf16[4,1792]{1,0:T(4,128)(2,1)S(1)}, u32[]{:S(2)}, u32[]{:S(2)}) collective-permute-start(bf16[4,1792]{1,0:T(4,128)(2,1)S(1)} %get-tuple-element.89), channel_id=1, source_target_pairs={{0,8},{4,12},{8,0},{12,4},{1,9},{5,13},{9,1},{13,5},{2,10},{6,14},... | collective-permute-start | bytes 43016 | tf_op jit(solution)/shard_map/ppermute | solution.py:111
  51.2 4.6 %collective-permute-start.16 = (bf16[4,1792]{1,0:T(4,128)(2,1)S(1)}, bf16[4,1792]{1,0:T(4,128)(2,1)S(1)}, u32[]{:S(2)}, u32[]{:S(2)}) collective-permute-start(bf16[4,1792]{1,0:T(4,128)(2,1)S(1)} %get-tuple-element.90), channel_id=1, source_target_pairs={{0,4},{4,0},{8,12},{12,8},{1,5},{5,1},{9,13},{13,9},{2,6},{6,2},{1... | collective-permute-start | bytes 43016 | tf_op jit(solution)/shard_map/ppermute | solution.py:111

commit v7 on v6

--- a/solution.py
+++ b/solution.py
@@ -111,7 +111,7 @@
     return lax.ppermute(value, axis, [(i, i ^ step) for i in range(size)])
 
 
-def kernel(body, name, outs, specs, args, limit=8, flops=0, aliases=None):
+def kernel(body, name, outs, specs, args, limit=8, flops=0, aliases=None, scratch=()):
     near = [a for a, spec in zip(args, specs) if spec is VM]
     size = sum(a.size * a.dtype.itemsize for a in near + list(outs))
     return pl.pallas_call(
@@ -120,6 +120,7 @@
         in_specs=specs,
         out_specs=[VM] * len(outs),
         input_output_aliases=aliases or {},
+        scratch_shapes=list(scratch),
         compiler_params=pltpu.CompilerParams(vmem_limit_bytes=limit * MIB),
         cost_estimate=pl.CostEstimate(flops=flops, bytes_accessed=size, transcendentals=0),
         name=name,
@@ -203,28 +204,15 @@
     tokens = toks * 2
     sds = jax.ShapeDtypeStruct
 
-    def inner(value):
-        value = value.reshape((blks, 2, tok_dev) + value.shape[1:])
-        return jnp.swapaxes(value, 0, 1).reshape((tokens,) + value.shape[3:])
-
-    valid_tok, masked_tok = token_masks(cand_lengths, masked_pos, tokens)
-    base_state = inner(jnp.where(masked_tok[:, None], mask_embed[None, :], dec_state))
-    keep_mask = valid_tok.astype(F32)
-    keep_inner = inner(keep_mask)[:, None]
-    own_start = (blk * 2 + row) * tok_dev
-    keep_own = lax.dynamic_slice_in_dim(keep_mask, own_start, tok_dev, 0)[:, None]
-    gain = norm_gain[None, :]
-
-    (queries_near,) = fetch([], [queries], "fetch_queries")
+    queries_near, dec_state, mask_embed, norm_gain, masked_pos = fetch(
+        [], [queries, dec_state, mask_embed, norm_gain, masked_pos], "fetch_small"
+    )
     blocks = [queries_near] * blks
-    for s in [1] + list(reversed(range(2, blks))):
+    for s in reversed(range(1, blks)):
         piece = hop(queries, "blk", blks, s)
         blocks = [jnp.where(blk == (k ^ s), piece, block) for k, block in enumerate(blocks)]
         blocks = list(lax.optimization_barrier(tuple(blocks)))
     q_all = jnp.concatenate(blocks, axis=0)
-    q_all, base_state, keep_inner, keep_own, gain = lax.optimization_barrier(
-        (q_all, base_state, keep_inner, keep_own, gain)
-    )
     grouped = q_all.reshape(toks, kv_local, group_size, head_size)
     scores = (
         jnp.einsum("tgjd,kgd->tgjk", grouped, src_keys, preferred_element_type=F32) * score_scale
@@ -242,7 +230,7 @@
     side = jnp.concatenate(parts_of(level, 3), axis=1)
     side = jnp.pad(side, ((0, 0), (0, head_size - side.shape[1])))
     note = jnp.concatenate([partial, side], axis=0)
-    notes = [note] + [hop(note, "blk", blks, s) for s in range(1, blks)]
+    notes = [note] + [hop(note, "blk", blks, s) for s in reversed(range(1, blks))]
     proj_near, gate_near = fetch([note], [out_weight.T, gate_weight], "fetch_proj_gate")
 
     def combine(*refs):
@@ -319,11 +307,37 @@
 
     lanes = -(-(width + 2) // 128) * 128
 
+    inner = [b * 2 + r for r in range(2) for b in range(blks)]
+    outer = [r * blks + b for b in range(blks) for r in range(2)]
+
+    def shuffled(value, order, scratch):
+        for at, k in enumerate(order):
+            scratch[at * tok_dev : (at + 1) * tok_dev] = value[k * tok_dev : (k + 1) * tok_dev]
+        return scratch[...]
+
     def middle(
-        base_ref, keep_ref, gain_ref, own_ref, other_ref, gate_ref, up_ref, stream_ref, note_ref, *_
+        dec_ref,
+        embed_ref,
+        gain_ref,
+        masked_ref,
+        own_ref,
+        other_ref,
+        gate_ref,
+        up_ref,
+        mid_ref,
+        note_ref,
+        gate_out,
+        up_out,
+        base_ref,
     ):
-        mid = base_ref[...].astype(F32) + (own_ref[...].astype(F32) + other_ref[...].astype(F32))
-        stream_ref[...] = (mid * keep_ref[...]).astype(BF)
+        slots = lax.broadcasted_iota(jnp.int32, (tokens, 1), 0)
+        hits = jnp.where(slots == masked_ref[...], 1.0, 0.0)
+        masked = jnp.max(hits, axis=1, keepdims=True) > 0.0
+        base = jnp.where(masked, embed_ref[...].astype(F32), dec_ref[...].astype(F32))
+        mid = shuffled(base, inner, base_ref) + (
+            own_ref[...].astype(F32) + other_ref[...].astype(F32)
+        )
+        mid_ref[...] = mid
         note_ref[:, :width] = (mid * gain_ref[...].astype(F32)).astype(BF)
         squares = jnp.sum(mid * mid, axis=1, keepdims=True)
         high, low = split_in(squares, 2)
@@ -332,18 +346,45 @@
             lane == 0, high.astype(F32), jnp.where(lane == 1, low.astype(F32), 0.0)
         ).astype(BF)
 
-    stream, note, gate_near, up_near = kernel(
+    mid, note, gate_near, up_near = kernel(
         middle,
         "middle",
         [
-            sds((tokens, width), BF),
+            sds((tokens, width), F32),
             sds((tokens, lanes), BF),
             sds(gate_near.shape, BF),
             sds(up_near.shape, BF),
         ],
-        [VM] * 7,
-        [base_state, keep_inner, gain, proj, proj_other, gate_near, up_near],
-        aliases={5: 2, 6: 3},
+        [VM] * 8,
+        [
+            dec_state,
+            mask_embed[None, :],
+            norm_gain[None, :],
+            masked_pos,
+            proj,
+            proj_other,
+            gate_near,
+            up_near,
+        ],
+        aliases={6: 2, 7: 3},
+        scratch=[pltpu.VMEM((tokens, width), F32)],
+    )
+
+    def residual(mid_ref, length_ref, stream_ref, keep_ref, order_ref):
+        slots = lax.broadcasted_iota(jnp.int32, (tokens, 1), 0)
+        keep = jnp.where(slots < length_ref[...], 1.0, 0.0)
+        stream_ref[...] = (shuffled(mid_ref[...], outer, order_ref) * keep).astype(BF)
+        first = (lax.axis_index("blk") * 2 + lax.axis_index("rows")) * tok_dev
+        owned = first + lax.broadcasted_iota(jnp.int32, (tok_dev, 1), 0)
+        keep_ref[...] = jnp.where(owned < length_ref[...], 1.0, 0.0)
+
+    stream, keep_own = kernel(
+        residual,
+        "residual",
+        [sds((tokens, width), BF), sds((tok_dev, 1), F32)],
+        [VM] * 2,
+        [mid, cand_lengths[None, :]],
+        scratch=[pltpu.VMEM((tokens, width), F32)],
     )
 
     far_pairs, near_pairs = [], []
@@ -363,7 +404,7 @@
     )
     lanes_all = note.shape[1]
 
-    def pick(own_ref, near_ref, far_ref, gate_ref, up_ref, out_ref):
+    def pick(own_ref, far_ref, near_ref, gate_ref, up_ref, out_ref):
         at = lax.axis_index("blk")
         inside = at // half == lax.axis_index("heads")
         odd = at % 2 == 1
@@ -377,7 +418,7 @@
         "pick",
         [sds((half, tokens, lanes_all), BF)],
         [VM, VM, VM, ANY, ANY],
-        [note, near, far, gate_near, up_near],
+        [note, far, near, gate_near, up_near],
     )
     theirs = hop(mine, "rows", 2, 1)
     rows_in = gate_weight.shape[0]
@@ -523,13 +564,19 @@
     for s in reversed(range(1, blks)):
         own = own + hop(sends[s - 1], "blk", blks, s).astype(F32)
     branch = (own * keep_own).astype(BF)
-    stream = stream.reshape(2, blks, tok_dev, width).swapaxes(0, 1).reshape(tokens, width)
     return (stream, branch)
 
 
 def solution(mesh):
     size = dict(mesh.shape)
-    direct = size["blk"] == 4 and size["heads"] == 2 and size["rows"] == 2
+    few = size["blk"] == 4 and size["heads"] == 2 and size["rows"] == 2
+
+    def shards(*args):
+        queries, cand_lengths = args[0], args[-2]
+        toks = queries.shape[0] * size["blk"]
+        direct = few and toks % 16 == 0 and toks * 2 <= LEN and cand_lengths.shape[0] == 1
+        return (shards_direct if direct else shards_any)(*args)
+
     placed = (
         P(("groups", "blk", "rows"), "heads", None),
         P(("groups", "blk"), "heads", None),
@@ -545,7 +592,7 @@
         P("groups", None),
     )
     return jax.shard_map(
-        shards_direct if direct else shards_any,
+        shards,
         mesh=mesh,
         in_specs=placed,
         out_specs=(P("groups", ("blk", "rows")), P(("groups", "blk", "rows"), "heads")),

time: 56.9 us -> 55.4 us (0.974)
  local copies, waits for them, and re-layouts: 1.9 us -> 0.18 us
  waiting for transfers between devices: 9.88 us -> 11.4 us
  other arithmetic: 2.7 us -> 1.21 us
  Pallas kernels: 16.6 us -> 17.6 us
  starting transfers between devices: 22.1 us -> 21.4 us
    ppermute x15, waiting for transfers between devices: 7.77 us -> 9.25 us  [hop(): return lax.ppermute(value, axis, [(i, i ^ step) for i in range(size)])]
    select_n x1 -> x0, other arithmetic: 0.84 us -> none  [shards_direct(): jnp.where(masked_tok[:, None], mask_embed[None, :], dec_state)]
    pallas_call x11 -> x12, Pallas kernels: 5.82 us -> 6.59 us  [kernel(): pl.pallas_call(body, out_shape=outs, in_specs=specs, out_specs=[VM] * len...]
    broadcast_in_dim x3 -> x2, local copies, waits for them, and re-layouts: 0.76 us -> 0.01 us  [the longest x1 0.01 us: shards_direct(): mask_embed[None, :]]
    reduce_or x1 -> x0, other arithmetic: 0.74 us -> none  [token_masks(): jnp.any(masked_pos[:, :, None] == slots[None, None, :], axis=1).reshape(-1)]
    reshape x5 -> x0, local copies, waits for them, and re-layouts: 0.71 us -> none  [the longest x2 0.65 us: shards_direct(): stream.reshape(2, blks, tok_dev, width).swapaxes(0, 1)]
  transfers between devices with their start and end apart: 17 -> 17, of which waited for: 12 -> 11; matrix products, arithmetic and copies ran while one was open for 6% -> 0% of each run, Pallas kernels for 25% -> 27%
where the time goes in v7:
time: 55.4 us; the launch traced here: 55.1 us
  starting transfers between devices  21.4 us (39%)
  Pallas kernels  17.6 us (32%)
  waiting for transfers between devices  11.4 us (21%)
  matrix products  1.82 us (3%)
  between operations  1.48 us (3%)
  other arithmetic  1.21 us (2%)
    ppermute x15, starting transfers between devices, hop(): return lax.ppermute(value, axis, [(i, i ^ step) for i in range(size)])  19.4 us
    pallas_call x5, Pallas kernels, fetch(): pl.pallas_call(body, out_shape=[jax.ShapeDtypeStruct(a.shape, a.dtype) fo...  11 us
    ppermute x15, waiting for transfers between devices, hop(): return lax.ppermute(value, axis, [(i, i ^ step) for i in range(size)])  9.25 us
    pallas_call x12, Pallas kernels, kernel(): pl.pallas_call(body, out_shape=outs, in_specs=specs, out_specs=[VM] * len...  6.59 us
    ppermute x1, starting transfers between devices, shards_direct(): far = lax.ppermute(note, ('blk', 'heads'), far_pairs)  1.94 us
    ppermute x1, waiting for transfers between devices, shards_direct(): far = lax.ppermute(note, ('blk', 'heads'), far_pairs)  1.87 us
    dot_general x1, matrix products, shards_direct(): jnp.einsum('tgjd,kgd->tgjk', grouped, src_keys, preferred_element_type=F32)  1.13 us
  transfers between devices with their start and end apart: 17, of which 11 were waited for; matrix products, arithmetic and copies ran while one was open for 0% of the time, Pallas kernels for 27%

profile of v7, /device:TPU:0, one launch (start us, length us, event | category | flops | bytes accessed | tf_op | source)
XLA Modules:
  0.0 55.1 jit_solution(16584245891485815114)
XLA Ops:
  0.6 5.1 %collective-permute-start.2 = (bf16[4,8,256]{2,1,0:T(8,128)(2,1)}, bf16[4,8,256]{2,1,0:T(8,128)(2,1)S(1)}, u32[]{:S(2)}, u32[]{:S(2)}) collective-permute-start(bf16[4,8,256]{2,1,0:T(8,128)(2,1)} %refs_0_.1), channel_id=1, source_target_pairs={{0,12},{4,8},{8,4},{12,0},{1,13},{5,9},{9,5},{13,1},{2,14},{6,10},... | collective-permute-start | bytes 49160 | tf_op jit(solution)/shard_map/ppermute | solution.py:111
  5.8 0.6 %collective-permute-start = (bf16[4,8,256]{2,1,0:T(8,128)(2,1)}, bf16[4,8,256]{2,1,0:T(8,128)(2,1)S(1)}, u32[]{:S(2)}, u32[]{:S(2)}) collective-permute-start(bf16[4,8,256]{2,1,0:T(8,128)(2,1)} %refs_0_.1), channel_id=1, source_target_pairs={{0,4},{4,0},{8,12},{12,8},{1,5},{5,1},{9,13},{13,9},{2,6},{6,2},{1... | collective-permute-start | bytes 49160 | tf_op jit(solution)/shard_map/ppermute | solution.py:111
  6.4 1.0 %fetch_small.1 = (bf16[4,8,256]{2,1,0:T(8,128)(2,1)S(1)}, bf16[32,448]{1,0:T(8,128)(2,1)S(1)}, bf16[448]{0:T(512)(128)(2,1)S(1)}, bf16[448]{0:T(512)(128)(2,1)S(1)}, s32[1,48]{1,0:T(1,128)S(1)}) custom-call(bf16[4,8,256]{2,1,0:T(8,128)(2,1)} %refs_0_.1, bf16[32,448]{1,0:T(8,128)(2,1)} %refs_1_.4, bf16[448]{0:T(512)(128)(2,1)} %refs_2_.2, ...), custom_call_target="tpu_custom_call" | custom-call | bytes 94080 | tf_op jit(solution)/shard_map/fetch_small/pallas_call | solution.py:148
  7.4 0.3 collective-permute-done.2
  7.7 2.9 %collective-permute-done.1 = bf16[4,8,256]{2,1,0:T(8,128)(2,1)S(1)} collective-permute-done((bf16[4,8,256]{2,1,0:T(8,128)(2,1)}, bf16[4,8,256]{2,1,0:T(8,128)(2,1)S(1)}, u32[]{:S(2)}, u32[]{:S(2)}) %collective-permute-start.1) | collective-permute-done | bytes 16416 | tf_op jit(solution)/shard_map/ppermute | solution.py:111
  10.7 1.1 %fusion.30 = (f32[16,4,2]{0,2,1:T(2,128)S(1)}, f32[16,4,2,1536]{3,0,2,1:T(8,128)S(1)}) fusion(bf16[16,4,2,256]{3,0,2,1:T(8,128)(2,1)S(1)} %bitcast.23, bf16[1536,4,256,1]{2,1,0,3:T(4,128)(2,1)S(1)} %bitcast.21), kind=kOutput, calls=%fused_computation.39 | convolution fusion | flops 101056384 | bytes 3998208 | tf_op jit(solution)/shard_map/tgjd,kgd->tgjk/dot_general | solution.py:218
  11.8 0.3 fusion.19
  12.1 0.7 %fusion.16 = bf16[4,2,16,256]{3,2,1,0:T(8,128)(2,1)S(1)} fusion(bf16[1536,4,256,1]{2,1,0,3:T(4,128)(2,1)S(1)} %bitcast.30, f32[16,4,2,1536]{3,0,2,1:T(8,128)S(1)} %get-tuple-element.112, f32[16,4,2]{0,2,1:T(2,128)S(1)} %get-tuple-element.67, f32[4,2,16]{2,1,0:T(2,128)S(1)} %bitcast.28), kind=kOutput, calls=%fused_computation.8 | convolution fusion | flops 101122048 | bytes 3998720 | tf_op jit(solution)/shard_map/tgjk,kgd->tgjd/dot_general | solution.py:223
  12.8 0.1 copy.35
  12.9 0.1 copy.34
  13.0 0.1 fusion.29
  13.1 1.5 %collective-permute-start.3 = (bf16[144,256]{1,0:T(8,128)(2,1)S(1)}, bf16[144,256]{1,0:T(8,128)(2,1)S(1)}, u32[]{:S(2)}, u32[]{:S(2)}) collective-permute-start(bf16[144,256]{1,0:T(8,128)(2,1)S(1)} %pad_maximum_fusion.refs_0_), channel_id=1, source_target_pairs={{0,12},{4,8},{8,4},{12,0},{1,13},{5,9},{9,5},{13,1},{2,14},{6,10},... | collective-permute-start | bytes 221192 | tf_op jit(solution)/shard_map/ppermute | solution.py:111
  14.6 0.6 %collective-permute-start.4 = (bf16[144,256]{1,0:T(8,128)(2,1)S(1)}, bf16[144,256]{1,0:T(8,128)(2,1)S(1)}, u32[]{:S(2)}, u32[]{:S(2)}) collective-permute-start(bf16[144,256]{1,0:T(8,128)(2,1)S(1)} %pad_maximum_fusion.refs_0_), channel_id=1, source_target_pairs={{0,8},{4,12},{8,0},{12,4},{1,9},{5,13},{9,1},{13,5},{2,10},{6,14},... | collective-permute-start | bytes 221192 | tf_op jit(solution)/shard_map/ppermute | solution.py:111
  15.2 2.3 %collective-permute-start.5 = (bf16[144,256]{1,0:T(8,128)(2,1)S(1)}, bf16[144,256]{1,0:T(8,128)(2,1)S(1)}, u32[]{:S(2)}, u32[]{:S(2)}) collective-permute-start(bf16[144,256]{1,0:T(8,128)(2,1)S(1)} %pad_maximum_fusion.refs_0_), channel_id=1, source_target_pairs={{0,4},{4,0},{8,12},{12,8},{1,5},{5,1},{9,13},{13,9},{2,6},{6,2},{1... | collective-permute-start | bytes 221192 | tf_op jit(solution)/shard_map/ppermute | solution.py:111
  17.5 3.4 %fetch_proj_gate.1 = (bf16[448,2048]{1,0:T(8,128)(2,1)S(1)}, bf16[1792,1792]{1,0:T(8,128)(2,1)S(1)}) custom-call(bf16[144,256]{1,0:T(8,128)(2,1)S(1)} %pad_maximum_fusion.refs_0_, bf16[448,2048]{1,0:T(8,128)(2,1)} %bitcast.22, bf16[1792,1792]{1,0:T(8,128)(2,1)} %refs_2_.3), custom_call_target="tpu_custom_call" | custom-call | bytes 16515072 | tf_op jit(solution)/shard_map/fetch_proj_gate/pallas_call | solution.py:148
  21.0 0.5 collective-permute-done.4.refs_2_
  21.5 0.2 combine.1
  21.7 0.1 collective-permute-start.6
  21.8 0.6 %project_own.1 = (f32[16,448]{1,0:T(8,128)S(1)}, bf16[1792,1792]{1,0:T(8,128)(2,1)S(1)}) custom-call(bf16[16,2048]{1,0:T(8,128)(2,1)S(1)} %get-tuple-element.71.own_ref, bf16[448,2048]{1,0:T(8,128)(2,1)S(1)} %get-tuple-element.72.weight_ref, bf16[1792,1792]{1,0:T(8,128)(2,1)S(1)} %get-tuple-element.73.gate_ref), custom_call_target="tpu_custom_call", output_to_operand_aliasing={{1}: (2, {})} | custom-call | bytes 14774272 | tf_op jit(solution)/shard_map/project_own/pallas_call | solution.py:117
  22.4 0.7 %collective-permute-done.6.other_ref = bf16[16,2048]{1,0:T(8,128)(2,1)S(1)} collective-permute-done((bf16[16,2048]{1,0:T(8,128)(2,1)S(1)}, bf16[16,2048]{1,0:T(8,128)(2,1)S(1)}, u32[]{:S(2)}, u32[]{:S(2)}) %collective-permute-start.6) | collective-permute-done | bytes 65568 | tf_op jit(solution)/shard_map/ppermute | solution.py:111
  23.1 0.6 %project.1 = (bf16[32,448]{1,0:T(8,128)(2,1)S(1)}, bf16[1792,1792]{1,0:T(8,128)(2,1)S(1)}) custom-call(f32[16,448]{1,0:T(8,128)S(1)} %get-tuple-element.74.own_ref, bf16[16,2048]{1,0:T(8,128)(2,1)S(1)} %collective-permute-done.6.other_ref, bf16[448,2048]{1,0:T(8,128)(2,1)S(1)} %get-tuple-element.72.weight_ref, ...), custom_call_target="tpu_custom_call", output_to_operand_aliasing={{1}: (3, {})} | custom-call | bytes 14802944 | tf_op jit(solution)/shard_map/project/pallas_call | solution.py:117
  23.6 1.5 %collective-permute-start.7 = (bf16[32,448]{1,0:T(8,128)(2,1)S(1)}, bf16[32,448]{1,0:T(8,128)(2,1)S(1)}, u32[]{:S(2)}, u32[]{:S(2)}) collective-permute-start(bf16[32,448]{1,0:T(8,128)(2,1)S(1)} %get-tuple-element.76.refs_0_.own_ref), channel_id=1, source_target_pairs={{0,2},{2,0},{1,3},{3,1},{4,6},{6,4},{5,7},{7,5},{8,10},{10,8},{9,1... | collective-permute-start | bytes 86024 | tf_op jit(solution)/shard_map/ppermute | solution.py:111
  25.2 1.9 %fetch_up_first.1.up_ref = bf16[1792,1792]{1,0:T(8,128)(2,1)S(1)} custom-call(bf16[32,448]{1,0:T(8,128)(2,1)S(1)} %get-tuple-element.76.refs_0_.own_ref, bf16[1792,1792]{1,0:T(8,128)(2,1)} %refs_1_.6), custom_call_target="tpu_custom_call" | custom-call | bytes 12845056 | tf_op jit(solution)/shard_map/fetch_up_first/pallas_call | solution.py:148
  27.1 0.5 collective-permute-done.7.other_ref
  27.6 0.2 middle.1
  27.8 1.9 %collective-permute-start.8 = (bf16[32,512]{1,0:T(8,128)(2,1)S(1)}, bf16[32,512]{1,0:T(8,128)(2,1)S(1)}, u32[]{:S(2)}, u32[]{:S(2)}) collective-permute-start(bf16[32,512]{1,0:T(8,128)(2,1)S(1)} %get-tuple-element.80.refs_0_.own_ref), channel_id=1, source_target_pairs={{0,12},{2,14},{4,8},{6,10},{8,4},{10,6},{12,0},{14,2},{1,13},{3,15... | collective-permute-start | bytes 98312 | tf_op jit(solution)/shard_map/ppermute | solution.py:397
  29.8 1.9 %fetch_up_last.1.up_ref.refs_4_ = bf16[1792,1792]{1,0:T(8,128)(2,1)S(1)} custom-call(bf16[32,512]{1,0:T(8,128)(2,1)S(1)} %get-tuple-element.80.refs_0_.own_ref, bf16[1792,1792]{1,0:T(8,128)(2,1)} %refs_1_.6, bf16[1792,1792]{1,0:T(8,128)(2,1)S(1)} %get-tuple-element.82.refs_2_), custom_call_target="tpu_custom_call", output_to_operand_aliasing={{}: (2, {})} | custom-call | bytes 12845056 | tf_op jit(solution)/shard_map/fetch_up_last/pallas_call | solution.py:148
  31.7 1.9 %collective-permute-done.8.far_ref = bf16[32,512]{1,0:T(8,128)(2,1)S(1)} collective-permute-done((bf16[32,512]{1,0:T(8,128)(2,1)S(1)}, bf16[32,512]{1,0:T(8,128)(2,1)S(1)}, u32[]{:S(2)}, u32[]{:S(2)}) %collective-permute-start.8) | collective-permute-done | bytes 32800 | tf_op jit(solution)/shard_map/ppermute | solution.py:397
  33.6 0.3 collective-permute-done.9.near_ref
  33.9 0.1 collective-permute-start.10
  34.0 1.2 %inner_products.1 = (f32[32,1792]{1,0:T(8,128)S(1)}, f32[32,1792]{1,0:T(8,128)S(1)}) custom-call(bf16[2,32,512]{2,1,0:T(8,128)(2,1)S(1)} %pick.1.mine_ref.refs_5_, bf16[1792,1792]{1,0:T(8,128)(2,1)S(1)} %get-tuple-element.81.gate_ref.refs_3_, bf16[1792,1792]{1,0:T(8,128)(2,1)S(1)} %fetch_up_last.1.up_ref.refs_4_), custom_call_target="tpu_custom_call" | custom-call | flops 205520896 | bytes 13369344 | tf_op jit(solution)/shard_map/inner_products/pallas_call | solution.py:117
  35.2 0.8 %gate_up_0.1 = (f32[32,2176]{1,0:T(8,128)S(1)}, bf16[32,2176]{1,0:T(8,128)(2,1)S(1)}) custom-call(bf16[2,32,512]{2,1,0:T(8,128)(2,1)S(1)} %collective-permute-done.10.refs_0_, f32[32,1792]{1,0:T(8,128)S(1)} %get-tuple-element.83.refs_1_, f32[32,1792]{1,0:T(8,128)S(1)} %get-tuple-element.84.refs_2_, ...), custom_call_target="tpu_custom_call" | custom-call | flops 102760448 | bytes 13852672 | tf_op jit(solution)/shard_map/gate_up_0/pallas_call | solution.py:117
  36.0 3.0 %collective-permute-start.12 = (bf16[32,2176]{1,0:T(8,128)(2,1)S(1)}, bf16[32,2176]{1,0:T(8,128)(2,1)S(1)}, u32[]{:S(2)}, u32[]{:S(2)}) collective-permute-start(bf16[32,2176]{1,0:T(8,128)(2,1)S(1)} %get-tuple-element.88), channel_id=1, source_target_pairs={{0,2},{2,0},{1,3},{3,1},{4,6},{6,4},{5,7},{7,5},{8,10},{10,8},{9,1... | collective-permute-start | bytes 417800 | tf_op jit(solution)/shard_map/ppermute | solution.py:111
  39.0 0.6 %gate_up_1.1 = (f32[32,1536]{1,0:T(8,128)S(1)}, bf16[32,1536]{1,0:T(8,128)(2,1)S(1)}) custom-call(bf16[2,32,512]{2,1,0:T(8,128)(2,1)S(1)} %collective-permute-done.10.refs_0_, f32[32,1792]{1,0:T(8,128)S(1)} %get-tuple-element.83.refs_1_, f32[32,1792]{1,0:T(8,128)S(1)} %get-tuple-element.84.refs_2_, ...), custom_call_target="tpu_custom_call" | custom-call | flops 102760448 | bytes 13664256 | tf_op jit(solution)/shard_map/gate_up_1/pallas_call | solution.py:117
  39.6 0.1 collective-permute-start.11
  39.7 2.8 %fetch_down.1.weight_ref = bf16[1792,1792]{1,0:T(8,128)(2,1)S(1)} custom-call(bf16[32,1536]{1,0:T(8,128)(2,1)S(1)} %get-tuple-element.86.refs_0_, bf16[1792,1792]{1,0:T(8,128)(2,1)} %refs_1_.7), custom_call_target="tpu_custom_call" | custom-call | bytes 12845056 | tf_op jit(solution)/shard_map/fetch_down/pallas_call | solution.py:148
  42.5 1.0 %collective-permute-done.12.other_ref.first_other_ref = bf16[32,2176]{1,0:T(8,128)(2,1)S(1)} collective-permute-done((bf16[32,2176]{1,0:T(8,128)(2,1)S(1)}, bf16[32,2176]{1,0:T(8,128)(2,1)S(1)}, u32[]{:S(2)}, u32[]{:S(2)}) %collective-permute-start.12) | collective-permute-done | bytes 139296 | tf_op jit(solution)/shard_map/ppermute | solution.py:111
  43.5 0.8 %down_first.1.part_ref = f32[32,1792]{1,0:T(8,128)S(1)} custom-call(f32[32,2176]{1,0:T(8,128)S(1)} %get-tuple-element.87.own_ref.first_ref, bf16[32,2176]{1,0:T(8,128)(2,1)S(1)} %collective-permute-done.12.other_ref.first_other_ref, bf16[1792,1792]{1,0:T(8,128)(2,1)S(1)} %fetch_down.1.weight_ref), custom_call_target="tpu_custom_call" | custom-call | flops 102760448 | bytes 7069696 | tf_op jit(solution)/shard_map/down_first/pallas_call | solution.py:117
  44.4 1.1 %collective-permute-done.11.other_ref = bf16[32,1536]{1,0:T(8,128)(2,1)S(1)} collective-permute-done((bf16[32,1536]{1,0:T(8,128)(2,1)S(1)}, bf16[32,1536]{1,0:T(8,128)(2,1)S(1)}, u32[]{:S(2)}, u32[]{:S(2)}) %collective-permute-start.11) | collective-permute-done | bytes 98336 | tf_op jit(solution)/shard_map/ppermute | solution.py:111
  45.4 0.7 %down_last.1 = (f32[16,1792]{1,0:T(8,128)S(1)}, bf16[16,1792]{1,0:T(8,128)(2,1)S(1)}) custom-call(f32[32,1536]{1,0:T(8,128)S(1)} %get-tuple-element.85.own_ref, bf16[32,1536]{1,0:T(8,128)(2,1)S(1)} %collective-permute-done.11.other_ref, f32[32,2176]{1,0:T(8,128)S(1)} %get-tuple-element.87.own_ref.first_ref, ...), custom_call_target="tpu_custom_call" | custom-call | bytes 7536640 | tf_op jit(solution)/shard_map/down_last/pallas_call | solution.py:117
  46.2 1.2 %collective-permute-done.13.back_ref = bf16[16,1792]{1,0:T(8,128)(2,1)S(1)} collective-permute-done((bf16[16,1792]{1,0:T(8,128)(2,1)S(1)}, bf16[16,1792]{1,0:T(8,128)(2,1)S(1)}, u32[]{:S(2)}, u32[]{:S(2)}) %collective-permute-start.13) | collective-permute-done | bytes 57376 | tf_op jit(solution)/shard_map/ppermute | solution.py:111
  47.4 0.1 owners.1
  47.5 2.4 %collective-permute-start.14 = (bf16[4,1792]{1,0:T(4,128)(2,1)S(1)}, bf16[4,1792]{1,0:T(4,128)(2,1)S(1)}, u32[]{:S(2)}, u32[]{:S(2)}) collective-permute-start(bf16[4,1792]{1,0:T(4,128)(2,1)S(1)} %get-tuple-element.92), channel_id=1, source_target_pairs={{0,12},{4,8},{8,4},{12,0},{1,13},{5,9},{9,5},{13,1},{2,14},{6,10},... | collective-permute-start | bytes 43016 | tf_op jit(solution)/shard_map/ppermute | solution.py:111
  49.8 2.1 %collective-permute-start.16 = (bf16[4,1792]{1,0:T(4,128)(2,1)S(1)}, bf16[4,1792]{1,0:T(4,128)(2,1)S(1)}, u32[]{:S(2)}, u32[]{:S(2)}) collective-permute-start(bf16[4,1792]{1,0:T(4,128)(2,1)S(1)} %get-tuple-element.94), channel_id=1, source_target_pairs={{0,4},{4,0},{8,12},{12,8},{1,5},{5,1},{9,13},{13,9},{2,6},{6,2},{1... | collective-permute-start | bytes 43016 | tf_op jit(solution)/shard_map/ppermute | solution.py:111
  52.6 0.7 %residual.1 = (bf16[32,448]{1,0:T(8,128)(2,1)}, f32[4,1]{1,0:T(4,128)S(1)}) custom-call(f32[32,448]{1,0:T(8,128)S(1)} %get-tuple-element.78.mid_ref, s32[1,1]{1,0:T(1,128)} %bitcast.20.length_ref), custom_call_target="tpu_custom_call" | custom-call | bytes 86036 | tf_op jit(solution)/shard_map/residual/pallas_call | solution.py:117
  53.3 0.1 reduce
  53.4 1.1 %collective-permute-done.15 = bf16[4,1792]{1,0:T(4,128)(2,1)S(1)} collective-permute-done((bf16[4,1792]{1,0:T(4,128)(2,1)S(1)}, bf16[4,1792]{1,0:T(4,128)(2,1)S(1)}, u32[]{:S(2)}, u32[]{:S(2)}) %collective-permute-start.15) | collective-permute-done | bytes 14368 | tf_op jit(solution)/shard_map/ppermute | solution.py:111
  54.5 0.7 %multiply_convert_fusion = bf16[4,1792]{1,0:T(4,128)(2,1)} fusion(bf16[4,1792]{1,0:T(4,128)(2,1)S(1)} %collective-permute-done.16, bf16[4,1792]{1,0:T(4,128)(2,1)S(1)} %collective-permute-done.15, f32[4,1792]{1,0:T(4,128)S(1)} %get-tuple-element.91, bf16[4,1792]{1,0:T(4,128)(2,1)S(1)} %collective-permute-done.14, f32[4]{0:T(128)S(1)} %reduce), kind=kLoop, calls=%fused_computation.15 | loop fusion | flops 57344 | bytes 86032 | tf_op jit(solution)/shard_map/convert_element_type | solution.py:566
  (26 shorter events, 0.2 us)
Async XLA Ops:
  0.6 10.1 %copy-start = (bf16[1536,4,256]{2,1,0:T(4,128)(2,1)S(1)}, bf16[1536,4,256]{2,1,0:T(4,128)(2,1)}, u32[]{:S(2)}) copy-start(bf16[1536,4,256]{2,1,0:T(4,128)(2,1)} %param.13) | copy-start | bytes 9437188
  0.6 7.0 %collective-permute-start.2 = (bf16[4,8,256]{2,1,0:T(8,128)(2,1)}, bf16[4,8,256]{2,1,0:T(8,128)(2,1)S(1)}, u32[]{:S(2)}, u32[]{:S(2)}) collective-permute-start(bf16[4,8,256]{2,1,0:T(8,128)(2,1)} %refs_0_.1), channel_id=1, source_target_pairs={{0,12},{4,8},{8,4},{12,0},{1,13},{5,9},{9,5},{13,1},{2,14},{6,10},... | collective-permute-start | bytes 49160 | tf_op jit(solution)/shard_map/ppermute | solution.py:111
  5.8 4.8 %collective-permute-start.1 = (bf16[4,8,256]{2,1,0:T(8,128)(2,1)}, bf16[4,8,256]{2,1,0:T(8,128)(2,1)S(1)}, u32[]{:S(2)}, u32[]{:S(2)}) collective-permute-start(bf16[4,8,256]{2,1,0:T(8,128)(2,1)} %refs_0_.1), channel_id=1, source_target_pairs={{0,8},{4,12},{8,0},{12,4},{1,9},{5,13},{9,1},{13,5},{2,10},{6,14},... | collective-permute-start | bytes 49160 | tf_op jit(solution)/shard_map/ppermute | solution.py:111
  5.8 4.9 %collective-permute-start = (bf16[4,8,256]{2,1,0:T(8,128)(2,1)}, bf16[4,8,256]{2,1,0:T(8,128)(2,1)S(1)}, u32[]{:S(2)}, u32[]{:S(2)}) collective-permute-start(bf16[4,8,256]{2,1,0:T(8,128)(2,1)} %refs_0_.1), channel_id=1, source_target_pairs={{0,4},{4,0},{8,12},{12,8},{1,5},{5,1},{9,13},{13,9},{2,6},{6,2},{1... | collective-permute-start | bytes 49160 | tf_op jit(solution)/shard_map/ppermute | solution.py:111
  6.4 5.7 %copy-start.1 = (bf16[1536,4,256]{2,1,0:T(4,128)(2,1)S(1)}, bf16[1536,4,256]{2,1,0:T(4,128)(2,1)}, u32[]{:S(2)}) copy-start(bf16[1536,4,256]{2,1,0:T(4,128)(2,1)} %param.14) | copy-start | bytes 9437188
  13.1 7.9 %collective-permute-start.3 = (bf16[144,256]{1,0:T(8,128)(2,1)S(1)}, bf16[144,256]{1,0:T(8,128)(2,1)S(1)}, u32[]{:S(2)}, u32[]{:S(2)}) collective-permute-start(bf16[144,256]{1,0:T(8,128)(2,1)S(1)} %pad_maximum_fusion.refs_0_), channel_id=1, source_target_pairs={{0,12},{4,8},{8,4},{12,0},{1,13},{5,9},{9,5},{13,1},{2,14},{6,10},... | collective-permute-start | bytes 221192 | tf_op jit(solution)/shard_map/ppermute | solution.py:111
  14.6 6.9 %collective-permute-start.4 = (bf16[144,256]{1,0:T(8,128)(2,1)S(1)}, bf16[144,256]{1,0:T(8,128)(2,1)S(1)}, u32[]{:S(2)}, u32[]{:S(2)}) collective-permute-start(bf16[144,256]{1,0:T(8,128)(2,1)S(1)} %pad_maximum_fusion.refs_0_), channel_id=1, source_target_pairs={{0,8},{4,12},{8,0},{12,4},{1,9},{5,13},{9,1},{13,5},{2,10},{6,14},... | collective-permute-start | bytes 221192 | tf_op jit(solution)/shard_map/ppermute | solution.py:111
  15.2 6.3 %collective-permute-start.5 = (bf16[144,256]{1,0:T(8,128)(2,1)S(1)}, bf16[144,256]{1,0:T(8,128)(2,1)S(1)}, u32[]{:S(2)}, u32[]{:S(2)}) collective-permute-start(bf16[144,256]{1,0:T(8,128)(2,1)S(1)} %pad_maximum_fusion.refs_0_), channel_id=1, source_target_pairs={{0,4},{4,0},{8,12},{12,8},{1,5},{5,1},{9,13},{13,9},{2,6},{6,2},{1... | collective-permute-start | bytes 221192 | tf_op jit(solution)/shard_map/ppermute | solution.py:111
  21.7 1.3 %collective-permute-start.6 = (bf16[16,2048]{1,0:T(8,128)(2,1)S(1)}, bf16[16,2048]{1,0:T(8,128)(2,1)S(1)}, u32[]{:S(2)}, u32[]{:S(2)}) collective-permute-start(bf16[16,2048]{1,0:T(8,128)(2,1)S(1)} %get-tuple-element.71.own_ref), channel_id=1, source_target_pairs={{0,1},{1,0},{2,3},{3,2},{4,5},{5,4},{6,7},{7,6},{8,9},{9,8},{10,11... | collective-permute-start | bytes 196616 | tf_op jit(solution)/shard_map/ppermute | solution.py:111
  23.6 3.9 %collective-permute-start.7 = (bf16[32,448]{1,0:T(8,128)(2,1)S(1)}, bf16[32,448]{1,0:T(8,128)(2,1)S(1)}, u32[]{:S(2)}, u32[]{:S(2)}) collective-permute-start(bf16[32,448]{1,0:T(8,128)(2,1)S(1)} %get-tuple-element.76.refs_0_.own_ref), channel_id=1, source_target_pairs={{0,2},{2,0},{1,3},{3,1},{4,6},{6,4},{5,7},{7,5},{8,10},{10,8},{9,1... | collective-permute-start | bytes 86024 | tf_op jit(solution)/shard_map/ppermute | solution.py:111
  27.8 5.7 %collective-permute-start.8 = (bf16[32,512]{1,0:T(8,128)(2,1)S(1)}, bf16[32,512]{1,0:T(8,128)(2,1)S(1)}, u32[]{:S(2)}, u32[]{:S(2)}) collective-permute-start(bf16[32,512]{1,0:T(8,128)(2,1)S(1)} %get-tuple-element.80.refs_0_.own_ref), channel_id=1, source_target_pairs={{0,12},{2,14},{4,8},{6,10},{8,4},{10,6},{12,0},{14,2},{1,13},{3,15... | collective-permute-start | bytes 98312 | tf_op jit(solution)/shard_map/ppermute | solution.py:397
  29.8 4.1 %collective-permute-start.9 = (bf16[32,512]{1,0:T(8,128)(2,1)S(1)}, bf16[32,512]{1,0:T(8,128)(2,1)S(1)}, u32[]{:S(2)}, u32[]{:S(2)}) collective-permute-start(bf16[32,512]{1,0:T(8,128)(2,1)S(1)} %get-tuple-element.80.refs_0_.own_ref), channel_id=1, source_target_pairs={{0,4},{2,8},{4,0},{6,12},{8,2},{10,14},{12,6},{14,10},{1,5},{3,9},... | collective-permute-start | bytes 98312 | tf_op jit(solution)/shard_map/ppermute | solution.py:396
  33.9 1.3 %collective-permute-start.10 = (bf16[2,32,512]{2,1,0:T(8,128)(2,1)S(1)}, bf16[2,32,512]{2,1,0:T(8,128)(2,1)S(1)}, u32[]{:S(2)}, u32[]{:S(2)}) collective-permute-start(bf16[2,32,512]{2,1,0:T(8,128)(2,1)S(1)} %pick.1.mine_ref.refs_5_), channel_id=1, source_target_pairs={{0,1},{1,0},{2,3},{3,2},{4,5},{5,4},{6,7},{7,6},{8,9},{9,8},{10,11... | collective-permute-start | bytes 196616 | tf_op jit(solution)/shard_map/ppermute | solution.py:111
  36.0 7.5 %collective-permute-start.12 = (bf16[32,2176]{1,0:T(8,128)(2,1)S(1)}, bf16[32,2176]{1,0:T(8,128)(2,1)S(1)}, u32[]{:S(2)}, u32[]{:S(2)}) collective-permute-start(bf16[32,2176]{1,0:T(8,128)(2,1)S(1)} %get-tuple-element.88), channel_id=1, source_target_pairs={{0,2},{2,0},{1,3},{3,1},{4,6},{6,4},{5,7},{7,5},{8,10},{10,8},{9,1... | collective-permute-start | bytes 417800 | tf_op jit(solution)/shard_map/ppermute | solution.py:111
  39.6 5.8 %collective-permute-start.11 = (bf16[32,1536]{1,0:T(8,128)(2,1)S(1)}, bf16[32,1536]{1,0:T(8,128)(2,1)S(1)}, u32[]{:S(2)}, u32[]{:S(2)}) collective-permute-start(bf16[32,1536]{1,0:T(8,128)(2,1)S(1)} %get-tuple-element.86.refs_0_), channel_id=1, source_target_pairs={{0,2},{2,0},{1,3},{3,1},{4,6},{6,4},{5,7},{7,5},{8,10},{10,8},{9,1... | collective-permute-start | bytes 294920 | tf_op jit(solution)/shard_map/ppermute | solution.py:111
  46.1 1.3 %collective-permute-start.13 = (bf16[16,1792]{1,0:T(8,128)(2,1)S(1)}, bf16[16,1792]{1,0:T(8,128)(2,1)S(1)}, u32[]{:S(2)}, u32[]{:S(2)}) collective-permute-start(bf16[16,1792]{1,0:T(8,128)(2,1)S(1)} %get-tuple-element.90), channel_id=1, source_target_pairs={{0,1},{1,0},{2,3},{3,2},{4,5},{5,4},{6,7},{7,6},{8,9},{9,8},{10,11... | collective-permute-start | bytes 172040 | tf_op jit(solution)/shard_map/ppermute | solution.py:111
  47.5 5.9 %collective-permute-start.14 = (bf16[4,1792]{1,0:T(4,128)(2,1)S(1)}, bf16[4,1792]{1,0:T(4,128)(2,1)S(1)}, u32[]{:S(2)}, u32[]{:S(2)}) collective-permute-start(bf16[4,1792]{1,0:T(4,128)(2,1)S(1)} %get-tuple-element.92), channel_id=1, source_target_pairs={{0,12},{4,8},{8,4},{12,0},{1,13},{5,9},{9,5},{13,1},{2,14},{6,10},... | collective-permute-start | bytes 43016 | tf_op jit(solution)/shard_map/ppermute | solution.py:111
  49.8 4.6 %collective-permute-start.15 = (bf16[4,1792]{1,0:T(4,128)(2,1)S(1)}, bf16[4,1792]{1,0:T(4,128)(2,1)S(1)}, u32[]{:S(2)}, u32[]{:S(2)}) collective-permute-start(bf16[4,1792]{1,0:T(4,128)(2,1)S(1)} %get-tuple-element.93), channel_id=1, source_target_pairs={{0,8},{4,12},{8,0},{12,4},{1,9},{5,13},{9,1},{13,5},{2,10},{6,14},... | collective-permute-start | bytes 43016 | tf_op jit(solution)/shard_map/ppermute | solution.py:111
  49.8 4.6 %collective-permute-start.16 = (bf16[4,1792]{1,0:T(4,128)(2,1)S(1)}, bf16[4,1792]{1,0:T(4,128)(2,1)S(1)}, u32[]{:S(2)}, u32[]{:S(2)}) collective-permute-start(bf16[4,1792]{1,0:T(4,128)(2,1)S(1)} %get-tuple-element.94), channel_id=1, source_target_pairs={{0,4},{4,0},{8,12},{12,8},{1,5},{5,1},{9,13},{13,9},{2,6},{6,2},{1... | collective-permute-start | bytes 43016 | tf_op jit(solution)/shard_map/ppermute | solution.py:111

commit v8 on v7

--- a/solution.py
+++ b/solution.py
@@ -136,8 +136,8 @@
         targets, sems = refs[-1 - n : -1], refs[-1]
         copies = []
         for i, (source, target) in enumerate(zip(sources, targets)):
-            if rows is not None:
-                source, target = source.at[pl.ds(*rows)], target.at[pl.ds(*rows)]
+            if rows is not None and rows[i] is not None:
+                source, target = source.at[pl.ds(*rows[i])], target.at[pl.ds(*rows[i])]
             copies.append(pltpu.make_async_copy(source, target, sems.at[i]))
         for copy in copies:
             copy.start()
@@ -208,7 +208,7 @@
         [], [queries, dec_state, mask_embed, norm_gain, masked_pos], "fetch_small"
     )
     blocks = [queries_near] * blks
-    for s in reversed(range(1, blks)):
+    for s in [blks - 1] + list(range(1, blks - 1)):
         piece = hop(queries, "blk", blks, s)
         blocks = [jnp.where(blk == (k ^ s), piece, block) for k, block in enumerate(blocks)]
         blocks = list(lax.optimization_barrier(tuple(blocks)))
@@ -231,7 +231,10 @@
     side = jnp.pad(side, ((0, 0), (0, head_size - side.shape[1])))
     note = jnp.concatenate([partial, side], axis=0)
     notes = [note] + [hop(note, "blk", blks, s) for s in reversed(range(1, blks))]
-    proj_near, gate_near = fetch([note], [out_weight.T, gate_weight], "fetch_proj_gate")
+    gate_cut = gate_weight.shape[0] * 2 // 48 * 16
+    proj_near, gate_near = fetch(
+        [note], [out_weight.T, gate_weight], "fetch_proj_gate", rows=[None, (0, gate_cut)]
+    )
 
     def combine(*refs):
         ins, out = refs[:blks], refs[blks + 2]
@@ -302,8 +305,13 @@
         aliases={3: 1},
     )
     proj_other = hop(proj, "heads", 2, 1)
-    up_cut = up_weight.shape[0] // 32 * 16
-    (up_near,) = fetch([proj], [up_weight], "fetch_up_first", rows=(0, up_cut))
+    (gate_near,) = fetch(
+        [proj],
+        [gate_weight],
+        "fetch_gate_last",
+        rows=[(gate_cut, gate_weight.shape[0] - gate_cut)],
+        into=[gate_near],
+    )
 
     lanes = -(-(width + 2) // 128) * 128
 
@@ -323,11 +331,9 @@
         own_ref,
         other_ref,
         gate_ref,
-        up_ref,
         mid_ref,
         note_ref,
         gate_out,
-        up_out,
         base_ref,
     ):
         slots = lax.broadcasted_iota(jnp.int32, (tokens, 1), 0)
@@ -346,16 +352,15 @@
             lane == 0, high.astype(F32), jnp.where(lane == 1, low.astype(F32), 0.0)
         ).astype(BF)
 
-    mid, note, gate_near, up_near = kernel(
+    mid, note, gate_near = kernel(
         middle,
         "middle",
         [
             sds((tokens, width), F32),
             sds((tokens, lanes), BF),
             sds(gate_near.shape, BF),
-            sds(up_near.shape, BF),
         ],
-        [VM] * 8,
+        [VM] * 7,
         [
             dec_state,
             mask_embed[None, :],
@@ -364,9 +369,8 @@
             proj,
             proj_other,
             gate_near,
-            up_near,
         ],
-        aliases={6: 2, 7: 3},
+        aliases={6: 2},
         scratch=[pltpu.VMEM((tokens, width), F32)],
     )
 
@@ -395,13 +399,7 @@
             near_pairs.append((b * head_parts + h, to[0] * head_parts + to[1]))
     near = lax.ppermute(note, ("blk", "heads"), near_pairs)
     far = lax.ppermute(note, ("blk", "heads"), far_pairs)
-    (up_near,) = fetch(
-        [note],
-        [up_weight],
-        "fetch_up_last",
-        rows=(up_cut, up_weight.shape[0] - up_cut),
-        into=[up_near],
-    )
+    (up_near,) = fetch([note], [up_weight], "fetch_up")
     lanes_all = note.shape[1]
 
     def pick(own_ref, far_ref, near_ref, gate_ref, up_ref, out_ref):
@@ -561,7 +559,7 @@
         [VM, VM],
         [keep, back],
     )
-    for s in reversed(range(1, blks)):
+    for s in range(1, blks):
         own = own + hop(sends[s - 1], "blk", blks, s).astype(F32)
     branch = (own * keep_own).astype(BF)
     return (stream, branch)

time: 55.4 us -> 55.3 us (level)
    ppermute x1, waiting for transfers between devices: 1.87 us -> 0.88 us  [shards_direct(): far = lax.ppermute(note, ('blk', 'heads'), far_pairs)]
    ppermute x15, waiting for transfers between devices: 9.25 us -> 10.1 us  [hop(): return lax.ppermute(value, axis, [(i, i ^ step) for i in range(size)])]
  transfers between devices with their start and end apart: 17 -> 17, of which waited for: 11 -> 12; matrix products, arithmetic and copies ran while one was open for 0% -> 0% of each run, Pallas kernels for 27% -> 27%
where the time goes in v8:
time: 55.3 us; the launch traced here: 55.1 us
  starting transfers between devices  21.5 us (39%)
  Pallas kernels  17.6 us (32%)
  waiting for transfers between devices  11.3 us (20%)
  matrix products  1.82 us (3%)
  between operations  1.47 us (3%)
  other arithmetic  1.2 us (2%)
    ppermute x15, starting transfers between devices, hop(): return lax.ppermute(value, axis, [(i, i ^ step) for i in range(size)])  19.5 us
    pallas_call x5, Pallas kernels, fetch(): pl.pallas_call(body, out_shape=[jax.ShapeDtypeStruct(a.shape, a.dtype) fo...  11 us
    ppermute x15, waiting for transfers between devices, hop(): return lax.ppermute(value, axis, [(i, i ^ step) for i in range(size)])  10.1 us
    pallas_call x12, Pallas kernels, kernel(): pl.pallas_call(body, out_shape=outs, in_specs=specs, out_specs=[VM] * len...  6.59 us
    ppermute x1, starting transfers between devices, shards_direct(): far = lax.ppermute(note, ('blk', 'heads'), far_pairs)  2.01 us
    dot_general x1, matrix products, shards_direct(): jnp.einsum('tgjd,kgd->tgjk', grouped, src_keys, preferred_element_type=F32)  1.13 us
  transfers between devices with their start and end apart: 17, of which 12 were waited for; matrix products, arithmetic and copies ran while one was open for 0% of the time, Pallas kernels for 27%

profile of v8, /device:TPU:0, one launch (start us, length us, event | category | flops | bytes accessed | tf_op | source)
XLA Modules:
  0.0 55.1 jit_solution(13169256399017774178)
XLA Ops:
  0.6 5.1 %collective-permute-start.2 = (bf16[4,8,256]{2,1,0:T(8,128)(2,1)}, bf16[4,8,256]{2,1,0:T(8,128)(2,1)S(1)}, u32[]{:S(2)}, u32[]{:S(2)}) collective-permute-start(bf16[4,8,256]{2,1,0:T(8,128)(2,1)} %refs_0_.1), channel_id=1, source_target_pairs={{0,12},{4,8},{8,4},{12,0},{1,13},{5,9},{9,5},{13,1},{2,14},{6,10},... | collective-permute-start | bytes 49160 | tf_op jit(solution)/shard_map/ppermute | solution.py:111
  5.8 0.6 %collective-permute-start.1 = (bf16[4,8,256]{2,1,0:T(8,128)(2,1)}, bf16[4,8,256]{2,1,0:T(8,128)(2,1)S(1)}, u32[]{:S(2)}, u32[]{:S(2)}) collective-permute-start(bf16[4,8,256]{2,1,0:T(8,128)(2,1)} %refs_0_.1), channel_id=1, source_target_pairs={{0,4},{4,0},{8,12},{12,8},{1,5},{5,1},{9,13},{13,9},{2,6},{6,2},{1... | collective-permute-start | bytes 49160 | tf_op jit(solution)/shard_map/ppermute | solution.py:111
  6.4 1.0 %fetch_small.1 = (bf16[4,8,256]{2,1,0:T(8,128)(2,1)S(1)}, bf16[32,448]{1,0:T(8,128)(2,1)S(1)}, bf16[448]{0:T(512)(128)(2,1)S(1)}, bf16[448]{0:T(512)(128)(2,1)S(1)}, s32[1,48]{1,0:T(1,128)S(1)}) custom-call(bf16[4,8,256]{2,1,0:T(8,128)(2,1)} %refs_0_.1, bf16[32,448]{1,0:T(8,128)(2,1)} %refs_1_.4, bf16[448]{0:T(512)(128)(2,1)} %refs_2_.2, ...), custom_call_target="tpu_custom_call" | custom-call | bytes 94080 | tf_op jit(solution)/shard_map/fetch_small/pallas_call | solution.py:148
  7.4 0.3 collective-permute-done.2
  7.7 2.0 %collective-permute-done.1 = bf16[4,8,256]{2,1,0:T(8,128)(2,1)S(1)} collective-permute-done((bf16[4,8,256]{2,1,0:T(8,128)(2,1)}, bf16[4,8,256]{2,1,0:T(8,128)(2,1)S(1)}, u32[]{:S(2)}, u32[]{:S(2)}) %collective-permute-start.1) | collective-permute-done | bytes 16416 | tf_op jit(solution)/shard_map/ppermute | solution.py:111
  9.7 0.9 %collective-permute-done = bf16[4,8,256]{2,1,0:T(8,128)(2,1)S(1)} collective-permute-done((bf16[4,8,256]{2,1,0:T(8,128)(2,1)}, bf16[4,8,256]{2,1,0:T(8,128)(2,1)S(1)}, u32[]{:S(2)}, u32[]{:S(2)}) %collective-permute-start) | collective-permute-done | bytes 16416 | tf_op jit(solution)/shard_map/ppermute | solution.py:111
  10.7 1.1 %fusion.30 = (f32[16,4,2]{0,2,1:T(2,128)S(1)}, f32[16,4,2,1536]{3,0,2,1:T(8,128)S(1)}) fusion(bf16[16,4,2,256]{3,0,2,1:T(8,128)(2,1)S(1)} %bitcast.23, bf16[1536,4,256,1]{2,1,0,3:T(4,128)(2,1)S(1)} %bitcast.21), kind=kOutput, calls=%fused_computation.39 | convolution fusion | flops 101056384 | bytes 3998208 | tf_op jit(solution)/shard_map/tgjd,kgd->tgjk/dot_general | solution.py:218
  11.8 0.3 fusion.19
  12.1 0.7 %fusion.16 = bf16[4,2,16,256]{3,2,1,0:T(8,128)(2,1)S(1)} fusion(bf16[1536,4,256,1]{2,1,0,3:T(4,128)(2,1)S(1)} %bitcast.30, f32[16,4,2,1536]{3,0,2,1:T(8,128)S(1)} %get-tuple-element.110, f32[16,4,2]{0,2,1:T(2,128)S(1)} %get-tuple-element.66, f32[4,2,16]{2,1,0:T(2,128)S(1)} %bitcast.28), kind=kOutput, calls=%fused_computation.8 | convolution fusion | flops 101122048 | bytes 3998720 | tf_op jit(solution)/shard_map/tgjk,kgd->tgjd/dot_general | solution.py:223
  12.8 0.1 copy.34
  12.9 0.1 copy.33
  13.0 0.1 fusion.29
  13.1 1.6 %collective-permute-start.3 = (bf16[144,256]{1,0:T(8,128)(2,1)S(1)}, bf16[144,256]{1,0:T(8,128)(2,1)S(1)}, u32[]{:S(2)}, u32[]{:S(2)}) collective-permute-start(bf16[144,256]{1,0:T(8,128)(2,1)S(1)} %pad_maximum_fusion.refs_0_), channel_id=1, source_target_pairs={{0,12},{4,8},{8,4},{12,0},{1,13},{5,9},{9,5},{13,1},{2,14},{6,10},... | collective-permute-start | bytes 221192 | tf_op jit(solution)/shard_map/ppermute | solution.py:111
  14.7 0.6 %collective-permute-start.4 = (bf16[144,256]{1,0:T(8,128)(2,1)S(1)}, bf16[144,256]{1,0:T(8,128)(2,1)S(1)}, u32[]{:S(2)}, u32[]{:S(2)}) collective-permute-start(bf16[144,256]{1,0:T(8,128)(2,1)S(1)} %pad_maximum_fusion.refs_0_), channel_id=1, source_target_pairs={{0,8},{4,12},{8,0},{12,4},{1,9},{5,13},{9,1},{13,5},{2,10},{6,14},... | collective-permute-start | bytes 221192 | tf_op jit(solution)/shard_map/ppermute | solution.py:111
  15.3 2.3 %collective-permute-start.5 = (bf16[144,256]{1,0:T(8,128)(2,1)S(1)}, bf16[144,256]{1,0:T(8,128)(2,1)S(1)}, u32[]{:S(2)}, u32[]{:S(2)}) collective-permute-start(bf16[144,256]{1,0:T(8,128)(2,1)S(1)} %pad_maximum_fusion.refs_0_), channel_id=1, source_target_pairs={{0,4},{4,0},{8,12},{12,8},{1,5},{5,1},{9,13},{13,9},{2,6},{6,2},{1... | collective-permute-start | bytes 221192 | tf_op jit(solution)/shard_map/ppermute | solution.py:111
  17.5 2.8 %fetch_proj_gate.1 = (bf16[448,2048]{1,0:T(8,128)(2,1)S(1)}, bf16[1792,1792]{1,0:T(8,128)(2,1)S(1)}) custom-call(bf16[144,256]{1,0:T(8,128)(2,1)S(1)} %pad_maximum_fusion.refs_0_, bf16[448,2048]{1,0:T(8,128)(2,1)} %bitcast.22, bf16[1792,1792]{1,0:T(8,128)(2,1)} %refs_1_.5), custom_call_target="tpu_custom_call" | custom-call | bytes 16515072 | tf_op jit(solution)/shard_map/fetch_proj_gate/pallas_call | solution.py:148
  20.3 1.1 %collective-permute-done.4.refs_2_ = bf16[144,256]{1,0:T(8,128)(2,1)S(1)} collective-permute-done((bf16[144,256]{1,0:T(8,128)(2,1)S(1)}, bf16[144,256]{1,0:T(8,128)(2,1)S(1)}, u32[]{:S(2)}, u32[]{:S(2)}) %collective-permute-start.4) | collective-permute-done | bytes 73760 | tf_op jit(solution)/shard_map/ppermute | solution.py:111
  21.4 0.2 combine.1
  21.7 0.1 collective-permute-start.6
  21.8 0.6 %project_own.1 = (f32[16,448]{1,0:T(8,128)S(1)}, bf16[1792,1792]{1,0:T(8,128)(2,1)S(1)}) custom-call(bf16[16,2048]{1,0:T(8,128)(2,1)S(1)} %get-tuple-element.70.own_ref, bf16[448,2048]{1,0:T(8,128)(2,1)S(1)} %get-tuple-element.71.weight_ref, bf16[1792,1792]{1,0:T(8,128)(2,1)S(1)} %get-tuple-element.72.gate_ref), custom_call_target="tpu_custom_call", output_to_operand_aliasing={{1}: (2, {})} | custom-call | bytes 14774272 | tf_op jit(solution)/shard_map/project_own/pallas_call | solution.py:117
  22.4 0.7 %collective-permute-done.6.other_ref = bf16[16,2048]{1,0:T(8,128)(2,1)S(1)} collective-permute-done((bf16[16,2048]{1,0:T(8,128)(2,1)S(1)}, bf16[16,2048]{1,0:T(8,128)(2,1)S(1)}, u32[]{:S(2)}, u32[]{:S(2)}) %collective-permute-start.6) | collective-permute-done | bytes 65568 | tf_op jit(solution)/shard_map/ppermute | solution.py:111
  23.0 0.6 %project.1 = (bf16[32,448]{1,0:T(8,128)(2,1)S(1)}, bf16[1792,1792]{1,0:T(8,128)(2,1)S(1)}) custom-call(f32[16,448]{1,0:T(8,128)S(1)} %get-tuple-element.73.own_ref, bf16[16,2048]{1,0:T(8,128)(2,1)S(1)} %collective-permute-done.6.other_ref, bf16[448,2048]{1,0:T(8,128)(2,1)S(1)} %get-tuple-element.71.weight_ref, ...), custom_call_target="tpu_custom_call", output_to_operand_aliasing={{1}: (3, {})} | custom-call | bytes 14802944 | tf_op jit(solution)/shard_map/project/pallas_call | solution.py:117
  23.6 1.5 %collective-permute-start.7 = (bf16[32,448]{1,0:T(8,128)(2,1)S(1)}, bf16[32,448]{1,0:T(8,128)(2,1)S(1)}, u32[]{:S(2)}, u32[]{:S(2)}) collective-permute-start(bf16[32,448]{1,0:T(8,128)(2,1)S(1)} %get-tuple-element.75.refs_0_.own_ref), channel_id=1, source_target_pairs={{0,2},{2,0},{1,3},{3,1},{4,6},{6,4},{5,7},{7,5},{8,10},{10,8},{9,1... | collective-permute-start | bytes 86024 | tf_op jit(solution)/shard_map/ppermute | solution.py:111
  25.1 1.6 %fetch_gate_last.1.gate_ref = bf16[1792,1792]{1,0:T(8,128)(2,1)S(1)} custom-call(bf16[32,448]{1,0:T(8,128)(2,1)S(1)} %get-tuple-element.75.refs_0_.own_ref, bf16[1792,1792]{1,0:T(8,128)(2,1)} %refs_1_.5, bf16[1792,1792]{1,0:T(8,128)(2,1)S(1)} %get-tuple-element.76.refs_2_), custom_call_target="tpu_custom_call", output_to_operand_aliasing={{}: (2, {})} | custom-call | bytes 12845056 | tf_op jit(solution)/shard_map/fetch_gate_last/pallas_call | solution.py:148
  26.8 0.8 %collective-permute-done.7.other_ref = bf16[32,448]{1,0:T(8,128)(2,1)S(1)} collective-permute-done((bf16[32,448]{1,0:T(8,128)(2,1)S(1)}, bf16[32,448]{1,0:T(8,128)(2,1)S(1)}, u32[]{:S(2)}, u32[]{:S(2)}) %collective-permute-start.7) | collective-permute-done | bytes 28704 | tf_op jit(solution)/shard_map/ppermute | solution.py:111
  27.5 0.2 middle.1
  27.8 2.0 %collective-permute-start.8 = (bf16[32,512]{1,0:T(8,128)(2,1)S(1)}, bf16[32,512]{1,0:T(8,128)(2,1)S(1)}, u32[]{:S(2)}, u32[]{:S(2)}) collective-permute-start(bf16[32,512]{1,0:T(8,128)(2,1)S(1)} %get-tuple-element.79.refs_0_.own_ref), channel_id=1, source_target_pairs={{0,12},{2,14},{4,8},{6,10},{8,4},{10,6},{12,0},{14,2},{1,13},{3,15... | collective-permute-start | bytes 98312 | tf_op jit(solution)/shard_map/ppermute | solution.py:401
  29.8 2.8 %fetch_up.1.up_ref.refs_4_ = bf16[1792,1792]{1,0:T(8,128)(2,1)S(1)} custom-call(bf16[32,512]{1,0:T(8,128)(2,1)S(1)} %get-tuple-element.79.refs_0_.own_ref, bf16[1792,1792]{1,0:T(8,128)(2,1)} %refs_1_.6), custom_call_target="tpu_custom_call" | custom-call | bytes 12845056 | tf_op jit(solution)/shard_map/fetch_up/pallas_call | solution.py:148
  32.6 0.9 %collective-permute-done.8.far_ref = bf16[32,512]{1,0:T(8,128)(2,1)S(1)} collective-permute-done((bf16[32,512]{1,0:T(8,128)(2,1)S(1)}, bf16[32,512]{1,0:T(8,128)(2,1)S(1)}, u32[]{:S(2)}, u32[]{:S(2)}) %collective-permute-start.8) | collective-permute-done | bytes 32800 | tf_op jit(solution)/shard_map/ppermute | solution.py:401
  33.5 0.3 collective-permute-done.9.near_ref
  33.9 0.1 collective-permute-start.10
  34.0 1.2 %inner_products.1 = (f32[32,1792]{1,0:T(8,128)S(1)}, f32[32,1792]{1,0:T(8,128)S(1)}) custom-call(bf16[2,32,512]{2,1,0:T(8,128)(2,1)S(1)} %pick.1.mine_ref.refs_5_, bf16[1792,1792]{1,0:T(8,128)(2,1)S(1)} %get-tuple-element.80.gate_ref.refs_3_, bf16[1792,1792]{1,0:T(8,128)(2,1)S(1)} %fetch_up.1.up_ref.refs_4_), custom_call_target="tpu_custom_call" | custom-call | flops 205520896 | bytes 13369344 | tf_op jit(solution)/shard_map/inner_products/pallas_call | solution.py:117
  35.2 0.8 %gate_up_0.1 = (f32[32,2176]{1,0:T(8,128)S(1)}, bf16[32,2176]{1,0:T(8,128)(2,1)S(1)}) custom-call(bf16[2,32,512]{2,1,0:T(8,128)(2,1)S(1)} %collective-permute-done.10.refs_0_, f32[32,1792]{1,0:T(8,128)S(1)} %get-tuple-element.81.refs_1_, f32[32,1792]{1,0:T(8,128)S(1)} %get-tuple-element.82.refs_2_, ...), custom_call_target="tpu_custom_call" | custom-call | flops 102760448 | bytes 13852672 | tf_op jit(solution)/shard_map/gate_up_0/pallas_call | solution.py:117
  36.0 3.0 %collective-permute-start.12 = (bf16[32,2176]{1,0:T(8,128)(2,1)S(1)}, bf16[32,2176]{1,0:T(8,128)(2,1)S(1)}, u32[]{:S(2)}, u32[]{:S(2)}) collective-permute-start(bf16[32,2176]{1,0:T(8,128)(2,1)S(1)} %get-tuple-element.86), channel_id=1, source_target_pairs={{0,2},{2,0},{1,3},{3,1},{4,6},{6,4},{5,7},{7,5},{8,10},{10,8},{9,1... | collective-permute-start | bytes 417800 | tf_op jit(solution)/shard_map/ppermute | solution.py:111
  39.0 0.6 %gate_up_1.1 = (f32[32,1536]{1,0:T(8,128)S(1)}, bf16[32,1536]{1,0:T(8,128)(2,1)S(1)}) custom-call(bf16[2,32,512]{2,1,0:T(8,128)(2,1)S(1)} %collective-permute-done.10.refs_0_, f32[32,1792]{1,0:T(8,128)S(1)} %get-tuple-element.81.refs_1_, f32[32,1792]{1,0:T(8,128)S(1)} %get-tuple-element.82.refs_2_, ...), custom_call_target="tpu_custom_call" | custom-call | flops 102760448 | bytes 13664256 | tf_op jit(solution)/shard_map/gate_up_1/pallas_call | solution.py:117
  39.6 0.1 collective-permute-start.11
  39.7 2.8 %fetch_down.1.weight_ref = bf16[1792,1792]{1,0:T(8,128)(2,1)S(1)} custom-call(bf16[32,1536]{1,0:T(8,128)(2,1)S(1)} %get-tuple-element.84.refs_0_, bf16[1792,1792]{1,0:T(8,128)(2,1)} %refs_1_.7), custom_call_target="tpu_custom_call" | custom-call | bytes 12845056 | tf_op jit(solution)/shard_map/fetch_down/pallas_call | solution.py:148
  42.5 1.0 %collective-permute-done.12.other_ref.first_other_ref = bf16[32,2176]{1,0:T(8,128)(2,1)S(1)} collective-permute-done((bf16[32,2176]{1,0:T(8,128)(2,1)S(1)}, bf16[32,2176]{1,0:T(8,128)(2,1)S(1)}, u32[]{:S(2)}, u32[]{:S(2)}) %collective-permute-start.12) | collective-permute-done | bytes 139296 | tf_op jit(solution)/shard_map/ppermute | solution.py:111
  43.5 0.8 %down_first.1.part_ref = f32[32,1792]{1,0:T(8,128)S(1)} custom-call(f32[32,2176]{1,0:T(8,128)S(1)} %get-tuple-element.85.own_ref.first_ref, bf16[32,2176]{1,0:T(8,128)(2,1)S(1)} %collective-permute-done.12.other_ref.first_other_ref, bf16[1792,1792]{1,0:T(8,128)(2,1)S(1)} %fetch_down.1.weight_ref), custom_call_target="tpu_custom_call" | custom-call | flops 102760448 | bytes 7069696 | tf_op jit(solution)/shard_map/down_first/pallas_call | solution.py:117
  44.4 1.1 %collective-permute-done.11.other_ref = bf16[32,1536]{1,0:T(8,128)(2,1)S(1)} collective-permute-done((bf16[32,1536]{1,0:T(8,128)(2,1)S(1)}, bf16[32,1536]{1,0:T(8,128)(2,1)S(1)}, u32[]{:S(2)}, u32[]{:S(2)}) %collective-permute-start.11) | collective-permute-done | bytes 98336 | tf_op jit(solution)/shard_map/ppermute | solution.py:111
  45.4 0.7 %down_last.1 = (f32[16,1792]{1,0:T(8,128)S(1)}, bf16[16,1792]{1,0:T(8,128)(2,1)S(1)}) custom-call(f32[32,1536]{1,0:T(8,128)S(1)} %get-tuple-element.83.own_ref, bf16[32,1536]{1,0:T(8,128)(2,1)S(1)} %collective-permute-done.11.other_ref, f32[32,2176]{1,0:T(8,128)S(1)} %get-tuple-element.85.own_ref.first_ref, ...), custom_call_target="tpu_custom_call" | custom-call | bytes 7536640 | tf_op jit(solution)/shard_map/down_last/pallas_call | solution.py:117
  46.2 1.2 %collective-permute-done.13.back_ref = bf16[16,1792]{1,0:T(8,128)(2,1)S(1)} collective-permute-done((bf16[16,1792]{1,0:T(8,128)(2,1)S(1)}, bf16[16,1792]{1,0:T(8,128)(2,1)S(1)}, u32[]{:S(2)}, u32[]{:S(2)}) %collective-permute-start.13) | collective-permute-done | bytes 57376 | tf_op jit(solution)/shard_map/ppermute | solution.py:111
  47.5 2.3 %collective-permute-start.16 = (bf16[4,1792]{1,0:T(4,128)(2,1)S(1)}, bf16[4,1792]{1,0:T(4,128)(2,1)S(1)}, u32[]{:S(2)}, u32[]{:S(2)}) collective-permute-start(bf16[4,1792]{1,0:T(4,128)(2,1)S(1)} %get-tuple-element.92), channel_id=1, source_target_pairs={{0,12},{4,8},{8,4},{12,0},{1,13},{5,9},{9,5},{13,1},{2,14},{6,10},... | collective-permute-start | bytes 43016 | tf_op jit(solution)/shard_map/ppermute | solution.py:111
  49.8 2.1 %collective-permute-start.14 = (bf16[4,1792]{1,0:T(4,128)(2,1)S(1)}, bf16[4,1792]{1,0:T(4,128)(2,1)S(1)}, u32[]{:S(2)}, u32[]{:S(2)}) collective-permute-start(bf16[4,1792]{1,0:T(4,128)(2,1)S(1)} %get-tuple-element.90), channel_id=1, source_target_pairs={{0,4},{4,0},{8,12},{12,8},{1,5},{5,1},{9,13},{13,9},{2,6},{6,2},{1... | collective-permute-start | bytes 43016 | tf_op jit(solution)/shard_map/ppermute | solution.py:111
  52.6 0.7 %residual.1 = (bf16[32,448]{1,0:T(8,128)(2,1)}, f32[4,1]{1,0:T(4,128)S(1)}) custom-call(f32[32,448]{1,0:T(8,128)S(1)} %get-tuple-element.77.mid_ref, s32[1,1]{1,0:T(1,128)} %bitcast.20.length_ref), custom_call_target="tpu_custom_call" | custom-call | bytes 86036 | tf_op jit(solution)/shard_map/residual/pallas_call | solution.py:117
  53.3 0.1 reduce
  53.4 1.0 %collective-permute-done.15 = bf16[4,1792]{1,0:T(4,128)(2,1)S(1)} collective-permute-done((bf16[4,1792]{1,0:T(4,128)(2,1)S(1)}, bf16[4,1792]{1,0:T(4,128)(2,1)S(1)}, u32[]{:S(2)}, u32[]{:S(2)}) %collective-permute-start.15) | collective-permute-done | bytes 14368 | tf_op jit(solution)/shard_map/ppermute | solution.py:111
  54.4 0.7 %multiply_convert_fusion = bf16[4,1792]{1,0:T(4,128)(2,1)} fusion(bf16[4,1792]{1,0:T(4,128)(2,1)S(1)} %collective-permute-done.16, bf16[4,1792]{1,0:T(4,128)(2,1)S(1)} %collective-permute-done.15, f32[4,1792]{1,0:T(4,128)S(1)} %get-tuple-element.89, bf16[4,1792]{1,0:T(4,128)(2,1)S(1)} %collective-permute-done.14, f32[4]{0:T(128)S(1)} %reduce), kind=kLoop, calls=%fused_computation.15 | loop fusion | flops 57344 | bytes 86032 | tf_op jit(solution)/shard_map/convert_element_type | solution.py:564
  (26 shorter events, 0.2 us)
Async XLA Ops:
  0.6 10.0 %copy-start = (bf16[1536,4,256]{2,1,0:T(4,128)(2,1)S(1)}, bf16[1536,4,256]{2,1,0:T(4,128)(2,1)}, u32[]{:S(2)}) copy-start(bf16[1536,4,256]{2,1,0:T(4,128)(2,1)} %param.13) | copy-start | bytes 9437188
  0.6 7.0 %collective-permute-start.2 = (bf16[4,8,256]{2,1,0:T(8,128)(2,1)}, bf16[4,8,256]{2,1,0:T(8,128)(2,1)S(1)}, u32[]{:S(2)}, u32[]{:S(2)}) collective-permute-start(bf16[4,8,256]{2,1,0:T(8,128)(2,1)} %refs_0_.1), channel_id=1, source_target_pairs={{0,12},{4,8},{8,4},{12,0},{1,13},{5,9},{9,5},{13,1},{2,14},{6,10},... | collective-permute-start | bytes 49160 | tf_op jit(solution)/shard_map/ppermute | solution.py:111
  5.8 4.8 %collective-permute-start = (bf16[4,8,256]{2,1,0:T(8,128)(2,1)}, bf16[4,8,256]{2,1,0:T(8,128)(2,1)S(1)}, u32[]{:S(2)}, u32[]{:S(2)}) collective-permute-start(bf16[4,8,256]{2,1,0:T(8,128)(2,1)} %refs_0_.1), channel_id=1, source_target_pairs={{0,8},{4,12},{8,0},{12,4},{1,9},{5,13},{9,1},{13,5},{2,10},{6,14},... | collective-permute-start | bytes 49160 | tf_op jit(solution)/shard_map/ppermute | solution.py:111
  5.8 3.9 %collective-permute-start.1 = (bf16[4,8,256]{2,1,0:T(8,128)(2,1)}, bf16[4,8,256]{2,1,0:T(8,128)(2,1)S(1)}, u32[]{:S(2)}, u32[]{:S(2)}) collective-permute-start(bf16[4,8,256]{2,1,0:T(8,128)(2,1)} %refs_0_.1), channel_id=1, source_target_pairs={{0,4},{4,0},{8,12},{12,8},{1,5},{5,1},{9,13},{13,9},{2,6},{6,2},{1... | collective-permute-start | bytes 49160 | tf_op jit(solution)/shard_map/ppermute | solution.py:111
  6.4 5.7 %copy-start.1 = (bf16[1536,4,256]{2,1,0:T(4,128)(2,1)S(1)}, bf16[1536,4,256]{2,1,0:T(4,128)(2,1)}, u32[]{:S(2)}) copy-start(bf16[1536,4,256]{2,1,0:T(4,128)(2,1)} %param.14) | copy-start | bytes 9437188
  13.1 7.2 %collective-permute-start.3 = (bf16[144,256]{1,0:T(8,128)(2,1)S(1)}, bf16[144,256]{1,0:T(8,128)(2,1)S(1)}, u32[]{:S(2)}, u32[]{:S(2)}) collective-permute-start(bf16[144,256]{1,0:T(8,128)(2,1)S(1)} %pad_maximum_fusion.refs_0_), channel_id=1, source_target_pairs={{0,12},{4,8},{8,4},{12,0},{1,13},{5,9},{9,5},{13,1},{2,14},{6,10},... | collective-permute-start | bytes 221192 | tf_op jit(solution)/shard_map/ppermute | solution.py:111
  14.7 6.8 %collective-permute-start.4 = (bf16[144,256]{1,0:T(8,128)(2,1)S(1)}, bf16[144,256]{1,0:T(8,128)(2,1)S(1)}, u32[]{:S(2)}, u32[]{:S(2)}) collective-permute-start(bf16[144,256]{1,0:T(8,128)(2,1)S(1)} %pad_maximum_fusion.refs_0_), channel_id=1, source_target_pairs={{0,8},{4,12},{8,0},{12,4},{1,9},{5,13},{9,1},{13,5},{2,10},{6,14},... | collective-permute-start | bytes 221192 | tf_op jit(solution)/shard_map/ppermute | solution.py:111
  15.3 6.2 %collective-permute-start.5 = (bf16[144,256]{1,0:T(8,128)(2,1)S(1)}, bf16[144,256]{1,0:T(8,128)(2,1)S(1)}, u32[]{:S(2)}, u32[]{:S(2)}) collective-permute-start(bf16[144,256]{1,0:T(8,128)(2,1)S(1)} %pad_maximum_fusion.refs_0_), channel_id=1, source_target_pairs={{0,4},{4,0},{8,12},{12,8},{1,5},{5,1},{9,13},{13,9},{2,6},{6,2},{1... | collective-permute-start | bytes 221192 | tf_op jit(solution)/shard_map/ppermute | solution.py:111
  21.7 1.3 %collective-permute-start.6 = (bf16[16,2048]{1,0:T(8,128)(2,1)S(1)}, bf16[16,2048]{1,0:T(8,128)(2,1)S(1)}, u32[]{:S(2)}, u32[]{:S(2)}) collective-permute-start(bf16[16,2048]{1,0:T(8,128)(2,1)S(1)} %get-tuple-element.70.own_ref), channel_id=1, source_target_pairs={{0,1},{1,0},{2,3},{3,2},{4,5},{5,4},{6,7},{7,6},{8,9},{9,8},{10,11... | collective-permute-start | bytes 196616 | tf_op jit(solution)/shard_map/ppermute | solution.py:111
  23.6 3.9 %collective-permute-start.7 = (bf16[32,448]{1,0:T(8,128)(2,1)S(1)}, bf16[32,448]{1,0:T(8,128)(2,1)S(1)}, u32[]{:S(2)}, u32[]{:S(2)}) collective-permute-start(bf16[32,448]{1,0:T(8,128)(2,1)S(1)} %get-tuple-element.75.refs_0_.own_ref), channel_id=1, source_target_pairs={{0,2},{2,0},{1,3},{3,1},{4,6},{6,4},{5,7},{7,5},{8,10},{10,8},{9,1... | collective-permute-start | bytes 86024 | tf_op jit(solution)/shard_map/ppermute | solution.py:111
  27.8 5.7 %collective-permute-start.8 = (bf16[32,512]{1,0:T(8,128)(2,1)S(1)}, bf16[32,512]{1,0:T(8,128)(2,1)S(1)}, u32[]{:S(2)}, u32[]{:S(2)}) collective-permute-start(bf16[32,512]{1,0:T(8,128)(2,1)S(1)} %get-tuple-element.79.refs_0_.own_ref), channel_id=1, source_target_pairs={{0,12},{2,14},{4,8},{6,10},{8,4},{10,6},{12,0},{14,2},{1,13},{3,15... | collective-permute-start | bytes 98312 | tf_op jit(solution)/shard_map/ppermute | solution.py:401
  29.8 4.1 %collective-permute-start.9 = (bf16[32,512]{1,0:T(8,128)(2,1)S(1)}, bf16[32,512]{1,0:T(8,128)(2,1)S(1)}, u32[]{:S(2)}, u32[]{:S(2)}) collective-permute-start(bf16[32,512]{1,0:T(8,128)(2,1)S(1)} %get-tuple-element.79.refs_0_.own_ref), channel_id=1, source_target_pairs={{0,4},{2,8},{4,0},{6,12},{8,2},{10,14},{12,6},{14,10},{1,5},{3,9},... | collective-permute-start | bytes 98312 | tf_op jit(solution)/shard_map/ppermute | solution.py:400
  33.9 1.3 %collective-permute-start.10 = (bf16[2,32,512]{2,1,0:T(8,128)(2,1)S(1)}, bf16[2,32,512]{2,1,0:T(8,128)(2,1)S(1)}, u32[]{:S(2)}, u32[]{:S(2)}) collective-permute-start(bf16[2,32,512]{2,1,0:T(8,128)(2,1)S(1)} %pick.1.mine_ref.refs_5_), channel_id=1, source_target_pairs={{0,1},{1,0},{2,3},{3,2},{4,5},{5,4},{6,7},{7,6},{8,9},{9,8},{10,11... | collective-permute-start | bytes 196616 | tf_op jit(solution)/shard_map/ppermute | solution.py:111
  36.0 7.6 %collective-permute-start.12 = (bf16[32,2176]{1,0:T(8,128)(2,1)S(1)}, bf16[32,2176]{1,0:T(8,128)(2,1)S(1)}, u32[]{:S(2)}, u32[]{:S(2)}) collective-permute-start(bf16[32,2176]{1,0:T(8,128)(2,1)S(1)} %get-tuple-element.86), channel_id=1, source_target_pairs={{0,2},{2,0},{1,3},{3,1},{4,6},{6,4},{5,7},{7,5},{8,10},{10,8},{9,1... | collective-permute-start | bytes 417800 | tf_op jit(solution)/shard_map/ppermute | solution.py:111
  39.6 5.8 %collective-permute-start.11 = (bf16[32,1536]{1,0:T(8,128)(2,1)S(1)}, bf16[32,1536]{1,0:T(8,128)(2,1)S(1)}, u32[]{:S(2)}, u32[]{:S(2)}) collective-permute-start(bf16[32,1536]{1,0:T(8,128)(2,1)S(1)} %get-tuple-element.84.refs_0_), channel_id=1, source_target_pairs={{0,2},{2,0},{1,3},{3,1},{4,6},{6,4},{5,7},{7,5},{8,10},{10,8},{9,1... | collective-permute-start | bytes 294920 | tf_op jit(solution)/shard_map/ppermute | solution.py:111
  46.2 1.3 %collective-permute-start.13 = (bf16[16,1792]{1,0:T(8,128)(2,1)S(1)}, bf16[16,1792]{1,0:T(8,128)(2,1)S(1)}, u32[]{:S(2)}, u32[]{:S(2)}) collective-permute-start(bf16[16,1792]{1,0:T(8,128)(2,1)S(1)} %get-tuple-element.88), channel_id=1, source_target_pairs={{0,1},{1,0},{2,3},{3,2},{4,5},{5,4},{6,7},{7,6},{8,9},{9,8},{10,11... | collective-permute-start | bytes 172040 | tf_op jit(solution)/shard_map/ppermute | solution.py:111
  47.5 5.9 %collective-permute-start.16 = (bf16[4,1792]{1,0:T(4,128)(2,1)S(1)}, bf16[4,1792]{1,0:T(4,128)(2,1)S(1)}, u32[]{:S(2)}, u32[]{:S(2)}) collective-permute-start(bf16[4,1792]{1,0:T(4,128)(2,1)S(1)} %get-tuple-element.92), channel_id=1, source_target_pairs={{0,12},{4,8},{8,4},{12,0},{1,13},{5,9},{9,5},{13,1},{2,14},{6,10},... | collective-permute-start | bytes 43016 | tf_op jit(solution)/shard_map/ppermute | solution.py:111
  49.8 4.6 %collective-permute-start.15 = (bf16[4,1792]{1,0:T(4,128)(2,1)S(1)}, bf16[4,1792]{1,0:T(4,128)(2,1)S(1)}, u32[]{:S(2)}, u32[]{:S(2)}) collective-permute-start(bf16[4,1792]{1,0:T(4,128)(2,1)S(1)} %get-tuple-element.91), channel_id=1, source_target_pairs={{0,8},{4,12},{8,0},{12,4},{1,9},{5,13},{9,1},{13,5},{2,10},{6,14},... | collective-permute-start | bytes 43016 | tf_op jit(solution)/shard_map/ppermute | solution.py:111
  49.8 4.6 %collective-permute-start.14 = (bf16[4,1792]{1,0:T(4,128)(2,1)S(1)}, bf16[4,1792]{1,0:T(4,128)(2,1)S(1)}, u32[]{:S(2)}, u32[]{:S(2)}) collective-permute-start(bf16[4,1792]{1,0:T(4,128)(2,1)S(1)} %get-tuple-element.90), channel_id=1, source_target_pairs={{0,4},{4,0},{8,12},{12,8},{1,5},{5,1},{9,13},{13,9},{2,6},{6,2},{1... | collective-permute-start | bytes 43016 | tf_op jit(solution)/shard_map/ppermute | solution.py:111

commit v9 on v8

--- a/solution.py
+++ b/solution.py
@@ -395,14 +395,14 @@
     for b in range(blks):
         for h in range(head_parts):
             far_pairs.append((b * head_parts + h, (b ^ 3) * head_parts + h))
-            to = (b ^ 1, h) if b // half == h else (b ^ 2, 1 - h)
+            to = (b ^ 2, h) if b // half == h else (b ^ 1, 1 - h)
             near_pairs.append((b * head_parts + h, to[0] * head_parts + to[1]))
     near = lax.ppermute(note, ("blk", "heads"), near_pairs)
     far = lax.ppermute(note, ("blk", "heads"), far_pairs)
     (up_near,) = fetch([note], [up_weight], "fetch_up")
     lanes_all = note.shape[1]
 
-    def pick(own_ref, far_ref, near_ref, gate_ref, up_ref, out_ref):
+    def pick(own_ref, near_ref, far_ref, gate_ref, up_ref, kept_ref, out_ref):
         at = lax.axis_index("blk")
         inside = at // half == lax.axis_index("heads")
         odd = at % 2 == 1
@@ -415,8 +415,8 @@
         pick,
         "pick",
         [sds((half, tokens, lanes_all), BF)],
-        [VM, VM, VM, ANY, ANY],
-        [note, far, near, gate_near, up_near],
+        [VM, VM, VM, ANY, ANY, ANY],
+        [note, near, far, gate_near, up_near, keep_own],
     )
     theirs = hop(mine, "rows", 2, 1)
     rows_in = gate_weight.shape[0]

time: 55.3 us -> 54.5 us (0.986)
  waiting for transfers between devices: 11.3 us -> 10.6 us
    ppermute x15, starting transfers between devices: 19.5 us -> 18.5 us  [hop(): return lax.ppermute(value, axis, [(i, i ^ step) for i in range(size)])]
    ppermute x1, waiting for transfers between devices: 0.88 us -> 0.01 us  [shards_direct(): far = lax.ppermute(note, ('blk', 'heads'), far_pairs)]
  transfers between devices with their start and end apart: 17 -> 17, of which waited for: 12 -> 12; matrix products, arithmetic and copies ran while one was open for 0% -> 0% of each run, Pallas kernels for 27% -> 28%
where the time goes in v9:
time: 54.5 us; the launch traced here: 54.3 us
  starting transfers between devices  21.4 us (39%)
  Pallas kernels  17.6 us (32%)
  waiting for transfers between devices  10.6 us (19%)
  matrix products  1.82 us (3%)
  between operations  1.47 us (3%)
  other arithmetic  1.2 us (2%)
    ppermute x15, starting transfers between devices, hop(): return lax.ppermute(value, axis, [(i, i ^ step) for i in range(size)])  18.5 us
    pallas_call x5, Pallas kernels, fetch(): pl.pallas_call(body, out_shape=[jax.ShapeDtypeStruct(a.shape, a.dtype) fo...  11 us
    ppermute x15, waiting for transfers between devices, hop(): return lax.ppermute(value, axis, [(i, i ^ step) for i in range(size)])  10.6 us
    pallas_call x12, Pallas kernels, kernel(): pl.pallas_call(body, out_shape=outs, in_specs=specs, out_specs=[VM] * len...  6.6 us
    ppermute x1, starting transfers between devices, shards_direct(): far = lax.ppermute(note, ('blk', 'heads'), far_pairs)  2.39 us
    dot_general x1, matrix products, shards_direct(): jnp.einsum('tgjd,kgd->tgjk', grouped, src_keys, preferred_element_type=F32)  1.13 us
  transfers between devices with their start and end apart: 17, of which 12 were waited for; matrix products, arithmetic and copies ran while one was open for 0% of the time, Pallas kernels for 28%

profile of v9, /device:TPU:0, one launch (start us, length us, event | category | flops | bytes accessed | tf_op | source)
XLA Modules:
  0.0 54.3 jit_solution(2647242823635117711)
XLA Ops:
  0.6 5.1 %collective-permute-start.2 = (bf16[4,8,256]{2,1,0:T(8,128)(2,1)}, bf16[4,8,256]{2,1,0:T(8,128)(2,1)S(1)}, u32[]{:S(2)}, u32[]{:S(2)}) collective-permute-start(bf16[4,8,256]{2,1,0:T(8,128)(2,1)} %refs_0_.1), channel_id=1, source_target_pairs={{0,12},{4,8},{8,4},{12,0},{1,13},{5,9},{9,5},{13,1},{2,14},{6,10},... | collective-permute-start | bytes 49160 | tf_op jit(solution)/shard_map/ppermute | solution.py:111
  5.8 0.6 %collective-permute-start.1 = (bf16[4,8,256]{2,1,0:T(8,128)(2,1)}, bf16[4,8,256]{2,1,0:T(8,128)(2,1)S(1)}, u32[]{:S(2)}, u32[]{:S(2)}) collective-permute-start(bf16[4,8,256]{2,1,0:T(8,128)(2,1)} %refs_0_.1), channel_id=1, source_target_pairs={{0,4},{4,0},{8,12},{12,8},{1,5},{5,1},{9,13},{13,9},{2,6},{6,2},{1... | collective-permute-start | bytes 49160 | tf_op jit(solution)/shard_map/ppermute | solution.py:111
  6.4 1.0 %fetch_small.1 = (bf16[4,8,256]{2,1,0:T(8,128)(2,1)S(1)}, bf16[32,448]{1,0:T(8,128)(2,1)S(1)}, bf16[448]{0:T(512)(128)(2,1)S(1)}, bf16[448]{0:T(512)(128)(2,1)S(1)}, s32[1,48]{1,0:T(1,128)S(1)}) custom-call(bf16[4,8,256]{2,1,0:T(8,128)(2,1)} %refs_0_.1, bf16[32,448]{1,0:T(8,128)(2,1)} %refs_1_.4, bf16[448]{0:T(512)(128)(2,1)} %refs_2_.2, ...), custom_call_target="tpu_custom_call" | custom-call | bytes 94080 | tf_op jit(solution)/shard_map/fetch_small/pallas_call | solution.py:148
  7.4 0.3 collective-permute-done.2
  7.7 2.0 %collective-permute-done.1 = bf16[4,8,256]{2,1,0:T(8,128)(2,1)S(1)} collective-permute-done((bf16[4,8,256]{2,1,0:T(8,128)(2,1)}, bf16[4,8,256]{2,1,0:T(8,128)(2,1)S(1)}, u32[]{:S(2)}, u32[]{:S(2)}) %collective-permute-start.1) | collective-permute-done | bytes 16416 | tf_op jit(solution)/shard_map/ppermute | solution.py:111
  9.7 0.9 %collective-permute-done = bf16[4,8,256]{2,1,0:T(8,128)(2,1)S(1)} collective-permute-done((bf16[4,8,256]{2,1,0:T(8,128)(2,1)}, bf16[4,8,256]{2,1,0:T(8,128)(2,1)S(1)}, u32[]{:S(2)}, u32[]{:S(2)}) %collective-permute-start) | collective-permute-done | bytes 16416 | tf_op jit(solution)/shard_map/ppermute | solution.py:111
  10.7 1.1 %fusion.30 = (f32[16,4,2]{0,2,1:T(2,128)S(1)}, f32[16,4,2,1536]{3,0,2,1:T(8,128)S(1)}) fusion(bf16[16,4,2,256]{3,0,2,1:T(8,128)(2,1)S(1)} %bitcast.23, bf16[1536,4,256,1]{2,1,0,3:T(4,128)(2,1)S(1)} %bitcast.21), kind=kOutput, calls=%fused_computation.39 | convolution fusion | flops 101056384 | bytes 3998208 | tf_op jit(solution)/shard_map/tgjd,kgd->tgjk/dot_general | solution.py:218
  11.8 0.3 fusion.19
  12.1 0.7 %fusion.16 = bf16[4,2,16,256]{3,2,1,0:T(8,128)(2,1)S(1)} fusion(bf16[1536,4,256,1]{2,1,0,3:T(4,128)(2,1)S(1)} %bitcast.30, f32[16,4,2,1536]{3,0,2,1:T(8,128)S(1)} %get-tuple-element.110, f32[16,4,2]{0,2,1:T(2,128)S(1)} %get-tuple-element.66, f32[4,2,16]{2,1,0:T(2,128)S(1)} %bitcast.28), kind=kOutput, calls=%fused_computation.8 | convolution fusion | flops 101122048 | bytes 3998720 | tf_op jit(solution)/shard_map/tgjk,kgd->tgjd/dot_general | solution.py:223
  12.8 0.1 copy.34
  12.9 0.1 copy.33
  13.0 0.1 fusion.29
  13.1 1.6 %collective-permute-start.3 = (bf16[144,256]{1,0:T(8,128)(2,1)S(1)}, bf16[144,256]{1,0:T(8,128)(2,1)S(1)}, u32[]{:S(2)}, u32[]{:S(2)}) collective-permute-start(bf16[144,256]{1,0:T(8,128)(2,1)S(1)} %pad_maximum_fusion.refs_0_), channel_id=1, source_target_pairs={{0,12},{4,8},{8,4},{12,0},{1,13},{5,9},{9,5},{13,1},{2,14},{6,10},... | collective-permute-start | bytes 221192 | tf_op jit(solution)/shard_map/ppermute | solution.py:111
  14.7 0.6 %collective-permute-start.4 = (bf16[144,256]{1,0:T(8,128)(2,1)S(1)}, bf16[144,256]{1,0:T(8,128)(2,1)S(1)}, u32[]{:S(2)}, u32[]{:S(2)}) collective-permute-start(bf16[144,256]{1,0:T(8,128)(2,1)S(1)} %pad_maximum_fusion.refs_0_), channel_id=1, source_target_pairs={{0,8},{4,12},{8,0},{12,4},{1,9},{5,13},{9,1},{13,5},{2,10},{6,14},... | collective-permute-start | bytes 221192 | tf_op jit(solution)/shard_map/ppermute | solution.py:111
  15.3 2.3 %collective-permute-start.5 = (bf16[144,256]{1,0:T(8,128)(2,1)S(1)}, bf16[144,256]{1,0:T(8,128)(2,1)S(1)}, u32[]{:S(2)}, u32[]{:S(2)}) collective-permute-start(bf16[144,256]{1,0:T(8,128)(2,1)S(1)} %pad_maximum_fusion.refs_0_), channel_id=1, source_target_pairs={{0,4},{4,0},{8,12},{12,8},{1,5},{5,1},{9,13},{13,9},{2,6},{6,2},{1... | collective-permute-start | bytes 221192 | tf_op jit(solution)/shard_map/ppermute | solution.py:111
  17.5 2.8 %fetch_proj_gate.1 = (bf16[448,2048]{1,0:T(8,128)(2,1)S(1)}, bf16[1792,1792]{1,0:T(8,128)(2,1)S(1)}) custom-call(bf16[144,256]{1,0:T(8,128)(2,1)S(1)} %pad_maximum_fusion.refs_0_, bf16[448,2048]{1,0:T(8,128)(2,1)} %bitcast.22, bf16[1792,1792]{1,0:T(8,128)(2,1)} %refs_1_.5), custom_call_target="tpu_custom_call" | custom-call | bytes 16515072 | tf_op jit(solution)/shard_map/fetch_proj_gate/pallas_call | solution.py:148
  20.3 1.1 %collective-permute-done.4.refs_2_ = bf16[144,256]{1,0:T(8,128)(2,1)S(1)} collective-permute-done((bf16[144,256]{1,0:T(8,128)(2,1)S(1)}, bf16[144,256]{1,0:T(8,128)(2,1)S(1)}, u32[]{:S(2)}, u32[]{:S(2)}) %collective-permute-start.4) | collective-permute-done | bytes 73760 | tf_op jit(solution)/shard_map/ppermute | solution.py:111
  21.4 0.2 combine.1
  21.8 0.6 %project_own.1 = (f32[16,448]{1,0:T(8,128)S(1)}, bf16[1792,1792]{1,0:T(8,128)(2,1)S(1)}) custom-call(bf16[16,2048]{1,0:T(8,128)(2,1)S(1)} %get-tuple-element.70.own_ref, bf16[448,2048]{1,0:T(8,128)(2,1)S(1)} %get-tuple-element.71.weight_ref, bf16[1792,1792]{1,0:T(8,128)(2,1)S(1)} %get-tuple-element.72.gate_ref), custom_call_target="tpu_custom_call", output_to_operand_aliasing={{1}: (2, {})} | custom-call | bytes 14774272 | tf_op jit(solution)/shard_map/project_own/pallas_call | solution.py:117
  22.4 0.7 %collective-permute-done.6.other_ref = bf16[16,2048]{1,0:T(8,128)(2,1)S(1)} collective-permute-done((bf16[16,2048]{1,0:T(8,128)(2,1)S(1)}, bf16[16,2048]{1,0:T(8,128)(2,1)S(1)}, u32[]{:S(2)}, u32[]{:S(2)}) %collective-permute-start.6) | collective-permute-done | bytes 65568 | tf_op jit(solution)/shard_map/ppermute | solution.py:111
  23.0 0.6 %project.1 = (bf16[32,448]{1,0:T(8,128)(2,1)S(1)}, bf16[1792,1792]{1,0:T(8,128)(2,1)S(1)}) custom-call(f32[16,448]{1,0:T(8,128)S(1)} %get-tuple-element.73.own_ref, bf16[16,2048]{1,0:T(8,128)(2,1)S(1)} %collective-permute-done.6.other_ref, bf16[448,2048]{1,0:T(8,128)(2,1)S(1)} %get-tuple-element.71.weight_ref, ...), custom_call_target="tpu_custom_call", output_to_operand_aliasing={{1}: (3, {})} | custom-call | bytes 14802944 | tf_op jit(solution)/shard_map/project/pallas_call | solution.py:117
  23.6 1.5 %collective-permute-start.7 = (bf16[32,448]{1,0:T(8,128)(2,1)S(1)}, bf16[32,448]{1,0:T(8,128)(2,1)S(1)}, u32[]{:S(2)}, u32[]{:S(2)}) collective-permute-start(bf16[32,448]{1,0:T(8,128)(2,1)S(1)} %get-tuple-element.75.refs_0_.own_ref), channel_id=1, source_target_pairs={{0,2},{2,0},{1,3},{3,1},{4,6},{6,4},{5,7},{7,5},{8,10},{10,8},{9,1... | collective-permute-start | bytes 86024 | tf_op jit(solution)/shard_map/ppermute | solution.py:111
  25.1 1.6 %fetch_gate_last.1.gate_ref = bf16[1792,1792]{1,0:T(8,128)(2,1)S(1)} custom-call(bf16[32,448]{1,0:T(8,128)(2,1)S(1)} %get-tuple-element.75.refs_0_.own_ref, bf16[1792,1792]{1,0:T(8,128)(2,1)} %refs_1_.5, bf16[1792,1792]{1,0:T(8,128)(2,1)S(1)} %get-tuple-element.76.refs_2_), custom_call_target="tpu_custom_call", output_to_operand_aliasing={{}: (2, {})} | custom-call | bytes 12845056 | tf_op jit(solution)/shard_map/fetch_gate_last/pallas_call | solution.py:148
  26.8 0.8 %collective-permute-done.7.other_ref = bf16[32,448]{1,0:T(8,128)(2,1)S(1)} collective-permute-done((bf16[32,448]{1,0:T(8,128)(2,1)S(1)}, bf16[32,448]{1,0:T(8,128)(2,1)S(1)}, u32[]{:S(2)}, u32[]{:S(2)}) %collective-permute-start.7) | collective-permute-done | bytes 28704 | tf_op jit(solution)/shard_map/ppermute | solution.py:111
  27.5 0.2 middle.1
  27.8 0.5 collective-permute-start.8
  28.3 2.4 %collective-permute-start.9 = (bf16[32,512]{1,0:T(8,128)(2,1)S(1)}, bf16[32,512]{1,0:T(8,128)(2,1)S(1)}, u32[]{:S(2)}, u32[]{:S(2)}) collective-permute-start(bf16[32,512]{1,0:T(8,128)(2,1)S(1)} %get-tuple-element.79.refs_0_.own_ref), channel_id=1, source_target_pairs={{0,12},{2,14},{4,8},{6,10},{8,4},{10,6},{12,0},{14,2},{1,13},{3,15... | collective-permute-start | bytes 98312 | tf_op jit(solution)/shard_map/ppermute | solution.py:401
  31.3 2.8 %fetch_up.1.up_ref.refs_4_ = bf16[1792,1792]{1,0:T(8,128)(2,1)S(1)} custom-call(bf16[32,512]{1,0:T(8,128)(2,1)S(1)} %get-tuple-element.79.refs_0_.own_ref, bf16[1792,1792]{1,0:T(8,128)(2,1)} %refs_1_.6), custom_call_target="tpu_custom_call" | custom-call | bytes 12845056 | tf_op jit(solution)/shard_map/fetch_up/pallas_call | solution.py:148
  34.2 0.7 %residual.1 = (bf16[32,448]{1,0:T(8,128)(2,1)}, f32[4,1]{1,0:T(4,128)S(1)}) custom-call(f32[32,448]{1,0:T(8,128)S(1)} %get-tuple-element.77.mid_ref, s32[1,1]{1,0:T(1,128)} %bitcast.20.length_ref), custom_call_target="tpu_custom_call" | custom-call | bytes 86036 | tf_op jit(solution)/shard_map/residual/pallas_call | solution.py:117
  35.0 1.2 %inner_products.1 = (f32[32,1792]{1,0:T(8,128)S(1)}, f32[32,1792]{1,0:T(8,128)S(1)}) custom-call(bf16[2,32,512]{2,1,0:T(8,128)(2,1)S(1)} %pick.1.mine_ref.refs_5_, bf16[1792,1792]{1,0:T(8,128)(2,1)S(1)} %get-tuple-element.80.gate_ref.refs_3_, bf16[1792,1792]{1,0:T(8,128)(2,1)S(1)} %fetch_up.1.up_ref.refs_4_), custom_call_target="tpu_custom_call" | custom-call | flops 205520896 | bytes 13369344 | tf_op jit(solution)/shard_map/inner_products/pallas_call | solution.py:117
  36.2 0.8 %gate_up_0.1 = (f32[32,2176]{1,0:T(8,128)S(1)}, bf16[32,2176]{1,0:T(8,128)(2,1)S(1)}) custom-call(bf16[2,32,512]{2,1,0:T(8,128)(2,1)S(1)} %collective-permute-done.10.refs_0_, f32[32,1792]{1,0:T(8,128)S(1)} %get-tuple-element.82.refs_1_, f32[32,1792]{1,0:T(8,128)S(1)} %get-tuple-element.83.refs_2_, ...), custom_call_target="tpu_custom_call" | custom-call | flops 102760448 | bytes 13852672 | tf_op jit(solution)/shard_map/gate_up_0/pallas_call | solution.py:117
  37.0 1.5 %collective-permute-start.12 = (bf16[32,2176]{1,0:T(8,128)(2,1)S(1)}, bf16[32,2176]{1,0:T(8,128)(2,1)S(1)}, u32[]{:S(2)}, u32[]{:S(2)}) collective-permute-start(bf16[32,2176]{1,0:T(8,128)(2,1)S(1)} %get-tuple-element.87), channel_id=1, source_target_pairs={{0,2},{2,0},{1,3},{3,1},{4,6},{6,4},{5,7},{7,5},{8,10},{10,8},{9,1... | collective-permute-start | bytes 417800 | tf_op jit(solution)/shard_map/ppermute | solution.py:111
  38.4 0.6 %gate_up_1.1 = (f32[32,1536]{1,0:T(8,128)S(1)}, bf16[32,1536]{1,0:T(8,128)(2,1)S(1)}) custom-call(bf16[2,32,512]{2,1,0:T(8,128)(2,1)S(1)} %collective-permute-done.10.refs_0_, f32[32,1792]{1,0:T(8,128)S(1)} %get-tuple-element.82.refs_1_, f32[32,1792]{1,0:T(8,128)S(1)} %get-tuple-element.83.refs_2_, ...), custom_call_target="tpu_custom_call" | custom-call | flops 102760448 | bytes 13664256 | tf_op jit(solution)/shard_map/gate_up_1/pallas_call | solution.py:117
  39.0 0.7 %collective-permute-start.11 = (bf16[32,1536]{1,0:T(8,128)(2,1)S(1)}, bf16[32,1536]{1,0:T(8,128)(2,1)S(1)}, u32[]{:S(2)}, u32[]{:S(2)}) collective-permute-start(bf16[32,1536]{1,0:T(8,128)(2,1)S(1)} %get-tuple-element.85.refs_0_), channel_id=1, source_target_pairs={{0,2},{2,0},{1,3},{3,1},{4,6},{6,4},{5,7},{7,5},{8,10},{10,8},{9,1... | collective-permute-start | bytes 294920 | tf_op jit(solution)/shard_map/ppermute | solution.py:111
  39.7 2.8 %fetch_down.1.weight_ref = bf16[1792,1792]{1,0:T(8,128)(2,1)S(1)} custom-call(bf16[32,1536]{1,0:T(8,128)(2,1)S(1)} %get-tuple-element.85.refs_0_, bf16[1792,1792]{1,0:T(8,128)(2,1)} %refs_1_.7), custom_call_target="tpu_custom_call" | custom-call | bytes 12845056 | tf_op jit(solution)/shard_map/fetch_down/pallas_call | solution.py:148
  42.6 0.9 %collective-permute-done.12.other_ref.first_other_ref = bf16[32,2176]{1,0:T(8,128)(2,1)S(1)} collective-permute-done((bf16[32,2176]{1,0:T(8,128)(2,1)S(1)}, bf16[32,2176]{1,0:T(8,128)(2,1)S(1)}, u32[]{:S(2)}, u32[]{:S(2)}) %collective-permute-start.12) | collective-permute-done | bytes 139296 | tf_op jit(solution)/shard_map/ppermute | solution.py:111
  43.5 0.8 %down_first.1.part_ref = f32[32,1792]{1,0:T(8,128)S(1)} custom-call(f32[32,2176]{1,0:T(8,128)S(1)} %get-tuple-element.86.own_ref.first_ref, bf16[32,2176]{1,0:T(8,128)(2,1)S(1)} %collective-permute-done.12.other_ref.first_other_ref, bf16[1792,1792]{1,0:T(8,128)(2,1)S(1)} %fetch_down.1.weight_ref), custom_call_target="tpu_custom_call" | custom-call | flops 102760448 | bytes 7069696 | tf_op jit(solution)/shard_map/down_first/pallas_call | solution.py:117
  44.4 0.9 %collective-permute-done.11.other_ref = bf16[32,1536]{1,0:T(8,128)(2,1)S(1)} collective-permute-done((bf16[32,1536]{1,0:T(8,128)(2,1)S(1)}, bf16[32,1536]{1,0:T(8,128)(2,1)S(1)}, u32[]{:S(2)}, u32[]{:S(2)}) %collective-permute-start.11) | collective-permute-done | bytes 98336 | tf_op jit(solution)/shard_map/ppermute | solution.py:111
  45.2 0.7 %down_last.1 = (f32[16,1792]{1,0:T(8,128)S(1)}, bf16[16,1792]{1,0:T(8,128)(2,1)S(1)}) custom-call(f32[32,1536]{1,0:T(8,128)S(1)} %get-tuple-element.84.own_ref, bf16[32,1536]{1,0:T(8,128)(2,1)S(1)} %collective-permute-done.11.other_ref, f32[32,2176]{1,0:T(8,128)S(1)} %get-tuple-element.86.own_ref.first_ref, ...), custom_call_target="tpu_custom_call" | custom-call | bytes 7536640 | tf_op jit(solution)/shard_map/down_last/pallas_call | solution.py:117
  46.0 1.2 %collective-permute-done.13.back_ref = bf16[16,1792]{1,0:T(8,128)(2,1)S(1)} collective-permute-done((bf16[16,1792]{1,0:T(8,128)(2,1)S(1)}, bf16[16,1792]{1,0:T(8,128)(2,1)S(1)}, u32[]{:S(2)}, u32[]{:S(2)}) %collective-permute-start.13) | collective-permute-done | bytes 57376 | tf_op jit(solution)/shard_map/ppermute | solution.py:111
  47.3 1.6 %collective-permute-start.16 = (bf16[4,1792]{1,0:T(4,128)(2,1)S(1)}, bf16[4,1792]{1,0:T(4,128)(2,1)S(1)}, u32[]{:S(2)}, u32[]{:S(2)}) collective-permute-start(bf16[4,1792]{1,0:T(4,128)(2,1)S(1)} %get-tuple-element.93), channel_id=1, source_target_pairs={{0,12},{4,8},{8,4},{12,0},{1,13},{5,9},{9,5},{13,1},{2,14},{6,10},... | collective-permute-start | bytes 43016 | tf_op jit(solution)/shard_map/ppermute | solution.py:111
  48.8 1.0 %collective-permute-start.15 = (bf16[4,1792]{1,0:T(4,128)(2,1)S(1)}, bf16[4,1792]{1,0:T(4,128)(2,1)S(1)}, u32[]{:S(2)}, u32[]{:S(2)}) collective-permute-start(bf16[4,1792]{1,0:T(4,128)(2,1)S(1)} %get-tuple-element.92), channel_id=1, source_target_pairs={{0,8},{4,12},{8,0},{12,4},{1,9},{5,13},{9,1},{13,5},{2,10},{6,14},... | collective-permute-start | bytes 43016 | tf_op jit(solution)/shard_map/ppermute | solution.py:111
  49.8 1.9 %collective-permute-start.14 = (bf16[4,1792]{1,0:T(4,128)(2,1)S(1)}, bf16[4,1792]{1,0:T(4,128)(2,1)S(1)}, u32[]{:S(2)}, u32[]{:S(2)}) collective-permute-start(bf16[4,1792]{1,0:T(4,128)(2,1)S(1)} %get-tuple-element.91), channel_id=1, source_target_pairs={{0,4},{4,0},{8,12},{12,8},{1,5},{5,1},{9,13},{13,9},{2,6},{6,2},{1... | collective-permute-start | bytes 43016 | tf_op jit(solution)/shard_map/ppermute | solution.py:111
  51.7 0.1 reduce
  51.9 1.0 %collective-permute-done.16 = bf16[4,1792]{1,0:T(4,128)(2,1)S(1)} collective-permute-done((bf16[4,1792]{1,0:T(4,128)(2,1)S(1)}, bf16[4,1792]{1,0:T(4,128)(2,1)S(1)}, u32[]{:S(2)}, u32[]{:S(2)}) %collective-permute-start.16) | collective-permute-done | bytes 14368 | tf_op jit(solution)/shard_map/ppermute | solution.py:111
  52.9 0.6 %collective-permute-done.15 = bf16[4,1792]{1,0:T(4,128)(2,1)S(1)} collective-permute-done((bf16[4,1792]{1,0:T(4,128)(2,1)S(1)}, bf16[4,1792]{1,0:T(4,128)(2,1)S(1)}, u32[]{:S(2)}, u32[]{:S(2)}) %collective-permute-start.15) | collective-permute-done | bytes 14368 | tf_op jit(solution)/shard_map/ppermute | solution.py:111
  53.5 0.1 collective-permute-done.14
  53.6 0.7 %multiply_convert_fusion = bf16[4,1792]{1,0:T(4,128)(2,1)} fusion(bf16[4,1792]{1,0:T(4,128)(2,1)S(1)} %collective-permute-done.16, bf16[4,1792]{1,0:T(4,128)(2,1)S(1)} %collective-permute-done.15, f32[4,1792]{1,0:T(4,128)S(1)} %get-tuple-element.90, bf16[4,1792]{1,0:T(4,128)(2,1)S(1)} %collective-permute-done.14, f32[4]{0:T(128)S(1)} %reduce), kind=kLoop, calls=%fused_computation.15 | loop fusion | flops 57344 | bytes 86032 | tf_op jit(solution)/shard_map/convert_element_type | solution.py:564
  (26 shorter events, 0.4 us)
Async XLA Ops:
  0.6 10.0 %copy-start = (bf16[1536,4,256]{2,1,0:T(4,128)(2,1)S(1)}, bf16[1536,4,256]{2,1,0:T(4,128)(2,1)}, u32[]{:S(2)}) copy-start(bf16[1536,4,256]{2,1,0:T(4,128)(2,1)} %param.13) | copy-start | bytes 9437188
  0.6 7.0 %collective-permute-start.2 = (bf16[4,8,256]{2,1,0:T(8,128)(2,1)}, bf16[4,8,256]{2,1,0:T(8,128)(2,1)S(1)}, u32[]{:S(2)}, u32[]{:S(2)}) collective-permute-start(bf16[4,8,256]{2,1,0:T(8,128)(2,1)} %refs_0_.1), channel_id=1, source_target_pairs={{0,12},{4,8},{8,4},{12,0},{1,13},{5,9},{9,5},{13,1},{2,14},{6,10},... | collective-permute-start | bytes 49160 | tf_op jit(solution)/shard_map/ppermute | solution.py:111
  5.8 4.8 %collective-permute-start = (bf16[4,8,256]{2,1,0:T(8,128)(2,1)}, bf16[4,8,256]{2,1,0:T(8,128)(2,1)S(1)}, u32[]{:S(2)}, u32[]{:S(2)}) collective-permute-start(bf16[4,8,256]{2,1,0:T(8,128)(2,1)} %refs_0_.1), channel_id=1, source_target_pairs={{0,8},{4,12},{8,0},{12,4},{1,9},{5,13},{9,1},{13,5},{2,10},{6,14},... | collective-permute-start | bytes 49160 | tf_op jit(solution)/shard_map/ppermute | solution.py:111
  5.8 3.9 %collective-permute-start.1 = (bf16[4,8,256]{2,1,0:T(8,128)(2,1)}, bf16[4,8,256]{2,1,0:T(8,128)(2,1)S(1)}, u32[]{:S(2)}, u32[]{:S(2)}) collective-permute-start(bf16[4,8,256]{2,1,0:T(8,128)(2,1)} %refs_0_.1), channel_id=1, source_target_pairs={{0,4},{4,0},{8,12},{12,8},{1,5},{5,1},{9,13},{13,9},{2,6},{6,2},{1... | collective-permute-start | bytes 49160 | tf_op jit(solution)/shard_map/ppermute | solution.py:111
  6.4 5.7 %copy-start.1 = (bf16[1536,4,256]{2,1,0:T(4,128)(2,1)S(1)}, bf16[1536,4,256]{2,1,0:T(4,128)(2,1)}, u32[]{:S(2)}) copy-start(bf16[1536,4,256]{2,1,0:T(4,128)(2,1)} %param.14) | copy-start | bytes 9437188
  13.1 7.2 %collective-permute-start.3 = (bf16[144,256]{1,0:T(8,128)(2,1)S(1)}, bf16[144,256]{1,0:T(8,128)(2,1)S(1)}, u32[]{:S(2)}, u32[]{:S(2)}) collective-permute-start(bf16[144,256]{1,0:T(8,128)(2,1)S(1)} %pad_maximum_fusion.refs_0_), channel_id=1, source_target_pairs={{0,12},{4,8},{8,4},{12,0},{1,13},{5,9},{9,5},{13,1},{2,14},{6,10},... | collective-permute-start | bytes 221192 | tf_op jit(solution)/shard_map/ppermute | solution.py:111
  14.7 6.8 %collective-permute-start.4 = (bf16[144,256]{1,0:T(8,128)(2,1)S(1)}, bf16[144,256]{1,0:T(8,128)(2,1)S(1)}, u32[]{:S(2)}, u32[]{:S(2)}) collective-permute-start(bf16[144,256]{1,0:T(8,128)(2,1)S(1)} %pad_maximum_fusion.refs_0_), channel_id=1, source_target_pairs={{0,8},{4,12},{8,0},{12,4},{1,9},{5,13},{9,1},{13,5},{2,10},{6,14},... | collective-permute-start | bytes 221192 | tf_op jit(solution)/shard_map/ppermute | solution.py:111
  15.3 6.2 %collective-permute-start.5 = (bf16[144,256]{1,0:T(8,128)(2,1)S(1)}, bf16[144,256]{1,0:T(8,128)(2,1)S(1)}, u32[]{:S(2)}, u32[]{:S(2)}) collective-permute-start(bf16[144,256]{1,0:T(8,128)(2,1)S(1)} %pad_maximum_fusion.refs_0_), channel_id=1, source_target_pairs={{0,4},{4,0},{8,12},{12,8},{1,5},{5,1},{9,13},{13,9},{2,6},{6,2},{1... | collective-permute-start | bytes 221192 | tf_op jit(solution)/shard_map/ppermute | solution.py:111
  21.7 1.3 %collective-permute-start.6 = (bf16[16,2048]{1,0:T(8,128)(2,1)S(1)}, bf16[16,2048]{1,0:T(8,128)(2,1)S(1)}, u32[]{:S(2)}, u32[]{:S(2)}) collective-permute-start(bf16[16,2048]{1,0:T(8,128)(2,1)S(1)} %get-tuple-element.70.own_ref), channel_id=1, source_target_pairs={{0,1},{1,0},{2,3},{3,2},{4,5},{5,4},{6,7},{7,6},{8,9},{9,8},{10,11... | collective-permute-start | bytes 196616 | tf_op jit(solution)/shard_map/ppermute | solution.py:111
  23.6 3.9 %collective-permute-start.7 = (bf16[32,448]{1,0:T(8,128)(2,1)S(1)}, bf16[32,448]{1,0:T(8,128)(2,1)S(1)}, u32[]{:S(2)}, u32[]{:S(2)}) collective-permute-start(bf16[32,448]{1,0:T(8,128)(2,1)S(1)} %get-tuple-element.75.refs_0_.own_ref), channel_id=1, source_target_pairs={{0,2},{2,0},{1,3},{3,1},{4,6},{6,4},{5,7},{7,5},{8,10},{10,8},{9,1... | collective-permute-start | bytes 86024 | tf_op jit(solution)/shard_map/ppermute | solution.py:111
  27.8 7.1 %collective-permute-start.8 = (bf16[32,512]{1,0:T(8,128)(2,1)S(1)}, bf16[32,512]{1,0:T(8,128)(2,1)S(1)}, u32[]{:S(2)}, u32[]{:S(2)}) collective-permute-start(bf16[32,512]{1,0:T(8,128)(2,1)S(1)} %get-tuple-element.79.refs_0_.own_ref), channel_id=1, source_target_pairs={{0,8},{2,4},{4,12},{6,0},{8,14},{10,2},{12,10},{14,6},{1,9},{3,5},... | collective-permute-start | bytes 98312 | tf_op jit(solution)/shard_map/ppermute | solution.py:400
  28.3 6.6 %collective-permute-start.9 = (bf16[32,512]{1,0:T(8,128)(2,1)S(1)}, bf16[32,512]{1,0:T(8,128)(2,1)S(1)}, u32[]{:S(2)}, u32[]{:S(2)}) collective-permute-start(bf16[32,512]{1,0:T(8,128)(2,1)S(1)} %get-tuple-element.79.refs_0_.own_ref), channel_id=1, source_target_pairs={{0,12},{2,14},{4,8},{6,10},{8,4},{10,6},{12,0},{14,2},{1,13},{3,15... | collective-permute-start | bytes 98312 | tf_op jit(solution)/shard_map/ppermute | solution.py:401
  34.9 1.3 %collective-permute-start.10 = (bf16[2,32,512]{2,1,0:T(8,128)(2,1)S(1)}, bf16[2,32,512]{2,1,0:T(8,128)(2,1)S(1)}, u32[]{:S(2)}, u32[]{:S(2)}) collective-permute-start(bf16[2,32,512]{2,1,0:T(8,128)(2,1)S(1)} %pick.1.mine_ref.refs_5_), channel_id=1, source_target_pairs={{0,1},{1,0},{2,3},{3,2},{4,5},{5,4},{6,7},{7,6},{8,9},{9,8},{10,11... | collective-permute-start | bytes 196616 | tf_op jit(solution)/shard_map/ppermute | solution.py:111
  37.0 6.5 %collective-permute-start.12 = (bf16[32,2176]{1,0:T(8,128)(2,1)S(1)}, bf16[32,2176]{1,0:T(8,128)(2,1)S(1)}, u32[]{:S(2)}, u32[]{:S(2)}) collective-permute-start(bf16[32,2176]{1,0:T(8,128)(2,1)S(1)} %get-tuple-element.87), channel_id=1, source_target_pairs={{0,2},{2,0},{1,3},{3,1},{4,6},{6,4},{5,7},{7,5},{8,10},{10,8},{9,1... | collective-permute-start | bytes 417800 | tf_op jit(solution)/shard_map/ppermute | solution.py:111
  39.0 6.2 %collective-permute-start.11 = (bf16[32,1536]{1,0:T(8,128)(2,1)S(1)}, bf16[32,1536]{1,0:T(8,128)(2,1)S(1)}, u32[]{:S(2)}, u32[]{:S(2)}) collective-permute-start(bf16[32,1536]{1,0:T(8,128)(2,1)S(1)} %get-tuple-element.85.refs_0_), channel_id=1, source_target_pairs={{0,2},{2,0},{1,3},{3,1},{4,6},{6,4},{5,7},{7,5},{8,10},{10,8},{9,1... | collective-permute-start | bytes 294920 | tf_op jit(solution)/shard_map/ppermute | solution.py:111
  45.9 1.3 %collective-permute-start.13 = (bf16[16,1792]{1,0:T(8,128)(2,1)S(1)}, bf16[16,1792]{1,0:T(8,128)(2,1)S(1)}, u32[]{:S(2)}, u32[]{:S(2)}) collective-permute-start(bf16[16,1792]{1,0:T(8,128)(2,1)S(1)} %get-tuple-element.89), channel_id=1, source_target_pairs={{0,1},{1,0},{2,3},{3,2},{4,5},{5,4},{6,7},{7,6},{8,9},{9,8},{10,11... | collective-permute-start | bytes 172040 | tf_op jit(solution)/shard_map/ppermute | solution.py:111
  47.3 5.6 %collective-permute-start.16 = (bf16[4,1792]{1,0:T(4,128)(2,1)S(1)}, bf16[4,1792]{1,0:T(4,128)(2,1)S(1)}, u32[]{:S(2)}, u32[]{:S(2)}) collective-permute-start(bf16[4,1792]{1,0:T(4,128)(2,1)S(1)} %get-tuple-element.93), channel_id=1, source_target_pairs={{0,12},{4,8},{8,4},{12,0},{1,13},{5,9},{9,5},{13,1},{2,14},{6,10},... | collective-permute-start | bytes 43016 | tf_op jit(solution)/shard_map/ppermute | solution.py:111
  48.8 4.6 %collective-permute-start.15 = (bf16[4,1792]{1,0:T(4,128)(2,1)S(1)}, bf16[4,1792]{1,0:T(4,128)(2,1)S(1)}, u32[]{:S(2)}, u32[]{:S(2)}) collective-permute-start(bf16[4,1792]{1,0:T(4,128)(2,1)S(1)} %get-tuple-element.92), channel_id=1, source_target_pairs={{0,8},{4,12},{8,0},{12,4},{1,9},{5,13},{9,1},{13,5},{2,10},{6,14},... | collective-permute-start | bytes 43016 | tf_op jit(solution)/shard_map/ppermute | solution.py:111
  49.8 3.8 %collective-permute-start.14 = (bf16[4,1792]{1,0:T(4,128)(2,1)S(1)}, bf16[4,1792]{1,0:T(4,128)(2,1)S(1)}, u32[]{:S(2)}, u32[]{:S(2)}) collective-permute-start(bf16[4,1792]{1,0:T(4,128)(2,1)S(1)} %get-tuple-element.91), channel_id=1, source_target_pairs={{0,4},{4,0},{8,12},{12,8},{1,5},{5,1},{9,13},{13,9},{2,6},{6,2},{1... | collective-permute-start | bytes 43016 | tf_op jit(solution)/shard_map/ppermute | solution.py:111

commit v10 on v9

--- a/solution.py
+++ b/solution.py
@@ -276,35 +276,33 @@
     def project_own(own_ref, weight_ref, gate_ref, out_ref, gate_out):
         out_ref[...] = lax.dot_general(
             own_ref[...], weight_ref[...], across, preferred_element_type=F32
-        )
+        ).astype(BF)
 
     proj_own, gate_near = kernel(
         project_own,
         "project_own",
-        [sds((toks, width), F32), sds(gate_near.shape, BF)],
+        [sds((toks, width), BF), sds(gate_near.shape, BF)],
         [VM] * 3,
         [attn, proj_near, gate_near],
         aliases={2: 1},
     )
 
-    def project(own_ref, other_ref, weight_ref, gate_ref, out_ref, gate_out):
-        first = lax.axis_index("rows") == 0
-        own = own_ref[...]
-        other = lax.dot_general(
+    proj_own_across = hop(proj_own, "heads", 2, 1)
+
+    def project(other_ref, weight_ref, gate_ref, out_ref, gate_out):
+        out_ref[...] = lax.dot_general(
             other_ref[...], weight_ref[...], across, preferred_element_type=F32
-        )
-        out_ref[:toks] = jnp.where(first, own, other).astype(BF)
-        out_ref[toks:] = jnp.where(first, other, own).astype(BF)
+        ).astype(BF)
 
     proj, gate_near = kernel(
         project,
         "project",
-        [sds((tokens, width), BF), sds(gate_near.shape, BF)],
-        [VM] * 4,
-        [proj_own, other, proj_near, gate_near],
-        aliases={3: 1},
-    )
-    proj_other = hop(proj, "heads", 2, 1)
+        [sds((toks, width), BF), sds(gate_near.shape, BF)],
+        [VM] * 3,
+        [other, proj_near, gate_near],
+        aliases={2: 1},
+    )
+    proj_across = hop(proj, "heads", 2, 1)
     (gate_near,) = fetch(
         [proj],
         [gate_weight],
@@ -329,7 +327,9 @@
         gain_ref,
         masked_ref,
         own_ref,
+        own_across_ref,
         other_ref,
+        other_across_ref,
         gate_ref,
         mid_ref,
         note_ref,
@@ -340,10 +340,13 @@
         hits = jnp.where(slots == masked_ref[...], 1.0, 0.0)
         masked = jnp.max(hits, axis=1, keepdims=True) > 0.0
         base = jnp.where(masked, embed_ref[...].astype(F32), dec_ref[...].astype(F32))
-        mid = shuffled(base, inner, base_ref) + (
-            own_ref[...].astype(F32) + other_ref[...].astype(F32)
-        )
-        mid_ref[...] = mid
+        base = shuffled(base, inner, base_ref)
+        own = own_ref[...].astype(F32) + own_across_ref[...].astype(F32)
+        other = other_ref[...].astype(F32) + other_across_ref[...].astype(F32)
+        first = lax.axis_index("rows") == 0
+        mid_ref[:toks] = base[:toks] + jnp.where(first, own, other)
+        mid_ref[toks:] = base[toks:] + jnp.where(first, other, own)
+        mid = mid_ref[...]
         note_ref[:, :width] = (mid * gain_ref[...].astype(F32)).astype(BF)
         squares = jnp.sum(mid * mid, axis=1, keepdims=True)
         high, low = split_in(squares, 2)
@@ -360,17 +363,19 @@
             sds((tokens, lanes), BF),
             sds(gate_near.shape, BF),
         ],
-        [VM] * 7,
+        [VM] * 9,
         [
             dec_state,
             mask_embed[None, :],
             norm_gain[None, :],
             masked_pos,
+            proj_own,
+            proj_own_across,
             proj,
-            proj_other,
+            proj_across,
             gate_near,
         ],
-        aliases={6: 2},
+        aliases={8: 2},
         scratch=[pltpu.VMEM((tokens, width), F32)],
     )
 

time: 54.5 us -> 55 us (level)
  waiting for transfers between devices: 10.6 us -> 11.2 us
    ppermute x1, starting transfers between devices: 2.39 us -> 1.54 us  [shards_direct(): far = lax.ppermute(note, ('blk', 'heads'), far_pairs)]
    ppermute x15 -> x16, starting transfers between devices: 18.5 us -> 19.2 us  [hop(): return lax.ppermute(value, axis, [(i, i ^ step) for i in range(size)])]
    ppermute x15 -> x16, waiting for transfers between devices: 10.6 us -> 11.2 us  [hop(): return lax.ppermute(value, axis, [(i, i ^ step) for i in range(size)])]
  transfers between devices with their start and end apart: 17 -> 18, of which waited for: 12 -> 10; matrix products, arithmetic and copies ran while one was open for 0% -> 0% of each run, Pallas kernels for 28% -> 28%
where the time goes in v10:
time: 55 us; the launch traced here: 54.8 us
  starting transfers between devices  21.2 us (39%)
  Pallas kernels  17.6 us (32%)
  waiting for transfers between devices  11.2 us (20%)
  matrix products  1.82 us (3%)
  between operations  1.48 us (3%)
  other arithmetic  1.2 us (2%)
    ppermute x16, starting transfers between devices, hop(): return lax.ppermute(value, axis, [(i, i ^ step) for i in range(size)])  19.2 us
    ppermute x16, waiting for transfers between devices, hop(): return lax.ppermute(value, axis, [(i, i ^ step) for i in range(size)])  11.2 us
    pallas_call x5, Pallas kernels, fetch(): pl.pallas_call(body, out_shape=[jax.ShapeDtypeStruct(a.shape, a.dtype) fo...  11 us
    pallas_call x12, Pallas kernels, kernel(): pl.pallas_call(body, out_shape=outs, in_specs=specs, out_specs=[VM] * len...  6.6 us
    ppermute x1, starting transfers between devices, shards_direct(): far = lax.ppermute(note, ('blk', 'heads'), far_pairs)  1.54 us
    dot_general x1, matrix products, shards_direct(): jnp.einsum('tgjd,kgd->tgjk', grouped, src_keys, preferred_element_type=F32)  1.13 us
  transfers between devices with their start and end apart: 18, of which 10 were waited for; matrix products, arithmetic and copies ran while one was open for 0% of the time, Pallas kernels for 28%

profile of v10, /device:TPU:0, one launch (start us, length us, event | category | flops | bytes accessed | tf_op | source)
XLA Modules:
  0.0 54.8 jit_solution(15189294708837062486)
XLA Ops:
  0.6 5.1 %collective-permute-start.2 = (bf16[4,8,256]{2,1,0:T(8,128)(2,1)}, bf16[4,8,256]{2,1,0:T(8,128)(2,1)S(1)}, u32[]{:S(2)}, u32[]{:S(2)}) collective-permute-start(bf16[4,8,256]{2,1,0:T(8,128)(2,1)} %refs_0_.1), channel_id=1, source_target_pairs={{0,12},{4,8},{8,4},{12,0},{1,13},{5,9},{9,5},{13,1},{2,14},{6,10},... | collective-permute-start | bytes 49160 | tf_op jit(solution)/shard_map/ppermute | solution.py:111
  5.8 0.6 %collective-permute-start.1 = (bf16[4,8,256]{2,1,0:T(8,128)(2,1)}, bf16[4,8,256]{2,1,0:T(8,128)(2,1)S(1)}, u32[]{:S(2)}, u32[]{:S(2)}) collective-permute-start(bf16[4,8,256]{2,1,0:T(8,128)(2,1)} %refs_0_.1), channel_id=1, source_target_pairs={{0,4},{4,0},{8,12},{12,8},{1,5},{5,1},{9,13},{13,9},{2,6},{6,2},{1... | collective-permute-start | bytes 49160 | tf_op jit(solution)/shard_map/ppermute | solution.py:111
  6.4 1.0 %fetch_small.1 = (bf16[4,8,256]{2,1,0:T(8,128)(2,1)S(1)}, bf16[32,448]{1,0:T(8,128)(2,1)S(1)}, bf16[448]{0:T(512)(128)(2,1)S(1)}, bf16[448]{0:T(512)(128)(2,1)S(1)}, s32[1,48]{1,0:T(1,128)S(1)}) custom-call(bf16[4,8,256]{2,1,0:T(8,128)(2,1)} %refs_0_.1, bf16[32,448]{1,0:T(8,128)(2,1)} %refs_1_.4, bf16[448]{0:T(512)(128)(2,1)} %refs_2_.2, ...), custom_call_target="tpu_custom_call" | custom-call | bytes 94080 | tf_op jit(solution)/shard_map/fetch_small/pallas_call | solution.py:148
  7.4 0.3 collective-permute-done.2
  7.7 2.0 %collective-permute-done.1 = bf16[4,8,256]{2,1,0:T(8,128)(2,1)S(1)} collective-permute-done((bf16[4,8,256]{2,1,0:T(8,128)(2,1)}, bf16[4,8,256]{2,1,0:T(8,128)(2,1)S(1)}, u32[]{:S(2)}, u32[]{:S(2)}) %collective-permute-start.1) | collective-permute-done | bytes 16416 | tf_op jit(solution)/shard_map/ppermute | solution.py:111
  9.7 0.9 %collective-permute-done = bf16[4,8,256]{2,1,0:T(8,128)(2,1)S(1)} collective-permute-done((bf16[4,8,256]{2,1,0:T(8,128)(2,1)}, bf16[4,8,256]{2,1,0:T(8,128)(2,1)S(1)}, u32[]{:S(2)}, u32[]{:S(2)}) %collective-permute-start) | collective-permute-done | bytes 16416 | tf_op jit(solution)/shard_map/ppermute | solution.py:111
  10.7 1.1 %fusion.30 = (f32[16,4,2]{0,2,1:T(2,128)S(1)}, f32[16,4,2,1536]{3,0,2,1:T(8,128)S(1)}) fusion(bf16[16,4,2,256]{3,0,2,1:T(8,128)(2,1)S(1)} %bitcast.23, bf16[1536,4,256,1]{2,1,0,3:T(4,128)(2,1)S(1)} %bitcast.21), kind=kOutput, calls=%fused_computation.39 | convolution fusion | flops 101056384 | bytes 3998208 | tf_op jit(solution)/shard_map/tgjd,kgd->tgjk/dot_general | solution.py:218
  11.8 0.3 fusion.19
  12.1 0.7 %fusion.16 = bf16[4,2,16,256]{3,2,1,0:T(8,128)(2,1)S(1)} fusion(bf16[1536,4,256,1]{2,1,0,3:T(4,128)(2,1)S(1)} %bitcast.30, f32[16,4,2,1536]{3,0,2,1:T(8,128)S(1)} %get-tuple-element.110, f32[16,4,2]{0,2,1:T(2,128)S(1)} %get-tuple-element.66, f32[4,2,16]{2,1,0:T(2,128)S(1)} %bitcast.28), kind=kOutput, calls=%fused_computation.8 | convolution fusion | flops 101122048 | bytes 3998720 | tf_op jit(solution)/shard_map/tgjk,kgd->tgjd/dot_general | solution.py:223
  12.8 0.1 copy.34
  12.9 0.1 copy.33
  13.0 0.1 fusion.29
  13.1 1.6 %collective-permute-start.3 = (bf16[144,256]{1,0:T(8,128)(2,1)S(1)}, bf16[144,256]{1,0:T(8,128)(2,1)S(1)}, u32[]{:S(2)}, u32[]{:S(2)}) collective-permute-start(bf16[144,256]{1,0:T(8,128)(2,1)S(1)} %pad_maximum_fusion.refs_0_), channel_id=1, source_target_pairs={{0,12},{4,8},{8,4},{12,0},{1,13},{5,9},{9,5},{13,1},{2,14},{6,10},... | collective-permute-start | bytes 221192 | tf_op jit(solution)/shard_map/ppermute | solution.py:111
  14.7 0.6 %collective-permute-start.4 = (bf16[144,256]{1,0:T(8,128)(2,1)S(1)}, bf16[144,256]{1,0:T(8,128)(2,1)S(1)}, u32[]{:S(2)}, u32[]{:S(2)}) collective-permute-start(bf16[144,256]{1,0:T(8,128)(2,1)S(1)} %pad_maximum_fusion.refs_0_), channel_id=1, source_target_pairs={{0,8},{4,12},{8,0},{12,4},{1,9},{5,13},{9,1},{13,5},{2,10},{6,14},... | collective-permute-start | bytes 221192 | tf_op jit(solution)/shard_map/ppermute | solution.py:111
  15.3 2.3 %collective-permute-start.5 = (bf16[144,256]{1,0:T(8,128)(2,1)S(1)}, bf16[144,256]{1,0:T(8,128)(2,1)S(1)}, u32[]{:S(2)}, u32[]{:S(2)}) collective-permute-start(bf16[144,256]{1,0:T(8,128)(2,1)S(1)} %pad_maximum_fusion.refs_0_), channel_id=1, source_target_pairs={{0,4},{4,0},{8,12},{12,8},{1,5},{5,1},{9,13},{13,9},{2,6},{6,2},{1... | collective-permute-start | bytes 221192 | tf_op jit(solution)/shard_map/ppermute | solution.py:111
  17.5 2.8 %fetch_proj_gate.1 = (bf16[448,2048]{1,0:T(8,128)(2,1)S(1)}, bf16[1792,1792]{1,0:T(8,128)(2,1)S(1)}) custom-call(bf16[144,256]{1,0:T(8,128)(2,1)S(1)} %pad_maximum_fusion.refs_0_, bf16[448,2048]{1,0:T(8,128)(2,1)} %bitcast.22, bf16[1792,1792]{1,0:T(8,128)(2,1)} %refs_1_.5), custom_call_target="tpu_custom_call" | custom-call | bytes 16515072 | tf_op jit(solution)/shard_map/fetch_proj_gate/pallas_call | solution.py:148
  20.3 1.1 %collective-permute-done.4.refs_2_ = bf16[144,256]{1,0:T(8,128)(2,1)S(1)} collective-permute-done((bf16[144,256]{1,0:T(8,128)(2,1)S(1)}, bf16[144,256]{1,0:T(8,128)(2,1)S(1)}, u32[]{:S(2)}, u32[]{:S(2)}) %collective-permute-start.4) | collective-permute-done | bytes 73760 | tf_op jit(solution)/shard_map/ppermute | solution.py:111
  21.4 0.2 combine.1
  21.7 0.1 collective-permute-start.7
  21.8 0.6 %project_own.1 = (bf16[16,448]{1,0:T(8,128)(2,1)S(1)}, bf16[1792,1792]{1,0:T(8,128)(2,1)S(1)}) custom-call(bf16[16,2048]{1,0:T(8,128)(2,1)S(1)} %get-tuple-element.70.own_ref, bf16[448,2048]{1,0:T(8,128)(2,1)S(1)} %get-tuple-element.71.weight_ref, bf16[1792,1792]{1,0:T(8,128)(2,1)S(1)} %get-tuple-element.72.gate_ref), custom_call_target="tpu_custom_call", output_to_operand_aliasing={{1}: (2, {})} | custom-call | bytes 14759936 | tf_op jit(solution)/shard_map/project_own/pallas_call | solution.py:117
  22.4 1.5 %collective-permute-start.6 = (bf16[16,448]{1,0:T(8,128)(2,1)S(1)}, bf16[16,448]{1,0:T(8,128)(2,1)S(1)}, u32[]{:S(2)}, u32[]{:S(2)}) collective-permute-start(bf16[16,448]{1,0:T(8,128)(2,1)S(1)} %get-tuple-element.73.own_ref), channel_id=1, source_target_pairs={{0,2},{2,0},{1,3},{3,1},{4,6},{6,4},{5,7},{7,5},{8,10},{10,8},{9,1... | collective-permute-start | bytes 43016 | tf_op jit(solution)/shard_map/ppermute | solution.py:111
  23.9 0.6 %project.1 = (bf16[16,448]{1,0:T(8,128)(2,1)S(1)}, bf16[1792,1792]{1,0:T(8,128)(2,1)S(1)}) custom-call(bf16[16,2048]{1,0:T(8,128)(2,1)S(1)} %collective-permute-done.7.other_ref, bf16[448,2048]{1,0:T(8,128)(2,1)S(1)} %get-tuple-element.71.weight_ref, bf16[1792,1792]{1,0:T(8,128)(2,1)S(1)} %get-tuple-element.74.gate_ref), custom_call_target="tpu_custom_call", output_to_operand_aliasing={{1}: (2, {})} | custom-call | bytes 14759936 | tf_op jit(solution)/shard_map/project/pallas_call | solution.py:117
  24.4 0.7 %collective-permute-start.8 = (bf16[16,448]{1,0:T(8,128)(2,1)S(1)}, bf16[16,448]{1,0:T(8,128)(2,1)S(1)}, u32[]{:S(2)}, u32[]{:S(2)}) collective-permute-start(bf16[16,448]{1,0:T(8,128)(2,1)S(1)} %get-tuple-element.75.refs_0_.other_ref), channel_id=1, source_target_pairs={{0,2},{2,0},{1,3},{3,1},{4,6},{6,4},{5,7},{7,5},{8,10},{10,8},{9,1... | collective-permute-start | bytes 43016 | tf_op jit(solution)/shard_map/ppermute | solution.py:111
  25.1 1.6 %fetch_gate_last.1.gate_ref = bf16[1792,1792]{1,0:T(8,128)(2,1)S(1)} custom-call(bf16[16,448]{1,0:T(8,128)(2,1)S(1)} %get-tuple-element.75.refs_0_.other_ref, bf16[1792,1792]{1,0:T(8,128)(2,1)} %refs_1_.5, bf16[1792,1792]{1,0:T(8,128)(2,1)S(1)} %get-tuple-element.76.refs_2_), custom_call_target="tpu_custom_call", output_to_operand_aliasing={{}: (2, {})} | custom-call | bytes 12845056 | tf_op jit(solution)/shard_map/fetch_gate_last/pallas_call | solution.py:148
  26.8 1.4 %collective-permute-done.8.other_across_ref = bf16[16,448]{1,0:T(8,128)(2,1)S(1)} collective-permute-done((bf16[16,448]{1,0:T(8,128)(2,1)S(1)}, bf16[16,448]{1,0:T(8,128)(2,1)S(1)}, u32[]{:S(2)}, u32[]{:S(2)}) %collective-permute-start.8) | collective-permute-done | bytes 14368 | tf_op jit(solution)/shard_map/ppermute | solution.py:111
  28.2 0.3 middle.1
  28.5 0.5 collective-permute-start.9
  28.9 1.5 %collective-permute-start.10 = (bf16[32,512]{1,0:T(8,128)(2,1)S(1)}, bf16[32,512]{1,0:T(8,128)(2,1)S(1)}, u32[]{:S(2)}, u32[]{:S(2)}) collective-permute-start(bf16[32,512]{1,0:T(8,128)(2,1)S(1)} %get-tuple-element.79.refs_0_.own_ref), channel_id=1, source_target_pairs={{0,12},{2,14},{4,8},{6,10},{8,4},{10,6},{12,0},{14,2},{1,13},{3,15... | collective-permute-start | bytes 98312 | tf_op jit(solution)/shard_map/ppermute | solution.py:406
  31.1 2.8 %fetch_up.1.up_ref.refs_4_ = bf16[1792,1792]{1,0:T(8,128)(2,1)S(1)} custom-call(bf16[32,512]{1,0:T(8,128)(2,1)S(1)} %get-tuple-element.79.refs_0_.own_ref, bf16[1792,1792]{1,0:T(8,128)(2,1)} %refs_1_.6), custom_call_target="tpu_custom_call" | custom-call | bytes 12845056 | tf_op jit(solution)/shard_map/fetch_up/pallas_call | solution.py:148
  34.0 0.7 %residual.1 = (bf16[32,448]{1,0:T(8,128)(2,1)}, f32[4,1]{1,0:T(4,128)S(1)}) custom-call(f32[32,448]{1,0:T(8,128)S(1)} %get-tuple-element.77.mid_ref, s32[1,1]{1,0:T(1,128)} %bitcast.20.length_ref), custom_call_target="tpu_custom_call" | custom-call | bytes 86036 | tf_op jit(solution)/shard_map/residual/pallas_call | solution.py:117
  34.8 1.2 %inner_products.1 = (f32[32,1792]{1,0:T(8,128)S(1)}, f32[32,1792]{1,0:T(8,128)S(1)}) custom-call(bf16[2,32,512]{2,1,0:T(8,128)(2,1)S(1)} %pick.1.mine_ref.refs_5_, bf16[1792,1792]{1,0:T(8,128)(2,1)S(1)} %get-tuple-element.80.gate_ref.refs_3_, bf16[1792,1792]{1,0:T(8,128)(2,1)S(1)} %fetch_up.1.up_ref.refs_4_), custom_call_target="tpu_custom_call" | custom-call | flops 205520896 | bytes 13369344 | tf_op jit(solution)/shard_map/inner_products/pallas_call | solution.py:117
  36.0 0.8 %gate_up_0.1 = (f32[32,2176]{1,0:T(8,128)S(1)}, bf16[32,2176]{1,0:T(8,128)(2,1)S(1)}) custom-call(bf16[2,32,512]{2,1,0:T(8,128)(2,1)S(1)} %collective-permute-done.11.refs_0_, f32[32,1792]{1,0:T(8,128)S(1)} %get-tuple-element.82.refs_1_, f32[32,1792]{1,0:T(8,128)S(1)} %get-tuple-element.83.refs_2_, ...), custom_call_target="tpu_custom_call" | custom-call | flops 102760448 | bytes 13852672 | tf_op jit(solution)/shard_map/gate_up_0/pallas_call | solution.py:117
  36.8 1.5 %collective-permute-start.13 = (bf16[32,2176]{1,0:T(8,128)(2,1)S(1)}, bf16[32,2176]{1,0:T(8,128)(2,1)S(1)}, u32[]{:S(2)}, u32[]{:S(2)}) collective-permute-start(bf16[32,2176]{1,0:T(8,128)(2,1)S(1)} %get-tuple-element.87), channel_id=1, source_target_pairs={{0,2},{2,0},{1,3},{3,1},{4,6},{6,4},{5,7},{7,5},{8,10},{10,8},{9,1... | collective-permute-start | bytes 417800 | tf_op jit(solution)/shard_map/ppermute | solution.py:111
  38.3 0.6 %gate_up_1.1 = (f32[32,1536]{1,0:T(8,128)S(1)}, bf16[32,1536]{1,0:T(8,128)(2,1)S(1)}) custom-call(bf16[2,32,512]{2,1,0:T(8,128)(2,1)S(1)} %collective-permute-done.11.refs_0_, f32[32,1792]{1,0:T(8,128)S(1)} %get-tuple-element.82.refs_1_, f32[32,1792]{1,0:T(8,128)S(1)} %get-tuple-element.83.refs_2_, ...), custom_call_target="tpu_custom_call" | custom-call | flops 102760448 | bytes 13664256 | tf_op jit(solution)/shard_map/gate_up_1/pallas_call | solution.py:117
  38.9 0.7 %collective-permute-start.12 = (bf16[32,1536]{1,0:T(8,128)(2,1)S(1)}, bf16[32,1536]{1,0:T(8,128)(2,1)S(1)}, u32[]{:S(2)}, u32[]{:S(2)}) collective-permute-start(bf16[32,1536]{1,0:T(8,128)(2,1)S(1)} %get-tuple-element.85.refs_0_), channel_id=1, source_target_pairs={{0,2},{2,0},{1,3},{3,1},{4,6},{6,4},{5,7},{7,5},{8,10},{10,8},{9,1... | collective-permute-start | bytes 294920 | tf_op jit(solution)/shard_map/ppermute | solution.py:111
  39.6 2.8 %fetch_down.1.weight_ref = bf16[1792,1792]{1,0:T(8,128)(2,1)S(1)} custom-call(bf16[32,1536]{1,0:T(8,128)(2,1)S(1)} %get-tuple-element.85.refs_0_, bf16[1792,1792]{1,0:T(8,128)(2,1)} %refs_1_.7), custom_call_target="tpu_custom_call" | custom-call | bytes 12845056 | tf_op jit(solution)/shard_map/fetch_down/pallas_call | solution.py:148
  42.4 0.9 %collective-permute-done.13.other_ref.first_other_ref = bf16[32,2176]{1,0:T(8,128)(2,1)S(1)} collective-permute-done((bf16[32,2176]{1,0:T(8,128)(2,1)S(1)}, bf16[32,2176]{1,0:T(8,128)(2,1)S(1)}, u32[]{:S(2)}, u32[]{:S(2)}) %collective-permute-start.13) | collective-permute-done | bytes 139296 | tf_op jit(solution)/shard_map/ppermute | solution.py:111
  43.3 0.8 %down_first.1.part_ref = f32[32,1792]{1,0:T(8,128)S(1)} custom-call(f32[32,2176]{1,0:T(8,128)S(1)} %get-tuple-element.86.own_ref.first_ref, bf16[32,2176]{1,0:T(8,128)(2,1)S(1)} %collective-permute-done.13.other_ref.first_other_ref, bf16[1792,1792]{1,0:T(8,128)(2,1)S(1)} %fetch_down.1.weight_ref), custom_call_target="tpu_custom_call" | custom-call | flops 102760448 | bytes 7069696 | tf_op jit(solution)/shard_map/down_first/pallas_call | solution.py:117
  44.2 0.9 %collective-permute-done.12.other_ref = bf16[32,1536]{1,0:T(8,128)(2,1)S(1)} collective-permute-done((bf16[32,1536]{1,0:T(8,128)(2,1)S(1)}, bf16[32,1536]{1,0:T(8,128)(2,1)S(1)}, u32[]{:S(2)}, u32[]{:S(2)}) %collective-permute-start.12) | collective-permute-done | bytes 98336 | tf_op jit(solution)/shard_map/ppermute | solution.py:111
  45.0 0.7 %down_last.1 = (f32[16,1792]{1,0:T(8,128)S(1)}, bf16[16,1792]{1,0:T(8,128)(2,1)S(1)}) custom-call(f32[32,1536]{1,0:T(8,128)S(1)} %get-tuple-element.84.own_ref, bf16[32,1536]{1,0:T(8,128)(2,1)S(1)} %collective-permute-done.12.other_ref, f32[32,2176]{1,0:T(8,128)S(1)} %get-tuple-element.86.own_ref.first_ref, ...), custom_call_target="tpu_custom_call" | custom-call | bytes 7536640 | tf_op jit(solution)/shard_map/down_last/pallas_call | solution.py:117
  45.8 1.2 %collective-permute-done.14.back_ref = bf16[16,1792]{1,0:T(8,128)(2,1)S(1)} collective-permute-done((bf16[16,1792]{1,0:T(8,128)(2,1)S(1)}, bf16[16,1792]{1,0:T(8,128)(2,1)S(1)}, u32[]{:S(2)}, u32[]{:S(2)}) %collective-permute-start.14) | collective-permute-done | bytes 57376 | tf_op jit(solution)/shard_map/ppermute | solution.py:111
  47.1 2.3 %collective-permute-start.17 = (bf16[4,1792]{1,0:T(4,128)(2,1)S(1)}, bf16[4,1792]{1,0:T(4,128)(2,1)S(1)}, u32[]{:S(2)}, u32[]{:S(2)}) collective-permute-start(bf16[4,1792]{1,0:T(4,128)(2,1)S(1)} %get-tuple-element.93), channel_id=1, source_target_pairs={{0,12},{4,8},{8,4},{12,0},{1,13},{5,9},{9,5},{13,1},{2,14},{6,10},... | collective-permute-start | bytes 43016 | tf_op jit(solution)/shard_map/ppermute | solution.py:111
  49.5 0.3 collective-permute-start.16
  49.7 1.8 %collective-permute-start.15 = (bf16[4,1792]{1,0:T(4,128)(2,1)S(1)}, bf16[4,1792]{1,0:T(4,128)(2,1)S(1)}, u32[]{:S(2)}, u32[]{:S(2)}) collective-permute-start(bf16[4,1792]{1,0:T(4,128)(2,1)S(1)} %get-tuple-element.91), channel_id=1, source_target_pairs={{0,4},{4,0},{8,12},{12,8},{1,5},{5,1},{9,13},{13,9},{2,6},{6,2},{1... | collective-permute-start | bytes 43016 | tf_op jit(solution)/shard_map/ppermute | solution.py:111
  51.6 0.1 reduce
  51.7 1.0 %collective-permute-done.17 = bf16[4,1792]{1,0:T(4,128)(2,1)S(1)} collective-permute-done((bf16[4,1792]{1,0:T(4,128)(2,1)S(1)}, bf16[4,1792]{1,0:T(4,128)(2,1)S(1)}, u32[]{:S(2)}, u32[]{:S(2)}) %collective-permute-start.17) | collective-permute-done | bytes 14368 | tf_op jit(solution)/shard_map/ppermute | solution.py:111
  52.7 1.4 %collective-permute-done.16 = bf16[4,1792]{1,0:T(4,128)(2,1)S(1)} collective-permute-done((bf16[4,1792]{1,0:T(4,128)(2,1)S(1)}, bf16[4,1792]{1,0:T(4,128)(2,1)S(1)}, u32[]{:S(2)}, u32[]{:S(2)}) %collective-permute-start.16) | collective-permute-done | bytes 14368 | tf_op jit(solution)/shard_map/ppermute | solution.py:111
  54.1 0.7 %multiply_convert_fusion = bf16[4,1792]{1,0:T(4,128)(2,1)} fusion(bf16[4,1792]{1,0:T(4,128)(2,1)S(1)} %collective-permute-done.17, bf16[4,1792]{1,0:T(4,128)(2,1)S(1)} %collective-permute-done.16, f32[4,1792]{1,0:T(4,128)S(1)} %get-tuple-element.90, bf16[4,1792]{1,0:T(4,128)(2,1)S(1)} %collective-permute-done.15, f32[4]{0:T(128)S(1)} %reduce), kind=kLoop, calls=%fused_computation.15 | loop fusion | flops 57344 | bytes 86032 | tf_op jit(solution)/shard_map/convert_element_type | solution.py:569
  (28 shorter events, 0.3 us)
Async XLA Ops:
  0.6 10.0 %copy-start = (bf16[1536,4,256]{2,1,0:T(4,128)(2,1)S(1)}, bf16[1536,4,256]{2,1,0:T(4,128)(2,1)}, u32[]{:S(2)}) copy-start(bf16[1536,4,256]{2,1,0:T(4,128)(2,1)} %param.13) | copy-start | bytes 9437188
  0.6 7.0 %collective-permute-start.2 = (bf16[4,8,256]{2,1,0:T(8,128)(2,1)}, bf16[4,8,256]{2,1,0:T(8,128)(2,1)S(1)}, u32[]{:S(2)}, u32[]{:S(2)}) collective-permute-start(bf16[4,8,256]{2,1,0:T(8,128)(2,1)} %refs_0_.1), channel_id=1, source_target_pairs={{0,12},{4,8},{8,4},{12,0},{1,13},{5,9},{9,5},{13,1},{2,14},{6,10},... | collective-permute-start | bytes 49160 | tf_op jit(solution)/shard_map/ppermute | solution.py:111
  5.8 4.8 %collective-permute-start = (bf16[4,8,256]{2,1,0:T(8,128)(2,1)}, bf16[4,8,256]{2,1,0:T(8,128)(2,1)S(1)}, u32[]{:S(2)}, u32[]{:S(2)}) collective-permute-start(bf16[4,8,256]{2,1,0:T(8,128)(2,1)} %refs_0_.1), channel_id=1, source_target_pairs={{0,8},{4,12},{8,0},{12,4},{1,9},{5,13},{9,1},{13,5},{2,10},{6,14},... | collective-permute-start | bytes 49160 | tf_op jit(solution)/shard_map/ppermute | solution.py:111
  5.8 3.9 %collective-permute-start.1 = (bf16[4,8,256]{2,1,0:T(8,128)(2,1)}, bf16[4,8,256]{2,1,0:T(8,128)(2,1)S(1)}, u32[]{:S(2)}, u32[]{:S(2)}) collective-permute-start(bf16[4,8,256]{2,1,0:T(8,128)(2,1)} %refs_0_.1), channel_id=1, source_target_pairs={{0,4},{4,0},{8,12},{12,8},{1,5},{5,1},{9,13},{13,9},{2,6},{6,2},{1... | collective-permute-start | bytes 49160 | tf_op jit(solution)/shard_map/ppermute | solution.py:111
  6.4 5.7 %copy-start.1 = (bf16[1536,4,256]{2,1,0:T(4,128)(2,1)S(1)}, bf16[1536,4,256]{2,1,0:T(4,128)(2,1)}, u32[]{:S(2)}) copy-start(bf16[1536,4,256]{2,1,0:T(4,128)(2,1)} %param.14) | copy-start | bytes 9437188
  13.1 7.2 %collective-permute-start.3 = (bf16[144,256]{1,0:T(8,128)(2,1)S(1)}, bf16[144,256]{1,0:T(8,128)(2,1)S(1)}, u32[]{:S(2)}, u32[]{:S(2)}) collective-permute-start(bf16[144,256]{1,0:T(8,128)(2,1)S(1)} %pad_maximum_fusion.refs_0_), channel_id=1, source_target_pairs={{0,12},{4,8},{8,4},{12,0},{1,13},{5,9},{9,5},{13,1},{2,14},{6,10},... | collective-permute-start | bytes 221192 | tf_op jit(solution)/shard_map/ppermute | solution.py:111
  14.7 6.8 %collective-permute-start.4 = (bf16[144,256]{1,0:T(8,128)(2,1)S(1)}, bf16[144,256]{1,0:T(8,128)(2,1)S(1)}, u32[]{:S(2)}, u32[]{:S(2)}) collective-permute-start(bf16[144,256]{1,0:T(8,128)(2,1)S(1)} %pad_maximum_fusion.refs_0_), channel_id=1, source_target_pairs={{0,8},{4,12},{8,0},{12,4},{1,9},{5,13},{9,1},{13,5},{2,10},{6,14},... | collective-permute-start | bytes 221192 | tf_op jit(solution)/shard_map/ppermute | solution.py:111
  15.3 6.2 %collective-permute-start.5 = (bf16[144,256]{1,0:T(8,128)(2,1)S(1)}, bf16[144,256]{1,0:T(8,128)(2,1)S(1)}, u32[]{:S(2)}, u32[]{:S(2)}) collective-permute-start(bf16[144,256]{1,0:T(8,128)(2,1)S(1)} %pad_maximum_fusion.refs_0_), channel_id=1, source_target_pairs={{0,4},{4,0},{8,12},{12,8},{1,5},{5,1},{9,13},{13,9},{2,6},{6,2},{1... | collective-permute-start | bytes 221192 | tf_op jit(solution)/shard_map/ppermute | solution.py:111
  21.7 2.2 %collective-permute-start.7 = (bf16[16,2048]{1,0:T(8,128)(2,1)S(1)}, bf16[16,2048]{1,0:T(8,128)(2,1)S(1)}, u32[]{:S(2)}, u32[]{:S(2)}) collective-permute-start(bf16[16,2048]{1,0:T(8,128)(2,1)S(1)} %get-tuple-element.70.own_ref), channel_id=1, source_target_pairs={{0,1},{1,0},{2,3},{3,2},{4,5},{5,4},{6,7},{7,6},{8,9},{9,8},{10,11... | collective-permute-start | bytes 196616 | tf_op jit(solution)/shard_map/ppermute | solution.py:111
  22.4 4.4 %collective-permute-start.6 = (bf16[16,448]{1,0:T(8,128)(2,1)S(1)}, bf16[16,448]{1,0:T(8,128)(2,1)S(1)}, u32[]{:S(2)}, u32[]{:S(2)}) collective-permute-start(bf16[16,448]{1,0:T(8,128)(2,1)S(1)} %get-tuple-element.73.own_ref), channel_id=1, source_target_pairs={{0,2},{2,0},{1,3},{3,1},{4,6},{6,4},{5,7},{7,5},{8,10},{10,8},{9,1... | collective-permute-start | bytes 43016 | tf_op jit(solution)/shard_map/ppermute | solution.py:111
  24.4 3.8 %collective-permute-start.8 = (bf16[16,448]{1,0:T(8,128)(2,1)S(1)}, bf16[16,448]{1,0:T(8,128)(2,1)S(1)}, u32[]{:S(2)}, u32[]{:S(2)}) collective-permute-start(bf16[16,448]{1,0:T(8,128)(2,1)S(1)} %get-tuple-element.75.refs_0_.other_ref), channel_id=1, source_target_pairs={{0,2},{2,0},{1,3},{3,1},{4,6},{6,4},{5,7},{7,5},{8,10},{10,8},{9,1... | collective-permute-start | bytes 43016 | tf_op jit(solution)/shard_map/ppermute | solution.py:111
  28.5 6.2 %collective-permute-start.9 = (bf16[32,512]{1,0:T(8,128)(2,1)S(1)}, bf16[32,512]{1,0:T(8,128)(2,1)S(1)}, u32[]{:S(2)}, u32[]{:S(2)}) collective-permute-start(bf16[32,512]{1,0:T(8,128)(2,1)S(1)} %get-tuple-element.79.refs_0_.own_ref), channel_id=1, source_target_pairs={{0,8},{2,4},{4,12},{6,0},{8,14},{10,2},{12,10},{14,6},{1,9},{3,5},... | collective-permute-start | bytes 98312 | tf_op jit(solution)/shard_map/ppermute | solution.py:405
  28.9 5.7 %collective-permute-start.10 = (bf16[32,512]{1,0:T(8,128)(2,1)S(1)}, bf16[32,512]{1,0:T(8,128)(2,1)S(1)}, u32[]{:S(2)}, u32[]{:S(2)}) collective-permute-start(bf16[32,512]{1,0:T(8,128)(2,1)S(1)} %get-tuple-element.79.refs_0_.own_ref), channel_id=1, source_target_pairs={{0,12},{2,14},{4,8},{6,10},{8,4},{10,6},{12,0},{14,2},{1,13},{3,15... | collective-permute-start | bytes 98312 | tf_op jit(solution)/shard_map/ppermute | solution.py:406
  34.7 1.3 %collective-permute-start.11 = (bf16[2,32,512]{2,1,0:T(8,128)(2,1)S(1)}, bf16[2,32,512]{2,1,0:T(8,128)(2,1)S(1)}, u32[]{:S(2)}, u32[]{:S(2)}) collective-permute-start(bf16[2,32,512]{2,1,0:T(8,128)(2,1)S(1)} %pick.1.mine_ref.refs_5_), channel_id=1, source_target_pairs={{0,1},{1,0},{2,3},{3,2},{4,5},{5,4},{6,7},{7,6},{8,9},{9,8},{10,11... | collective-permute-start | bytes 196616 | tf_op jit(solution)/shard_map/ppermute | solution.py:111
  36.8 6.5 %collective-permute-start.13 = (bf16[32,2176]{1,0:T(8,128)(2,1)S(1)}, bf16[32,2176]{1,0:T(8,128)(2,1)S(1)}, u32[]{:S(2)}, u32[]{:S(2)}) collective-permute-start(bf16[32,2176]{1,0:T(8,128)(2,1)S(1)} %get-tuple-element.87), channel_id=1, source_target_pairs={{0,2},{2,0},{1,3},{3,1},{4,6},{6,4},{5,7},{7,5},{8,10},{10,8},{9,1... | collective-permute-start | bytes 417800 | tf_op jit(solution)/shard_map/ppermute | solution.py:111
  38.9 6.2 %collective-permute-start.12 = (bf16[32,1536]{1,0:T(8,128)(2,1)S(1)}, bf16[32,1536]{1,0:T(8,128)(2,1)S(1)}, u32[]{:S(2)}, u32[]{:S(2)}) collective-permute-start(bf16[32,1536]{1,0:T(8,128)(2,1)S(1)} %get-tuple-element.85.refs_0_), channel_id=1, source_target_pairs={{0,2},{2,0},{1,3},{3,1},{4,6},{6,4},{5,7},{7,5},{8,10},{10,8},{9,1... | collective-permute-start | bytes 294920 | tf_op jit(solution)/shard_map/ppermute | solution.py:111
  45.8 1.3 %collective-permute-start.14 = (bf16[16,1792]{1,0:T(8,128)(2,1)S(1)}, bf16[16,1792]{1,0:T(8,128)(2,1)S(1)}, u32[]{:S(2)}, u32[]{:S(2)}) collective-permute-start(bf16[16,1792]{1,0:T(8,128)(2,1)S(1)} %get-tuple-element.89), channel_id=1, source_target_pairs={{0,1},{1,0},{2,3},{3,2},{4,5},{5,4},{6,7},{7,6},{8,9},{9,8},{10,11... | collective-permute-start | bytes 172040 | tf_op jit(solution)/shard_map/ppermute | solution.py:111
  47.1 5.6 %collective-permute-start.17 = (bf16[4,1792]{1,0:T(4,128)(2,1)S(1)}, bf16[4,1792]{1,0:T(4,128)(2,1)S(1)}, u32[]{:S(2)}, u32[]{:S(2)}) collective-permute-start(bf16[4,1792]{1,0:T(4,128)(2,1)S(1)} %get-tuple-element.93), channel_id=1, source_target_pairs={{0,12},{4,8},{8,4},{12,0},{1,13},{5,9},{9,5},{13,1},{2,14},{6,10},... | collective-permute-start | bytes 43016 | tf_op jit(solution)/shard_map/ppermute | solution.py:111
  49.5 4.6 %collective-permute-start.16 = (bf16[4,1792]{1,0:T(4,128)(2,1)S(1)}, bf16[4,1792]{1,0:T(4,128)(2,1)S(1)}, u32[]{:S(2)}, u32[]{:S(2)}) collective-permute-start(bf16[4,1792]{1,0:T(4,128)(2,1)S(1)} %get-tuple-element.92), channel_id=1, source_target_pairs={{0,8},{4,12},{8,0},{12,4},{1,9},{5,13},{9,1},{13,5},{2,10},{6,14},... | collective-permute-start | bytes 43016 | tf_op jit(solution)/shard_map/ppermute | solution.py:111
  49.7 4.4 %collective-permute-start.15 = (bf16[4,1792]{1,0:T(4,128)(2,1)S(1)}, bf16[4,1792]{1,0:T(4,128)(2,1)S(1)}, u32[]{:S(2)}, u32[]{:S(2)}) collective-permute-start(bf16[4,1792]{1,0:T(4,128)(2,1)S(1)} %get-tuple-element.91), channel_id=1, source_target_pairs={{0,4},{4,0},{8,12},{12,8},{1,5},{5,1},{9,13},{13,9},{2,6},{6,2},{1... | collective-permute-start | bytes 43016 | tf_op jit(solution)/shard_map/ppermute | solution.py:111

commit v11 on v9

--- a/solution.py
+++ b/solution.py
@@ -446,8 +446,8 @@
         flops=2 * tokens * rows_in * hidden_width,
     )
 
-    cut = -(-hidden_width // 512) * 256
-    pieces_at = [(0, cut), (cut, hidden_width)]
+    cut, next_cut = 3 * hidden_width // 7, 5 * hidden_width // 7
+    pieces_at = [(0, cut), (cut, next_cut), (next_cut, hidden_width)]
 
     def gate_up(lo, hi, with_squares):
         span = hi - lo
@@ -522,11 +522,25 @@
         flops=tokens * hidden_width * out_width,
     )
 
+    def down_next(own_ref, other_ref, first_ref, first_other_ref, part_ref, weight_ref, out_ref):
+        out_ref[...] = part_ref[...] + down_piece(
+            1, own_ref, other_ref, first_ref, first_other_ref, weight_ref
+        )
+
+    (down_part,) = kernel(
+        down_next,
+        "down_next",
+        [sds((tokens, out_width), F32)],
+        [VM] * 6,
+        [sums[1], sum_others[1], sums[0], sum_others[0], down_part, down_near],
+        flops=tokens * hidden_width * out_width,
+    )
+
     def down_last(
         own_ref, other_ref, first_ref, first_other_ref, part_ref, weight_ref, keep_ref, away_ref
     ):
         down = part_ref[...] + down_piece(
-            1, own_ref, other_ref, first_ref, first_other_ref, weight_ref
+            2, own_ref, other_ref, first_ref, first_other_ref, weight_ref
         )
         first = lax.axis_index("rows") == 0
         keep_ref[...] = jnp.where(first, down[:toks], down[toks:])
@@ -537,7 +551,7 @@
         "down_last",
         [sds((toks, out_width), F32), sds((toks, out_width), BF)],
         [VM] * 6,
-        [sums[1], sum_others[1], sums[0], sum_others[0], down_part, down_near],
+        [sums[2], sum_others[2], sums[0], sum_others[0], down_part, down_near],
         limit=12,
     )
     back = hop(away, "rows", 2, 1)

time: 54.5 us -> 54.6 us (level)
  waiting for transfers between devices: 10.6 us -> 8.77 us
  starting transfers between devices: 21.4 us -> 22.9 us
    ppermute x15 -> x16, waiting for transfers between devices: 10.6 us -> 8.77 us  [hop(): return lax.ppermute(value, axis, [(i, i ^ step) for i in range(size)])]
    ppermute x15 -> x16, starting transfers between devices: 18.5 us -> 20 us  [hop(): return lax.ppermute(value, axis, [(i, i ^ step) for i in range(size)])]
    pallas_call x12 -> x14, Pallas kernels: 6.6 us -> 6.94 us  [kernel(): pl.pallas_call(body, out_shape=outs, in_specs=specs, out_specs=[VM] * len...]
  transfers between devices with their start and end apart: 17 -> 18, of which waited for: 12 -> 9; matrix products, arithmetic and copies ran while one was open for 0% -> 0% of each run, Pallas kernels for 28% -> 29%
where the time goes in v11:
time: 54.6 us; the launch traced here: 54.3 us
  starting transfers between devices  22.9 us (42%)
  Pallas kernels  18 us (33%)
  waiting for transfers between devices  8.77 us (16%)
  matrix products  1.82 us (3%)
  between operations  1.49 us (3%)
  other arithmetic  1.2 us (2%)
    ppermute x16, starting transfers between devices, hop(): return lax.ppermute(value, axis, [(i, i ^ step) for i in range(size)])  20 us
    pallas_call x5, Pallas kernels, fetch(): pl.pallas_call(body, out_shape=[jax.ShapeDtypeStruct(a.shape, a.dtype) fo...  11 us
    ppermute x16, waiting for transfers between devices, hop(): return lax.ppermute(value, axis, [(i, i ^ step) for i in range(size)])  8.77 us
    pallas_call x14, Pallas kernels, kernel(): pl.pallas_call(body, out_shape=outs, in_specs=specs, out_specs=[VM] * len...  6.94 us
    ppermute x1, starting transfers between devices, shards_direct(): far = lax.ppermute(note, ('blk', 'heads'), far_pairs)  2.39 us
    dot_general x1, matrix products, shards_direct(): jnp.einsum('tgjd,kgd->tgjk', grouped, src_keys, preferred_element_type=F32)  1.13 us
  transfers between devices with their start and end apart: 18, of which 9 were waited for; matrix products, arithmetic and copies ran while one was open for 0% of the time, Pallas kernels for 29%

profile of v11, /device:TPU:0, one launch (start us, length us, event | category | flops | bytes accessed | tf_op | source)
XLA Modules:
  0.0 54.3 jit_solution(9089095866103731037)
XLA Ops:
  0.6 5.1 %collective-permute-start.2 = (bf16[4,8,256]{2,1,0:T(8,128)(2,1)}, bf16[4,8,256]{2,1,0:T(8,128)(2,1)S(1)}, u32[]{:S(2)}, u32[]{:S(2)}) collective-permute-start(bf16[4,8,256]{2,1,0:T(8,128)(2,1)} %refs_0_.1), channel_id=1, source_target_pairs={{0,12},{4,8},{8,4},{12,0},{1,13},{5,9},{9,5},{13,1},{2,14},{6,10},... | collective-permute-start | bytes 49160 | tf_op jit(solution)/shard_map/ppermute | solution.py:111
  5.8 0.6 %collective-permute-start.1 = (bf16[4,8,256]{2,1,0:T(8,128)(2,1)}, bf16[4,8,256]{2,1,0:T(8,128)(2,1)S(1)}, u32[]{:S(2)}, u32[]{:S(2)}) collective-permute-start(bf16[4,8,256]{2,1,0:T(8,128)(2,1)} %refs_0_.1), channel_id=1, source_target_pairs={{0,4},{4,0},{8,12},{12,8},{1,5},{5,1},{9,13},{13,9},{2,6},{6,2},{1... | collective-permute-start | bytes 49160 | tf_op jit(solution)/shard_map/ppermute | solution.py:111
  6.4 1.0 %fetch_small.1 = (bf16[4,8,256]{2,1,0:T(8,128)(2,1)S(1)}, bf16[32,448]{1,0:T(8,128)(2,1)S(1)}, bf16[448]{0:T(512)(128)(2,1)S(1)}, bf16[448]{0:T(512)(128)(2,1)S(1)}, s32[1,48]{1,0:T(1,128)S(1)}) custom-call(bf16[4,8,256]{2,1,0:T(8,128)(2,1)} %refs_0_.1, bf16[32,448]{1,0:T(8,128)(2,1)} %refs_1_.4, bf16[448]{0:T(512)(128)(2,1)} %refs_2_.2, ...), custom_call_target="tpu_custom_call" | custom-call | bytes 94080 | tf_op jit(solution)/shard_map/fetch_small/pallas_call | solution.py:148
  7.4 0.3 collective-permute-done.2
  7.7 2.0 %collective-permute-done.1 = bf16[4,8,256]{2,1,0:T(8,128)(2,1)S(1)} collective-permute-done((bf16[4,8,256]{2,1,0:T(8,128)(2,1)}, bf16[4,8,256]{2,1,0:T(8,128)(2,1)S(1)}, u32[]{:S(2)}, u32[]{:S(2)}) %collective-permute-start.1) | collective-permute-done | bytes 16416 | tf_op jit(solution)/shard_map/ppermute | solution.py:111
  9.7 0.9 %collective-permute-done = bf16[4,8,256]{2,1,0:T(8,128)(2,1)S(1)} collective-permute-done((bf16[4,8,256]{2,1,0:T(8,128)(2,1)}, bf16[4,8,256]{2,1,0:T(8,128)(2,1)S(1)}, u32[]{:S(2)}, u32[]{:S(2)}) %collective-permute-start) | collective-permute-done | bytes 16416 | tf_op jit(solution)/shard_map/ppermute | solution.py:111
  10.7 1.1 %fusion.30 = (f32[16,4,2]{0,2,1:T(2,128)S(1)}, f32[16,4,2,1536]{3,0,2,1:T(8,128)S(1)}) fusion(bf16[16,4,2,256]{3,0,2,1:T(8,128)(2,1)S(1)} %bitcast.23, bf16[1536,4,256,1]{2,1,0,3:T(4,128)(2,1)S(1)} %bitcast.21), kind=kOutput, calls=%fused_computation.39 | convolution fusion | flops 101056384 | bytes 3998208 | tf_op jit(solution)/shard_map/tgjd,kgd->tgjk/dot_general | solution.py:218
  11.8 0.3 fusion.19
  12.1 0.7 %fusion.16 = bf16[4,2,16,256]{3,2,1,0:T(8,128)(2,1)S(1)} fusion(bf16[1536,4,256,1]{2,1,0,3:T(4,128)(2,1)S(1)} %bitcast.30, f32[16,4,2,1536]{3,0,2,1:T(8,128)S(1)} %get-tuple-element.114, f32[16,4,2]{0,2,1:T(2,128)S(1)} %get-tuple-element.68, f32[4,2,16]{2,1,0:T(2,128)S(1)} %bitcast.28), kind=kOutput, calls=%fused_computation.8 | convolution fusion | flops 101122048 | bytes 3998720 | tf_op jit(solution)/shard_map/tgjk,kgd->tgjd/dot_general | solution.py:223
  12.8 0.1 copy.34
  12.9 0.1 copy.33
  13.0 0.1 fusion.29
  13.1 1.6 %collective-permute-start.3 = (bf16[144,256]{1,0:T(8,128)(2,1)S(1)}, bf16[144,256]{1,0:T(8,128)(2,1)S(1)}, u32[]{:S(2)}, u32[]{:S(2)}) collective-permute-start(bf16[144,256]{1,0:T(8,128)(2,1)S(1)} %pad_maximum_fusion.refs_0_), channel_id=1, source_target_pairs={{0,12},{4,8},{8,4},{12,0},{1,13},{5,9},{9,5},{13,1},{2,14},{6,10},... | collective-permute-start | bytes 221192 | tf_op jit(solution)/shard_map/ppermute | solution.py:111
  14.7 0.6 %collective-permute-start.4 = (bf16[144,256]{1,0:T(8,128)(2,1)S(1)}, bf16[144,256]{1,0:T(8,128)(2,1)S(1)}, u32[]{:S(2)}, u32[]{:S(2)}) collective-permute-start(bf16[144,256]{1,0:T(8,128)(2,1)S(1)} %pad_maximum_fusion.refs_0_), channel_id=1, source_target_pairs={{0,8},{4,12},{8,0},{12,4},{1,9},{5,13},{9,1},{13,5},{2,10},{6,14},... | collective-permute-start | bytes 221192 | tf_op jit(solution)/shard_map/ppermute | solution.py:111
  15.3 2.3 %collective-permute-start.5 = (bf16[144,256]{1,0:T(8,128)(2,1)S(1)}, bf16[144,256]{1,0:T(8,128)(2,1)S(1)}, u32[]{:S(2)}, u32[]{:S(2)}) collective-permute-start(bf16[144,256]{1,0:T(8,128)(2,1)S(1)} %pad_maximum_fusion.refs_0_), channel_id=1, source_target_pairs={{0,4},{4,0},{8,12},{12,8},{1,5},{5,1},{9,13},{13,9},{2,6},{6,2},{1... | collective-permute-start | bytes 221192 | tf_op jit(solution)/shard_map/ppermute | solution.py:111
  17.5 2.8 %fetch_proj_gate.1 = (bf16[448,2048]{1,0:T(8,128)(2,1)S(1)}, bf16[1792,1792]{1,0:T(8,128)(2,1)S(1)}) custom-call(bf16[144,256]{1,0:T(8,128)(2,1)S(1)} %pad_maximum_fusion.refs_0_, bf16[448,2048]{1,0:T(8,128)(2,1)} %bitcast.22, bf16[1792,1792]{1,0:T(8,128)(2,1)} %refs_1_.5), custom_call_target="tpu_custom_call" | custom-call | bytes 16515072 | tf_op jit(solution)/shard_map/fetch_proj_gate/pallas_call | solution.py:148
  20.3 1.1 %collective-permute-done.4.refs_2_ = bf16[144,256]{1,0:T(8,128)(2,1)S(1)} collective-permute-done((bf16[144,256]{1,0:T(8,128)(2,1)S(1)}, bf16[144,256]{1,0:T(8,128)(2,1)S(1)}, u32[]{:S(2)}, u32[]{:S(2)}) %collective-permute-start.4) | collective-permute-done | bytes 73760 | tf_op jit(solution)/shard_map/ppermute | solution.py:111
  21.4 0.2 combine.1
  21.8 0.6 %project_own.1 = (f32[16,448]{1,0:T(8,128)S(1)}, bf16[1792,1792]{1,0:T(8,128)(2,1)S(1)}) custom-call(bf16[16,2048]{1,0:T(8,128)(2,1)S(1)} %get-tuple-element.72.own_ref, bf16[448,2048]{1,0:T(8,128)(2,1)S(1)} %get-tuple-element.73.weight_ref, bf16[1792,1792]{1,0:T(8,128)(2,1)S(1)} %get-tuple-element.74.gate_ref), custom_call_target="tpu_custom_call", output_to_operand_aliasing={{1}: (2, {})} | custom-call | bytes 14774272 | tf_op jit(solution)/shard_map/project_own/pallas_call | solution.py:117
  22.4 0.7 %collective-permute-done.6.other_ref = bf16[16,2048]{1,0:T(8,128)(2,1)S(1)} collective-permute-done((bf16[16,2048]{1,0:T(8,128)(2,1)S(1)}, bf16[16,2048]{1,0:T(8,128)(2,1)S(1)}, u32[]{:S(2)}, u32[]{:S(2)}) %collective-permute-start.6) | collective-permute-done | bytes 65568 | tf_op jit(solution)/shard_map/ppermute | solution.py:111
  23.0 0.6 %project.1 = (bf16[32,448]{1,0:T(8,128)(2,1)S(1)}, bf16[1792,1792]{1,0:T(8,128)(2,1)S(1)}) custom-call(f32[16,448]{1,0:T(8,128)S(1)} %get-tuple-element.75.own_ref, bf16[16,2048]{1,0:T(8,128)(2,1)S(1)} %collective-permute-done.6.other_ref, bf16[448,2048]{1,0:T(8,128)(2,1)S(1)} %get-tuple-element.73.weight_ref, ...), custom_call_target="tpu_custom_call", output_to_operand_aliasing={{1}: (3, {})} | custom-call | bytes 14802944 | tf_op jit(solution)/shard_map/project/pallas_call | solution.py:117
  23.6 1.5 %collective-permute-start.7 = (bf16[32,448]{1,0:T(8,128)(2,1)S(1)}, bf16[32,448]{1,0:T(8,128)(2,1)S(1)}, u32[]{:S(2)}, u32[]{:S(2)}) collective-permute-start(bf16[32,448]{1,0:T(8,128)(2,1)S(1)} %get-tuple-element.77.refs_0_.own_ref), channel_id=1, source_target_pairs={{0,2},{2,0},{1,3},{3,1},{4,6},{6,4},{5,7},{7,5},{8,10},{10,8},{9,1... | collective-permute-start | bytes 86024 | tf_op jit(solution)/shard_map/ppermute | solution.py:111
  25.1 1.6 %fetch_gate_last.1.gate_ref = bf16[1792,1792]{1,0:T(8,128)(2,1)S(1)} custom-call(bf16[32,448]{1,0:T(8,128)(2,1)S(1)} %get-tuple-element.77.refs_0_.own_ref, bf16[1792,1792]{1,0:T(8,128)(2,1)} %refs_1_.5, bf16[1792,1792]{1,0:T(8,128)(2,1)S(1)} %get-tuple-element.78.refs_2_), custom_call_target="tpu_custom_call", output_to_operand_aliasing={{}: (2, {})} | custom-call | bytes 12845056 | tf_op jit(solution)/shard_map/fetch_gate_last/pallas_call | solution.py:148
  26.8 0.8 %collective-permute-done.7.other_ref = bf16[32,448]{1,0:T(8,128)(2,1)S(1)} collective-permute-done((bf16[32,448]{1,0:T(8,128)(2,1)S(1)}, bf16[32,448]{1,0:T(8,128)(2,1)S(1)}, u32[]{:S(2)}, u32[]{:S(2)}) %collective-permute-start.7) | collective-permute-done | bytes 28704 | tf_op jit(solution)/shard_map/ppermute | solution.py:111
  27.5 0.3 middle.1
  27.8 0.5 collective-permute-start.8
  28.3 2.4 %collective-permute-start.9 = (bf16[32,512]{1,0:T(8,128)(2,1)S(1)}, bf16[32,512]{1,0:T(8,128)(2,1)S(1)}, u32[]{:S(2)}, u32[]{:S(2)}) collective-permute-start(bf16[32,512]{1,0:T(8,128)(2,1)S(1)} %get-tuple-element.81.refs_0_.own_ref), channel_id=1, source_target_pairs={{0,12},{2,14},{4,8},{6,10},{8,4},{10,6},{12,0},{14,2},{1,13},{3,15... | collective-permute-start | bytes 98312 | tf_op jit(solution)/shard_map/ppermute | solution.py:401
  31.3 2.8 %fetch_up.1.up_ref.refs_4_ = bf16[1792,1792]{1,0:T(8,128)(2,1)S(1)} custom-call(bf16[32,512]{1,0:T(8,128)(2,1)S(1)} %get-tuple-element.81.refs_0_.own_ref, bf16[1792,1792]{1,0:T(8,128)(2,1)} %refs_1_.6), custom_call_target="tpu_custom_call" | custom-call | bytes 12845056 | tf_op jit(solution)/shard_map/fetch_up/pallas_call | solution.py:148
  34.2 0.7 %residual.1 = (bf16[32,448]{1,0:T(8,128)(2,1)}, f32[4,1]{1,0:T(4,128)S(1)}) custom-call(f32[32,448]{1,0:T(8,128)S(1)} %get-tuple-element.79.mid_ref, s32[1,1]{1,0:T(1,128)} %bitcast.20.length_ref), custom_call_target="tpu_custom_call" | custom-call | bytes 86036 | tf_op jit(solution)/shard_map/residual/pallas_call | solution.py:117
  35.0 1.2 %inner_products.1 = (f32[32,1792]{1,0:T(8,128)S(1)}, f32[32,1792]{1,0:T(8,128)S(1)}) custom-call(bf16[2,32,512]{2,1,0:T(8,128)(2,1)S(1)} %pick.1.mine_ref.refs_5_, bf16[1792,1792]{1,0:T(8,128)(2,1)S(1)} %get-tuple-element.82.gate_ref.refs_3_, bf16[1792,1792]{1,0:T(8,128)(2,1)S(1)} %fetch_up.1.up_ref.refs_4_), custom_call_target="tpu_custom_call" | custom-call | flops 205520896 | bytes 13369344 | tf_op jit(solution)/shard_map/inner_products/pallas_call | solution.py:117
  36.2 0.6 %gate_up_0.1 = (f32[32,1664]{1,0:T(8,128)S(1)}, bf16[32,1664]{1,0:T(8,128)(2,1)S(1)}) custom-call(bf16[2,32,512]{2,1,0:T(8,128)(2,1)S(1)} %collective-permute-done.10.refs_0_, f32[32,1792]{1,0:T(8,128)S(1)} %get-tuple-element.84.refs_1_, f32[32,1792]{1,0:T(8,128)S(1)} %get-tuple-element.85.refs_2_, ...), custom_call_target="tpu_custom_call" | custom-call | flops 102760448 | bytes 13754368 | tf_op jit(solution)/shard_map/gate_up_0/pallas_call | solution.py:117
  36.8 1.5 %collective-permute-start.12 = (bf16[32,1664]{1,0:T(8,128)(2,1)S(1)}, bf16[32,1664]{1,0:T(8,128)(2,1)S(1)}, u32[]{:S(2)}, u32[]{:S(2)}) collective-permute-start(bf16[32,1664]{1,0:T(8,128)(2,1)S(1)} %get-tuple-element.89), channel_id=1, source_target_pairs={{0,2},{2,0},{1,3},{3,1},{4,6},{6,4},{5,7},{7,5},{8,10},{10,8},{9,1... | collective-permute-start | bytes 319496 | tf_op jit(solution)/shard_map/ppermute | solution.py:111
  38.3 0.4 gate_up_1.1
  38.7 0.7 %collective-permute-start.13 = (bf16[32,1024]{1,0:T(8,128)(2,1)S(1)}, bf16[32,1024]{1,0:T(8,128)(2,1)S(1)}, u32[]{:S(2)}, u32[]{:S(2)}) collective-permute-start(bf16[32,1024]{1,0:T(8,128)(2,1)S(1)} %get-tuple-element.91), channel_id=1, source_target_pairs={{0,2},{2,0},{1,3},{3,1},{4,6},{6,4},{5,7},{7,5},{8,10},{10,8},{9,1... | collective-permute-start | bytes 196616 | tf_op jit(solution)/shard_map/ppermute | solution.py:111
  39.4 0.4 gate_up_2.1
  39.8 1.5 %collective-permute-start.11 = (bf16[32,1024]{1,0:T(8,128)(2,1)S(1)}, bf16[32,1024]{1,0:T(8,128)(2,1)S(1)}, u32[]{:S(2)}, u32[]{:S(2)}) collective-permute-start(bf16[32,1024]{1,0:T(8,128)(2,1)S(1)} %get-tuple-element.87.refs_0_), channel_id=1, source_target_pairs={{0,2},{2,0},{1,3},{3,1},{4,6},{6,4},{5,7},{7,5},{8,10},{10,8},{9,1... | collective-permute-start | bytes 196616 | tf_op jit(solution)/shard_map/ppermute | solution.py:111
  41.3 2.8 %fetch_down.1.weight_ref = bf16[1792,1792]{1,0:T(8,128)(2,1)S(1)} custom-call(bf16[32,1024]{1,0:T(8,128)(2,1)S(1)} %get-tuple-element.87.refs_0_, bf16[1792,1792]{1,0:T(8,128)(2,1)} %refs_1_.7), custom_call_target="tpu_custom_call" | custom-call | bytes 12845056 | tf_op jit(solution)/shard_map/fetch_down/pallas_call | solution.py:148
  44.2 0.7 %down_first.1.part_ref = f32[32,1792]{1,0:T(8,128)S(1)} custom-call(f32[32,1664]{1,0:T(8,128)S(1)} %get-tuple-element.88.own_ref.first_ref, bf16[32,1664]{1,0:T(8,128)(2,1)S(1)} %collective-permute-done.12.other_ref.first_other_ref, bf16[1792,1792]{1,0:T(8,128)(2,1)S(1)} %fetch_down.1.weight_ref), custom_call_target="tpu_custom_call" | custom-call | flops 102760448 | bytes 6971392 | tf_op jit(solution)/shard_map/down_first/pallas_call | solution.py:117
  44.9 0.5 %down_next.1.part_ref = f32[32,1792]{1,0:T(8,128)S(1)} custom-call(f32[32,1024]{1,0:T(8,128)S(1)} %get-tuple-element.90.own_ref, bf16[32,1024]{1,0:T(8,128)(2,1)S(1)} %collective-permute-done.13.other_ref, f32[32,1664]{1,0:T(8,128)S(1)} %get-tuple-element.88.own_ref.first_ref, bf16[32,1664]{1,0:T(8,128)(2,1)S(1)} %collective-permute-done.12.other_ref.first_other_ref, ...), custom_call_target="tpu_custom_call" | custom-call | flops 102760448 | bytes 7397376 | tf_op jit(solution)/shard_map/down_next/pallas_call | solution.py:117
  45.4 0.5 down_last.1
  46.1 1.2 %collective-permute-done.14.back_ref = bf16[16,1792]{1,0:T(8,128)(2,1)S(1)} collective-permute-done((bf16[16,1792]{1,0:T(8,128)(2,1)S(1)}, bf16[16,1792]{1,0:T(8,128)(2,1)S(1)}, u32[]{:S(2)}, u32[]{:S(2)}) %collective-permute-start.14) | collective-permute-done | bytes 57376 | tf_op jit(solution)/shard_map/ppermute | solution.py:111
  47.3 1.6 %collective-permute-start.17 = (bf16[4,1792]{1,0:T(4,128)(2,1)S(1)}, bf16[4,1792]{1,0:T(4,128)(2,1)S(1)}, u32[]{:S(2)}, u32[]{:S(2)}) collective-permute-start(bf16[4,1792]{1,0:T(4,128)(2,1)S(1)} %get-tuple-element.97), channel_id=1, source_target_pairs={{0,12},{4,8},{8,4},{12,0},{1,13},{5,9},{9,5},{13,1},{2,14},{6,10},... | collective-permute-start | bytes 43016 | tf_op jit(solution)/shard_map/ppermute | solution.py:111
  48.9 0.7 %collective-permute-start.16 = (bf16[4,1792]{1,0:T(4,128)(2,1)S(1)}, bf16[4,1792]{1,0:T(4,128)(2,1)S(1)}, u32[]{:S(2)}, u32[]{:S(2)}) collective-permute-start(bf16[4,1792]{1,0:T(4,128)(2,1)S(1)} %get-tuple-element.96), channel_id=1, source_target_pairs={{0,8},{4,12},{8,0},{12,4},{1,9},{5,13},{9,1},{13,5},{2,10},{6,14},... | collective-permute-start | bytes 43016 | tf_op jit(solution)/shard_map/ppermute | solution.py:111
  49.6 2.2 %collective-permute-start.15 = (bf16[4,1792]{1,0:T(4,128)(2,1)S(1)}, bf16[4,1792]{1,0:T(4,128)(2,1)S(1)}, u32[]{:S(2)}, u32[]{:S(2)}) collective-permute-start(bf16[4,1792]{1,0:T(4,128)(2,1)S(1)} %get-tuple-element.95), channel_id=1, source_target_pairs={{0,4},{4,0},{8,12},{12,8},{1,5},{5,1},{9,13},{13,9},{2,6},{6,2},{1... | collective-permute-start | bytes 43016 | tf_op jit(solution)/shard_map/ppermute | solution.py:111
  51.8 0.1 reduce
  51.9 1.0 %collective-permute-done.17 = bf16[4,1792]{1,0:T(4,128)(2,1)S(1)} collective-permute-done((bf16[4,1792]{1,0:T(4,128)(2,1)S(1)}, bf16[4,1792]{1,0:T(4,128)(2,1)S(1)}, u32[]{:S(2)}, u32[]{:S(2)}) %collective-permute-start.17) | collective-permute-done | bytes 14368 | tf_op jit(solution)/shard_map/ppermute | solution.py:111
  52.9 0.7 %collective-permute-done.16 = bf16[4,1792]{1,0:T(4,128)(2,1)S(1)} collective-permute-done((bf16[4,1792]{1,0:T(4,128)(2,1)S(1)}, bf16[4,1792]{1,0:T(4,128)(2,1)S(1)}, u32[]{:S(2)}, u32[]{:S(2)}) %collective-permute-start.16) | collective-permute-done | bytes 14368 | tf_op jit(solution)/shard_map/ppermute | solution.py:111
  53.6 0.7 %multiply_convert_fusion = bf16[4,1792]{1,0:T(4,128)(2,1)} fusion(bf16[4,1792]{1,0:T(4,128)(2,1)S(1)} %collective-permute-done.17, bf16[4,1792]{1,0:T(4,128)(2,1)S(1)} %collective-permute-done.16, f32[4,1792]{1,0:T(4,128)S(1)} %get-tuple-element.94, bf16[4,1792]{1,0:T(4,128)(2,1)S(1)} %collective-permute-done.15, f32[4]{0:T(128)S(1)} %reduce), kind=kLoop, calls=%fused_computation.15 | loop fusion | flops 57344 | bytes 86032 | tf_op jit(solution)/shard_map/convert_element_type | solution.py:578
  (30 shorter events, 0.4 us)
Async XLA Ops:
  0.6 10.0 %copy-start = (bf16[1536,4,256]{2,1,0:T(4,128)(2,1)S(1)}, bf16[1536,4,256]{2,1,0:T(4,128)(2,1)}, u32[]{:S(2)}) copy-start(bf16[1536,4,256]{2,1,0:T(4,128)(2,1)} %param.13) | copy-start | bytes 9437188
  0.6 7.0 %collective-permute-start.2 = (bf16[4,8,256]{2,1,0:T(8,128)(2,1)}, bf16[4,8,256]{2,1,0:T(8,128)(2,1)S(1)}, u32[]{:S(2)}, u32[]{:S(2)}) collective-permute-start(bf16[4,8,256]{2,1,0:T(8,128)(2,1)} %refs_0_.1), channel_id=1, source_target_pairs={{0,12},{4,8},{8,4},{12,0},{1,13},{5,9},{9,5},{13,1},{2,14},{6,10},... | collective-permute-start | bytes 49160 | tf_op jit(solution)/shard_map/ppermute | solution.py:111
  5.8 4.8 %collective-permute-start = (bf16[4,8,256]{2,1,0:T(8,128)(2,1)}, bf16[4,8,256]{2,1,0:T(8,128)(2,1)S(1)}, u32[]{:S(2)}, u32[]{:S(2)}) collective-permute-start(bf16[4,8,256]{2,1,0:T(8,128)(2,1)} %refs_0_.1), channel_id=1, source_target_pairs={{0,8},{4,12},{8,0},{12,4},{1,9},{5,13},{9,1},{13,5},{2,10},{6,14},... | collective-permute-start | bytes 49160 | tf_op jit(solution)/shard_map/ppermute | solution.py:111
  5.8 3.9 %collective-permute-start.1 = (bf16[4,8,256]{2,1,0:T(8,128)(2,1)}, bf16[4,8,256]{2,1,0:T(8,128)(2,1)S(1)}, u32[]{:S(2)}, u32[]{:S(2)}) collective-permute-start(bf16[4,8,256]{2,1,0:T(8,128)(2,1)} %refs_0_.1), channel_id=1, source_target_pairs={{0,4},{4,0},{8,12},{12,8},{1,5},{5,1},{9,13},{13,9},{2,6},{6,2},{1... | collective-permute-start | bytes 49160 | tf_op jit(solution)/shard_map/ppermute | solution.py:111
  6.4 5.7 %copy-start.1 = (bf16[1536,4,256]{2,1,0:T(4,128)(2,1)S(1)}, bf16[1536,4,256]{2,1,0:T(4,128)(2,1)}, u32[]{:S(2)}) copy-start(bf16[1536,4,256]{2,1,0:T(4,128)(2,1)} %param.14) | copy-start | bytes 9437188
  13.1 7.2 %collective-permute-start.3 = (bf16[144,256]{1,0:T(8,128)(2,1)S(1)}, bf16[144,256]{1,0:T(8,128)(2,1)S(1)}, u32[]{:S(2)}, u32[]{:S(2)}) collective-permute-start(bf16[144,256]{1,0:T(8,128)(2,1)S(1)} %pad_maximum_fusion.refs_0_), channel_id=1, source_target_pairs={{0,12},{4,8},{8,4},{12,0},{1,13},{5,9},{9,5},{13,1},{2,14},{6,10},... | collective-permute-start | bytes 221192 | tf_op jit(solution)/shard_map/ppermute | solution.py:111
  14.7 6.8 %collective-permute-start.4 = (bf16[144,256]{1,0:T(8,128)(2,1)S(1)}, bf16[144,256]{1,0:T(8,128)(2,1)S(1)}, u32[]{:S(2)}, u32[]{:S(2)}) collective-permute-start(bf16[144,256]{1,0:T(8,128)(2,1)S(1)} %pad_maximum_fusion.refs_0_), channel_id=1, source_target_pairs={{0,8},{4,12},{8,0},{12,4},{1,9},{5,13},{9,1},{13,5},{2,10},{6,14},... | collective-permute-start | bytes 221192 | tf_op jit(solution)/shard_map/ppermute | solution.py:111
  15.3 6.2 %collective-permute-start.5 = (bf16[144,256]{1,0:T(8,128)(2,1)S(1)}, bf16[144,256]{1,0:T(8,128)(2,1)S(1)}, u32[]{:S(2)}, u32[]{:S(2)}) collective-permute-start(bf16[144,256]{1,0:T(8,128)(2,1)S(1)} %pad_maximum_fusion.refs_0_), channel_id=1, source_target_pairs={{0,4},{4,0},{8,12},{12,8},{1,5},{5,1},{9,13},{13,9},{2,6},{6,2},{1... | collective-permute-start | bytes 221192 | tf_op jit(solution)/shard_map/ppermute | solution.py:111
  21.7 1.3 %collective-permute-start.6 = (bf16[16,2048]{1,0:T(8,128)(2,1)S(1)}, bf16[16,2048]{1,0:T(8,128)(2,1)S(1)}, u32[]{:S(2)}, u32[]{:S(2)}) collective-permute-start(bf16[16,2048]{1,0:T(8,128)(2,1)S(1)} %get-tuple-element.72.own_ref), channel_id=1, source_target_pairs={{0,1},{1,0},{2,3},{3,2},{4,5},{5,4},{6,7},{7,6},{8,9},{9,8},{10,11... | collective-permute-start | bytes 196616 | tf_op jit(solution)/shard_map/ppermute | solution.py:111
  23.6 3.9 %collective-permute-start.7 = (bf16[32,448]{1,0:T(8,128)(2,1)S(1)}, bf16[32,448]{1,0:T(8,128)(2,1)S(1)}, u32[]{:S(2)}, u32[]{:S(2)}) collective-permute-start(bf16[32,448]{1,0:T(8,128)(2,1)S(1)} %get-tuple-element.77.refs_0_.own_ref), channel_id=1, source_target_pairs={{0,2},{2,0},{1,3},{3,1},{4,6},{6,4},{5,7},{7,5},{8,10},{10,8},{9,1... | collective-permute-start | bytes 86024 | tf_op jit(solution)/shard_map/ppermute | solution.py:111
  27.8 7.1 %collective-permute-start.8 = (bf16[32,512]{1,0:T(8,128)(2,1)S(1)}, bf16[32,512]{1,0:T(8,128)(2,1)S(1)}, u32[]{:S(2)}, u32[]{:S(2)}) collective-permute-start(bf16[32,512]{1,0:T(8,128)(2,1)S(1)} %get-tuple-element.81.refs_0_.own_ref), channel_id=1, source_target_pairs={{0,8},{2,4},{4,12},{6,0},{8,14},{10,2},{12,10},{14,6},{1,9},{3,5},... | collective-permute-start | bytes 98312 | tf_op jit(solution)/shard_map/ppermute | solution.py:400
  28.3 6.6 %collective-permute-start.9 = (bf16[32,512]{1,0:T(8,128)(2,1)S(1)}, bf16[32,512]{1,0:T(8,128)(2,1)S(1)}, u32[]{:S(2)}, u32[]{:S(2)}) collective-permute-start(bf16[32,512]{1,0:T(8,128)(2,1)S(1)} %get-tuple-element.81.refs_0_.own_ref), channel_id=1, source_target_pairs={{0,12},{2,14},{4,8},{6,10},{8,4},{10,6},{12,0},{14,2},{1,13},{3,15... | collective-permute-start | bytes 98312 | tf_op jit(solution)/shard_map/ppermute | solution.py:401
  34.9 1.3 %collective-permute-start.10 = (bf16[2,32,512]{2,1,0:T(8,128)(2,1)S(1)}, bf16[2,32,512]{2,1,0:T(8,128)(2,1)S(1)}, u32[]{:S(2)}, u32[]{:S(2)}) collective-permute-start(bf16[2,32,512]{2,1,0:T(8,128)(2,1)S(1)} %pick.1.mine_ref.refs_5_), channel_id=1, source_target_pairs={{0,1},{1,0},{2,3},{3,2},{4,5},{5,4},{6,7},{7,6},{8,9},{9,8},{10,11... | collective-permute-start | bytes 196616 | tf_op jit(solution)/shard_map/ppermute | solution.py:111
  36.8 7.3 %collective-permute-start.12 = (bf16[32,1664]{1,0:T(8,128)(2,1)S(1)}, bf16[32,1664]{1,0:T(8,128)(2,1)S(1)}, u32[]{:S(2)}, u32[]{:S(2)}) collective-permute-start(bf16[32,1664]{1,0:T(8,128)(2,1)S(1)} %get-tuple-element.89), channel_id=1, source_target_pairs={{0,2},{2,0},{1,3},{3,1},{4,6},{6,4},{5,7},{7,5},{8,10},{10,8},{9,1... | collective-permute-start | bytes 319496 | tf_op jit(solution)/shard_map/ppermute | solution.py:111
  38.7 6.1 %collective-permute-start.13 = (bf16[32,1024]{1,0:T(8,128)(2,1)S(1)}, bf16[32,1024]{1,0:T(8,128)(2,1)S(1)}, u32[]{:S(2)}, u32[]{:S(2)}) collective-permute-start(bf16[32,1024]{1,0:T(8,128)(2,1)S(1)} %get-tuple-element.91), channel_id=1, source_target_pairs={{0,2},{2,0},{1,3},{3,1},{4,6},{6,4},{5,7},{7,5},{8,10},{10,8},{9,1... | collective-permute-start | bytes 196616 | tf_op jit(solution)/shard_map/ppermute | solution.py:111
  39.8 5.6 %collective-permute-start.11 = (bf16[32,1024]{1,0:T(8,128)(2,1)S(1)}, bf16[32,1024]{1,0:T(8,128)(2,1)S(1)}, u32[]{:S(2)}, u32[]{:S(2)}) collective-permute-start(bf16[32,1024]{1,0:T(8,128)(2,1)S(1)} %get-tuple-element.87.refs_0_), channel_id=1, source_target_pairs={{0,2},{2,0},{1,3},{3,1},{4,6},{6,4},{5,7},{7,5},{8,10},{10,8},{9,1... | collective-permute-start | bytes 196616 | tf_op jit(solution)/shard_map/ppermute | solution.py:111
  46.0 1.3 %collective-permute-start.14 = (bf16[16,1792]{1,0:T(8,128)(2,1)S(1)}, bf16[16,1792]{1,0:T(8,128)(2,1)S(1)}, u32[]{:S(2)}, u32[]{:S(2)}) collective-permute-start(bf16[16,1792]{1,0:T(8,128)(2,1)S(1)} %get-tuple-element.93), channel_id=1, source_target_pairs={{0,1},{1,0},{2,3},{3,2},{4,5},{5,4},{6,7},{7,6},{8,9},{9,8},{10,11... | collective-permute-start | bytes 172040 | tf_op jit(solution)/shard_map/ppermute | solution.py:111
  47.3 5.6 %collective-permute-start.17 = (bf16[4,1792]{1,0:T(4,128)(2,1)S(1)}, bf16[4,1792]{1,0:T(4,128)(2,1)S(1)}, u32[]{:S(2)}, u32[]{:S(2)}) collective-permute-start(bf16[4,1792]{1,0:T(4,128)(2,1)S(1)} %get-tuple-element.97), channel_id=1, source_target_pairs={{0,12},{4,8},{8,4},{12,0},{1,13},{5,9},{9,5},{13,1},{2,14},{6,10},... | collective-permute-start | bytes 43016 | tf_op jit(solution)/shard_map/ppermute | solution.py:111
  48.9 4.7 %collective-permute-start.16 = (bf16[4,1792]{1,0:T(4,128)(2,1)S(1)}, bf16[4,1792]{1,0:T(4,128)(2,1)S(1)}, u32[]{:S(2)}, u32[]{:S(2)}) collective-permute-start(bf16[4,1792]{1,0:T(4,128)(2,1)S(1)} %get-tuple-element.96), channel_id=1, source_target_pairs={{0,8},{4,12},{8,0},{12,4},{1,9},{5,13},{9,1},{13,5},{2,10},{6,14},... | collective-permute-start | bytes 43016 | tf_op jit(solution)/shard_map/ppermute | solution.py:111
  49.6 4.1 %collective-permute-start.15 = (bf16[4,1792]{1,0:T(4,128)(2,1)S(1)}, bf16[4,1792]{1,0:T(4,128)(2,1)S(1)}, u32[]{:S(2)}, u32[]{:S(2)}) collective-permute-start(bf16[4,1792]{1,0:T(4,128)(2,1)S(1)} %get-tuple-element.95), channel_id=1, source_target_pairs={{0,4},{4,0},{8,12},{12,8},{1,5},{5,1},{9,13},{13,9},{2,6},{6,2},{1... | collective-permute-start | bytes 43016 | tf_op jit(solution)/shard_map/ppermute | solution.py:111
